TPU v7x, 32 devices: a whole 2x2x4 slice. The times are simulated.
32 devices in a mesh: grp: 2 (over y), lon: 8 (over z, x), lat: 2 (over core).
Axes of the slice: x: 2, y: 2, z: 4, core: 2. Of those that a mesh axis runs over, the one named last changes fastest.
Arguments:
- right_side: bfloat16 [64, 32768], P(None, ('grp', 'lon', 'lat')), parts along dimension 1, may hold values from -21 to 21
- stiffness_blocks: bfloat16 [768, 128, 128], P(('grp', 'lon', 'lat')), parts along dimension 0, may hold values from -0.21875 to 0.21875
- block_pattern: int32 [768, 2], P(('grp', 'lon', 'lat')), parts along dimension 0, may hold values from 0 to 7
- reaction: float32 [32768], P(('grp', 'lon', 'lat')), parts along dimension 0, may hold values from 1 to 4
- lumped_mass: float32 [32768], P(('grp', 'lon', 'lat')), parts along dimension 0, may hold values from 0.5 to 2
- obs_precision: float32 [32768], P(('grp', 'lon', 'lat')), parts along dimension 0, may hold values from 0.5 to 2
- coupling: bfloat16 [4096, 128], P(('grp', 'lon', 'lat')), parts along dimension 0, may hold values from -0.375 to 0.375
- east_rows: int32 [32, 128], P(('grp', 'lon', 'lat')), parts along dimension 0, may hold values from 0 to 1023
- west_rows: int32 [32, 128], P(('grp', 'lon', 'lat')), parts along dimension 0, may hold values from 0 to 1023
- iface_count: int32 [32], P(('grp', 'lon', 'lat')), parts along dimension 0, may hold values from 32 to 128, as said below
- node_count: int32 [32], P(('grp', 'lon', 'lat')), parts along dimension 0, may hold values from 512 to 1024, as said below
- deflation: bfloat16 [64, 32768], P(None, ('grp', 'lon', 'lat')), parts along dimension 1, may hold values from -0.1875 to 0.1875
- coarse_inverse: bfloat16 [2048, 1024], P(('grp', 'lon', 'lat')), parts along dimension 0, may hold values from -1 to 7, as said below
Outputs:
- solution: float32 [64, 32768], P(None, ('grp', 'lon', 'lat')), parts along dimension 1
There are 2 independent parts, one for each index of `grp`. A program takes and returns all parts, laid end to end along the dimension named above; each array names one. Nothing has to cross between parts.
Inputs may be any that keep to these rules, and one draw needn't show every extreme that they name: `iface_count`: some subdomain uses all 128 interface slots. `node_count`: some subdomain has all of its nodes live. `coarse_inverse`: symmetric positive definite.
All inputs are finite; a program needn't handle non-finite values.
Results may differ from a plain program's by a relative error of at most 0.0046.
Values may be sent and summed in bfloat16 or wider, within the bound.
No kernel may reach another device: no remote copies, remote signals or barrier semaphores. Data moves between devices by JAX's collectives and lax.ppermute only.
A program may use at most 64 MiB of HBM per device.

v0:
```python
import jax
import jax.numpy as jnp
from jax import lax
from jax.sharding import PartitionSpec as P

ITERS = 2


def from_behind(array, axis, by):
    size = lax.axis_size(axis)
    return lax.ppermute(array, axis, [(i, (i + by) % size) for i in range(size)])


def body(
    right_side,
    stiffness_blocks,
    block_pattern,
    reaction,
    lumped_mass,
    obs_precision,
    coupling,
    east_rows,
    west_rows,
    iface_count,
    node_count,
    deflation,
    coarse_inverse,
):
    samples, per_domain = right_side.shape
    block = stiffness_blocks.shape[1]
    nblocks = per_domain // block
    slots = coupling.shape[0]
    active = (jnp.arange(per_domain) < node_count[0]).astype(jnp.float32)
    live = jnp.arange(slots) < iface_count[0]
    coupler = jnp.where(live[:, None] & live[None, :], coupling, jnp.zeros_like(coupling))
    row_onehot = (block_pattern[:, 0:1] == jnp.arange(nblocks)[None, :]).astype(jnp.float32)
    col_onehot = (block_pattern[:, 1:2] == jnp.arange(nblocks)[None, :]).astype(jnp.float32)
    east_index = east_rows[0]
    west_index = west_rows[0]
    jacobi = 1.0 / (obs_precision + reaction * reaction / lumped_mass)
    contract_last = (((1,), (1,)), ((), ()))

    def stiffness(field):
        rounded = field.astype(jnp.bfloat16)
        arrived = from_behind(jnp.take(rounded, west_index, axis=1), "lon", -1)
        outgoing = jnp.dot(
            jnp.take(rounded, east_index, axis=1), coupler, preferred_element_type=jnp.float32
        )
        incoming = from_behind(outgoing.astype(jnp.bfloat16), "lon", 1).astype(outgoing.dtype)
        shaped = rounded.reshape(samples, nblocks, block)
        from_cols = jnp.take(shaped, block_pattern[:, 1], axis=1)
        from_rows = jnp.take(shaped, block_pattern[:, 0], axis=1)
        forward = jnp.einsum(
            "skj,kij->ski", from_cols, stiffness_blocks, preferred_element_type=jnp.float32
        )
        backward = jnp.einsum(
            "ski,kij->skj", from_rows, stiffness_blocks, preferred_element_type=jnp.float32
        )
        summed = jnp.einsum("kn,ski->sni", row_onehot, forward, precision=lax.Precision.HIGHEST)
        summed = summed + jnp.einsum(
            "kn,ski->sni", col_onehot, backward, precision=lax.Precision.HIGHEST
        )
        result = reaction * field + summed.reshape(samples, per_domain)
        into_east = lax.dot_general(
            arrived, coupler, contract_last, preferred_element_type=jnp.float32
        )
        result = result.at[:, east_index].add(into_east)
        return result.at[:, west_index].add(incoming)

    def coarse_solve(coarse_local):
        gathered = lax.all_gather(coarse_local, ("lon", "lat"), axis=1, tiled=True)
        return lax.dot_general(
            gathered, coarse_inverse, contract_last, preferred_element_type=jnp.float32
        )

    def precondition(residual):
        coarse_local = lax.dot_general(
            residual.astype(jnp.bfloat16),
            deflation,
            contract_last,
            preferred_element_type=jnp.float32,
        ).astype(jnp.bfloat16)
        coarse_fix = coarse_solve(coarse_local).astype(jnp.bfloat16)
        spread = jnp.dot(coarse_fix, deflation, preferred_element_type=jnp.float32)
        return active * (jacobi * residual + spread)

    def local_dot(first, second):
        return jnp.sum(first * second, axis=1)

    def reduce_products(values):
        return lax.psum(values, ("lon", "lat"))

    residual = active * right_side.astype(jnp.float32)
    solution = jnp.zeros_like(residual)
    smoothed = precondition(residual)
    direction = smoothed
    norm_now = reduce_products(local_dot(residual, smoothed))
    for iteration in range(ITERS):
        inner = stiffness(active * direction) / lumped_mass
        image = active * (stiffness(inner) + obs_precision * direction)
        step_size = norm_now / reduce_products(local_dot(direction, image))
        solution = solution + step_size[:, None] * direction
        residual = residual - step_size[:, None] * image
        if iteration + 1 < ITERS:
            smoothed = precondition(residual)
            norm_next = reduce_products(local_dot(residual, smoothed))
            direction = smoothed + (norm_next / norm_now)[:, None] * direction
            norm_now = norm_next
    return solution


def solution(mesh):
    placed = (
        P(None, ("grp", "lon", "lat")),
        P(("grp", "lon", "lat"), None, None),
        P(("grp", "lon", "lat"), None),
        P(("grp", "lon", "lat")),
        P(("grp", "lon", "lat")),
        P(("grp", "lon", "lat")),
        P(("grp", "lon", "lat"), None),
        P(("grp", "lon", "lat"), None),
        P(("grp", "lon", "lat"), None),
        P(("grp", "lon", "lat")),
        P(("grp", "lon", "lat")),
        P(None, ("grp", "lon", "lat")),
        P(("grp", "lon", "lat"), None),
    )
    return jax.shard_map(
        body, mesh=mesh, in_specs=placed, out_specs=P(None, ("grp", "lon", "lat")), check_vma=False
    )
```

profile of v0, /device:TPU:0, one launch (start us, length us, event | category | flops | bytes accessed | tf_op | source)
XLA Modules:
  0.0 201.7 jit_solution(13160157740179570907)
XLA Ops:
  0.0 0.7 compare_select_fusion.1
  1.4 1.2 convolution_convert_fusion.5
  2.8 23.9 %all_gather.6 = bf16[64,1024]{0,1:T(8,128)(2,1)S(1)} all-gather(bf16[64,64]{0,1:T(8,128)(2,1)S(1)} %copy.70), channel_id=1, replica_groups=mesh['grp'=2,'lon'=8,'lat'=2] {'lon','lat'}, dimensions={1}, use_global_device_ids=true | all-gather | bytes 139264 | tf_op jit(solution)/shard_map/all_gather | solution.py:71
  30.4 1.6 collective-permute-start.1
  34.0 0.8 fusion.12
  35.2 0.8 convolution_add_fusion.4
  37.2 1.5 scatter_fusion
  38.7 1.5 scatter_fusion.1
  41.8 0.7 gather_fusion.6
  43.9 0.8 fusion.9
  45.1 0.8 convolution_add_fusion.3
  46.6 4.7 %collective-permute-start.2 = (bf16[64,128]{0,1:T(8,128)(2,1)S(1)}, bf16[64,128]{0,1:T(8,128)(2,1)S(1)}, u32[]{:S(2)}, u32[]{:S(2)}) collective-permute-start(bf16[64,128]{0,1:T(8,128)(2,1)S(1)} %select_bitcast_fusion.2), channel_id=1, source_target_pairs={{0,14},{2,0},{4,2},{6,4},{8,6},{10,8},{12,10},{14,12},{1,15},{3,1}... | collective-permute-start | bytes 49160 | tf_op jit(solution)/shard_map/ppermute | solution.py:11
  51.4 1.4 collective-permute-done.3
  53.2 1.5 scatter_fusion.2
  54.6 1.5 scatter_fusion.3
  56.5 31.9 %all-reduce = (f32[64]{0:T(128)S(1)}, f32[64]{0:T(128)S(1)}) all-reduce(f32[64]{0:T(128)S(1)} %get-tuple-element.8, f32[64]{0:T(128)S(1)} %get-tuple-element.6), channel_id=1, replica_groups=mesh['grp'=2,'lon'=8,'lat'=2] {'lon','lat'}, use_global_device_ids=true, to_apply=%region_1.2 | all-reduce | flops 128 | bytes 1024 | tf_op jit(solution)/shard_map/psum | solution.py:91
  88.7 17.8 %all_gather.7 = bf16[64,1024]{0,1:T(8,128)(2,1)S(1)} all-gather(bf16[64,64]{0,1:T(8,128)(2,1)S(1)} %copy.91), channel_id=1, replica_groups=mesh['grp'=2,'lon'=8,'lat'=2] {'lon','lat'}, dimensions={1}, use_global_device_ids=true | all-gather | bytes 139264 | tf_op jit(solution)/shard_map/all_gather | solution.py:71
  107.1 31.7 %psum.30 = f32[64]{0:T(128)S(1)} all-reduce(f32[64]{0:T(128)S(1)} %get-tuple-element.23), channel_id=1, replica_groups=mesh['grp'=2,'lon'=8,'lat'=2] {'lon','lat'}, use_global_device_ids=true, to_apply=%region_9.12 | all-reduce | flops 64 | bytes 512 | tf_op jit(solution)/shard_map/psum | solution.py:91
  142.5 0.8 fusion.6
  143.9 0.8 convolution_add_fusion.1
  145.1 4.8 %collective-permute-start.4 = (bf16[64,128]{0,1:T(8,128)(2,1)S(1)}, bf16[64,128]{0,1:T(8,128)(2,1)S(1)}, u32[]{:S(2)}, u32[]{:S(2)}) collective-permute-start(bf16[64,128]{0,1:T(8,128)(2,1)S(1)} %select_bitcast_fusion.1), channel_id=1, source_target_pairs={{0,14},{2,0},{4,2},{6,4},{8,6},{10,8},{12,10},{14,12},{1,15},{3,1}... | collective-permute-start | bytes 49160 | tf_op jit(solution)/shard_map/ppermute | solution.py:11
  150.5 1.0 collective-permute-done.4
  151.7 1.5 scatter_fusion.4
  153.2 1.5 scatter_fusion.5
  158.4 0.8 fusion.3
  159.6 0.8 convolution_add_fusion
  161.1 5.1 %collective-permute-start.6 = (bf16[64,128]{0,1:T(8,128)(2,1)S(1)}, bf16[64,128]{0,1:T(8,128)(2,1)S(1)}, u32[]{:S(2)}, u32[]{:S(2)}) collective-permute-start(bf16[64,128]{0,1:T(8,128)(2,1)S(1)} %select_bitcast_fusion), channel_id=1, source_target_pairs={{0,14},{2,0},{4,2},{6,4},{8,6},{10,8},{12,10},{14,12},{1,15},{3,1}... | collective-permute-start | bytes 49160 | tf_op jit(solution)/shard_map/ppermute | solution.py:11
  166.2 1.4 collective-permute-done.7
  168.0 1.5 scatter_fusion.6
  169.4 1.5 scatter_fusion.7
  171.2 29.7 %psum.31 = f32[64]{0:T(128)S(1)} all-reduce(f32[64]{0:T(128)S(1)} %multiply_reduce_fusion), channel_id=1, replica_groups=mesh['grp'=2,'lon'=8,'lat'=2] {'lon','lat'}, use_global_device_ids=true, to_apply=%region_15.18 | all-reduce | flops 64 | bytes 512 | tf_op jit(solution)/shard_map/psum | solution.py:91
  200.9 0.8 multiply_add_fusion
  (120 shorter events, 23.2 us)
Async XLA Ops:
  0.0 33.3 %copy-start = (bf16[24,128,128]{2,1,0:T(8,128)(2,1)S(1)}, bf16[24,128,128]{2,1,0:T(8,128)(2,1)}, u32[]{:S(2)}) copy-start(bf16[24,128,128]{2,1,0:T(8,128)(2,1)} %param.18) | copy-start | bytes 2359300
  0.0 0.7 copy-start.10
  1.4 25.3 %copy-start.4 = (bf16[64,1024]{1,0:T(8,128)(2,1)S(1)}, bf16[64,1024]{1,0:T(8,128)(2,1)}, u32[]{:S(2)}) copy-start(bf16[64,1024]{1,0:T(8,128)(2,1)} %param.29) | copy-start | bytes 393220
  2.7 24.0 %copy-start.5 = (f32[1024]{0:T(1024)S(1)}, f32[1024]{0:T(1024)}, u32[]{:S(2)}) copy-start(f32[1024]{0:T(1024)} %param.21) | copy-start | bytes 12292
  2.7 24.0 %copy-start.6 = (f32[1024]{0:T(1024)S(1)}, f32[1024]{0:T(1024)}, u32[]{:S(2)}) copy-start(f32[1024]{0:T(1024)} %param.20) | copy-start | bytes 12292
  2.7 24.0 %copy-start.7 = (f32[1024]{0:T(1024)S(1)}, f32[1024]{0:T(1024)}, u32[]{:S(2)}) copy-start(f32[1024]{0:T(1024)} %param.22) | copy-start | bytes 12292
  2.7 24.0 %copy-start.1 = (bf16[64,1024]{1,0:T(8,128)(2,1)S(1)}, bf16[64,1024]{1,0:T(8,128)(2,1)}, u32[]{:S(2)}) copy-start(bf16[64,1024]{1,0:T(8,128)(2,1)} %param.17) | copy-start | bytes 393220
  2.8 24.0 %copy-start.2 = (bf16[64,1024]{1,0:T(8,128)(2,1)S(1)}, bf16[64,1024]{1,0:T(8,128)(2,1)}, u32[]{:S(2)}) copy-start(bf16[64,1024]{1,0:T(8,128)(2,1)} %param.28) | copy-start | bytes 393220
  28.0 0.7 copy-start.9
  28.1 8.8 %collective-permute-start = (bf16[64,128]{0,1:T(8,128)(2,1)S(1)}, bf16[64,128]{0,1:T(8,128)(2,1)S(1)}, u32[]{:S(2)}, u32[]{:S(2)}) collective-permute-start(bf16[64,128]{0,1:T(8,128)(2,1)S(1)} %select_bitcast_fusion.3), channel_id=1, source_target_pairs={{0,14},{2,0},{4,2},{6,4},{8,6},{10,8},{12,10},{14,12},{1,15},{3,1}... | collective-permute-start | bytes 49160 | tf_op jit(solution)/shard_map/ppermute | solution.py:11
  29.4 0.8 copy-start.3
  30.4 1.6 copy-start.8
  30.4 6.5 %collective-permute-start.1 = (bf16[64,128]{1,0:T(8,128)(2,1)S(1)}, bf16[64,128]{1,0:T(8,128)(2,1)S(1)}, u32[]{:S(2)}, u32[]{:S(2)}) collective-permute-start(bf16[64,128]{1,0:T(8,128)(2,1)S(1)} %convolution_convert_fusion.4), channel_id=1, source_target_pairs={{0,2},{2,4},{4,6},{6,8},{8,10},{10,12},{12,14},{14,0},{1,3},{3,5},... | collective-permute-start | bytes 49160 | tf_op jit(solution)/shard_map/ppermute | solution.py:11
  46.3 6.4 %collective-permute-start.3 = (bf16[64,128]{1,0:T(8,128)(2,1)S(1)}, bf16[64,128]{1,0:T(8,128)(2,1)S(1)}, u32[]{:S(2)}, u32[]{:S(2)}) collective-permute-start(bf16[64,128]{1,0:T(8,128)(2,1)S(1)} %convolution_convert_fusion.3), channel_id=1, source_target_pairs={{0,2},{2,4},{4,6},{6,8},{8,10},{10,12},{12,14},{14,0},{1,3},{3,5},... | collective-permute-start | bytes 49160 | tf_op jit(solution)/shard_map/ppermute | solution.py:11
  46.6 6.3 %collective-permute-start.2 = (bf16[64,128]{0,1:T(8,128)(2,1)S(1)}, bf16[64,128]{0,1:T(8,128)(2,1)S(1)}, u32[]{:S(2)}, u32[]{:S(2)}) collective-permute-start(bf16[64,128]{0,1:T(8,128)(2,1)S(1)} %select_bitcast_fusion.2), channel_id=1, source_target_pairs={{0,14},{2,0},{4,2},{6,4},{8,6},{10,8},{12,10},{14,12},{1,15},{3,1}... | collective-permute-start | bytes 49160 | tf_op jit(solution)/shard_map/ppermute | solution.py:11
  143.9 6.4 %collective-permute-start.5 = (bf16[64,128]{1,0:T(8,128)(2,1)S(1)}, bf16[64,128]{1,0:T(8,128)(2,1)S(1)}, u32[]{:S(2)}, u32[]{:S(2)}) collective-permute-start(bf16[64,128]{1,0:T(8,128)(2,1)S(1)} %convolution_convert_fusion.1), channel_id=1, source_target_pairs={{0,2},{2,4},{4,6},{6,8},{8,10},{10,12},{12,14},{14,0},{1,3},{3,5},... | collective-permute-start | bytes 49160 | tf_op jit(solution)/shard_map/ppermute | solution.py:11
  145.1 6.4 %collective-permute-start.4 = (bf16[64,128]{0,1:T(8,128)(2,1)S(1)}, bf16[64,128]{0,1:T(8,128)(2,1)S(1)}, u32[]{:S(2)}, u32[]{:S(2)}) collective-permute-start(bf16[64,128]{0,1:T(8,128)(2,1)S(1)} %select_bitcast_fusion.1), channel_id=1, source_target_pairs={{0,14},{2,0},{4,2},{6,4},{8,6},{10,8},{12,10},{14,12},{1,15},{3,1}... | collective-permute-start | bytes 49160 | tf_op jit(solution)/shard_map/ppermute | solution.py:11
  160.8 6.7 %collective-permute-start.7 = (bf16[64,128]{1,0:T(8,128)(2,1)S(1)}, bf16[64,128]{1,0:T(8,128)(2,1)S(1)}, u32[]{:S(2)}, u32[]{:S(2)}) collective-permute-start(bf16[64,128]{1,0:T(8,128)(2,1)S(1)} %convolution_convert_fusion), channel_id=1, source_target_pairs={{0,2},{2,4},{4,6},{6,8},{8,10},{10,12},{12,14},{14,0},{1,3},{3,5},... | collective-permute-start | bytes 49160 | tf_op jit(solution)/shard_map/ppermute | solution.py:11
  161.1 6.7 %collective-permute-start.6 = (bf16[64,128]{0,1:T(8,128)(2,1)S(1)}, bf16[64,128]{0,1:T(8,128)(2,1)S(1)}, u32[]{:S(2)}, u32[]{:S(2)}) collective-permute-start(bf16[64,128]{0,1:T(8,128)(2,1)S(1)} %select_bitcast_fusion), channel_id=1, source_target_pairs={{0,14},{2,0},{4,2},{6,4},{8,6},{10,8},{12,10},{14,12},{1,15},{3,1}... | collective-permute-start | bytes 49160 | tf_op jit(solution)/shard_map/ppermute | solution.py:11
where the time goes:
time: 202 us
  blocking collectives  135 us (67%)
  starting transfers between devices  16.3 us (8%)
  matrix products  14.8 us (7%)
  other arithmetic  14.5 us (7%)
  local copies, waits for them, and re-layouts  14 us (7%)
  waiting for transfers between devices  5.05 us (2%)
    psum x3, blocking collectives, reduce_products(): return lax.psum(values, ('lon', 'lat'))  93.3 us
    all_gather x2, blocking collectives, coarse_solve(): gathered = lax.all_gather(coarse_local, ('lon', 'lat'), axis=1, tiled=True)  41.8 us
    ppermute x8, starting transfers between devices, from_behind(): lax.ppermute(array, axis, [(i, (i + by) % size) for i in range(size)])  16.3 us
    scatter-add x4, other arithmetic, stiffness(): return result.at[:, west_index].add(incoming)  5.84 us
    scatter-add x4, other arithmetic, stiffness(): result = result.at[:, east_index].add(into_east)  5.82 us
    ppermute x8, waiting for transfers between devices, from_behind(): lax.ppermute(array, axis, [(i, (i + by) % size) for i in range(size)])  5.05 us
  transfers between devices with their start and end apart: 8, of which 7 were waited for; matrix products, arithmetic and copies ran while one was open for 4% of the time, Pallas kernels for 0%

commit v1 on v0

--- a/solution.py
+++ b/solution.py
@@ -3,12 +3,18 @@
 from jax import lax
 from jax.sharding import PartitionSpec as P
 
-ITERS = 2
+AXES = ("lon", "lat")
 
 
 def from_behind(array, axis, by):
     size = lax.axis_size(axis)
     return lax.ppermute(array, axis, [(i, (i + by) % size) for i in range(size)])
+
+
+def exchange(chunk):
+    domains = lax.axis_size("lon") * lax.axis_size("lat")
+    copies = jnp.broadcast_to(chunk[None], (domains,) + chunk.shape)
+    return lax.all_to_all(copies, AXES, split_axis=0, concat_axis=0, tiled=True)
 
 
 def body(
@@ -30,6 +36,8 @@
     block = stiffness_blocks.shape[1]
     nblocks = per_domain // block
     slots = coupling.shape[0]
+    vectors = deflation.shape[0]
+    domains = lax.axis_size("lon") * lax.axis_size("lat")
     active = (jnp.arange(per_domain) < node_count[0]).astype(jnp.float32)
     live = jnp.arange(slots) < iface_count[0]
     coupler = jnp.where(live[:, None] & live[None, :], coupling, jnp.zeros_like(coupling))
@@ -39,6 +47,7 @@
     west_index = west_rows[0]
     jacobi = 1.0 / (obs_precision + reaction * reaction / lumped_mass)
     contract_last = (((1,), (1,)), ((), ()))
+    inverse_parts = coarse_inverse.reshape(vectors, domains, vectors)
 
     def stiffness(field):
         rounded = field.astype(jnp.bfloat16)
@@ -67,46 +76,58 @@
         result = result.at[:, east_index].add(into_east)
         return result.at[:, west_index].add(incoming)
 
-    def coarse_solve(coarse_local):
-        gathered = lax.all_gather(coarse_local, ("lon", "lat"), axis=1, tiled=True)
+    def precision(field):
+        inner = stiffness(active * field) / lumped_mass
+        return active * (stiffness(inner) + obs_precision * field)
+
+    def coarse_of(values):
         return lax.dot_general(
-            gathered, coarse_inverse, contract_last, preferred_element_type=jnp.float32
+            values.astype(jnp.bfloat16), deflation, contract_last, preferred_element_type=jnp.float32
         )
 
-    def precondition(residual):
-        coarse_local = lax.dot_general(
-            residual.astype(jnp.bfloat16),
-            deflation,
-            contract_last,
-            preferred_element_type=jnp.float32,
+    def precondition(residual, coarse_all):
+        coarse_fix = jnp.einsum(
+            "dsk,jdk->sj", coarse_all, inverse_parts, preferred_element_type=jnp.float32
         ).astype(jnp.bfloat16)
-        coarse_fix = coarse_solve(coarse_local).astype(jnp.bfloat16)
         spread = jnp.dot(coarse_fix, deflation, preferred_element_type=jnp.float32)
         return active * (jacobi * residual + spread)
 
     def local_dot(first, second):
         return jnp.sum(first * second, axis=1)
 
-    def reduce_products(values):
-        return lax.psum(values, ("lon", "lat"))
-
     residual = active * right_side.astype(jnp.float32)
-    solution = jnp.zeros_like(residual)
-    smoothed = precondition(residual)
-    direction = smoothed
-    norm_now = reduce_products(local_dot(residual, smoothed))
-    for iteration in range(ITERS):
-        inner = stiffness(active * direction) / lumped_mass
-        image = active * (stiffness(inner) + obs_precision * direction)
-        step_size = norm_now / reduce_products(local_dot(direction, image))
-        solution = solution + step_size[:, None] * direction
-        residual = residual - step_size[:, None] * image
-        if iteration + 1 < ITERS:
-            smoothed = precondition(residual)
-            norm_next = reduce_products(local_dot(residual, smoothed))
-            direction = smoothed + (norm_next / norm_now)[:, None] * direction
-            norm_now = norm_next
-    return solution
+    coarse0 = exchange(coarse_of(residual).astype(jnp.bfloat16))
+    direction = precondition(residual, coarse0)
+    image = precision(direction)
+    packed = jnp.concatenate(
+        [
+            coarse_of(image),
+            local_dot(residual, direction)[:, None],
+            local_dot(direction, image)[:, None],
+            jnp.zeros((samples, 62), jnp.float32),
+        ],
+        axis=1,
+    )
+    second = exchange(packed)
+    sums = jnp.sum(second[:, :, vectors : vectors + 2], axis=0)
+    norm0, curved0 = sums[:, 0], sums[:, 1]
+    step0 = norm0 / curved0
+    residual = residual - step0[:, None] * image
+    coarse1 = coarse0.astype(jnp.float32) - step0[None, :, None] * second[:, :, :vectors]
+    smoothed = precondition(residual, coarse1.astype(jnp.bfloat16))
+    smooth_image = precision(smoothed)
+    partial = jnp.stack(
+        [
+            local_dot(residual, smoothed),
+            local_dot(smoothed, smooth_image),
+            local_dot(smoothed, image),
+        ]
+    )
+    norm1, curved, cross = jnp.sum(exchange(partial), axis=0)
+    beta = norm1 / norm0
+    curved1 = curved + beta * (2.0 * cross + beta * curved0)
+    step1 = norm1 / curved1
+    return (step0 + step1 * beta)[:, None] * direction + step1[:, None] * smoothed
 
 
 def solution(mesh):

time: 202 us -> 121 us (0.60)
  blocking collectives: 135 us -> 33.3 us
  starting transfers between devices: 16.3 us -> 27.2 us
  waiting for transfers between devices: 5.05 us -> 11.1 us
  local copies, waits for them, and re-layouts: 14 us -> 17.6 us
    psum x3 -> x0, blocking collectives: 93.3 us -> none  [reduce_products(): return lax.psum(values, ('lon', 'lat'))]
    all_gather x2 -> x0, blocking collectives: 41.8 us -> none  [coarse_solve(): gathered = lax.all_gather(coarse_local, ('lon', 'lat'), axis=1, tiled=True)]
    all_to_all x0 -> x2, blocking collectives: none -> 33.3 us  [exchange(): return lax.all_to_all(copies, AXES, split_axis=0, concat_axis=0, tiled=True)]
    all_to_all x0 -> x1, starting transfers between devices: none -> 7.49 us  [exchange(): return lax.all_to_all(copies, AXES, split_axis=0, concat_axis=0, tiled=True)]
    all_to_all x0 -> x1, waiting for transfers between devices: none -> 5.11 us  [exchange(): return lax.all_to_all(copies, AXES, split_axis=0, concat_axis=0, tiled=True)]
    ppermute x8, starting transfers between devices: 16.3 us -> 19.7 us  [from_behind(): lax.ppermute(array, axis, [(i, (i + by) % size) for i in range(size)])]
    unnamed x22 -> x28, local copies, waits for them, and re-layouts: 0.58 us -> 3.19 us
  transfers between devices with their start and end apart: 8 -> 9, of which waited for: 7 -> 8; matrix products, arithmetic and copies ran while one was open for 4% -> 5% of each run, Pallas kernels for 0% -> 0%
where the time goes in v1:
time: 121 us
  blocking collectives  33.3 us (28%)
  starting transfers between devices  27.2 us (22%)
  local copies, waits for them, and re-layouts  17.6 us (15%)
  other arithmetic  14.8 us (12%)
  matrix products  14.7 us (12%)
  waiting for transfers between devices  11.1 us (9%)
  between operations  2.08 us (2%)
    all_to_all x2, blocking collectives, exchange(): return lax.all_to_all(copies, AXES, split_axis=0, concat_axis=0, tiled=True)  33.3 us
    ppermute x8, starting transfers between devices, from_behind(): lax.ppermute(array, axis, [(i, (i + by) % size) for i in range(size)])  19.7 us
    all_to_all x1, starting transfers between devices, exchange(): return lax.all_to_all(copies, AXES, split_axis=0, concat_axis=0, tiled=True)  7.49 us
    ppermute x8, waiting for transfers between devices, from_behind(): lax.ppermute(array, axis, [(i, (i + by) % size) for i in range(size)])  5.98 us
    scatter-add x4, other arithmetic, stiffness(): return result.at[:, west_index].add(incoming)  5.84 us
    scatter-add x4, other arithmetic, stiffness(): result = result.at[:, east_index].add(into_east)  5.81 us
    all_to_all x1, waiting for transfers between devices, exchange(): return lax.all_to_all(copies, AXES, split_axis=0, concat_axis=0, tiled=True)  5.11 us
    dot_general x4, matrix products, stiffness(): jnp.einsum('kn,ski->sni', col_onehot, backward, precision=lax.Precision.H...  3.25 us
  transfers between devices with their start and end apart: 9, of which 8 were waited for; matrix products, arithmetic and copies ran while one was open for 5% of the time, Pallas kernels for 0%

profile of v1, /device:TPU:0, one launch (start us, length us, event | category | flops | bytes accessed | tf_op | source)
XLA Modules:
  0.0 120.8 jit_solution(13789573717450902763)
XLA Ops:
  0.7 1.1 convolution_convert_fusion.4
  1.9 0.9 reshape.393
  2.8 7.5 %all-to-all-start = ((bf16[16,2,2048]{2,1,0:T(2,128)(2,1)}), bf16[16,2,2048]{2,1,0:T(2,128)(2,1)S(1)}, u32[]{:S(2)}, u32[]{:S(2)}) async-start(bf16[16,2,2048]{2,1,0:T(2,128)(2,1)} %reshape.393), calls=%async_computation | async-start | bytes 262144 | tf_op jit(solution)/shard_map/all_to_all | solution.py:17
  13.2 5.1 %all-to-all-done = bf16[16,2,2048]{2,1,0:T(2,128)(2,1)S(1)} async-done(((bf16[16,2,2048]{2,1,0:T(2,128)(2,1)}), bf16[16,2,2048]{2,1,0:T(2,128)(2,1)S(1)}, u32[]{:S(2)}, u32[]{:S(2)}) %all-to-all-start) | async-done | bytes 131104 | tf_op jit(solution)/shard_map/all_to_all | solution.py:17
  22.8 0.8 fusion.14
  24.0 0.8 convolution_add_fusion.4
  25.2 4.8 %collective-permute-start = (bf16[64,128]{0,1:T(8,128)(2,1)S(1)}, bf16[64,128]{0,1:T(8,128)(2,1)S(1)}, u32[]{:S(2)}, u32[]{:S(2)}) collective-permute-start(bf16[64,128]{0,1:T(8,128)(2,1)S(1)} %select_bitcast_fusion.3), channel_id=1, source_target_pairs={{0,14},{2,0},{4,2},{6,4},{8,6},{10,8},{12,10},{14,12},{1,15},{3,1}... | collective-permute-start | bytes 49160 | tf_op jit(solution)/shard_map/ppermute | solution.py:11
  30.1 1.5 %collective-permute-done = bf16[64,128]{0,1:T(8,128)(2,1)S(1)} collective-permute-done((bf16[64,128]{0,1:T(8,128)(2,1)S(1)}, bf16[64,128]{0,1:T(8,128)(2,1)S(1)}, u32[]{:S(2)}, u32[]{:S(2)}) %collective-permute-start) | collective-permute-done | bytes 16416 | tf_op jit(solution)/shard_map/ppermute | solution.py:11
  31.8 1.5 %scatter_fusion = f32[64,1024]{0,1:T(8,128)S(1)} fusion(f32[64,1024]{0,1:T(8,128)S(1)} %copy.125, s32[128]{0:T(128)S(1)} %fusion.102, f32[128,64]{1,0:T(8,128)S(1)} %fusion.122), kind=kCustom, calls=%fused_computation.16 | custom fusion | flops 8192 | bytes 98816 | tf_op jit(solution)/shard_map/scatter-add | solution.py:76
  33.2 1.5 %scatter_fusion.1 = f32[64,1024]{0,1:T(8,128)S(1)} fusion(f32[64,1024]{0,1:T(8,128)S(1)} %scatter_fusion, s32[128]{0:T(128)S(1)} %fusion.103, f32[128,64]{1,0:T(8,128)S(1)} %copy.128), kind=kCustom, calls=%fused_computation.17 | custom fusion | flops 8192 | bytes 98816 | tf_op jit(solution)/shard_map/scatter-add | solution.py:77
  38.5 0.8 fusion.11
  39.7 0.8 convolution_add_fusion.3
  41.2 5.1 %collective-permute-start.2 = (bf16[64,128]{0,1:T(8,128)(2,1)S(1)}, bf16[64,128]{0,1:T(8,128)(2,1)S(1)}, u32[]{:S(2)}, u32[]{:S(2)}) collective-permute-start(bf16[64,128]{0,1:T(8,128)(2,1)S(1)} %select_bitcast_fusion.2), channel_id=1, source_target_pairs={{0,14},{2,0},{4,2},{6,4},{8,6},{10,8},{12,10},{14,12},{1,15},{3,1}... | collective-permute-start | bytes 49160 | tf_op jit(solution)/shard_map/ppermute | solution.py:11
  46.2 1.4 %collective-permute-done.3 = bf16[64,128]{1,0:T(8,128)(2,1)S(1)} collective-permute-done((bf16[64,128]{1,0:T(8,128)(2,1)S(1)}, bf16[64,128]{1,0:T(8,128)(2,1)S(1)}, u32[]{:S(2)}, u32[]{:S(2)}) %collective-permute-start.3) | collective-permute-done | bytes 16416 | tf_op jit(solution)/shard_map/ppermute | solution.py:11
  48.0 1.5 %scatter_fusion.2 = f32[64,1024]{0,1:T(8,128)S(1)} fusion(f32[64,1024]{0,1:T(8,128)S(1)} %copy.135, s32[128]{0:T(128)S(1)} %fusion.102, f32[128,64]{1,0:T(8,128)S(1)} %fusion.121), kind=kCustom, calls=%fused_computation.18 | custom fusion | flops 8192 | bytes 98816 | tf_op jit(solution)/shard_map/scatter-add | solution.py:76
  49.5 1.5 %scatter_fusion.3 = f32[64,1024]{0,1:T(8,128)S(1)} fusion(f32[64,1024]{0,1:T(8,128)S(1)} %scatter_fusion.2, s32[128]{0:T(128)S(1)} %fusion.103, f32[128,64]{1,0:T(8,128)S(1)} %copy.138), kind=kCustom, calls=%fused_computation.19 | custom fusion | flops 8192 | bytes 98816 | tf_op jit(solution)/shard_map/scatter-add | solution.py:77
  51.8 20.7 %all_to_all.15 = f32[16,64,128]{2,1,0:T(8,128)S(1)} all-to-all(f32[16,64,128]{2,1,0:T(8,128)S(1)} %broadcast_in_dim.37), channel_id=1, replica_groups=mesh['grp'=2,'lon'=8,'lat'=2] {'lon','lat'}, dimensions={0} | all-to-all | bytes 1048576 | tf_op jit(solution)/shard_map/all_to_all | solution.py:17
  77.0 0.8 fusion.8
  78.9 0.8 convolution_add_fusion.1
  80.1 4.4 %collective-permute-start.4 = (bf16[64,128]{0,1:T(8,128)(2,1)S(1)}, bf16[64,128]{0,1:T(8,128)(2,1)S(1)}, u32[]{:S(2)}, u32[]{:S(2)}) collective-permute-start(bf16[64,128]{0,1:T(8,128)(2,1)S(1)} %select_bitcast_fusion.1), channel_id=1, source_target_pairs={{0,14},{2,0},{4,2},{6,4},{8,6},{10,8},{12,10},{14,12},{1,15},{3,1}... | collective-permute-start | bytes 49160 | tf_op jit(solution)/shard_map/ppermute | solution.py:11
  85.0 1.0 collective-permute-done.4
  86.2 1.5 %scatter_fusion.4 = f32[64,1024]{0,1:T(8,128)S(1)} fusion(f32[64,1024]{0,1:T(8,128)S(1)} %copy.149, s32[128]{0:T(128)S(1)} %fusion.102, f32[128,64]{1,0:T(8,128)S(1)} %fusion.120), kind=kCustom, calls=%fused_computation.20 | custom fusion | flops 8192 | bytes 98816 | tf_op jit(solution)/shard_map/scatter-add | solution.py:76
  87.7 1.5 %scatter_fusion.5 = f32[64,1024]{0,1:T(8,128)S(1)} fusion(f32[64,1024]{0,1:T(8,128)S(1)} %scatter_fusion.4, s32[128]{0:T(128)S(1)} %fusion.103, f32[128,64]{1,0:T(8,128)S(1)} %copy.152), kind=kCustom, calls=%fused_computation.21 | custom fusion | flops 8192 | bytes 98816 | tf_op jit(solution)/shard_map/scatter-add | solution.py:77
  92.9 0.8 fusion.5
  94.2 0.8 convolution_add_fusion
  95.3 1.1 collective-permute-start.7
  96.7 4.0 %collective-permute-start.6 = (bf16[64,128]{0,1:T(8,128)(2,1)S(1)}, bf16[64,128]{0,1:T(8,128)(2,1)S(1)}, u32[]{:S(2)}, u32[]{:S(2)}) collective-permute-start(bf16[64,128]{0,1:T(8,128)(2,1)S(1)} %select_bitcast_fusion), channel_id=1, source_target_pairs={{0,14},{2,0},{4,2},{6,4},{8,6},{10,8},{12,10},{14,12},{1,15},{3,1}... | collective-permute-start | bytes 49160 | tf_op jit(solution)/shard_map/ppermute | solution.py:11
  100.7 1.4 %collective-permute-done.7 = bf16[64,128]{1,0:T(8,128)(2,1)S(1)} collective-permute-done((bf16[64,128]{1,0:T(8,128)(2,1)S(1)}, bf16[64,128]{1,0:T(8,128)(2,1)S(1)}, u32[]{:S(2)}, u32[]{:S(2)}) %collective-permute-start.7) | collective-permute-done | bytes 16416 | tf_op jit(solution)/shard_map/ppermute | solution.py:11
  102.5 1.5 %scatter_fusion.6 = f32[64,1024]{0,1:T(8,128)S(1)} fusion(f32[64,1024]{0,1:T(8,128)S(1)} %copy.159, s32[128]{0:T(128)S(1)} %fusion.102, f32[128,64]{1,0:T(8,128)S(1)} %fusion.119), kind=kCustom, calls=%fused_computation.22 | custom fusion | flops 8192 | bytes 98816 | tf_op jit(solution)/shard_map/scatter-add | solution.py:76
  104.0 1.5 %scatter_fusion.7 = f32[64,1024]{0,1:T(8,128)S(1)} fusion(f32[64,1024]{0,1:T(8,128)S(1)} %scatter_fusion.6, s32[128]{0:T(128)S(1)} %fusion.103, f32[128,64]{1,0:T(8,128)S(1)} %copy.162), kind=kCustom, calls=%fused_computation.23 | custom fusion | flops 8192 | bytes 98816 | tf_op jit(solution)/shard_map/scatter-add | solution.py:77
  106.0 12.7 %all_to_all.16 = f32[16,1,192]{2,1,0:T(1,128)S(1)} all-to-all(f32[16,1,192]{2,1,0:T(1,128)S(1)} %reshape.395), channel_id=1, replica_groups=mesh['grp'=2,'lon'=8,'lat'=2] {'lon','lat'}, dimensions={0} | all-to-all | bytes 24576 | tf_op jit(solution)/shard_map/all_to_all | solution.py:17
  120.0 0.8 multiply_add_fusion
  (136 shorter events, 27.3 us)
Async XLA Ops:
  0.0 22.1 %copy-start = (bf16[24,128,128]{2,1,0:T(8,128)(2,1)S(1)}, bf16[24,128,128]{2,1,0:T(8,128)(2,1)}, u32[]{:S(2)}) copy-start(bf16[24,128,128]{2,1,0:T(8,128)(2,1)} %param.18) | copy-start | bytes 2359300
  2.8 7.5 %copy-start.8 = (s32[24,2]{0,1:T(2,128)S(1)}, s32[24,2]{0,1:T(2,128)}, u32[]{:S(2)}) copy-start(s32[24,2]{0,1:T(2,128)} %param.19) | copy-start | bytes 580
  2.8 9.6 %copy-start.5 = (bf16[64,1024]{1,0:T(8,128)(2,1)S(1)}, bf16[64,1024]{1,0:T(8,128)(2,1)}, u32[]{:S(2)}) copy-start(bf16[64,1024]{1,0:T(8,128)(2,1)} %param.29) | copy-start | bytes 393220
  2.8 15.4 %all-to-all-start = ((bf16[16,2,2048]{2,1,0:T(2,128)(2,1)}), bf16[16,2,2048]{2,1,0:T(2,128)(2,1)S(1)}, u32[]{:S(2)}, u32[]{:S(2)}) async-start(bf16[16,2,2048]{2,1,0:T(2,128)(2,1)} %reshape.393), calls=%async_computation | async-start | bytes 262144 | tf_op jit(solution)/shard_map/all_to_all | solution.py:17
  10.4 0.7 copy-start.10
  11.0 0.7 copy-start.9
  12.4 0.7 copy-start.4
  12.4 0.7 copy-start.6
  12.5 0.7 copy-start.7
  13.2 5.3 %copy-start.1 = (bf16[64,1024]{1,0:T(8,128)(2,1)S(1)}, bf16[64,1024]{1,0:T(8,128)(2,1)}, u32[]{:S(2)}) copy-start(bf16[64,1024]{1,0:T(8,128)(2,1)} %param.17) | copy-start | bytes 393220
  13.2 5.3 %copy-start.2 = (bf16[64,1024]{1,0:T(8,128)(2,1)S(1)}, bf16[64,1024]{1,0:T(8,128)(2,1)}, u32[]{:S(2)}) copy-start(bf16[64,1024]{1,0:T(8,128)(2,1)} %param.28) | copy-start | bytes 393220
  21.1 0.8 copy-start.3
  22.1 7.9 %collective-permute-start.1 = (bf16[64,128]{1,0:T(8,128)(2,1)S(1)}, bf16[64,128]{1,0:T(8,128)(2,1)S(1)}, u32[]{:S(2)}, u32[]{:S(2)}) collective-permute-start(bf16[64,128]{1,0:T(8,128)(2,1)S(1)} %convolution_convert_fusion.3), channel_id=1, source_target_pairs={{0,2},{2,4},{4,6},{6,8},{8,10},{10,12},{12,14},{14,0},{1,3},{3,5},... | collective-permute-start | bytes 49160 | tf_op jit(solution)/shard_map/ppermute | solution.py:11
  25.2 6.4 %collective-permute-start = (bf16[64,128]{0,1:T(8,128)(2,1)S(1)}, bf16[64,128]{0,1:T(8,128)(2,1)S(1)}, u32[]{:S(2)}, u32[]{:S(2)}) collective-permute-start(bf16[64,128]{0,1:T(8,128)(2,1)S(1)} %select_bitcast_fusion.3), channel_id=1, source_target_pairs={{0,14},{2,0},{4,2},{6,4},{8,6},{10,8},{12,10},{14,12},{1,15},{3,1}... | collective-permute-start | bytes 49160 | tf_op jit(solution)/shard_map/ppermute | solution.py:11
  40.9 6.7 %collective-permute-start.3 = (bf16[64,128]{1,0:T(8,128)(2,1)S(1)}, bf16[64,128]{1,0:T(8,128)(2,1)S(1)}, u32[]{:S(2)}, u32[]{:S(2)}) collective-permute-start(bf16[64,128]{1,0:T(8,128)(2,1)S(1)} %convolution_convert_fusion.2), channel_id=1, source_target_pairs={{0,2},{2,4},{4,6},{6,8},{8,10},{10,12},{12,14},{14,0},{1,3},{3,5},... | collective-permute-start | bytes 49160 | tf_op jit(solution)/shard_map/ppermute | solution.py:11
  41.2 6.7 %collective-permute-start.2 = (bf16[64,128]{0,1:T(8,128)(2,1)S(1)}, bf16[64,128]{0,1:T(8,128)(2,1)S(1)}, u32[]{:S(2)}, u32[]{:S(2)}) collective-permute-start(bf16[64,128]{0,1:T(8,128)(2,1)S(1)} %select_bitcast_fusion.2), channel_id=1, source_target_pairs={{0,14},{2,0},{4,2},{6,4},{8,6},{10,8},{12,10},{14,12},{1,15},{3,1}... | collective-permute-start | bytes 49160 | tf_op jit(solution)/shard_map/ppermute | solution.py:11
  78.5 6.4 %collective-permute-start.5 = (bf16[64,128]{1,0:T(8,128)(2,1)S(1)}, bf16[64,128]{1,0:T(8,128)(2,1)S(1)}, u32[]{:S(2)}, u32[]{:S(2)}) collective-permute-start(bf16[64,128]{1,0:T(8,128)(2,1)S(1)} %convolution_convert_fusion.1), channel_id=1, source_target_pairs={{0,2},{2,4},{4,6},{6,8},{8,10},{10,12},{12,14},{14,0},{1,3},{3,5},... | collective-permute-start | bytes 49160 | tf_op jit(solution)/shard_map/ppermute | solution.py:11
  80.1 6.0 %collective-permute-start.4 = (bf16[64,128]{0,1:T(8,128)(2,1)S(1)}, bf16[64,128]{0,1:T(8,128)(2,1)S(1)}, u32[]{:S(2)}, u32[]{:S(2)}) collective-permute-start(bf16[64,128]{0,1:T(8,128)(2,1)S(1)} %select_bitcast_fusion.1), channel_id=1, source_target_pairs={{0,14},{2,0},{4,2},{6,4},{8,6},{10,8},{12,10},{14,12},{1,15},{3,1}... | collective-permute-start | bytes 49160 | tf_op jit(solution)/shard_map/ppermute | solution.py:11
  95.3 6.7 %collective-permute-start.7 = (bf16[64,128]{1,0:T(8,128)(2,1)S(1)}, bf16[64,128]{1,0:T(8,128)(2,1)S(1)}, u32[]{:S(2)}, u32[]{:S(2)}) collective-permute-start(bf16[64,128]{1,0:T(8,128)(2,1)S(1)} %convolution_convert_fusion), channel_id=1, source_target_pairs={{0,2},{2,4},{4,6},{6,8},{8,10},{10,12},{12,14},{14,0},{1,3},{3,5},... | collective-permute-start | bytes 49160 | tf_op jit(solution)/shard_map/ppermute | solution.py:11
  96.7 5.6 %collective-permute-start.6 = (bf16[64,128]{0,1:T(8,128)(2,1)S(1)}, bf16[64,128]{0,1:T(8,128)(2,1)S(1)}, u32[]{:S(2)}, u32[]{:S(2)}) collective-permute-start(bf16[64,128]{0,1:T(8,128)(2,1)S(1)} %select_bitcast_fusion), channel_id=1, source_target_pairs={{0,14},{2,0},{4,2},{6,4},{8,6},{10,8},{12,10},{14,12},{1,15},{3,1}... | collective-permute-start | bytes 49160 | tf_op jit(solution)/shard_map/ppermute | solution.py:11

commit v2 on v0

v2 whole, which is shorter than its diff:
```python
import jax
import jax.numpy as jnp
import numpy as np
from jax import lax
from jax.experimental import pallas as pl
from jax.experimental.pallas import tpu as pltpu
from jax.sharding import PartitionSpec as P

F32 = jnp.float32
BF16 = jnp.bfloat16
VMEM = pl.BlockSpec(memory_space=pltpu.VMEM)
SMEM = pl.BlockSpec(memory_space=pltpu.SMEM)
LANES = 128


def dot(a, b, ca=1, cb=0):
    return lax.dot_general(a, b, (((ca,), (cb,)), ((), ())), preferred_element_type=F32)


def call(kernel, outs, specs, args, flops, scratch=()):
    moved = sum(int(np.prod(a.shape)) * a.dtype.itemsize for a in args)
    return pl.pallas_call(
        kernel,
        out_shape=[jax.ShapeDtypeStruct(s, t) for s, t in outs],
        in_specs=specs,
        out_specs=[VMEM] * len(outs),
        scratch_shapes=list(scratch),
        compiler_params=pltpu.CompilerParams(vmem_limit_bytes=32 * 1024 * 1024),
        cost_estimate=pl.CostEstimate(flops=flops, bytes_accessed=moved, transcendentals=0),
    )(*args)


def active_of(count_ref, nodes):
    return (lax.broadcasted_iota(jnp.int32, (1, nodes), 1) < count_ref[0]).astype(F32)


def fold(values):
    half = values.shape[0] // 2
    return jnp.concatenate([values[:half], values[half:]], axis=1)


def column_of(row):
    return jnp.transpose(jnp.broadcast_to(row, (LANES, LANES)))[:, 0:1]


def row_of(first, second):
    both = jnp.concatenate([first, second], axis=0)
    return jnp.transpose(jnp.broadcast_to(both, (LANES, LANES)))[0:1]


def row_sum(first, second):
    return jnp.sum(first * second, axis=1, keepdims=True)


def coarse_kernel(count_ref, right_ref, vectors_ref, chunk_ref):
    active = active_of(count_ref, right_ref.shape[1]).astype(BF16)
    coarse = dot(vectors_ref[...], right_ref[...] * active, 1, 1)
    chunk_ref[...] = fold(coarse).astype(BF16)


def dense_kernel(pattern_ref, blocks_ref, dense_ref, total_ref):
    count, block, _ = blocks_ref.shape
    nodes = dense_ref.shape[0]

    def clear(i, carry):
        total_ref[pl.ds(pl.multiple_of(i * block, block), block), :] = jnp.zeros((block, nodes), F32)
        return carry

    lax.fori_loop(0, nodes // block, clear, 0)

    def place(k, carry):
        rows = pl.ds(pl.multiple_of(pattern_ref[k, 0] * block, block), block)
        cols = pl.ds(pl.multiple_of(pattern_ref[k, 1] * block, block), block)
        values = blocks_ref[k].astype(F32)
        total_ref[rows, cols] += values
        total_ref[cols, rows] += jnp.transpose(values)
        return carry

    lax.fori_loop(0, count, place, 0)

    def narrow(i, carry):
        rows = pl.ds(pl.multiple_of(i * block, block), block)
        dense_ref[rows, :] = total_ref[rows, :].astype(BF16)
        return carry

    lax.fori_loop(0, nodes // block, narrow, 0)


def edge_kernel(iface_ref, coupling_ref, east_ref, west_ref, mass_ref, edge_ref, to_west_ref, to_east_ref):
    slots = coupling_ref.shape[0]
    nodes = mass_ref.shape[1]
    live_a = lax.broadcasted_iota(jnp.int32, (slots, slots), 0) < iface_ref[0]
    live_b = lax.broadcasted_iota(jnp.int32, (slots, slots), 1) < iface_ref[0]
    link = jnp.where(live_a & live_b, coupling_ref[...], jnp.zeros((slots, slots), BF16))
    node = lax.broadcasted_iota(jnp.int32, (slots, nodes), 1).astype(F32)
    east = column_of(east_ref[...].astype(F32))
    west = column_of(west_ref[...].astype(F32))
    east_hot = jnp.where(node == east, 1.0, 0.0).astype(BF16)
    west_hot = jnp.where(node == west, 1.0, 0.0).astype(BF16)
    spread = dot(link, east_hot, 0, 0).astype(BF16)
    edge_ref[0:slots, :] = spread
    edge_ref[slots : 2 * slots, :] = west_hot
    edges = edge_ref[...]
    scaled = (edges.astype(F32) * (1.0 / mass_ref[...])).astype(BF16)
    both = dot(scaled, edges, 1, 1).astype(BF16)
    to_east_ref[...] = both[:, 0:slots]
    to_west_ref[...] = both[:, slots:]


def unfold(place_ref, count, piece, coarse_ref):
    half = coarse_ref.shape[0] // count // 2

    def move(d, carry):
        values = piece(place_ref[d])
        at = pl.multiple_of(d * 2 * half, 2 * half)
        coarse_ref[pl.ds(at, half), :] = values[:, 0 : LANES // 2]
        coarse_ref[pl.ds(at + half, half), :] = values[:, LANES // 2 :]
        return carry

    lax.fori_loop(0, count, move, 0, unroll=min(count, 16))


def first_level(field, coarse_ref, inverse_ref, vectors_ref, dense_ref, edge_ref, react, mass, obs, active,
                z_ref, scaled_ref, level_ref):
    fix = dot(inverse_ref[...], coarse_ref[...]).astype(BF16)
    spread = dot(fix, vectors_ref[...], 0, 0)
    z = active * (field / (obs + react * react / mass) + spread)
    z_ref[...] = z
    w = z.astype(BF16)
    scaled = (dot(w, dense_ref[...]) + react * z) / mass
    scaled_ref[...] = scaled
    edges = edge_ref[...]
    level1 = dot(w, edges, 1, 1).astype(BF16)
    level2 = dot(scaled.astype(BF16), edges, 1, 1).astype(BF16)
    level_ref[...] = jnp.concatenate([level1, level2], axis=0)
    return z


def start_kernel(place_ref, count_ref, pieces_ref, inverse_ref, right_ref, vectors_ref, dense_ref, edge_ref,
                 react_ref, mass_ref, obs_ref, to_west_ref, to_east_ref,
                 z_ref, scaled_ref, west_msg_ref, east_msg_ref, far_west_ref, far_east_ref,
                 coarse_ref, level_ref):
    samples, nodes = right_ref.shape
    unfold(place_ref, pieces_ref.shape[0], lambda at: pieces_ref[at], coarse_ref)
    active = active_of(count_ref, nodes)
    first_level(active * right_ref[...].astype(F32), coarse_ref, inverse_ref, vectors_ref, dense_ref, edge_ref,
                react_ref[...], mass_ref[...], obs_ref[...], active, z_ref, scaled_ref, level_ref)
    slots = edge_ref.shape[0] // 2
    east_msg_ref[0 : 2 * samples, :] = level_ref[:, 0:slots]
    west_msg_ref[0 : 2 * samples, :] = level_ref[:, slots:]
    east_msg_ref[2 * samples :, :] = to_east_ref[...]
    west_msg_ref[2 * samples :, :] = to_west_ref[...]
    far_east_ref[...] = level_ref[0:samples, 0:slots]
    far_west_ref[...] = level_ref[0:samples, slots:]


def second_level(from_east_ref, from_west_ref, beyond_east_ref, beyond_west_ref, own_west_ref, own_east_ref,
                 corr_east, corr_west, z, scaled_ref, dense_ref, edge_ref, react, mass, obs, active):
    samples = z.shape[0]
    edges = edge_ref[...]
    arrived = jnp.concatenate([from_east_ref[0:samples, :], from_west_ref[0:samples, :]], axis=1)
    inner = scaled_ref[...] + dot(arrived, edges) / mass
    east_terms = jnp.concatenate([beyond_east_ref[...], own_east_ref[...]], axis=1)
    west_terms = jnp.concatenate([own_west_ref[...], beyond_west_ref[...]], axis=1)
    second_east = from_east_ref[samples : 2 * samples, :].astype(F32) + dot(east_terms, corr_east)
    second_west = from_west_ref[samples : 2 * samples, :].astype(F32) + dot(west_terms, corr_west)
    arrived2 = jnp.concatenate([second_east, second_west], axis=1).astype(BF16)
    image = dot(inner.astype(BF16), dense_ref[...]) + dot(arrived2, edges) + react * inner
    return active * (image + obs * z)


def image_kernel(count_ref, from_east_ref, from_west_ref, beyond_east_ref, beyond_west_ref, own_west_ref, own_east_ref,
                 z_ref, scaled_ref, dense_ref, edge_ref, react_ref, mass_ref, obs_ref, right_ref, vectors_ref,
                 image_ref, chunk_ref):
    samples, nodes = z_ref.shape
    active = active_of(count_ref, nodes)
    z = z_ref[...]
    image = second_level(from_east_ref, from_west_ref, beyond_east_ref, beyond_west_ref, own_west_ref, own_east_ref,
                         from_east_ref[2 * samples :, :], from_west_ref[2 * samples :, :], z, scaled_ref, dense_ref,
                         edge_ref, react_ref[...], mass_ref[...], obs_ref[...], active)
    image_ref[...] = image
    coarse = fold(dot(vectors_ref[...], image.astype(BF16), 1, 1))
    half = coarse.shape[0]
    sums = row_of(row_sum(active * right_ref[...].astype(F32), z), row_sum(z, image))
    chunk_ref[0:half, :] = coarse
    chunk_ref[half:, :] = jnp.broadcast_to(sums, (chunk_ref.shape[0] - half, LANES))


def middle_kernel(place_ref, count_ref, pieces_ref, second_ref, inverse_ref, right_ref, image_ref, vectors_ref,
                  dense_ref, edge_ref, react_ref, mass_ref, obs_ref,
                  z_ref, scaled_ref, west_msg_ref, east_msg_ref, far_west_ref, far_east_ref, sums_ref,
                  coarse_ref, level_ref):
    samples, nodes = right_ref.shape
    count, half, _ = pieces_ref.shape

    def add(d, total):
        return total + second_ref[d, half : half + 1, :]

    sums = lax.fori_loop(0, count, add, jnp.zeros((1, LANES), F32), unroll=min(count, 16))
    step = sums[:, 0 : LANES // 2] / sums[:, LANES // 2 :]
    step = jnp.concatenate([step, step], axis=1)

    def piece(at):
        return (pieces_ref[at].astype(F32) - step * second_ref[at, 0:half, :]).astype(BF16)

    unfold(place_ref, count, piece, coarse_ref)
    active = active_of(count_ref, nodes)
    residual = active * right_ref[...].astype(F32) - column_of(step)[0:samples] * image_ref[...]
    z = first_level(residual, coarse_ref, inverse_ref, vectors_ref, dense_ref, edge_ref,
                    react_ref[...], mass_ref[...], obs_ref[...], active, z_ref, scaled_ref, level_ref)
    slots = edge_ref.shape[0] // 2
    east_msg_ref[...] = level_ref[:, 0:slots]
    west_msg_ref[...] = level_ref[:, slots:]
    far_east_ref[...] = level_ref[0:samples, 0:slots]
    far_west_ref[...] = level_ref[0:samples, slots:]
    norm = row_sum(residual, z)
    row = lax.broadcasted_iota(jnp.int32, (8, LANES), 0)
    sums_ref[...] = jnp.where(row == 0, sums, jnp.where(row == 1, row_of(norm, norm), 0.0))


def last_kernel(count_ref, from_east_ref, from_west_ref, beyond_east_ref, beyond_west_ref, own_west_ref, own_east_ref,
                corr_east_ref, corr_west_ref, z_ref, scaled_ref, dense_ref, edge_ref, react_ref, mass_ref, obs_ref,
                first_image_ref, sums_ref, partial_ref):
    samples, nodes = z_ref.shape
    active = active_of(count_ref, nodes)
    z = z_ref[...]
    image = second_level(from_east_ref, from_west_ref, beyond_east_ref, beyond_west_ref, own_west_ref, own_east_ref,
                         corr_east_ref[2 * samples :, :], corr_west_ref[2 * samples :, :], z, scaled_ref, dense_ref,
                         edge_ref, react_ref[...], mass_ref[...], obs_ref[...], active)
    curves = row_of(row_sum(z, image), row_sum(z, first_image_ref[...]))
    row = lax.broadcasted_iota(jnp.int32, (8, LANES), 0)
    partial_ref[...] = jnp.where(row == 0, curves, jnp.where(row == 1, sums_ref[1:2, :], 0.0))


def finish_kernel(sums_ref, totals_ref, first_ref, second_ref, out_ref):
    samples = first_ref.shape[0]
    half = LANES // 2
    norm0, curve0 = sums_ref[0:1, 0:half], sums_ref[0:1, half:]
    curve, cross = totals_ref[0:1, 0:half], totals_ref[0:1, half:]
    norm1 = totals_ref[1:2, 0:half]
    beta = norm1 / norm0
    step0 = norm0 / curve0
    step1 = norm1 / (curve + beta * (2.0 * cross + beta * curve0))
    scales = column_of(jnp.concatenate([step0 + step1 * beta, step1], axis=1))
    out_ref[...] = scales[0:samples] * first_ref[...] + scales[samples : 2 * samples] * second_ref[...]


def shift(array, by):
    size = lax.axis_size("lon")
    return lax.ppermute(array, "lon", [(i, (i + by) % size) for i in range(size)])


def rounds():
    steps = []
    for axis in ("lon", "lat"):
        by = lax.axis_size(axis) // 2
        while by:
            steps.append((axis, by))
            by //= 2
    return steps


def swap(array, axis, by):
    return lax.ppermute(array, axis, [(i, i ^ by) for i in range(lax.axis_size(axis))])


def gather(chunk):
    pieces = chunk[None]
    for axis, by in rounds():
        pieces = jnp.concatenate([pieces, swap(pieces, axis, by)], axis=0)
    return pieces


def total(values):
    for axis, by in rounds():
        values = values + swap(values, axis, by)
    return values


def places():
    lats = lax.axis_size("lat")
    domains = lax.axis_size("lon") * lats
    me = lax.axis_index("lon") * lats + lax.axis_index("lat")
    apart = jnp.arange(domains, dtype=jnp.int32) ^ me
    place = jnp.zeros_like(apart)
    for i, (axis, by) in enumerate(rounds()):
        mask = by * lats if axis == "lon" else by
        place = place + jnp.where((apart & mask) != 0, 1 << i, 0)
    return place


def body(
    right_side,
    stiffness_blocks,
    block_pattern,
    reaction,
    lumped_mass,
    obs_precision,
    coupling,
    east_rows,
    west_rows,
    iface_count,
    node_count,
    deflation,
    coarse_inverse,
):
    samples, nodes = right_side.shape
    slots = coupling.shape[0]
    vectors = deflation.shape[0]
    domains = lax.axis_size("lon") * lax.axis_size("lat")
    half = vectors // 2
    react, mass, obs = reaction[None], lumped_mass[None], obs_precision[None]
    fields = [((samples, nodes), F32)] * 2
    far = [((samples, slots), BF16)] * 2
    coarse_scratch = pltpu.VMEM((domains * vectors, samples), BF16)
    level_scratch = pltpu.VMEM((2 * samples, 2 * slots), BF16)
    apply_cost = 2 * samples * nodes * nodes
    place = places()

    (chunk,) = call(coarse_kernel, [((half, LANES), BF16)], [SMEM, VMEM, VMEM],
                    (node_count, right_side, deflation), 2 * samples * vectors * nodes)
    edge, corr_west, corr_east = call(
        edge_kernel,
        [((2 * slots, nodes), BF16), ((2 * slots, slots), BF16), ((2 * slots, slots), BF16)],
        [SMEM, VMEM, VMEM, VMEM, VMEM],
        (iface_count, coupling, east_rows, west_rows, mass),
        8 * slots * slots * nodes,
    )
    (dense,) = call(dense_kernel, [((nodes, nodes), BF16)], [SMEM, VMEM], (block_pattern, stiffness_blocks),
                    apply_cost, [pltpu.VMEM((nodes, nodes), F32)])

    pieces = gather(chunk)
    z0, scaled, west_msg, east_msg, far_west, far_east = call(
        start_kernel,
        fields + [((2 * samples + 2 * slots, slots), BF16)] * 2 + far,
        [SMEM, SMEM] + [VMEM] * 11,
        (place, node_count, pieces, coarse_inverse, right_side, deflation, dense, edge, react, mass, obs,
         corr_west, corr_east),
        apply_cost,
        [coarse_scratch, level_scratch],
    )
    from_west = shift(east_msg, 1)
    from_east = shift(west_msg, -1)
    beyond_west = shift(far_east, 2)
    beyond_east = shift(far_west, -2)
    image, chunk = call(
        image_kernel,
        [((samples, nodes), F32), ((half + 8, LANES), F32)],
        [SMEM] + [VMEM] * 15,
        (node_count, from_east, from_west, beyond_east, beyond_west, far_west, far_east, z0, scaled, dense, edge,
         react, mass, obs, right_side, deflation),
        apply_cost,
    )
    second = gather(chunk)
    z1, scaled, west_msg, east_msg, far_west, far_east, sums = call(
        middle_kernel,
        fields + [((2 * samples, slots), BF16)] * 2 + far + [((8, LANES), F32)],
        [SMEM, SMEM] + [VMEM] * 11,
        (place, node_count, pieces, second, coarse_inverse, right_side, image, deflation, dense, edge, react, mass,
         obs),
        apply_cost,
        [coarse_scratch, level_scratch],
    )
    corr_from_east, corr_from_west = from_east, from_west
    from_west = shift(east_msg, 1)
    from_east = shift(west_msg, -1)
    beyond_west = shift(far_east, 2)
    beyond_east = shift(far_west, -2)
    (partial,) = call(
        last_kernel,
        [((8, LANES), F32)],
        [SMEM] + [VMEM] * 17,
        (node_count, from_east, from_west, beyond_east, beyond_west, far_west, far_east, corr_from_east,
         corr_from_west, z1, scaled, dense, edge, react, mass, obs, image, sums),
        apply_cost,
    )
    totals = total(partial)
    (out,) = call(finish_kernel, [((samples, nodes), F32)], [VMEM] * 4, (sums, totals, z0, z1), 4 * samples * nodes)
    return out


def solution(mesh):
    placed = (
        P(None, ("grp", "lon", "lat")),
        P(("grp", "lon", "lat"), None, None),
        P(("grp", "lon", "lat"), None),
        P(("grp", "lon", "lat")),
        P(("grp", "lon", "lat")),
        P(("grp", "lon", "lat")),
        P(("grp", "lon", "lat"), None),
        P(("grp", "lon", "lat"), None),
        P(("grp", "lon", "lat"), None),
        P(("grp", "lon", "lat")),
        P(("grp", "lon", "lat")),
        P(None, ("grp", "lon", "lat")),
        P(("grp", "lon", "lat"), None),
    )
    return jax.shard_map(
        body, mesh=mesh, in_specs=placed, out_specs=P(None, ("grp", "lon", "lat")), check_vma=False
    )
```

time: 202 us -> 79.4 us (0.39)
  blocking collectives: 135 us -> 0 us
  waiting for transfers between devices: 5.05 us -> 38.4 us
  matrix products: 14.8 us -> 0 us
  other arithmetic: 14.5 us -> 0.07 us
  Pallas kernels: 0 us -> 11.7 us
  local copies, waits for them, and re-layouts: 14 us -> 3.8 us
  starting transfers between devices: 16.3 us -> 23.6 us
    psum x3 -> x0, blocking collectives: 93.3 us -> none  [reduce_products(): return lax.psum(values, ('lon', 'lat'))]
    all_gather x2 -> x0, blocking collectives: 41.8 us -> none  [coarse_solve(): gathered = lax.all_gather(coarse_local, ('lon', 'lat'), axis=1, tiled=True)]
    ppermute x8 -> x20, waiting for transfers between devices: 5.05 us -> 38.4 us  [the longest x12 28.7 us: swap(): lax.ppermute(array, axis, [(i, i ^ by) for i in range(lax.axis_size(axis))])]
    dot_general x28 -> x0, matrix products: 14.8 us -> none  [the longest x4 3.25 us: stiffness(): jnp.einsum('kn,ski->sni', col_onehot, backward, precision=lax.Precision.H...]
    pallas_call x0 -> x8, Pallas kernels: none -> 11.7 us  [call(): pl.pallas_call(kernel, out_shape=[jax.ShapeDtypeStruct(s, t) for s, t in...]
    scatter-add x8 -> x0, other arithmetic: 11.7 us -> none  [the longest x4 5.84 us: stiffness(): return result.at[:, west_index].add(incoming)]
    gather x16 -> x0, local copies, waits for them, and re-layouts: 10.7 us -> none  [the longest x4 2.86 us: stiffness(): arrived = from_behind(jnp.take(rounded, west_index, axis=1), 'lon', -1)]
    ppermute x8 -> x20, starting transfers between devices: 16.3 us -> 23.6 us  [the longest x12 15.1 us: swap(): lax.ppermute(array, axis, [(i, i ^ by) for i in range(lax.axis_size(axis))])]
  transfers between devices with their start and end apart: 8 -> 20, of which waited for: 7 -> 16; matrix products, arithmetic and copies ran while one was open for 4% -> 1% of each run, Pallas kernels for 0% -> 6%
where the time goes in v2:
time: 79.4 us; the launch traced here: 79.2 us
  waiting for transfers between devices  38.4 us (48%)
  starting transfers between devices  23.6 us (30%)
  Pallas kernels  11.7 us (15%)
  local copies, waits for them, and re-layouts  3.8 us (5%)
  between operations  1.58 us (2%)
    ppermute x12, waiting for transfers between devices, swap(): lax.ppermute(array, axis, [(i, i ^ by) for i in range(lax.axis_size(axis))])  28.7 us
    ppermute x12, starting transfers between devices, swap(): lax.ppermute(array, axis, [(i, i ^ by) for i in range(lax.axis_size(axis))])  15.1 us
    pallas_call x8, Pallas kernels, call(): pl.pallas_call(kernel, out_shape=[jax.ShapeDtypeStruct(s, t) for s, t in...  11.7 us
    ppermute x8, waiting for transfers between devices, shift(): lax.ppermute(array, 'lon', [(i, (i + by) % size) for i in range(size)])  9.69 us
    ppermute x8, starting transfers between devices, shift(): lax.ppermute(array, 'lon', [(i, (i + by) % size) for i in range(size)])  8.53 us
    unnamed x33, local copies, waits for them, and re-layouts  3.77 us
  transfers between devices with their start and end apart: 20, of which 16 were waited for; matrix products, arithmetic and copies ran while one was open for 1% of the time, Pallas kernels for 6%

profile of v2, /device:TPU:0, one launch (start us, length us, event | category | flops | bytes accessed | tf_op | source)
XLA Modules:
  0.0 79.2 jit_solution(4129868234931069382)
XLA Ops:
  2.8 4.1 %collective-permute-start = (bf16[1,32,128]{2,1,0:T(8,128)(2,1)S(1)}, bf16[1,32,128]{2,1,0:T(8,128)(2,1)S(1)}, u32[]{:S(2)}, u32[]{:S(2)}) collective-permute-start(bf16[1,32,128]{2,1,0:T(8,128)(2,1)S(1)} %bitcast.11), channel_id=1, source_target_pairs={{0,8},{2,10},{4,12},{6,14},{8,0},{10,2},{12,4},{14,6},{1,9},{3,11}... | collective-permute-start | bytes 24584 | tf_op jit(solution)/shard_map/ppermute | solution.py:264
  8.3 1.1 %copy-done.4 = bf16[24,128,128]{2,1,0:T(8,128)(2,1)S(1)} copy-done((bf16[24,128,128]{2,1,0:T(8,128)(2,1)S(1)}, bf16[24,128,128]{2,1,0:T(8,128)(2,1)}, u32[]{:S(2)}) %copy-start.4) | copy-done | bytes 786456
  9.4 3.7 %shard_map.128.dense_ref = bf16[1024,1024]{1,0:T(8,128)(2,1)S(1)} custom-call(s32[24,2]{1,0:T(8,128)S(1)} %copy.14.pattern_ref, bf16[24,128,128]{2,1,0:T(8,128)(2,1)S(1)} %copy-done.4), custom_call_target="tpu_custom_call" | custom-call | flops 134217728 | bytes 786624 | tf_op jit(solution)/shard_map/pallas_call | solution.py:22
  13.9 1.6 %collective-permute-start.1 = (bf16[2,32,128]{2,1,0:T(8,128)(2,1)S(1)}, bf16[2,32,128]{2,1,0:T(8,128)(2,1)S(1)}, u32[]{:S(2)}, u32[]{:S(2)}) collective-permute-start(bf16[2,32,128]{2,1,0:T(8,128)(2,1)S(1)} %pad_maximum_fusion.5), channel_id=1, source_target_pairs={{0,4},{2,6},{4,0},{6,2},{8,12},{10,14},{12,8},{14,10},{1,5},{3,7},... | collective-permute-start | bytes 49160 | tf_op jit(solution)/shard_map/ppermute | solution.py:264
  15.5 2.2 %collective-permute-done.1 = bf16[2,32,128]{2,1,0:T(8,128)(2,1)S(1)} collective-permute-done((bf16[2,32,128]{2,1,0:T(8,128)(2,1)S(1)}, bf16[2,32,128]{2,1,0:T(8,128)(2,1)S(1)}, u32[]{:S(2)}, u32[]{:S(2)}) %collective-permute-start.1) | collective-permute-done | bytes 16416 | tf_op jit(solution)/shard_map/ppermute | solution.py:264
  17.7 1.5 %collective-permute-start.2 = (bf16[4,32,128]{2,1,0:T(8,128)(2,1)S(1)}, bf16[4,32,128]{2,1,0:T(8,128)(2,1)S(1)}, u32[]{:S(2)}, u32[]{:S(2)}) collective-permute-start(bf16[4,32,128]{2,1,0:T(8,128)(2,1)S(1)} %pad_maximum_fusion.4), channel_id=1, source_target_pairs={{0,2},{2,0},{4,6},{6,4},{8,10},{10,8},{12,14},{14,12},{1,3},{3,1},... | collective-permute-start | bytes 98312 | tf_op jit(solution)/shard_map/ppermute | solution.py:264
  19.2 2.4 %collective-permute-done.2 = bf16[4,32,128]{2,1,0:T(8,128)(2,1)S(1)} collective-permute-done((bf16[4,32,128]{2,1,0:T(8,128)(2,1)S(1)}, bf16[4,32,128]{2,1,0:T(8,128)(2,1)S(1)}, u32[]{:S(2)}, u32[]{:S(2)}) %collective-permute-start.2) | collective-permute-done | bytes 32800 | tf_op jit(solution)/shard_map/ppermute | solution.py:264
  21.7 1.2 %collective-permute-done.3 = bf16[8,32,128]{2,1,0:T(8,128)(2,1)S(1)} collective-permute-done((bf16[8,32,128]{2,1,0:T(8,128)(2,1)S(1)}, bf16[8,32,128]{2,1,0:T(8,128)(2,1)S(1)}, u32[]{:S(2)}, u32[]{:S(2)}) %collective-permute-start.3) | collective-permute-done | bytes 65568 | tf_op jit(solution)/shard_map/ppermute | solution.py:264
  23.0 1.8 %shard_map.130 = (f32[64,1024]{1,0:T(8,128)S(1)}, f32[64,1024]{1,0:T(8,128)S(1)}, bf16[384,128]{1,0:T(8,128)(2,1)S(1)}, bf16[384,128]{1,0:T(8,128)(2,1)S(1)}, bf...) custom-call(s32[16]{0:T(128)S(1)} %fusion.2.place_ref, s32[1]{0:T(128)S(6)} %copy.24.count_ref, ...), custom_call_target="tpu_custom_call" | custom-call | flops 134217728 | bytes 3289156 | tf_op jit(solution)/shard_map/pallas_call | solution.py:22
  24.8 2.3 %collective-permute-start.4 = (bf16[384,128]{1,0:T(8,128)(2,1)S(1)}, bf16[384,128]{1,0:T(8,128)(2,1)S(1)}, u32[]{:S(2)}, u32[]{:S(2)}) collective-permute-start(bf16[384,128]{1,0:T(8,128)(2,1)S(1)} %get-tuple-element.26), channel_id=1, source_target_pairs={{0,14},{2,0},{4,2},{6,4},{8,6},{10,8},{12,10},{14,12},{1,15},{3,1}... | collective-permute-start | bytes 294920 | tf_op jit(solution)/shard_map/ppermute | solution.py:250
  27.2 1.1 %collective-permute-start.6 = (bf16[64,128]{1,0:T(8,128)(2,1)S(1)}, bf16[64,128]{1,0:T(8,128)(2,1)S(1)}, u32[]{:S(2)}, u32[]{:S(2)}) collective-permute-start(bf16[64,128]{1,0:T(8,128)(2,1)S(1)} %get-tuple-element.28.own_west_ref), channel_id=1, source_target_pairs={{0,12},{2,14},{4,0},{6,2},{8,4},{10,6},{12,8},{14,10},{1,13},{3,15... | collective-permute-start | bytes 49160 | tf_op jit(solution)/shard_map/ppermute | solution.py:250
  28.3 0.9 %collective-permute-start.7 = (bf16[64,128]{1,0:T(8,128)(2,1)S(1)}, bf16[64,128]{1,0:T(8,128)(2,1)S(1)}, u32[]{:S(2)}, u32[]{:S(2)}) collective-permute-start(bf16[64,128]{1,0:T(8,128)(2,1)S(1)} %get-tuple-element.29.own_east_ref), channel_id=1, source_target_pairs={{0,4},{2,6},{4,8},{6,10},{8,12},{10,14},{12,0},{14,2},{1,5},{3,7},... | collective-permute-start | bytes 49160 | tf_op jit(solution)/shard_map/ppermute | solution.py:250
  29.2 1.9 %collective-permute-done.6.beyond_east_ref = bf16[64,128]{1,0:T(8,128)(2,1)S(1)} collective-permute-done((bf16[64,128]{1,0:T(8,128)(2,1)S(1)}, bf16[64,128]{1,0:T(8,128)(2,1)S(1)}, u32[]{:S(2)}, u32[]{:S(2)}) %collective-permute-start.6) | collective-permute-done | bytes 16416 | tf_op jit(solution)/shard_map/ppermute | solution.py:250
  31.1 2.7 %collective-permute-done.7.beyond_west_ref = bf16[64,128]{1,0:T(8,128)(2,1)S(1)} collective-permute-done((bf16[64,128]{1,0:T(8,128)(2,1)S(1)}, bf16[64,128]{1,0:T(8,128)(2,1)S(1)}, u32[]{:S(2)}, u32[]{:S(2)}) %collective-permute-start.7) | collective-permute-done | bytes 16416 | tf_op jit(solution)/shard_map/ppermute | solution.py:250
  34.6 1.1 %shard_map.131 = (f32[64,1024]{1,0:T(8,128)S(1)}, f32[40,128]{1,0:T(8,128)S(1)}) custom-call(s32[1]{0:T(128)S(6)} %copy.24.count_ref, bf16[384,128]{1,0:T(8,128)(2,1)S(1)} %collective-permute-done.4.from_east_ref.corr_east_ref, bf16[384,128]{1,0:T(8,128)(2,1)S(1)} %collective-permute-done.5.from_west_ref.corr_west_ref, ...), custom_call_target="tpu_custom_call" | custom-call | flops 134217728 | bytes 3682308 | tf_op jit(solution)/shard_map/pallas_call | solution.py:22
  35.8 4.7 %collective-permute-done.8 = f32[1,40,128]{2,1,0:T(8,128)S(1)} collective-permute-done((f32[1,40,128]{2,1,0:T(8,128)S(1)}, f32[1,40,128]{2,1,0:T(8,128)S(1)}, u32[]{:S(2)}, u32[]{:S(2)}) %collective-permute-start.8) | collective-permute-done | bytes 20512 | tf_op jit(solution)/shard_map/ppermute | solution.py:264
  40.5 4.0 %collective-permute-done.9 = f32[2,40,128]{2,1,0:T(8,128)S(1)} collective-permute-done((f32[2,40,128]{2,1,0:T(8,128)S(1)}, f32[2,40,128]{2,1,0:T(8,128)S(1)}, u32[]{:S(2)}, u32[]{:S(2)}) %collective-permute-start.9) | collective-permute-done | bytes 40992 | tf_op jit(solution)/shard_map/ppermute | solution.py:264
  44.5 3.5 %collective-permute-start.10 = (f32[4,40,128]{2,1,0:T(8,128)S(1)}, f32[4,40,128]{2,1,0:T(8,128)S(1)}, u32[]{:S(2)}, u32[]{:S(2)}) collective-permute-start(f32[4,40,128]{2,1,0:T(8,128)S(1)} %pad_maximum_fusion.1), channel_id=1, source_target_pairs={{0,2},{2,0},{4,6},{6,4},{8,10},{10,8},{12,14},{14,12},{1,3},{3,1},... | collective-permute-start | bytes 245768 | tf_op jit(solution)/shard_map/ppermute | solution.py:264
  47.9 2.4 %collective-permute-done.10 = f32[4,40,128]{2,1,0:T(8,128)S(1)} collective-permute-done((f32[4,40,128]{2,1,0:T(8,128)S(1)}, f32[4,40,128]{2,1,0:T(8,128)S(1)}, u32[]{:S(2)}, u32[]{:S(2)}) %collective-permute-start.10) | collective-permute-done | bytes 81952 | tf_op jit(solution)/shard_map/ppermute | solution.py:264
  50.5 1.4 %collective-permute-done.11 = f32[8,40,128]{2,1,0:T(8,128)S(1)} collective-permute-done((f32[8,40,128]{2,1,0:T(8,128)S(1)}, f32[8,40,128]{2,1,0:T(8,128)S(1)}, u32[]{:S(2)}, u32[]{:S(2)}) %collective-permute-start.11) | collective-permute-done | bytes 163872 | tf_op jit(solution)/shard_map/ppermute | solution.py:264
  51.8 2.0 %shard_map.132 = (f32[64,1024]{1,0:T(8,128)S(1)}, f32[64,1024]{1,0:T(8,128)S(1)}, bf16[128,128]{1,0:T(8,128)(2,1)S(1)}, bf16[128,128]{1,0:T(8,128)(2,1)S(1)}, bf...) custom-call(s32[16]{0:T(128)S(1)} %fusion.2.place_ref, s32[1]{0:T(128)S(6)} %copy.24.count_ref, ...), custom_call_target="tpu_custom_call" | custom-call | flops 134217728 | bytes 3747908 | tf_op jit(solution)/shard_map/pallas_call | solution.py:22
  53.9 1.4 %collective-permute-start.12 = (bf16[128,128]{1,0:T(8,128)(2,1)S(1)}, bf16[128,128]{1,0:T(8,128)(2,1)S(1)}, u32[]{:S(2)}, u32[]{:S(2)}) collective-permute-start(bf16[128,128]{1,0:T(8,128)(2,1)S(1)} %get-tuple-element.35), channel_id=1, source_target_pairs={{0,14},{2,0},{4,2},{6,4},{8,6},{10,8},{12,10},{14,12},{1,15},{3,1}... | collective-permute-start | bytes 98312 | tf_op jit(solution)/shard_map/ppermute | solution.py:250
  56.7 1.3 %collective-permute-start.15 = (bf16[64,128]{1,0:T(8,128)(2,1)S(1)}, bf16[64,128]{1,0:T(8,128)(2,1)S(1)}, u32[]{:S(2)}, u32[]{:S(2)}) collective-permute-start(bf16[64,128]{1,0:T(8,128)(2,1)S(1)} %get-tuple-element.38.own_east_ref), channel_id=1, source_target_pairs={{0,4},{2,6},{4,8},{6,10},{8,12},{10,14},{12,0},{14,2},{1,5},{3,7},... | collective-permute-start | bytes 49160 | tf_op jit(solution)/shard_map/ppermute | solution.py:250
  58.0 1.7 %collective-permute-done.14.beyond_east_ref = bf16[64,128]{1,0:T(8,128)(2,1)S(1)} collective-permute-done((bf16[64,128]{1,0:T(8,128)(2,1)S(1)}, bf16[64,128]{1,0:T(8,128)(2,1)S(1)}, u32[]{:S(2)}, u32[]{:S(2)}) %collective-permute-start.14) | collective-permute-done | bytes 16416 | tf_op jit(solution)/shard_map/ppermute | solution.py:250
  59.8 2.5 %collective-permute-done.15.beyond_west_ref = bf16[64,128]{1,0:T(8,128)(2,1)S(1)} collective-permute-done((bf16[64,128]{1,0:T(8,128)(2,1)S(1)}, bf16[64,128]{1,0:T(8,128)(2,1)S(1)}, u32[]{:S(2)}, u32[]{:S(2)}) %collective-permute-start.15) | collective-permute-done | bytes 16416 | tf_op jit(solution)/shard_map/ppermute | solution.py:250
  62.3 1.0 %shard_map.133 = f32[8,128]{1,0:T(8,128)S(1)} custom-call(s32[1]{0:T(128)S(6)} %copy.24.count_ref, bf16[128,128]{1,0:T(8,128)(2,1)S(1)} %collective-permute-done.12.from_east_ref, bf16[128,128]{1,0:T(8,128)(2,1)S(1)} %collective-permute-done.13.from_west_ref, bf16[64,128]{1,0:T(8,128)(2,1)S(1)} %collective-permute-done.14.beyond_east_ref, ...), custom_call_target="tpu_custom_call" | custom-call | flops 134217728 | bytes 3751940 | tf_op jit(solution)/shard_map/pallas_call | solution.py:22
  63.7 4.2 %collective-permute-done.16 = f32[8,128]{1,0:T(8,128)S(1)} collective-permute-done((f32[8,128]{1,0:T(8,128)S(1)}, f32[8,128]{1,0:T(8,128)S(1)}, u32[]{:S(2)}, u32[]{:S(2)}) %collective-permute-start.16) | collective-permute-done | bytes 4128 | tf_op jit(solution)/shard_map/ppermute | solution.py:264
  67.8 3.6 %collective-permute-done.17 = f32[8,128]{1,0:T(8,128)S(1)} collective-permute-done((f32[8,128]{1,0:T(8,128)S(1)}, f32[8,128]{1,0:T(8,128)S(1)}, u32[]{:S(2)}, u32[]{:S(2)}) %collective-permute-start.17) | collective-permute-done | bytes 4128 | tf_op jit(solution)/shard_map/ppermute | solution.py:264
  71.5 3.8 %collective-permute-start.18 = (f32[8,128]{1,0:T(8,128)S(1)}, f32[8,128]{1,0:T(8,128)S(1)}, u32[]{:S(2)}, u32[]{:S(2)}) collective-permute-start(f32[8,128]{1,0:T(8,128)S(1)} %add.29), channel_id=1, source_target_pairs={{0,2},{2,0},{4,6},{6,4},{8,10},{10,8},{12,14},{14,12},{1,3},{3,1},... | collective-permute-start | bytes 12296 | tf_op jit(solution)/shard_map/ppermute | solution.py:264
  75.3 1.6 %collective-permute-done.18 = f32[8,128]{1,0:T(8,128)S(1)} collective-permute-done((f32[8,128]{1,0:T(8,128)S(1)}, f32[8,128]{1,0:T(8,128)S(1)}, u32[]{:S(2)}, u32[]{:S(2)}) %collective-permute-start.18) | collective-permute-done | bytes 4128 | tf_op jit(solution)/shard_map/ppermute | solution.py:264
  76.9 1.2 %collective-permute-done.19 = f32[8,128]{1,0:T(8,128)S(1)} collective-permute-done((f32[8,128]{1,0:T(8,128)S(1)}, f32[8,128]{1,0:T(8,128)S(1)}, u32[]{:S(2)}, u32[]{:S(2)}) %collective-permute-start.19) | collective-permute-done | bytes 4128 | tf_op jit(solution)/shard_map/ppermute | solution.py:264
  78.0 1.2 %shard_map.134 = f32[64,1024]{1,0:T(8,128)} custom-call(f32[8,128]{1,0:T(8,128)S(1)} %get-tuple-element.34.sums_ref, f32[8,128]{1,0:T(8,128)S(1)} %add.31.totals_ref, f32[64,1024]{1,0:T(8,128)S(1)} %get-tuple-element.30.z_ref.first_ref, f32[64,1024]{1,0:T(8,128)S(1)} %get-tuple-element.39.z_ref.second_ref), custom_call_target="tpu_custom_call" | custom-call | flops 262144 | bytes 532480 | tf_op jit(solution)/shard_map/pallas_call | solution.py:22
  (62 shorter events, 6.5 us)
Async XLA Ops:
  0.0 13.1 %copy-start.10 = (s32[1,128]{1,0:T(1,128)S(1)}, s32[1,128]{1,0:T(1,128)}, u32[]{:S(2)}) copy-start(s32[1,128]{1,0:T(1,128)} %east_ref.1) | copy-start | bytes 1540
  0.0 13.1 %copy-start.11 = (s32[1,128]{1,0:T(1,128)S(1)}, s32[1,128]{1,0:T(1,128)}, u32[]{:S(2)}) copy-start(s32[1,128]{1,0:T(1,128)} %west_ref.1) | copy-start | bytes 1540
  0.7 0.9 %copy-start = (bf16[64,1024]{1,0:T(8,128)(2,1)S(1)}, bf16[64,1024]{1,0:T(8,128)(2,1)}, u32[]{:S(2)}) copy-start(bf16[64,1024]{1,0:T(8,128)(2,1)} %right_ref.7) | copy-start | bytes 393220
  1.6 0.9 %copy-start.2 = (bf16[64,1024]{1,0:T(8,128)(2,1)S(1)}, bf16[64,1024]{1,0:T(8,128)(2,1)}, u32[]{:S(2)}) copy-start(bf16[64,1024]{1,0:T(8,128)(2,1)} %vectors_ref.7) | copy-start | bytes 393220
  2.5 10.7 %copy-start.6 = (f32[1024]{0:T(1024)S(1)}, f32[1024]{0:T(1024)}, u32[]{:S(2)}) copy-start(f32[1024]{0:T(1024)} %param.17) | copy-start | bytes 12292
  2.5 10.7 %copy-start.9 = (bf16[128,128]{1,0:T(8,128)(2,1)S(1)}, bf16[128,128]{1,0:T(8,128)(2,1)}, u32[]{:S(2)}) copy-start(bf16[128,128]{1,0:T(8,128)(2,1)} %coupling_ref.1) | copy-start | bytes 98308
  2.5 20.4 %copy-start.1 = (bf16[64,1024]{1,0:T(8,128)(2,1)S(1)}, bf16[64,1024]{1,0:T(8,128)(2,1)}, u32[]{:S(2)}) copy-start(bf16[64,1024]{1,0:T(8,128)(2,1)} %right_ref.7) | copy-start | bytes 393220
  2.5 20.4 %copy-start.3 = (bf16[64,1024]{1,0:T(8,128)(2,1)S(1)}, bf16[64,1024]{1,0:T(8,128)(2,1)}, u32[]{:S(2)}) copy-start(bf16[64,1024]{1,0:T(8,128)(2,1)} %vectors_ref.7) | copy-start | bytes 393220
  2.5 20.5 %copy-start.7 = (f32[1024]{0:T(1024)S(1)}, f32[1024]{0:T(1024)}, u32[]{:S(2)}) copy-start(f32[1024]{0:T(1024)} %param.16) | copy-start | bytes 12292
  2.5 20.5 %copy-start.8 = (f32[1024]{0:T(1024)S(1)}, f32[1024]{0:T(1024)}, u32[]{:S(2)}) copy-start(f32[1024]{0:T(1024)} %param.18) | copy-start | bytes 12292
  2.8 11.1 %collective-permute-start = (bf16[1,32,128]{2,1,0:T(8,128)(2,1)S(1)}, bf16[1,32,128]{2,1,0:T(8,128)(2,1)S(1)}, u32[]{:S(2)}, u32[]{:S(2)}) collective-permute-start(bf16[1,32,128]{2,1,0:T(8,128)(2,1)S(1)} %bitcast.11), channel_id=1, source_target_pairs={{0,8},{2,10},{4,12},{6,14},{8,0},{10,2},{12,4},{14,6},{1,9},{3,11}... | collective-permute-start | bytes 24584 | tf_op jit(solution)/shard_map/ppermute | solution.py:264
  8.2 1.1 %copy-start.4 = (bf16[24,128,128]{2,1,0:T(8,128)(2,1)S(1)}, bf16[24,128,128]{2,1,0:T(8,128)(2,1)}, u32[]{:S(2)}) copy-start(bf16[24,128,128]{2,1,0:T(8,128)(2,1)} %blocks_ref.1) | copy-start | bytes 2359300
  9.4 13.6 %copy-start.5 = (bf16[64,1024]{1,0:T(8,128)(2,1)S(1)}, bf16[64,1024]{1,0:T(8,128)(2,1)}, u32[]{:S(2)}) copy-start(bf16[64,1024]{1,0:T(8,128)(2,1)} %inverse_ref.3) | copy-start | bytes 393220
  13.9 3.8 %collective-permute-start.1 = (bf16[2,32,128]{2,1,0:T(8,128)(2,1)S(1)}, bf16[2,32,128]{2,1,0:T(8,128)(2,1)S(1)}, u32[]{:S(2)}, u32[]{:S(2)}) collective-permute-start(bf16[2,32,128]{2,1,0:T(8,128)(2,1)S(1)} %pad_maximum_fusion.5), channel_id=1, source_target_pairs={{0,4},{2,6},{4,0},{6,2},{8,12},{10,14},{12,8},{14,10},{1,5},{3,7},... | collective-permute-start | bytes 49160 | tf_op jit(solution)/shard_map/ppermute | solution.py:264
  17.7 3.9 %collective-permute-start.2 = (bf16[4,32,128]{2,1,0:T(8,128)(2,1)S(1)}, bf16[4,32,128]{2,1,0:T(8,128)(2,1)S(1)}, u32[]{:S(2)}, u32[]{:S(2)}) collective-permute-start(bf16[4,32,128]{2,1,0:T(8,128)(2,1)S(1)} %pad_maximum_fusion.4), channel_id=1, source_target_pairs={{0,2},{2,0},{4,6},{6,4},{8,10},{10,8},{12,14},{14,12},{1,3},{3,1},... | collective-permute-start | bytes 98312 | tf_op jit(solution)/shard_map/ppermute | solution.py:264
  21.6 1.3 %collective-permute-start.3 = (bf16[8,32,128]{2,1,0:T(8,128)(2,1)S(1)}, bf16[8,32,128]{2,1,0:T(8,128)(2,1)S(1)}, u32[]{:S(2)}, u32[]{:S(2)}) collective-permute-start(bf16[8,32,128]{2,1,0:T(8,128)(2,1)S(1)} %pad_maximum_fusion.2), channel_id=1, source_target_pairs={{0,1},{1,0},{2,3},{3,2},{4,5},{5,4},{6,7},{7,6},{8,9},{9,8},{10,11... | collective-permute-start | bytes 196616 | tf_op jit(solution)/shard_map/ppermute | solution.py:264
  24.8 9.0 %collective-permute-start.4 = (bf16[384,128]{1,0:T(8,128)(2,1)S(1)}, bf16[384,128]{1,0:T(8,128)(2,1)S(1)}, u32[]{:S(2)}, u32[]{:S(2)}) collective-permute-start(bf16[384,128]{1,0:T(8,128)(2,1)S(1)} %get-tuple-element.26), channel_id=1, source_target_pairs={{0,14},{2,0},{4,2},{6,4},{8,6},{10,8},{12,10},{14,12},{1,15},{3,1}... | collective-permute-start | bytes 294920 | tf_op jit(solution)/shard_map/ppermute | solution.py:250
  27.2 7.5 %collective-permute-start.5 = (bf16[384,128]{1,0:T(8,128)(2,1)S(1)}, bf16[384,128]{1,0:T(8,128)(2,1)S(1)}, u32[]{:S(2)}, u32[]{:S(2)}) collective-permute-start(bf16[384,128]{1,0:T(8,128)(2,1)S(1)} %get-tuple-element.27), channel_id=1, source_target_pairs={{0,2},{2,4},{4,6},{6,8},{8,10},{10,12},{12,14},{14,0},{1,3},{3,5},... | collective-permute-start | bytes 294920 | tf_op jit(solution)/shard_map/ppermute | solution.py:250
  27.2 3.9 %collective-permute-start.6 = (bf16[64,128]{1,0:T(8,128)(2,1)S(1)}, bf16[64,128]{1,0:T(8,128)(2,1)S(1)}, u32[]{:S(2)}, u32[]{:S(2)}) collective-permute-start(bf16[64,128]{1,0:T(8,128)(2,1)S(1)} %get-tuple-element.28.own_west_ref), channel_id=1, source_target_pairs={{0,12},{2,14},{4,0},{6,2},{8,4},{10,6},{12,8},{14,10},{1,13},{3,15... | collective-permute-start | bytes 49160 | tf_op jit(solution)/shard_map/ppermute | solution.py:250
  28.3 5.5 %collective-permute-start.7 = (bf16[64,128]{1,0:T(8,128)(2,1)S(1)}, bf16[64,128]{1,0:T(8,128)(2,1)S(1)}, u32[]{:S(2)}, u32[]{:S(2)}) collective-permute-start(bf16[64,128]{1,0:T(8,128)(2,1)S(1)} %get-tuple-element.29.own_east_ref), channel_id=1, source_target_pairs={{0,4},{2,6},{4,8},{6,10},{8,12},{10,14},{12,0},{14,2},{1,5},{3,7},... | collective-permute-start | bytes 49160 | tf_op jit(solution)/shard_map/ppermute | solution.py:250
  35.7 4.7 %collective-permute-start.8 = (f32[1,40,128]{2,1,0:T(8,128)S(1)}, f32[1,40,128]{2,1,0:T(8,128)S(1)}, u32[]{:S(2)}, u32[]{:S(2)}) collective-permute-start(f32[1,40,128]{2,1,0:T(8,128)S(1)} %bitcast.7), channel_id=1, source_target_pairs={{0,8},{2,10},{4,12},{6,14},{8,0},{10,2},{12,4},{14,6},{1,9},{3,11}... | collective-permute-start | bytes 61448 | tf_op jit(solution)/shard_map/ppermute | solution.py:264
  40.5 4.0 %collective-permute-start.9 = (f32[2,40,128]{2,1,0:T(8,128)S(1)}, f32[2,40,128]{2,1,0:T(8,128)S(1)}, u32[]{:S(2)}, u32[]{:S(2)}) collective-permute-start(f32[2,40,128]{2,1,0:T(8,128)S(1)} %pad_maximum_fusion.3), channel_id=1, source_target_pairs={{0,4},{2,6},{4,0},{6,2},{8,12},{10,14},{12,8},{14,10},{1,5},{3,7},... | collective-permute-start | bytes 122888 | tf_op jit(solution)/shard_map/ppermute | solution.py:264
  44.5 5.9 %collective-permute-start.10 = (f32[4,40,128]{2,1,0:T(8,128)S(1)}, f32[4,40,128]{2,1,0:T(8,128)S(1)}, u32[]{:S(2)}, u32[]{:S(2)}) collective-permute-start(f32[4,40,128]{2,1,0:T(8,128)S(1)} %pad_maximum_fusion.1), channel_id=1, source_target_pairs={{0,2},{2,0},{4,6},{6,4},{8,10},{10,8},{12,14},{14,12},{1,3},{3,1},... | collective-permute-start | bytes 245768 | tf_op jit(solution)/shard_map/ppermute | solution.py:264
  50.4 1.5 %collective-permute-start.11 = (f32[8,40,128]{2,1,0:T(8,128)S(1)}, f32[8,40,128]{2,1,0:T(8,128)S(1)}, u32[]{:S(2)}, u32[]{:S(2)}) collective-permute-start(f32[8,40,128]{2,1,0:T(8,128)S(1)} %pad_maximum_fusion), channel_id=1, source_target_pairs={{0,1},{1,0},{2,3},{3,2},{4,5},{5,4},{6,7},{7,6},{8,9},{9,8},{10,11... | collective-permute-start | bytes 491528 | tf_op jit(solution)/shard_map/ppermute | solution.py:264
  53.9 8.4 %collective-permute-start.12 = (bf16[128,128]{1,0:T(8,128)(2,1)S(1)}, bf16[128,128]{1,0:T(8,128)(2,1)S(1)}, u32[]{:S(2)}, u32[]{:S(2)}) collective-permute-start(bf16[128,128]{1,0:T(8,128)(2,1)S(1)} %get-tuple-element.35), channel_id=1, source_target_pairs={{0,14},{2,0},{4,2},{6,4},{8,6},{10,8},{12,10},{14,12},{1,15},{3,1}... | collective-permute-start | bytes 98312 | tf_op jit(solution)/shard_map/ppermute | solution.py:250
  55.3 7.0 %collective-permute-start.13 = (bf16[128,128]{1,0:T(8,128)(2,1)S(1)}, bf16[128,128]{1,0:T(8,128)(2,1)S(1)}, u32[]{:S(2)}, u32[]{:S(2)}) collective-permute-start(bf16[128,128]{1,0:T(8,128)(2,1)S(1)} %get-tuple-element.36), channel_id=1, source_target_pairs={{0,2},{2,4},{4,6},{6,8},{8,10},{10,12},{12,14},{14,0},{1,3},{3,5},... | collective-permute-start | bytes 98312 | tf_op jit(solution)/shard_map/ppermute | solution.py:250
  56.0 3.7 %collective-permute-start.14 = (bf16[64,128]{1,0:T(8,128)(2,1)S(1)}, bf16[64,128]{1,0:T(8,128)(2,1)S(1)}, u32[]{:S(2)}, u32[]{:S(2)}) collective-permute-start(bf16[64,128]{1,0:T(8,128)(2,1)S(1)} %get-tuple-element.37.own_west_ref), channel_id=1, source_target_pairs={{0,12},{2,14},{4,0},{6,2},{8,4},{10,6},{12,8},{14,10},{1,13},{3,15... | collective-permute-start | bytes 49160 | tf_op jit(solution)/shard_map/ppermute | solution.py:250
  56.7 5.5 %collective-permute-start.15 = (bf16[64,128]{1,0:T(8,128)(2,1)S(1)}, bf16[64,128]{1,0:T(8,128)(2,1)S(1)}, u32[]{:S(2)}, u32[]{:S(2)}) collective-permute-start(bf16[64,128]{1,0:T(8,128)(2,1)S(1)} %get-tuple-element.38.own_east_ref), channel_id=1, source_target_pairs={{0,4},{2,6},{4,8},{6,10},{8,12},{10,14},{12,0},{14,2},{1,5},{3,7},... | collective-permute-start | bytes 49160 | tf_op jit(solution)/shard_map/ppermute | solution.py:250
  63.3 4.5 %collective-permute-start.16 = (f32[8,128]{1,0:T(8,128)S(1)}, f32[8,128]{1,0:T(8,128)S(1)}, u32[]{:S(2)}, u32[]{:S(2)}) collective-permute-start(f32[8,128]{1,0:T(8,128)S(1)} %shard_map.133), channel_id=1, source_target_pairs={{0,8},{2,10},{4,12},{6,14},{8,0},{10,2},{12,4},{14,6},{1,9},{3,11}... | collective-permute-start | bytes 12296 | tf_op jit(solution)/shard_map/ppermute | solution.py:264
  67.8 3.6 %collective-permute-start.17 = (f32[8,128]{1,0:T(8,128)S(1)}, f32[8,128]{1,0:T(8,128)S(1)}, u32[]{:S(2)}, u32[]{:S(2)}) collective-permute-start(f32[8,128]{1,0:T(8,128)S(1)} %add.28), channel_id=1, source_target_pairs={{0,4},{2,6},{4,0},{6,2},{8,12},{10,14},{12,8},{14,10},{1,5},{3,7},... | collective-permute-start | bytes 12296 | tf_op jit(solution)/shard_map/ppermute | solution.py:264
  71.5 5.4 %collective-permute-start.18 = (f32[8,128]{1,0:T(8,128)S(1)}, f32[8,128]{1,0:T(8,128)S(1)}, u32[]{:S(2)}, u32[]{:S(2)}) collective-permute-start(f32[8,128]{1,0:T(8,128)S(1)} %add.29), channel_id=1, source_target_pairs={{0,2},{2,0},{4,6},{6,4},{8,10},{10,8},{12,14},{14,12},{1,3},{3,1},... | collective-permute-start | bytes 12296 | tf_op jit(solution)/shard_map/ppermute | solution.py:264
  76.9 1.2 %collective-permute-start.19 = (f32[8,128]{1,0:T(8,128)S(1)}, f32[8,128]{1,0:T(8,128)S(1)}, u32[]{:S(2)}, u32[]{:S(2)}) collective-permute-start(f32[8,128]{1,0:T(8,128)S(1)} %add.30), channel_id=1, source_target_pairs={{0,1},{1,0},{2,3},{3,2},{4,5},{5,4},{6,7},{7,6},{8,9},{9,8},{10,11... | collective-permute-start | bytes 12296 | tf_op jit(solution)/shard_map/ppermute | solution.py:264

commit v3 on v2

v3 whole, which is shorter than its diff:
```python
import jax
import jax.numpy as jnp
import numpy as np
from jax import lax
from jax.experimental import pallas as pl
from jax.experimental.pallas import tpu as pltpu
from jax.sharding import PartitionSpec as P

F32 = jnp.float32
BF16 = jnp.bfloat16
VMEM = pl.BlockSpec(memory_space=pltpu.VMEM)
SMEM = pl.BlockSpec(memory_space=pltpu.SMEM)
HBM = pl.BlockSpec(memory_space=pltpu.HBM)
LANES = 128


def dot(a, b, ca=1, cb=0):
    return lax.dot_general(a, b, (((ca,), (cb,)), ((), ())), preferred_element_type=F32)


def call(kernel, outs, specs, args, flops, scratch=()):
    moved = sum(int(np.prod(a.shape)) * a.dtype.itemsize for a in args)
    return pl.pallas_call(
        kernel,
        out_shape=[jax.ShapeDtypeStruct(s, t) for s, t in outs],
        in_specs=specs,
        out_specs=[VMEM] * len(outs),
        scratch_shapes=list(scratch),
        compiler_params=pltpu.CompilerParams(vmem_limit_bytes=32 * 1024 * 1024),
        cost_estimate=pl.CostEstimate(flops=flops, bytes_accessed=moved, transcendentals=0),
    )(*args)


def active_of(count_ref, nodes):
    return (lax.broadcasted_iota(jnp.int32, (1, nodes), 1) < count_ref[0]).astype(F32)


def fold(values):
    half = values.shape[0] // 2
    return jnp.concatenate([values[:half], values[half:]], axis=1)


def column_of(row):
    return jnp.transpose(jnp.broadcast_to(row, (LANES, LANES)))[:, 0:1]


def row_of(first, second):
    both = jnp.concatenate([first, second], axis=0)
    return jnp.transpose(jnp.broadcast_to(both, (LANES, LANES)))[0:1]


def row_sum(first, second):
    return jnp.sum(first * second, axis=1, keepdims=True)


def coarse_kernel(count_ref, right_hbm, vectors_hbm, chunks_ref, right_ref, vectors_ref, sems):
    copies = [
        pltpu.make_async_copy(right_hbm, right_ref, sems.at[0]),
        pltpu.make_async_copy(vectors_hbm, vectors_ref, sems.at[1]),
    ]
    for copy in copies:
        copy.start()
    for copy in copies:
        copy.wait()
    active = active_of(count_ref, right_ref.shape[1]).astype(BF16)
    coarse = fold(dot(vectors_ref[...], right_ref[...] * active, 1, 1)).astype(BF16)
    chunks_ref[...] = jnp.broadcast_to(coarse[None], chunks_ref.shape)


def dense_kernel(pattern_ref, blocks_ref, dense_ref, total_ref):
    count, block, _ = blocks_ref.shape
    nodes = dense_ref.shape[0]

    def clear(i, carry):
        total_ref[pl.ds(pl.multiple_of(i * block, block), block), :] = jnp.zeros((block, nodes), F32)
        return carry

    lax.fori_loop(0, nodes // block, clear, 0)

    def place(k, carry):
        rows = pl.ds(pl.multiple_of(pattern_ref[k, 0] * block, block), block)
        cols = pl.ds(pl.multiple_of(pattern_ref[k, 1] * block, block), block)
        values = blocks_ref[k].astype(F32)
        total_ref[rows, cols] += values
        total_ref[cols, rows] += jnp.transpose(values)
        return carry

    lax.fori_loop(0, count, place, 0)

    def narrow(i, carry):
        rows = pl.ds(pl.multiple_of(i * block, block), block)
        dense_ref[rows, :] = total_ref[rows, :].astype(BF16)
        return carry

    lax.fori_loop(0, nodes // block, narrow, 0)


def edge_kernel(iface_ref, coupling_ref, east_ref, west_ref, mass_ref, edge_ref, to_west_ref, to_east_ref):
    slots = coupling_ref.shape[0]
    nodes = mass_ref.shape[1]
    live_a = lax.broadcasted_iota(jnp.int32, (slots, slots), 0) < iface_ref[0]
    live_b = lax.broadcasted_iota(jnp.int32, (slots, slots), 1) < iface_ref[0]
    link = jnp.where(live_a & live_b, coupling_ref[...], jnp.zeros((slots, slots), BF16))
    node = lax.broadcasted_iota(jnp.int32, (slots, nodes), 1).astype(F32)
    east = column_of(east_ref[...].astype(F32))
    west = column_of(west_ref[...].astype(F32))
    east_hot = jnp.where(node == east, 1.0, 0.0).astype(BF16)
    west_hot = jnp.where(node == west, 1.0, 0.0).astype(BF16)
    spread = dot(link, east_hot, 0, 0).astype(BF16)
    edge_ref[0:slots, :] = spread
    edge_ref[slots : 2 * slots, :] = west_hot
    edges = edge_ref[...]
    scaled = (edges.astype(F32) * (1.0 / mass_ref[...])).astype(BF16)
    both = dot(scaled, edges, 1, 1).astype(BF16)
    to_east_ref[...] = both[:, 0:slots]
    to_west_ref[...] = both[:, slots:]


def unfold(count, piece, coarse_ref):
    half = coarse_ref.shape[0] // count // 2

    def move(d, carry):
        values = piece(d)
        at = pl.multiple_of(d * 2 * half, 2 * half)
        coarse_ref[pl.ds(at, half), :] = values[:, 0 : LANES // 2]
        coarse_ref[pl.ds(at + half, half), :] = values[:, LANES // 2 :]
        return carry

    lax.fori_loop(0, count, move, 0, unroll=min(count, 16))


def smooth(field, coarse_ref, inverse_ref, vectors_ref, react, mass, obs, active):
    fix = dot(inverse_ref[...], coarse_ref[...]).astype(BF16)
    spread = dot(fix, vectors_ref[...], 0, 0)
    return active * (field / (obs + react * react / mass) + spread)


def start_kernel(at_ref, count_ref, pieces_ref, inverse_ref, right_ref, vectors_ref, dense_ref, edge_ref,
                 react_ref, mass_ref, obs_ref, to_west_ref, to_east_ref,
                 z_ref, scaled_ref, near_ref, across_ref, far_ref, beyond_ref, coarse_ref):
    samples, nodes = right_ref.shape
    unfold(pieces_ref.shape[0], lambda d: pieces_ref[d], coarse_ref)
    active = active_of(count_ref, nodes)
    react, mass = react_ref[...], mass_ref[...]
    z = smooth(active * right_ref[...].astype(F32), coarse_ref, inverse_ref, vectors_ref, react, mass, obs_ref[...],
               active)
    z_ref[...] = z
    w = z.astype(BF16)
    edges = edge_ref[...]
    scaled = (dot(w, dense_ref[...]) + react * z) / mass
    scaled_ref[...] = scaled
    level1 = dot(w, edges, 1, 1).astype(BF16)
    level2 = dot(scaled.astype(BF16), edges, 1, 1).astype(BF16)
    slots = edges.shape[0] // 2

    def send(east_ref, west_ref):
        for ref, cols, corr_ref in (
            (east_ref, slice(0, slots), to_east_ref),
            (west_ref, slice(slots, 2 * slots), to_west_ref),
        ):
            ref[0:samples, :] = level1[:, cols]
            ref[samples : 2 * samples, :] = level2[:, cols]
            ref[2 * samples :, :] = corr_ref[...]

    def send_far(east_ref, west_ref):
        east_ref[...] = level1[:, 0:slots]
        west_ref[...] = level1[:, slots:]

    pl.when(at_ref[0] == 0)(lambda: send(near_ref, across_ref))
    pl.when(at_ref[0] == 1)(lambda: send(across_ref, near_ref))
    pl.when(at_ref[1] == 0)(lambda: send_far(far_ref, beyond_ref))
    pl.when(at_ref[1] == 1)(lambda: send_far(beyond_ref, far_ref))


def pick(flag, first_ref, second_ref):
    first, second = first_ref[...].astype(F32), second_ref[...].astype(F32)
    keep = jnp.full((1, 1), flag, jnp.int32) == 0
    return jnp.where(keep, first, second).astype(BF16), jnp.where(keep, second, first).astype(BF16)


def image_kernel(at_ref, count_ref, near_ref, across_ref, far_ref, beyond_ref, own_far_ref, own_beyond_ref,
                 z_ref, scaled_ref, dense_ref, edge_ref, react_ref, mass_ref, obs_ref, right_ref, vectors_ref,
                 image_ref, chunks_ref):
    samples, nodes = z_ref.shape
    active = active_of(count_ref, nodes)
    z = z_ref[...]
    edges = edge_ref[...]
    from_east, from_west = pick(at_ref[0], near_ref, across_ref)
    beyond_east, beyond_west = pick(at_ref[1], far_ref, beyond_ref)
    own_east, own_west = pick(at_ref[1], own_far_ref, own_beyond_ref)
    arrived = jnp.concatenate([from_east[0:samples], from_west[0:samples]], axis=1)
    inner = scaled_ref[...] + dot(arrived, edges) / mass_ref[...]
    east_terms = jnp.concatenate([beyond_east, own_east], axis=1)
    west_terms = jnp.concatenate([own_west, beyond_west], axis=1)
    second_east = from_east[samples : 2 * samples].astype(F32) + dot(east_terms, from_east[2 * samples :])
    second_west = from_west[samples : 2 * samples].astype(F32) + dot(west_terms, from_west[2 * samples :])
    arrived2 = jnp.concatenate([second_east, second_west], axis=1).astype(BF16)
    stiff = dot(inner.astype(BF16), dense_ref[...]) + dot(arrived2, edges) + react_ref[...] * inner
    image = active * (stiff + obs_ref[...] * z)
    image_ref[...] = image
    coarse = fold(dot(vectors_ref[...], image.astype(BF16), 1, 1))
    half = coarse.shape[0]
    sums = row_of(row_sum(active * right_ref[...].astype(F32), z), row_sum(z, image))
    count, rows, _ = chunks_ref.shape
    chunks_ref[:, 0:half, :] = jnp.broadcast_to(coarse[None], (count, half, LANES))
    chunks_ref[:, half:, :] = jnp.broadcast_to(sums[None], (count, rows - half, LANES))


def middle_kernel(at_ref, count_ref, pieces_ref, second_ref, inverse_ref, right_ref, image_ref, vectors_ref,
                  dense_ref, edge_ref, react_ref, mass_ref, obs_ref,
                  z_ref, scaled_ref, near_ref, across_ref, sums_ref, coarse_ref):
    samples, nodes = right_ref.shape
    count, half, _ = pieces_ref.shape

    def add(d, total):
        return total + second_ref[d, half : half + 1, :]

    sums = lax.fori_loop(0, count, add, jnp.zeros((1, LANES), F32), unroll=min(count, 16))
    step = sums[:, 0 : LANES // 2] / sums[:, LANES // 2 :]
    step = jnp.concatenate([step, step], axis=1)

    def piece(d):
        return (pieces_ref[d].astype(F32) - step * second_ref[d, 0:half, :]).astype(BF16)

    unfold(count, piece, coarse_ref)
    active = active_of(count_ref, nodes)
    react, mass = react_ref[...], mass_ref[...]
    image = image_ref[...]
    residual = active * right_ref[...].astype(F32) - column_of(step)[0:samples] * image
    z = smooth(residual, coarse_ref, inverse_ref, vectors_ref, react, mass, obs_ref[...], active)
    z_ref[...] = z
    w = z.astype(BF16)
    level1 = dot(w, edge_ref[...], 1, 1).astype(BF16)
    slots = edge_ref.shape[0] // 2

    def send(east_ref, west_ref):
        east_ref[...] = level1[:, 0:slots]
        west_ref[...] = level1[:, slots:]

    pl.when(at_ref[0] == 0)(lambda: send(near_ref, across_ref))
    pl.when(at_ref[0] == 1)(lambda: send(across_ref, near_ref))
    scaled_ref[...] = dot(w, dense_ref[...]) + react * z
    products = row_of(row_sum(residual, z), row_sum(z, image))
    row = lax.broadcasted_iota(jnp.int32, (8, LANES), 0)
    sums_ref[...] = jnp.where(row == 0, products, sums)


def last_kernel(at_ref, near_ref, across_ref, z_ref, scaled_ref, edge_ref, mass_ref, obs_ref, sums_ref, chunks_ref):
    z = z_ref[...]
    from_east, from_west = pick(at_ref[0], near_ref, across_ref)
    stiff = scaled_ref[...] + dot(jnp.concatenate([from_east, from_west], axis=1), edge_ref[...])
    curve = jnp.sum(stiff * stiff / mass_ref[...] + obs_ref[...] * z * z, axis=1, keepdims=True)
    row = lax.broadcasted_iota(jnp.int32, (8, LANES), 0)
    chunk = jnp.where(row == 0, sums_ref[0:1, :], row_of(curve, curve))
    chunks_ref[...] = jnp.broadcast_to(chunk[None], chunks_ref.shape)


def finish_kernel(sums_ref, chunks_ref, first_ref, second_ref, out_ref):
    samples = first_ref.shape[0]
    half = LANES // 2
    totals = jnp.sum(chunks_ref[...], axis=0)
    norm0, curve0 = sums_ref[1:2, 0:half], sums_ref[1:2, half:]
    norm1, cross = totals[0:1, 0:half], totals[0:1, half:]
    curve = totals[1:2, 0:half]
    beta = norm1 / norm0
    step0 = norm0 / curve0
    step1 = norm1 / (curve + beta * (2.0 * cross + beta * curve0))
    scales = column_of(jnp.concatenate([step0 + step1 * beta, step1], axis=1))
    out_ref[...] = scales[0:samples] * first_ref[...] + scales[samples : 2 * samples] * second_ref[...]


def exchange(chunks):
    return lax.all_to_all(chunks, ("lon", "lat"), split_axis=0, concat_axis=0, tiled=True)


def swap(array, reach, inner):
    size = lax.axis_size("lon")
    pairs = []
    for i in range(size):
        up = (i // reach) % 2 == (0 if inner else 1)
        pairs.append((i, (i + (reach if up else -reach)) % size))
    return lax.ppermute(array, "lon", pairs)


def body(
    right_side,
    stiffness_blocks,
    block_pattern,
    reaction,
    lumped_mass,
    obs_precision,
    coupling,
    east_rows,
    west_rows,
    iface_count,
    node_count,
    deflation,
    coarse_inverse,
):
    samples, nodes = right_side.shape
    slots = coupling.shape[0]
    vectors = deflation.shape[0]
    domains = lax.axis_size("lon") * lax.axis_size("lat")
    half = vectors // 2
    react, mass, obs = reaction[None], lumped_mass[None], obs_precision[None]
    field = ((samples, nodes), F32)
    coarse_scratch = pltpu.VMEM((domains * vectors, samples), BF16)
    apply_cost = 2 * samples * nodes * nodes
    lon = lax.axis_index("lon")
    at = jnp.stack([lon % 2, (lon // 2) % 2]).astype(jnp.int32)

    (chunks,) = call(
        coarse_kernel,
        [((domains, half, LANES), BF16)],
        [SMEM, HBM, HBM],
        (node_count, right_side, deflation),
        2 * samples * vectors * nodes,
        [pltpu.VMEM((samples, nodes), BF16), pltpu.VMEM((vectors, nodes), BF16), pltpu.SemaphoreType.DMA((2,))],
    )
    edge, corr_west, corr_east = call(
        edge_kernel,
        [((2 * slots, nodes), BF16), ((2 * slots, slots), BF16), ((2 * slots, slots), BF16)],
        [SMEM, VMEM, VMEM, VMEM, VMEM],
        (iface_count, coupling, east_rows, west_rows, mass),
        8 * slots * slots * nodes,
    )
    (dense,) = call(dense_kernel, [((nodes, nodes), BF16)], [SMEM, VMEM], (block_pattern, stiffness_blocks),
                    apply_cost, [pltpu.VMEM((nodes, nodes), F32)])

    pieces = exchange(chunks)
    z0, scaled, near, across, far, beyond = call(
        start_kernel,
        [field] * 2 + [((2 * samples + 2 * slots, slots), BF16)] * 2 + [((samples, slots), BF16)] * 2,
        [SMEM, SMEM] + [VMEM] * 11,
        (at, node_count, pieces, coarse_inverse, right_side, deflation, dense, edge, react, mass, obs,
         corr_west, corr_east),
        apply_cost,
        [coarse_scratch],
    )
    across = swap(across, 1, False)
    got_beyond = swap(beyond, 2, False)
    got_far = swap(far, 2, True)
    near = swap(near, 1, True)
    image, chunks = call(
        image_kernel,
        [field, ((domains, half + 8, LANES), F32)],
        [SMEM, SMEM] + [VMEM] * 15,
        (at, node_count, near, across, got_far, got_beyond, far, beyond, z0, scaled, dense, edge,
         react, mass, obs, right_side, deflation),
        apply_cost,
    )
    second = exchange(chunks)
    z1, scaled, near, across, sums = call(
        middle_kernel,
        [field] * 2 + [((samples, slots), BF16)] * 2 + [((8, LANES), F32)],
        [SMEM, SMEM] + [VMEM] * 11,
        (at, node_count, pieces, second, coarse_inverse, right_side, image, deflation, dense, edge, react, mass, obs),
        apply_cost,
        [coarse_scratch],
    )
    across = swap(across, 1, False)
    near = swap(near, 1, True)
    (chunks,) = call(
        last_kernel,
        [((domains, 8, LANES), F32)],
        [SMEM] + [VMEM] * 8,
        (at, near, across, z1, scaled, edge, mass, obs, sums),
        apply_cost,
    )
    totals = exchange(chunks)
    (out,) = call(finish_kernel, [field], [VMEM] * 4, (sums, totals, z0, z1), 4 * samples * nodes)
    return out


def solution(mesh):
    placed = (
        P(None, ("grp", "lon", "lat")),
        P(("grp", "lon", "lat"), None, None),
        P(("grp", "lon", "lat"), None),
        P(("grp", "lon", "lat")),
        P(("grp", "lon", "lat")),
        P(("grp", "lon", "lat")),
        P(("grp", "lon", "lat"), None),
        P(("grp", "lon", "lat"), None),
        P(("grp", "lon", "lat"), None),
        P(("grp", "lon", "lat")),
        P(("grp", "lon", "lat")),
        P(None, ("grp", "lon", "lat")),
        P(("grp", "lon", "lat"), None),
    )
    return jax.shard_map(
        body, mesh=mesh, in_specs=placed, out_specs=P(None, ("grp", "lon", "lat")), check_vma=False
    )
```

time: 79.4 us -> 69.6 us (0.88)
  waiting for transfers between devices: 38.4 us -> 9.19 us
  blocking collectives: 0 us -> 25.8 us
  starting transfers between devices: 23.6 us -> 15.5 us
  Pallas kernels: 11.7 us -> 13.4 us
    ppermute x20 -> x6, waiting for transfers between devices: 38.4 us -> 8.37 us  [swap(): return lax.ppermute(array, 'lon', pairs)]
    all_to_all x0 -> x2, blocking collectives: none -> 25.8 us  [exchange(): lax.all_to_all(chunks, ('lon', 'lat'), split_axis=0, concat_axis=0, tiled...]
    ppermute x20 -> x6, starting transfers between devices: 23.6 us -> 8.17 us  [swap(): return lax.ppermute(array, 'lon', pairs)]
    all_to_all x0 -> x1, starting transfers between devices: none -> 7.37 us  [exchange(): lax.all_to_all(chunks, ('lon', 'lat'), split_axis=0, concat_axis=0, tiled...]
    pallas_call x8, Pallas kernels: 11.7 us -> 13.4 us  [call(): pl.pallas_call(kernel, out_shape=[jax.ShapeDtypeStruct(s, t) for s, t in...]
    all_to_all x0 -> x1, waiting for transfers between devices: none -> 0.82 us  [exchange(): lax.all_to_all(chunks, ('lon', 'lat'), split_axis=0, concat_axis=0, tiled...]
    unnamed x33 -> x25, local copies, waits for them, and re-layouts: 3.77 us -> 3.73 us
  transfers between devices with their start and end apart: 20 -> 7, of which waited for: 16 -> 5; matrix products, arithmetic and copies ran while one was open for 1% -> 1% of each run, Pallas kernels for 6% -> 6%
where the time goes in v3:
time: 69.6 us; the launch traced here: 69.2 us
  blocking collectives  25.8 us (37%)
  starting transfers between devices  15.5 us (22%)
  Pallas kernels  13.4 us (19%)
  waiting for transfers between devices  9.19 us (13%)
  local copies, waits for them, and re-layouts  3.73 us (5%)
  between operations  1.52 us (2%)
    all_to_all x2, blocking collectives, exchange(): lax.all_to_all(chunks, ('lon', 'lat'), split_axis=0, concat_axis=0, tiled...  25.8 us
    pallas_call x8, Pallas kernels, call(): pl.pallas_call(kernel, out_shape=[jax.ShapeDtypeStruct(s, t) for s, t in...  13.4 us
    ppermute x6, waiting for transfers between devices, swap(): return lax.ppermute(array, 'lon', pairs)  8.37 us
    ppermute x6, starting transfers between devices, swap(): return lax.ppermute(array, 'lon', pairs)  8.17 us
    all_to_all x1, starting transfers between devices, exchange(): lax.all_to_all(chunks, ('lon', 'lat'), split_axis=0, concat_axis=0, tiled...  7.37 us
    unnamed x25, local copies, waits for them, and re-layouts  3.73 us
  transfers between devices with their start and end apart: 7, of which 5 were waited for; matrix products, arithmetic and copies ran while one was open for 1% of the time, Pallas kernels for 6%

profile of v3, /device:TPU:0, one launch (start us, length us, event | category | flops | bytes accessed | tf_op | source)
XLA Modules:
  0.0 69.2 jit_solution(6087656988372759506)
XLA Ops:
  0.7 0.9 %copy-done = bf16[64,1024]{1,0:T(8,128)(2,1)S(1)} copy-done((bf16[64,1024]{1,0:T(8,128)(2,1)S(1)}, bf16[64,1024]{1,0:T(8,128)(2,1)}, u32[]{:S(2)}) %copy-start) | copy-done | bytes 131096
  1.6 0.9 %copy-done.2 = bf16[64,1024]{1,0:T(8,128)(2,1)S(1)} copy-done((bf16[64,1024]{1,0:T(8,128)(2,1)S(1)}, bf16[64,1024]{1,0:T(8,128)(2,1)}, u32[]{:S(2)}) %copy-start.2) | copy-done | bytes 131096
  2.5 1.3 %shard_map.127 = bf16[16,32,128]{2,1,0:T(8,128)(2,1)} custom-call(s32[1]{0:T(128)S(6)} %copy.16.count_ref, bf16[64,1024]{1,0:T(8,128)(2,1)S(1)} %copy-done, bf16[64,1024]{1,0:T(8,128)(2,1)S(1)} %copy-done.2), custom_call_target="tpu_custom_call" | custom-call | flops 8388608 | bytes 262148 | tf_op jit(solution)/shard_map/pallas_call | solution.py:23
  3.8 7.4 %all-to-all-start = ((bf16[16,32,128]{2,1,0:T(8,128)(2,1)}), bf16[16,32,128]{2,1,0:T(8,128)(2,1)S(1)}, u32[]{:S(2)}, u32[]{:S(2)}) async-start(bf16[16,32,128]{2,1,0:T(8,128)(2,1)} %shard_map.127), calls=%async_computation | async-start | bytes 262144 | tf_op jit(solution)/shard_map/all_to_all | solution.py:273
  11.9 0.8 %copy.14.pattern_ref = s32[24,2]{1,0:T(8,128)S(1)} copy(s32[24,2]{0,1:T(2,128)} %param.15) | data formatting | bytes 384 | tf_op args[2]
  12.6 1.1 %copy-done.4 = bf16[24,128,128]{2,1,0:T(8,128)(2,1)S(1)} copy-done((bf16[24,128,128]{2,1,0:T(8,128)(2,1)S(1)}, bf16[24,128,128]{2,1,0:T(8,128)(2,1)}, u32[]{:S(2)}) %copy-start.4) | copy-done | bytes 786456
  13.8 3.7 %shard_map.128.dense_ref = bf16[1024,1024]{1,0:T(8,128)(2,1)S(1)} custom-call(s32[24,2]{1,0:T(8,128)S(1)} %copy.14.pattern_ref, bf16[24,128,128]{2,1,0:T(8,128)(2,1)S(1)} %copy-done.4), custom_call_target="tpu_custom_call" | custom-call | flops 134217728 | bytes 786624 | tf_op jit(solution)/shard_map/pallas_call | solution.py:23
  17.5 0.7 shard_map.129
  18.2 0.1 pad_add_fusion.at_ref
  18.3 0.8 %all-to-all-done.pieces_ref = bf16[16,32,128]{2,1,0:T(8,128)(2,1)S(1)} async-done(((bf16[16,32,128]{2,1,0:T(8,128)(2,1)}), bf16[16,32,128]{2,1,0:T(8,128)(2,1)S(1)}, u32[]{:S(2)}, u32[]{:S(2)}) %all-to-all-start) | async-done | bytes 131104 | tf_op jit(solution)/shard_map/all_to_all | solution.py:273
  19.1 0.0 copy-done.5
  19.1 0.0 copy-done.7
  19.1 0.0 copy-done.8
  19.2 1.8 %shard_map.130 = (f32[64,1024]{1,0:T(8,128)S(1)}, f32[64,1024]{1,0:T(8,128)S(1)}, bf16[384,128]{1,0:T(8,128)(2,1)S(1)}, bf16[384,128]{1,0:T(8,128)(2,1)S(1)}, bf...) custom-call(s32[2]{0:T(128)S(1)} %pad_add_fusion.at_ref, s32[1]{0:T(128)S(6)} %copy.16.count_ref, ...), custom_call_target="tpu_custom_call" | custom-call | flops 134217728 | bytes 3289100 | tf_op jit(solution)/shard_map/pallas_call | solution.py:23
  21.0 1.2 %collective-permute-start = (bf16[384,128]{1,0:T(8,128)(2,1)S(1)}, bf16[384,128]{1,0:T(8,128)(2,1)S(1)}, u32[]{:S(2)}, u32[]{:S(2)}) collective-permute-start(bf16[384,128]{1,0:T(8,128)(2,1)S(1)} %get-tuple-element.24), channel_id=1, source_target_pairs={{0,2},{2,0},{4,6},{6,4},{8,10},{10,8},{12,14},{14,12},{1,3},{3,1},... | collective-permute-start | bytes 294920 | tf_op jit(solution)/shard_map/ppermute | solution.py:282
  22.2 3.3 %collective-permute-start.1 = (bf16[384,128]{1,0:T(8,128)(2,1)S(1)}, bf16[384,128]{1,0:T(8,128)(2,1)S(1)}, u32[]{:S(2)}, u32[]{:S(2)}) collective-permute-start(bf16[384,128]{1,0:T(8,128)(2,1)S(1)} %get-tuple-element.25), channel_id=1, source_target_pairs={{0,14},{2,4},{4,2},{6,8},{8,6},{10,12},{12,10},{14,0},{1,15},{3,5}... | collective-permute-start | bytes 294920 | tf_op jit(solution)/shard_map/ppermute | solution.py:282
  25.4 0.0 collective-permute-start.2
  25.4 1.1 %collective-permute-start.3 = (bf16[64,128]{1,0:T(8,128)(2,1)S(1)}, bf16[64,128]{1,0:T(8,128)(2,1)S(1)}, u32[]{:S(2)}, u32[]{:S(2)}) collective-permute-start(bf16[64,128]{1,0:T(8,128)(2,1)S(1)} %get-tuple-element.27.own_beyond_ref), channel_id=1, source_target_pairs={{0,12},{2,14},{4,8},{6,10},{8,4},{10,6},{12,0},{14,2},{1,13},{3,15... | collective-permute-start | bytes 49160 | tf_op jit(solution)/shard_map/ppermute | solution.py:282
  26.5 2.6 %collective-permute-done.2.far_ref = bf16[64,128]{1,0:T(8,128)(2,1)S(1)} collective-permute-done((bf16[64,128]{1,0:T(8,128)(2,1)S(1)}, bf16[64,128]{1,0:T(8,128)(2,1)S(1)}, u32[]{:S(2)}, u32[]{:S(2)}) %collective-permute-start.2) | collective-permute-done | bytes 16416 | tf_op jit(solution)/shard_map/ppermute | solution.py:282
  29.2 1.8 %collective-permute-done.3.beyond_ref = bf16[64,128]{1,0:T(8,128)(2,1)S(1)} collective-permute-done((bf16[64,128]{1,0:T(8,128)(2,1)S(1)}, bf16[64,128]{1,0:T(8,128)(2,1)S(1)}, u32[]{:S(2)}, u32[]{:S(2)}) %collective-permute-start.3) | collective-permute-done | bytes 16416 | tf_op jit(solution)/shard_map/ppermute | solution.py:282
  31.0 0.0 collective-permute-done.near_ref
  31.0 0.0 collective-permute-done.1.across_ref
  31.0 1.6 %shard_map.131 = (f32[64,1024]{1,0:T(8,128)S(1)}, f32[16,40,128]{2,1,0:T(8,128)S(1)}) custom-call(s32[2]{0:T(128)S(1)} %pad_add_fusion.at_ref, s32[1]{0:T(128)S(6)} %copy.16.count_ref, bf16[384,128]{1,0:T(8,128)(2,1)S(1)} %collective-permute-done.near_ref, bf16[384,128]{1,0:T(8,128)(2,1)S(1)} %collective-permute-done.1.across_ref, ...), custom_call_target="tpu_custom_call" | custom-call | flops 134217728 | bytes 3682316 | tf_op jit(solution)/shard_map/pallas_call | solution.py:23
  32.6 15.2 %all_to_all.15.second_ref = f32[16,40,128]{2,1,0:T(8,128)S(1)} all-to-all(f32[16,40,128]{2,1,0:T(8,128)S(1)} %get-tuple-element.30), channel_id=1, replica_groups=mesh['grp'=2,'lon'=8,'lat'=2] {'lon','lat'}, dimensions={0} | all-to-all | bytes 655360 | tf_op jit(solution)/shard_map/all_to_all | solution.py:273
  47.8 2.1 %shard_map.132 = (f32[64,1024]{1,0:T(8,128)S(1)}, f32[64,1024]{1,0:T(8,128)S(1)}, bf16[64,128]{1,0:T(8,128)(2,1)S(1)}, bf16[64,128]{1,0:T(8,128)(2,1)S(1)}, f32[8,128]{1,0:T(8,128)S(1)}) custom-call(s32[2]{0:T(128)S(1)} %pad_add_fusion.at_ref, s32[1]{0:T(128)S(6)} %copy.16.count_ref, bf16[16,32,128]{2,1,0:T(8,128)(2,1)S(1)} %all-to-all-done.pieces_ref, ...), custom_call_target="tpu_custom_call" | custom-call | flops 134217728 | bytes 3747852 | tf_op jit(solution)/shard_map/pallas_call | solution.py:23
  50.0 0.1 collective-permute-start.4
  50.0 2.6 %collective-permute-start.5 = (bf16[64,128]{1,0:T(8,128)(2,1)S(1)}, bf16[64,128]{1,0:T(8,128)(2,1)S(1)}, u32[]{:S(2)}, u32[]{:S(2)}) collective-permute-start(bf16[64,128]{1,0:T(8,128)(2,1)S(1)} %get-tuple-element.34), channel_id=1, source_target_pairs={{0,14},{2,4},{4,2},{6,8},{8,6},{10,12},{12,10},{14,0},{1,15},{3,5}... | collective-permute-start | bytes 49160 | tf_op jit(solution)/shard_map/ppermute | solution.py:282
  52.6 1.2 %collective-permute-done.4.near_ref = bf16[64,128]{1,0:T(8,128)(2,1)S(1)} collective-permute-done((bf16[64,128]{1,0:T(8,128)(2,1)S(1)}, bf16[64,128]{1,0:T(8,128)(2,1)S(1)}, u32[]{:S(2)}, u32[]{:S(2)}) %collective-permute-start.4) | collective-permute-done | bytes 16416 | tf_op jit(solution)/shard_map/ppermute | solution.py:282
  53.8 2.8 %collective-permute-done.5.across_ref = bf16[64,128]{1,0:T(8,128)(2,1)S(1)} collective-permute-done((bf16[64,128]{1,0:T(8,128)(2,1)S(1)}, bf16[64,128]{1,0:T(8,128)(2,1)S(1)}, u32[]{:S(2)}, u32[]{:S(2)}) %collective-permute-start.5) | collective-permute-done | bytes 16416 | tf_op jit(solution)/shard_map/ppermute | solution.py:282
  56.6 0.9 %shard_map.133 = f32[16,8,128]{2,1,0:T(8,128)S(1)} custom-call(s32[2]{0:T(128)S(1)} %pad_add_fusion.at_ref, bf16[64,128]{1,0:T(8,128)(2,1)S(1)} %collective-permute-done.4.near_ref, bf16[64,128]{1,0:T(8,128)(2,1)S(1)} %collective-permute-done.5.across_ref, f32[64,1024]{1,0:T(8,128)S(1)} %get-tuple-element.35.z_ref.second_ref, ...), custom_call_target="tpu_custom_call" | custom-call | flops 134217728 | bytes 1093640 | tf_op jit(solution)/shard_map/pallas_call | solution.py:23
  57.5 10.6 %all_to_all.16.chunks_ref = f32[16,8,128]{2,1,0:T(8,128)S(1)} all-to-all(f32[16,8,128]{2,1,0:T(8,128)S(1)} %shard_map.133), channel_id=1, replica_groups=mesh['grp'=2,'lon'=8,'lat'=2] {'lon','lat'}, dimensions={0} | all-to-all | bytes 131072 | tf_op jit(solution)/shard_map/all_to_all | solution.py:273
  68.1 1.2 %shard_map.134 = f32[64,1024]{1,0:T(8,128)} custom-call(f32[8,128]{1,0:T(8,128)S(1)} %get-tuple-element.32.sums_ref, f32[16,8,128]{2,1,0:T(8,128)S(1)} %all_to_all.16.chunks_ref, f32[64,1024]{1,0:T(8,128)S(1)} %get-tuple-element.28.z_ref.first_ref, f32[64,1024]{1,0:T(8,128)S(1)} %get-tuple-element.35.z_ref.second_ref), custom_call_target="tpu_custom_call" | custom-call | flops 262144 | bytes 593920 | tf_op jit(solution)/shard_map/pallas_call | solution.py:23
  (18 shorter events, 0.0 us)
Async XLA Ops:
  0.0 17.5 %copy-start.11 = (s32[1,128]{1,0:T(1,128)S(1)}, s32[1,128]{1,0:T(1,128)}, u32[]{:S(2)}) copy-start(s32[1,128]{1,0:T(1,128)} %west_ref.1) | copy-start | bytes 1540
  0.0 17.5 %copy-start.10 = (s32[1,128]{1,0:T(1,128)S(1)}, s32[1,128]{1,0:T(1,128)}, u32[]{:S(2)}) copy-start(s32[1,128]{1,0:T(1,128)} %east_ref.1) | copy-start | bytes 1540
  0.7 0.9 %copy-start = (bf16[64,1024]{1,0:T(8,128)(2,1)S(1)}, bf16[64,1024]{1,0:T(8,128)(2,1)}, u32[]{:S(2)}) copy-start(bf16[64,1024]{1,0:T(8,128)(2,1)} %right_ref.5) | copy-start | bytes 393220
  1.6 0.9 %copy-start.2 = (bf16[64,1024]{1,0:T(8,128)(2,1)S(1)}, bf16[64,1024]{1,0:T(8,128)(2,1)}, u32[]{:S(2)}) copy-start(bf16[64,1024]{1,0:T(8,128)(2,1)} %vectors_ref.5) | copy-start | bytes 393220
  2.5 15.0 %copy-start.6 = (f32[1024]{0:T(1024)S(1)}, f32[1024]{0:T(1024)}, u32[]{:S(2)}) copy-start(f32[1024]{0:T(1024)} %param.17) | copy-start | bytes 12292
  2.5 15.0 %copy-start.9 = (bf16[128,128]{1,0:T(8,128)(2,1)S(1)}, bf16[128,128]{1,0:T(8,128)(2,1)}, u32[]{:S(2)}) copy-start(bf16[128,128]{1,0:T(8,128)(2,1)} %coupling_ref.1) | copy-start | bytes 98308
  2.5 16.6 %copy-start.1 = (bf16[64,1024]{1,0:T(8,128)(2,1)S(1)}, bf16[64,1024]{1,0:T(8,128)(2,1)}, u32[]{:S(2)}) copy-start(bf16[64,1024]{1,0:T(8,128)(2,1)} %right_ref.5) | copy-start | bytes 393220
  2.5 16.6 %copy-start.3 = (bf16[64,1024]{1,0:T(8,128)(2,1)S(1)}, bf16[64,1024]{1,0:T(8,128)(2,1)}, u32[]{:S(2)}) copy-start(bf16[64,1024]{1,0:T(8,128)(2,1)} %vectors_ref.5) | copy-start | bytes 393220
  2.5 16.6 %copy-start.5 = (bf16[64,1024]{1,0:T(8,128)(2,1)S(1)}, bf16[64,1024]{1,0:T(8,128)(2,1)}, u32[]{:S(2)}) copy-start(bf16[64,1024]{1,0:T(8,128)(2,1)} %inverse_ref.3) | copy-start | bytes 393220
  2.5 16.6 %copy-start.7 = (f32[1024]{0:T(1024)S(1)}, f32[1024]{0:T(1024)}, u32[]{:S(2)}) copy-start(f32[1024]{0:T(1024)} %param.18) | copy-start | bytes 12292
  2.5 16.6 %copy-start.8 = (f32[1024]{0:T(1024)S(1)}, f32[1024]{0:T(1024)}, u32[]{:S(2)}) copy-start(f32[1024]{0:T(1024)} %param.16) | copy-start | bytes 12292
  3.8 15.3 %all-to-all-start = ((bf16[16,32,128]{2,1,0:T(8,128)(2,1)}), bf16[16,32,128]{2,1,0:T(8,128)(2,1)S(1)}, u32[]{:S(2)}, u32[]{:S(2)}) async-start(bf16[16,32,128]{2,1,0:T(8,128)(2,1)} %shard_map.127), calls=%async_computation | async-start | bytes 262144 | tf_op jit(solution)/shard_map/all_to_all | solution.py:273
  12.6 1.1 %copy-start.4 = (bf16[24,128,128]{2,1,0:T(8,128)(2,1)S(1)}, bf16[24,128,128]{2,1,0:T(8,128)(2,1)}, u32[]{:S(2)}) copy-start(bf16[24,128,128]{2,1,0:T(8,128)(2,1)} %blocks_ref.1) | copy-start | bytes 2359300
  21.0 10.0 %collective-permute-start = (bf16[384,128]{1,0:T(8,128)(2,1)S(1)}, bf16[384,128]{1,0:T(8,128)(2,1)S(1)}, u32[]{:S(2)}, u32[]{:S(2)}) collective-permute-start(bf16[384,128]{1,0:T(8,128)(2,1)S(1)} %get-tuple-element.24), channel_id=1, source_target_pairs={{0,2},{2,0},{4,6},{6,4},{8,10},{10,8},{12,14},{14,12},{1,3},{3,1},... | collective-permute-start | bytes 294920 | tf_op jit(solution)/shard_map/ppermute | solution.py:282
  22.2 8.8 %collective-permute-start.1 = (bf16[384,128]{1,0:T(8,128)(2,1)S(1)}, bf16[384,128]{1,0:T(8,128)(2,1)S(1)}, u32[]{:S(2)}, u32[]{:S(2)}) collective-permute-start(bf16[384,128]{1,0:T(8,128)(2,1)S(1)} %get-tuple-element.25), channel_id=1, source_target_pairs={{0,14},{2,4},{4,2},{6,8},{8,6},{10,12},{12,10},{14,0},{1,15},{3,5}... | collective-permute-start | bytes 294920 | tf_op jit(solution)/shard_map/ppermute | solution.py:282
  25.4 3.7 %collective-permute-start.2 = (bf16[64,128]{1,0:T(8,128)(2,1)S(1)}, bf16[64,128]{1,0:T(8,128)(2,1)S(1)}, u32[]{:S(2)}, u32[]{:S(2)}) collective-permute-start(bf16[64,128]{1,0:T(8,128)(2,1)S(1)} %get-tuple-element.26.own_far_ref), channel_id=1, source_target_pairs={{0,4},{2,6},{4,0},{6,2},{8,12},{10,14},{12,8},{14,10},{1,5},{3,7},... | collective-permute-start | bytes 49160 | tf_op jit(solution)/shard_map/ppermute | solution.py:282
  25.4 5.5 %collective-permute-start.3 = (bf16[64,128]{1,0:T(8,128)(2,1)S(1)}, bf16[64,128]{1,0:T(8,128)(2,1)S(1)}, u32[]{:S(2)}, u32[]{:S(2)}) collective-permute-start(bf16[64,128]{1,0:T(8,128)(2,1)S(1)} %get-tuple-element.27.own_beyond_ref), channel_id=1, source_target_pairs={{0,12},{2,14},{4,8},{6,10},{8,4},{10,6},{12,0},{14,2},{1,13},{3,15... | collective-permute-start | bytes 49160 | tf_op jit(solution)/shard_map/ppermute | solution.py:282
  50.0 3.8 %collective-permute-start.4 = (bf16[64,128]{1,0:T(8,128)(2,1)S(1)}, bf16[64,128]{1,0:T(8,128)(2,1)S(1)}, u32[]{:S(2)}, u32[]{:S(2)}) collective-permute-start(bf16[64,128]{1,0:T(8,128)(2,1)S(1)} %get-tuple-element.33), channel_id=1, source_target_pairs={{0,2},{2,0},{4,6},{6,4},{8,10},{10,8},{12,14},{14,12},{1,3},{3,1},... | collective-permute-start | bytes 49160 | tf_op jit(solution)/shard_map/ppermute | solution.py:282
  50.0 6.5 %collective-permute-start.5 = (bf16[64,128]{1,0:T(8,128)(2,1)S(1)}, bf16[64,128]{1,0:T(8,128)(2,1)S(1)}, u32[]{:S(2)}, u32[]{:S(2)}) collective-permute-start(bf16[64,128]{1,0:T(8,128)(2,1)S(1)} %get-tuple-element.34), channel_id=1, source_target_pairs={{0,14},{2,4},{4,2},{6,8},{8,6},{10,12},{12,10},{14,0},{1,15},{3,5}... | collective-permute-start | bytes 49160 | tf_op jit(solution)/shard_map/ppermute | solution.py:282

commit v4 on v3

--- a/solution.py
+++ b/solution.py
@@ -18,7 +18,7 @@
     return lax.dot_general(a, b, (((ca,), (cb,)), ((), ())), preferred_element_type=F32)
 
 
-def call(kernel, outs, specs, args, flops, scratch=()):
+def call(kernel, outs, specs, args, flops, scratch=(), limit=32):
     moved = sum(int(np.prod(a.shape)) * a.dtype.itemsize for a in args)
     return pl.pallas_call(
         kernel,
@@ -26,7 +26,7 @@
         in_specs=specs,
         out_specs=[VMEM] * len(outs),
         scratch_shapes=list(scratch),
-        compiler_params=pltpu.CompilerParams(vmem_limit_bytes=32 * 1024 * 1024),
+        compiler_params=pltpu.CompilerParams(vmem_limit_bytes=limit * 1024 * 1024),
         cost_estimate=pl.CostEstimate(flops=flops, bytes_accessed=moved, transcendentals=0),
     )(*args)
 
@@ -70,6 +70,9 @@
 def dense_kernel(pattern_ref, blocks_ref, dense_ref, total_ref):
     count, block, _ = blocks_ref.shape
     nodes = dense_ref.shape[0]
+    unit = (
+        lax.broadcasted_iota(jnp.int32, (block, block), 0) == lax.broadcasted_iota(jnp.int32, (block, block), 1)
+    ).astype(F32).astype(BF16)
 
     def clear(i, carry):
         total_ref[pl.ds(pl.multiple_of(i * block, block), block), :] = jnp.zeros((block, nodes), F32)
@@ -80,12 +83,12 @@
     def place(k, carry):
         rows = pl.ds(pl.multiple_of(pattern_ref[k, 0] * block, block), block)
         cols = pl.ds(pl.multiple_of(pattern_ref[k, 1] * block, block), block)
-        values = blocks_ref[k].astype(F32)
-        total_ref[rows, cols] += values
-        total_ref[cols, rows] += jnp.transpose(values)
+        values = blocks_ref[k]
+        total_ref[rows, cols] += values.astype(F32)
+        total_ref[cols, rows] += dot(unit, values, 1, 1)
         return carry
 
-    lax.fori_loop(0, count, place, 0)
+    lax.fori_loop(0, count, place, 0, unroll=8)
 
     def narrow(i, carry):
         rows = pl.ds(pl.multiple_of(i * block, block), block)
@@ -116,17 +119,18 @@
     to_west_ref[...] = both[:, slots:]
 
 
-def unfold(count, piece, coarse_ref):
-    half = coarse_ref.shape[0] // count // 2
+def unfold(lat, count, piece, coarse_ref):
+    half = coarse_ref.shape[0] // count // 4
 
     def move(d, carry):
-        values = piece(d)
-        at = pl.multiple_of(d * 2 * half, 2 * half)
-        coarse_ref[pl.ds(at, half), :] = values[:, 0 : LANES // 2]
-        coarse_ref[pl.ds(at + half, half), :] = values[:, LANES // 2 :]
+        for side in range(2):
+            values = piece(side, d)
+            at = pl.multiple_of((2 * d + (lat if side == 0 else 1 - lat)) * 2 * half, 2 * half)
+            coarse_ref[pl.ds(at, half), :] = values[:, 0 : LANES // 2]
+            coarse_ref[pl.ds(at + half, half), :] = values[:, LANES // 2 :]
         return carry
 
-    lax.fori_loop(0, count, move, 0, unroll=min(count, 16))
+    lax.fori_loop(0, count, move, 0, unroll=min(count, 8))
 
 
 def smooth(field, coarse_ref, inverse_ref, vectors_ref, react, mass, obs, active):
@@ -135,11 +139,11 @@
     return active * (field / (obs + react * react / mass) + spread)
 
 
-def start_kernel(at_ref, count_ref, pieces_ref, inverse_ref, right_ref, vectors_ref, dense_ref, edge_ref,
+def start_kernel(at_ref, count_ref, pieces_ref, others_ref, inverse_ref, right_ref, vectors_ref, dense_ref, edge_ref,
                  react_ref, mass_ref, obs_ref, to_west_ref, to_east_ref,
                  z_ref, scaled_ref, near_ref, across_ref, far_ref, beyond_ref, coarse_ref):
     samples, nodes = right_ref.shape
-    unfold(pieces_ref.shape[0], lambda d: pieces_ref[d], coarse_ref)
+    unfold(at_ref[2], pieces_ref.shape[0], lambda side, d: (pieces_ref, others_ref)[side][d], coarse_ref)
     active = active_of(count_ref, nodes)
     react, mass = react_ref[...], mass_ref[...]
     z = smooth(active * right_ref[...].astype(F32), coarse_ref, inverse_ref, vectors_ref, react, mass, obs_ref[...],
@@ -178,7 +182,7 @@
     return jnp.where(keep, first, second).astype(BF16), jnp.where(keep, second, first).astype(BF16)
 
 
-def image_kernel(at_ref, count_ref, near_ref, across_ref, far_ref, beyond_ref, own_far_ref, own_beyond_ref,
+def image_kernel(at_ref, count_ref, across_ref, beyond_ref, near_ref, far_ref, own_far_ref, own_beyond_ref,
                  z_ref, scaled_ref, dense_ref, edge_ref, react_ref, mass_ref, obs_ref, right_ref, vectors_ref,
                  image_ref, chunks_ref):
     samples, nodes = z_ref.shape
@@ -206,23 +210,24 @@
     chunks_ref[:, half:, :] = jnp.broadcast_to(sums[None], (count, rows - half, LANES))
 
 
-def middle_kernel(at_ref, count_ref, pieces_ref, second_ref, inverse_ref, right_ref, image_ref, vectors_ref,
+def middle_kernel(at_ref, count_ref, pieces_ref, others_ref, second_ref, second_others_ref, inverse_ref, right_ref, image_ref, vectors_ref,
                   dense_ref, edge_ref, react_ref, mass_ref, obs_ref,
                   z_ref, scaled_ref, near_ref, across_ref, sums_ref, coarse_ref):
     samples, nodes = right_ref.shape
     count, half, _ = pieces_ref.shape
 
     def add(d, total):
-        return total + second_ref[d, half : half + 1, :]
-
-    sums = lax.fori_loop(0, count, add, jnp.zeros((1, LANES), F32), unroll=min(count, 16))
+        return total + second_ref[d, half : half + 1, :] + second_others_ref[d, half : half + 1, :]
+
+    sums = lax.fori_loop(0, count, add, jnp.zeros((1, LANES), F32), unroll=min(count, 8))
     step = sums[:, 0 : LANES // 2] / sums[:, LANES // 2 :]
     step = jnp.concatenate([step, step], axis=1)
 
-    def piece(d):
-        return (pieces_ref[d].astype(F32) - step * second_ref[d, 0:half, :]).astype(BF16)
-
-    unfold(count, piece, coarse_ref)
+    def piece(side, d):
+        first, change = ((pieces_ref, second_ref), (others_ref, second_others_ref))[side]
+        return (first[d].astype(F32) - step * change[d, 0:half, :]).astype(BF16)
+
+    unfold(at_ref[2], count, piece, coarse_ref)
     active = active_of(count_ref, nodes)
     react, mass = react_ref[...], mass_ref[...]
     image = image_ref[...]
@@ -245,7 +250,7 @@
     sums_ref[...] = jnp.where(row == 0, products, sums)
 
 
-def last_kernel(at_ref, near_ref, across_ref, z_ref, scaled_ref, edge_ref, mass_ref, obs_ref, sums_ref, chunks_ref):
+def last_kernel(at_ref, across_ref, near_ref, z_ref, scaled_ref, edge_ref, mass_ref, obs_ref, sums_ref, chunks_ref):
     z = z_ref[...]
     from_east, from_west = pick(at_ref[0], near_ref, across_ref)
     stiff = scaled_ref[...] + dot(jnp.concatenate([from_east, from_west], axis=1), edge_ref[...])
@@ -255,10 +260,10 @@
     chunks_ref[...] = jnp.broadcast_to(chunk[None], chunks_ref.shape)
 
 
-def finish_kernel(sums_ref, chunks_ref, first_ref, second_ref, out_ref):
+def finish_kernel(sums_ref, chunks_ref, others_ref, first_ref, second_ref, out_ref):
     samples = first_ref.shape[0]
     half = LANES // 2
-    totals = jnp.sum(chunks_ref[...], axis=0)
+    totals = jnp.sum(chunks_ref[...] + others_ref[...], axis=0)
     norm0, curve0 = sums_ref[1:2, 0:half], sums_ref[1:2, half:]
     norm1, cross = totals[0:1, 0:half], totals[0:1, half:]
     curve = totals[1:2, 0:half]
@@ -270,7 +275,11 @@
 
 
 def exchange(chunks):
-    return lax.all_to_all(chunks, ("lon", "lat"), split_axis=0, concat_axis=0, tiled=True)
+    return lax.all_to_all(chunks, "lon", split_axis=0, concat_axis=0, tiled=True)
+
+
+def other_band(array):
+    return lax.ppermute(array, "lat", [(0, 1), (1, 0)])
 
 
 def swap(array, reach, inner):
@@ -300,22 +309,24 @@
     samples, nodes = right_side.shape
     slots = coupling.shape[0]
     vectors = deflation.shape[0]
-    domains = lax.axis_size("lon") * lax.axis_size("lat")
+    sectors = lax.axis_size("lon")
+    domains = sectors * lax.axis_size("lat")
     half = vectors // 2
     react, mass, obs = reaction[None], lumped_mass[None], obs_precision[None]
     field = ((samples, nodes), F32)
     coarse_scratch = pltpu.VMEM((domains * vectors, samples), BF16)
     apply_cost = 2 * samples * nodes * nodes
     lon = lax.axis_index("lon")
-    at = jnp.stack([lon % 2, (lon // 2) % 2]).astype(jnp.int32)
+    at = jnp.stack([lon & 1, (lon >> 1) & 1, lax.axis_index("lat")]).astype(jnp.int32)
 
     (chunks,) = call(
         coarse_kernel,
-        [((domains, half, LANES), BF16)],
+        [((sectors, half, LANES), BF16)],
         [SMEM, HBM, HBM],
         (node_count, right_side, deflation),
         2 * samples * vectors * nodes,
         [pltpu.VMEM((samples, nodes), BF16), pltpu.VMEM((vectors, nodes), BF16), pltpu.SemaphoreType.DMA((2,))],
+        64,
     )
     edge, corr_west, corr_east = call(
         edge_kernel,
@@ -327,12 +338,15 @@
     (dense,) = call(dense_kernel, [((nodes, nodes), BF16)], [SMEM, VMEM], (block_pattern, stiffness_blocks),
                     apply_cost, [pltpu.VMEM((nodes, nodes), F32)])
 
-    pieces = exchange(chunks)
+    pieces, dense, edge, corr_west, corr_east = lax.optimization_barrier(
+        (exchange(chunks), dense, edge, corr_west, corr_east)
+    )
+    others = other_band(pieces)
     z0, scaled, near, across, far, beyond = call(
         start_kernel,
         [field] * 2 + [((2 * samples + 2 * slots, slots), BF16)] * 2 + [((samples, slots), BF16)] * 2,
-        [SMEM, SMEM] + [VMEM] * 11,
-        (at, node_count, pieces, coarse_inverse, right_side, deflation, dense, edge, react, mass, obs,
+        [SMEM, SMEM] + [VMEM] * 12,
+        (at, node_count, pieces, others, coarse_inverse, right_side, deflation, dense, edge, react, mass, obs,
          corr_west, corr_east),
         apply_cost,
         [coarse_scratch],
@@ -343,18 +357,20 @@
     near = swap(near, 1, True)
     image, chunks = call(
         image_kernel,
-        [field, ((domains, half + 8, LANES), F32)],
+        [field, ((sectors, half + 8, LANES), F32)],
         [SMEM, SMEM] + [VMEM] * 15,
-        (at, node_count, near, across, got_far, got_beyond, far, beyond, z0, scaled, dense, edge,
+        (at, node_count, across, got_beyond, near, got_far, far, beyond, z0, scaled, dense, edge,
          react, mass, obs, right_side, deflation),
         apply_cost,
     )
     second = exchange(chunks)
+    second_others = other_band(second)
     z1, scaled, near, across, sums = call(
         middle_kernel,
         [field] * 2 + [((samples, slots), BF16)] * 2 + [((8, LANES), F32)],
-        [SMEM, SMEM] + [VMEM] * 11,
-        (at, node_count, pieces, second, coarse_inverse, right_side, image, deflation, dense, edge, react, mass, obs),
+        [SMEM, SMEM] + [VMEM] * 13,
+        (at, node_count, pieces, others, second, second_others, coarse_inverse, right_side, image, deflation, dense,
+         edge, react, mass, obs),
         apply_cost,
         [coarse_scratch],
     )
@@ -362,13 +378,14 @@
     near = swap(near, 1, True)
     (chunks,) = call(
         last_kernel,
-        [((domains, 8, LANES), F32)],
+        [((sectors, 8, LANES), F32)],
         [SMEM] + [VMEM] * 8,
-        (at, near, across, z1, scaled, edge, mass, obs, sums),
+        (at, across, near, z1, scaled, edge, mass, obs, sums),
         apply_cost,
     )
     totals = exchange(chunks)
-    (out,) = call(finish_kernel, [field], [VMEM] * 4, (sums, totals, z0, z1), 4 * samples * nodes)
+    other_totals = other_band(totals)
+    (out,) = call(finish_kernel, [field], [VMEM] * 5, (sums, totals, other_totals, z0, z1), 4 * samples * nodes)
     return out
 
 

time: 69.6 us -> 66.6 us (0.957)
  waiting for transfers between devices: 9.19 us -> 14.5 us
  blocking collectives: 25.8 us -> 21.4 us
  local copies, waits for them, and re-layouts: 3.73 us -> 1.94 us
  starting transfers between devices: 15.5 us -> 14.2 us
  Pallas kernels: 13.4 us -> 12.7 us
    all_to_all x2, blocking collectives: 25.8 us -> 21.4 us  [exchange(): lax.all_to_all(chunks, 'lon', split_axis=0, concat_axis=0, tiled=True)]
    ppermute x0 -> x3, waiting for transfers between devices: none -> 3.77 us  [other_band(): return lax.ppermute(array, 'lat', [(0, 1), (1, 0)])]
    unnamed x25 -> x21, local copies, waits for them, and re-layouts: 3.73 us -> 1.94 us
    ppermute x6, starting transfers between devices: 8.17 us -> 6.8 us  [swap(): return lax.ppermute(array, 'lon', pairs)]
    ppermute x6, waiting for transfers between devices: 8.37 us -> 9.49 us  [swap(): return lax.ppermute(array, 'lon', pairs)]
    pallas_call x8, Pallas kernels: 13.4 us -> 12.7 us  [call(): pl.pallas_call(kernel, out_shape=[jax.ShapeDtypeStruct(s, t) for s, t in...]
  transfers between devices with their start and end apart: 7 -> 10, of which waited for: 5 -> 7; matrix products, arithmetic and copies ran while one was open for 1% -> 1% of each run, Pallas kernels for 6% -> 5%
where the time goes in v4:
time: 66.6 us; the launch traced here: 66.2 us
  blocking collectives  21.4 us (32%)
  waiting for transfers between devices  14.5 us (22%)
  starting transfers between devices  14.2 us (21%)
  Pallas kernels  12.7 us (19%)
  local copies, waits for them, and re-layouts  1.94 us (3%)
  between operations  1.45 us (2%)
    all_to_all x2, blocking collectives, exchange(): lax.all_to_all(chunks, 'lon', split_axis=0, concat_axis=0, tiled=True)  21.4 us
    pallas_call x8, Pallas kernels, call(): pl.pallas_call(kernel, out_shape=[jax.ShapeDtypeStruct(s, t) for s, t in...  12.7 us
    ppermute x6, waiting for transfers between devices, swap(): return lax.ppermute(array, 'lon', pairs)  9.49 us
    all_to_all x1, starting transfers between devices, exchange(): lax.all_to_all(chunks, 'lon', split_axis=0, concat_axis=0, tiled=True)  7.4 us
    ppermute x6, starting transfers between devices, swap(): return lax.ppermute(array, 'lon', pairs)  6.8 us
    ppermute x3, waiting for transfers between devices, other_band(): return lax.ppermute(array, 'lat', [(0, 1), (1, 0)])  3.77 us
    unnamed x21, local copies, waits for them, and re-layouts  1.94 us
  transfers between devices with their start and end apart: 10, of which 7 were waited for; matrix products, arithmetic and copies ran while one was open for 1% of the time, Pallas kernels for 5%

profile of v4, /device:TPU:0, one launch (start us, length us, event | category | flops | bytes accessed | tf_op | source)
XLA Modules:
  0.0 66.2 jit_solution(4877894511775622337)
XLA Ops:
  0.7 1.9 %shard_map.127 = bf16[8,32,128]{2,1,0:T(8,128)(2,1)} custom-call(s32[1]{0:T(128)S(6)} %copy.16.count_ref, bf16[64,1024]{1,0:T(8,128)(2,1)} %right_ref.5, bf16[64,1024]{1,0:T(8,128)(2,1)} %vectors_ref.5), custom_call_target="tpu_custom_call" | custom-call | flops 8388608 | bytes 262148 | tf_op jit(solution)/shard_map/pallas_call | solution.py:23
  2.5 0.0 copy-start
  2.5 0.0 copy-start.1
  2.6 7.4 %all-to-all-start = ((bf16[8,32,128]{2,1,0:T(8,128)(2,1)}), bf16[8,32,128]{2,1,0:T(8,128)(2,1)S(1)}, u32[]{:S(2)}, u32[]{:S(2)}) async-start(bf16[8,32,128]{2,1,0:T(8,128)(2,1)} %shard_map.127), calls=%async_computation | async-start | bytes 131072 | tf_op jit(solution)/shard_map/all_to_all | solution.py:278
  10.6 0.8 %copy.14.pattern_ref = s32[24,2]{1,0:T(8,128)S(1)} copy(s32[24,2]{0,1:T(2,128)} %param.15) | data formatting | bytes 384 | tf_op args[2]
  11.4 1.1 %copy-done.2 = bf16[24,128,128]{2,1,0:T(8,128)(2,1)S(1)} copy-done((bf16[24,128,128]{2,1,0:T(8,128)(2,1)S(1)}, bf16[24,128,128]{2,1,0:T(8,128)(2,1)}, u32[]{:S(2)}) %copy-start.2) | copy-done | bytes 786456
  12.5 0.0 copy-start.3
  12.5 0.0 copy-start.5
  12.5 0.0 copy-start.6
  12.5 2.4 %shard_map.128.dense_ref = bf16[1024,1024]{1,0:T(8,128)(2,1)S(1)} custom-call(s32[24,2]{1,0:T(8,128)S(1)} %copy.14.pattern_ref, bf16[24,128,128]{2,1,0:T(8,128)(2,1)S(1)} %copy-done.2), custom_call_target="tpu_custom_call" | custom-call | flops 134217728 | bytes 786624 | tf_op jit(solution)/shard_map/pallas_call | solution.py:23
  15.0 0.7 %shard_map.129 = (bf16[256,1024]{1,0:T(8,128)(2,1)S(1)}, bf16[256,128]{1,0:T(8,128)(2,1)S(1)}, bf16[256,128]{1,0:T(8,128)(2,1)S(1)}) custom-call(s32[1]{0:T(128)S(6)} %copy.15.iface_ref, bf16[128,128]{1,0:T(8,128)(2,1)S(1)} %copy-done.7, s32[1,128]{1,0:T(1,128)S(1)} %copy-done.8, s32[1,128]{1,0:T(1,128)S(1)} %copy-done.9, f32[1,1024]{1,0:T(1,128)S(1)} %bitcast.6), custom_call_target="tpu_custom_call" | custom-call | flops 134217728 | bytes 37892 | tf_op jit(solution)/shard_map/pallas_call | solution.py:23
  15.7 1.2 %all-to-all-done.pieces_ref = bf16[8,32,128]{2,1,0:T(8,128)(2,1)S(1)} async-done(((bf16[8,32,128]{2,1,0:T(8,128)(2,1)}), bf16[8,32,128]{2,1,0:T(8,128)(2,1)S(1)}, u32[]{:S(2)}, u32[]{:S(2)}) %all-to-all-start) | async-done | bytes 65568 | tf_op jit(solution)/shard_map/all_to_all | solution.py:278
  16.9 0.0 collective-permute-start
  16.9 0.1 pad_add_fusion.at_ref
  16.9 1.2 %collective-permute-done.others_ref = bf16[8,32,128]{2,1,0:T(8,128)(2,1)S(1)} collective-permute-done((bf16[8,32,128]{2,1,0:T(8,128)(2,1)S(1)}, bf16[8,32,128]{2,1,0:T(8,128)(2,1)S(1)}, u32[]{:S(2)}, u32[]{:S(2)}) %collective-permute-start) | collective-permute-done | bytes 65568 | tf_op jit(solution)/shard_map/ppermute | solution.py:282
  18.1 1.8 %shard_map.130 = (f32[64,1024]{1,0:T(8,128)S(1)}, f32[64,1024]{1,0:T(8,128)S(1)}, bf16[384,128]{1,0:T(8,128)(2,1)S(1)}, bf16[384,128]{1,0:T(8,128)(2,1)S(1)}, bf...) custom-call(s32[3]{0:T(128)S(1)} %pad_add_fusion.at_ref, s32[1]{0:T(128)S(6)} %copy.16.count_ref, ...), custom_call_target="tpu_custom_call" | custom-call | flops 134217728 | bytes 3289104 | tf_op jit(solution)/shard_map/pallas_call | solution.py:23
  20.0 3.7 %collective-permute-start.1 = (bf16[384,128]{1,0:T(8,128)(2,1)S(1)}, bf16[384,128]{1,0:T(8,128)(2,1)S(1)}, u32[]{:S(2)}, u32[]{:S(2)}) collective-permute-start(bf16[384,128]{1,0:T(8,128)(2,1)S(1)} %get-tuple-element.34), channel_id=1, source_target_pairs={{0,14},{2,4},{4,2},{6,8},{8,6},{10,12},{12,10},{14,0},{1,15},{3,5}... | collective-permute-start | bytes 294920 | tf_op jit(solution)/shard_map/ppermute | solution.py:291
  23.7 1.6 %collective-permute-start.2 = (bf16[64,128]{1,0:T(8,128)(2,1)S(1)}, bf16[64,128]{1,0:T(8,128)(2,1)S(1)}, u32[]{:S(2)}, u32[]{:S(2)}) collective-permute-start(bf16[64,128]{1,0:T(8,128)(2,1)S(1)} %get-tuple-element.35.own_beyond_ref), channel_id=1, source_target_pairs={{0,12},{2,14},{4,8},{6,10},{8,4},{10,6},{12,0},{14,2},{1,13},{3,15... | collective-permute-start | bytes 49160 | tf_op jit(solution)/shard_map/ppermute | solution.py:291
  25.3 0.0 collective-permute-start.4
  25.4 3.9 %collective-permute-done.2.beyond_ref = bf16[64,128]{1,0:T(8,128)(2,1)S(1)} collective-permute-done((bf16[64,128]{1,0:T(8,128)(2,1)S(1)}, bf16[64,128]{1,0:T(8,128)(2,1)S(1)}, u32[]{:S(2)}, u32[]{:S(2)}) %collective-permute-start.2) | collective-permute-done | bytes 16416 | tf_op jit(solution)/shard_map/ppermute | solution.py:291
  29.3 0.5 collective-permute-done.3.near_ref
  29.8 1.6 %shard_map.131 = (f32[64,1024]{1,0:T(8,128)S(1)}, f32[8,40,128]{2,1,0:T(8,128)S(1)}) custom-call(s32[3]{0:T(128)S(1)} %pad_add_fusion.at_ref, s32[1]{0:T(128)S(6)} %copy.16.count_ref, bf16[384,128]{1,0:T(8,128)(2,1)S(1)} %collective-permute-done.1.across_ref, bf16[64,128]{1,0:T(8,128)(2,1)S(1)} %collective-permute-done.2.beyond_ref, ...), custom_call_target="tpu_custom_call" | custom-call | flops 134217728 | bytes 3682320 | tf_op jit(solution)/shard_map/pallas_call | solution.py:23
  31.4 11.6 %all_to_all.15.second_ref = f32[8,40,128]{2,1,0:T(8,128)S(1)} all-to-all(f32[8,40,128]{2,1,0:T(8,128)S(1)} %get-tuple-element.40), channel_id=1, replica_groups=mesh['grp'=2,'lon'=8,'lat'=2] {'lon'}, dimensions={0} | all-to-all | bytes 327680 | tf_op jit(solution)/shard_map/all_to_all | solution.py:278
  43.0 1.4 %collective-permute-done.5.second_others_ref = f32[8,40,128]{2,1,0:T(8,128)S(1)} collective-permute-done((f32[8,40,128]{2,1,0:T(8,128)S(1)}, f32[8,40,128]{2,1,0:T(8,128)S(1)}, u32[]{:S(2)}, u32[]{:S(2)}) %collective-permute-start.5) | collective-permute-done | bytes 163872 | tf_op jit(solution)/shard_map/ppermute | solution.py:282
  44.4 2.2 %shard_map.132 = (f32[64,1024]{1,0:T(8,128)S(1)}, f32[64,1024]{1,0:T(8,128)S(1)}, bf16[64,128]{1,0:T(8,128)(2,1)S(1)}, bf16[64,128]{1,0:T(8,128)(2,1)S(1)}, f32[8,128]{1,0:T(8,128)S(1)}) custom-call(s32[3]{0:T(128)S(1)} %pad_add_fusion.at_ref, s32[1]{0:T(128)S(6)} %copy.16.count_ref, bf16[8,32,128]{2,1,0:T(8,128)(2,1)S(1)} %all-to-all-done.pieces_ref, ...), custom_call_target="tpu_custom_call" | custom-call | flops 134217728 | bytes 3747856 | tf_op jit(solution)/shard_map/pallas_call | solution.py:23
  46.6 1.3 %collective-permute-start.6 = (bf16[64,128]{1,0:T(8,128)(2,1)S(1)}, bf16[64,128]{1,0:T(8,128)(2,1)S(1)}, u32[]{:S(2)}, u32[]{:S(2)}) collective-permute-start(bf16[64,128]{1,0:T(8,128)(2,1)S(1)} %get-tuple-element.43), channel_id=1, source_target_pairs={{0,14},{2,4},{4,2},{6,8},{8,6},{10,12},{12,10},{14,0},{1,15},{3,5}... | collective-permute-start | bytes 49160 | tf_op jit(solution)/shard_map/ppermute | solution.py:291
  47.9 0.1 collective-permute-start.7
  48.0 5.1 %collective-permute-done.6.across_ref = bf16[64,128]{1,0:T(8,128)(2,1)S(1)} collective-permute-done((bf16[64,128]{1,0:T(8,128)(2,1)S(1)}, bf16[64,128]{1,0:T(8,128)(2,1)S(1)}, u32[]{:S(2)}, u32[]{:S(2)}) %collective-permute-start.6) | collective-permute-done | bytes 16416 | tf_op jit(solution)/shard_map/ppermute | solution.py:291
  53.1 0.9 %shard_map.133 = f32[8,8,128]{2,1,0:T(8,128)S(1)} custom-call(s32[3]{0:T(128)S(1)} %pad_add_fusion.at_ref, bf16[64,128]{1,0:T(8,128)(2,1)S(1)} %collective-permute-done.6.across_ref, bf16[64,128]{1,0:T(8,128)(2,1)S(1)} %collective-permute-done.7.near_ref, f32[64,1024]{1,0:T(8,128)S(1)} %get-tuple-element.45.z_ref.second_ref, ...), custom_call_target="tpu_custom_call" | custom-call | flops 134217728 | bytes 1093644 | tf_op jit(solution)/shard_map/pallas_call | solution.py:23
  54.1 9.8 %all_to_all.16.chunks_ref = f32[8,8,128]{2,1,0:T(8,128)S(1)} all-to-all(f32[8,8,128]{2,1,0:T(8,128)S(1)} %shard_map.133), channel_id=1, replica_groups=mesh['grp'=2,'lon'=8,'lat'=2] {'lon'}, dimensions={0} | all-to-all | bytes 65536 | tf_op jit(solution)/shard_map/all_to_all | solution.py:278
  63.8 1.2 %collective-permute-done.8.others_ref = f32[8,8,128]{2,1,0:T(8,128)S(1)} collective-permute-done((f32[8,8,128]{2,1,0:T(8,128)S(1)}, f32[8,8,128]{2,1,0:T(8,128)S(1)}, u32[]{:S(2)}, u32[]{:S(2)}) %collective-permute-start.8) | collective-permute-done | bytes 32800 | tf_op jit(solution)/shard_map/ppermute | solution.py:282
  65.1 1.2 %shard_map.134 = f32[64,1024]{1,0:T(8,128)} custom-call(f32[8,128]{1,0:T(8,128)S(1)} %get-tuple-element.42.sums_ref, f32[8,8,128]{2,1,0:T(8,128)S(1)} %all_to_all.16.chunks_ref, f32[8,8,128]{2,1,0:T(8,128)S(1)} %collective-permute-done.8.others_ref, f32[64,1024]{1,0:T(8,128)S(1)} %get-tuple-element.38.z_ref.first_ref, ...), custom_call_target="tpu_custom_call" | custom-call | flops 262144 | bytes 593920 | tf_op jit(solution)/shard_map/pallas_call | solution.py:23
  (20 shorter events, 0.0 us)
Async XLA Ops:
  2.5 15.6 %copy-start = (bf16[64,1024]{1,0:T(8,128)(2,1)S(1)}, bf16[64,1024]{1,0:T(8,128)(2,1)}, u32[]{:S(2)}) copy-start(bf16[64,1024]{1,0:T(8,128)(2,1)} %right_ref.5) | copy-start | bytes 393220
  2.5 15.6 %copy-start.1 = (bf16[64,1024]{1,0:T(8,128)(2,1)S(1)}, bf16[64,1024]{1,0:T(8,128)(2,1)}, u32[]{:S(2)}) copy-start(bf16[64,1024]{1,0:T(8,128)(2,1)} %vectors_ref.5) | copy-start | bytes 393220
  2.6 14.3 %all-to-all-start = ((bf16[8,32,128]{2,1,0:T(8,128)(2,1)}), bf16[8,32,128]{2,1,0:T(8,128)(2,1)S(1)}, u32[]{:S(2)}, u32[]{:S(2)}) async-start(bf16[8,32,128]{2,1,0:T(8,128)(2,1)} %shard_map.127), calls=%async_computation | async-start | bytes 131072 | tf_op jit(solution)/shard_map/all_to_all | solution.py:278
  11.4 1.1 %copy-start.2 = (bf16[24,128,128]{2,1,0:T(8,128)(2,1)S(1)}, bf16[24,128,128]{2,1,0:T(8,128)(2,1)}, u32[]{:S(2)}) copy-start(bf16[24,128,128]{2,1,0:T(8,128)(2,1)} %blocks_ref.1) | copy-start | bytes 2359300
  12.5 2.4 %copy-start.4 = (f32[1024]{0:T(1024)S(1)}, f32[1024]{0:T(1024)}, u32[]{:S(2)}) copy-start(f32[1024]{0:T(1024)} %param.17) | copy-start | bytes 12292
  12.5 2.5 %copy-start.7 = (bf16[128,128]{1,0:T(8,128)(2,1)S(1)}, bf16[128,128]{1,0:T(8,128)(2,1)}, u32[]{:S(2)}) copy-start(bf16[128,128]{1,0:T(8,128)(2,1)} %coupling_ref.1) | copy-start | bytes 98308
  12.5 2.5 %copy-start.8 = (s32[1,128]{1,0:T(1,128)S(1)}, s32[1,128]{1,0:T(1,128)}, u32[]{:S(2)}) copy-start(s32[1,128]{1,0:T(1,128)} %east_ref.1) | copy-start | bytes 1540
  12.5 2.5 %copy-start.9 = (s32[1,128]{1,0:T(1,128)S(1)}, s32[1,128]{1,0:T(1,128)}, u32[]{:S(2)}) copy-start(s32[1,128]{1,0:T(1,128)} %west_ref.1) | copy-start | bytes 1540
  12.5 5.6 %copy-start.3 = (bf16[64,1024]{1,0:T(8,128)(2,1)S(1)}, bf16[64,1024]{1,0:T(8,128)(2,1)}, u32[]{:S(2)}) copy-start(bf16[64,1024]{1,0:T(8,128)(2,1)} %inverse_ref.3) | copy-start | bytes 393220
  12.5 5.6 %copy-start.5 = (f32[1024]{0:T(1024)S(1)}, f32[1024]{0:T(1024)}, u32[]{:S(2)}) copy-start(f32[1024]{0:T(1024)} %param.18) | copy-start | bytes 12292
  12.5 5.6 %copy-start.6 = (f32[1024]{0:T(1024)S(1)}, f32[1024]{0:T(1024)}, u32[]{:S(2)}) copy-start(f32[1024]{0:T(1024)} %param.16) | copy-start | bytes 12292
  16.9 1.3 %collective-permute-start = (bf16[8,32,128]{2,1,0:T(8,128)(2,1)S(1)}, bf16[8,32,128]{2,1,0:T(8,128)(2,1)S(1)}, u32[]{:S(2)}, u32[]{:S(2)}) collective-permute-start(bf16[8,32,128]{2,1,0:T(8,128)(2,1)S(1)} %all-to-all-done.pieces_ref), channel_id=1, source_target_pairs={{0,1},{1,0},{2,3},{3,2},{4,5},{5,4},{6,7},{7,6},{8,9},{9,8},{10,11... | collective-permute-start | bytes 196616 | tf_op jit(solution)/shard_map/ppermute | solution.py:282
  20.0 9.3 %collective-permute-start.1 = (bf16[384,128]{1,0:T(8,128)(2,1)S(1)}, bf16[384,128]{1,0:T(8,128)(2,1)S(1)}, u32[]{:S(2)}, u32[]{:S(2)}) collective-permute-start(bf16[384,128]{1,0:T(8,128)(2,1)S(1)} %get-tuple-element.34), channel_id=1, source_target_pairs={{0,14},{2,4},{4,2},{6,8},{8,6},{10,12},{12,10},{14,0},{1,15},{3,5}... | collective-permute-start | bytes 294920 | tf_op jit(solution)/shard_map/ppermute | solution.py:291
  23.7 6.1 %collective-permute-start.3 = (bf16[384,128]{1,0:T(8,128)(2,1)S(1)}, bf16[384,128]{1,0:T(8,128)(2,1)S(1)}, u32[]{:S(2)}, u32[]{:S(2)}) collective-permute-start(bf16[384,128]{1,0:T(8,128)(2,1)S(1)} %get-tuple-element.36), channel_id=1, source_target_pairs={{0,2},{2,0},{4,6},{6,4},{8,10},{10,8},{12,14},{14,12},{1,3},{3,1},... | collective-permute-start | bytes 294920 | tf_op jit(solution)/shard_map/ppermute | solution.py:291
  23.7 5.5 %collective-permute-start.2 = (bf16[64,128]{1,0:T(8,128)(2,1)S(1)}, bf16[64,128]{1,0:T(8,128)(2,1)S(1)}, u32[]{:S(2)}, u32[]{:S(2)}) collective-permute-start(bf16[64,128]{1,0:T(8,128)(2,1)S(1)} %get-tuple-element.35.own_beyond_ref), channel_id=1, source_target_pairs={{0,12},{2,14},{4,8},{6,10},{8,4},{10,6},{12,0},{14,2},{1,13},{3,15... | collective-permute-start | bytes 49160 | tf_op jit(solution)/shard_map/ppermute | solution.py:291
  25.3 3.9 %collective-permute-start.4 = (bf16[64,128]{1,0:T(8,128)(2,1)S(1)}, bf16[64,128]{1,0:T(8,128)(2,1)S(1)}, u32[]{:S(2)}, u32[]{:S(2)}) collective-permute-start(bf16[64,128]{1,0:T(8,128)(2,1)S(1)} %get-tuple-element.37.own_far_ref), channel_id=1, source_target_pairs={{0,4},{2,6},{4,0},{6,2},{8,12},{10,14},{12,8},{14,10},{1,5},{3,7},... | collective-permute-start | bytes 49160 | tf_op jit(solution)/shard_map/ppermute | solution.py:291
  43.0 1.4 %collective-permute-start.5 = (f32[8,40,128]{2,1,0:T(8,128)S(1)}, f32[8,40,128]{2,1,0:T(8,128)S(1)}, u32[]{:S(2)}, u32[]{:S(2)}) collective-permute-start(f32[8,40,128]{2,1,0:T(8,128)S(1)} %all_to_all.15.second_ref), channel_id=1, source_target_pairs={{0,1},{1,0},{2,3},{3,2},{4,5},{5,4},{6,7},{7,6},{8,9},{9,8},{10,11... | collective-permute-start | bytes 491528 | tf_op jit(solution)/shard_map/ppermute | solution.py:282
  46.6 6.5 %collective-permute-start.6 = (bf16[64,128]{1,0:T(8,128)(2,1)S(1)}, bf16[64,128]{1,0:T(8,128)(2,1)S(1)}, u32[]{:S(2)}, u32[]{:S(2)}) collective-permute-start(bf16[64,128]{1,0:T(8,128)(2,1)S(1)} %get-tuple-element.43), channel_id=1, source_target_pairs={{0,14},{2,4},{4,2},{6,8},{8,6},{10,12},{12,10},{14,0},{1,15},{3,5}... | collective-permute-start | bytes 49160 | tf_op jit(solution)/shard_map/ppermute | solution.py:291
  47.9 5.2 %collective-permute-start.7 = (bf16[64,128]{1,0:T(8,128)(2,1)S(1)}, bf16[64,128]{1,0:T(8,128)(2,1)S(1)}, u32[]{:S(2)}, u32[]{:S(2)}) collective-permute-start(bf16[64,128]{1,0:T(8,128)(2,1)S(1)} %get-tuple-element.44), channel_id=1, source_target_pairs={{0,2},{2,0},{4,6},{6,4},{8,10},{10,8},{12,14},{14,12},{1,3},{3,1},... | collective-permute-start | bytes 49160 | tf_op jit(solution)/shard_map/ppermute | solution.py:291
  63.8 1.2 %collective-permute-start.8 = (f32[8,8,128]{2,1,0:T(8,128)S(1)}, f32[8,8,128]{2,1,0:T(8,128)S(1)}, u32[]{:S(2)}, u32[]{:S(2)}) collective-permute-start(f32[8,8,128]{2,1,0:T(8,128)S(1)} %all_to_all.16.chunks_ref), channel_id=1, source_target_pairs={{0,1},{1,0},{2,3},{3,2},{4,5},{5,4},{6,7},{7,6},{8,9},{9,8},{10,11... | collective-permute-start | bytes 98312 | tf_op jit(solution)/shard_map/ppermute | solution.py:282

commit v5 on v4

--- a/solution.py
+++ b/solution.py
@@ -18,13 +18,13 @@
     return lax.dot_general(a, b, (((ca,), (cb,)), ((), ())), preferred_element_type=F32)
 
 
-def call(kernel, outs, specs, args, flops, scratch=(), limit=32):
+def call(kernel, outs, specs, args, flops, scratch=(), limit=32, placed=None):
     moved = sum(int(np.prod(a.shape)) * a.dtype.itemsize for a in args)
     return pl.pallas_call(
         kernel,
         out_shape=[jax.ShapeDtypeStruct(s, t) for s, t in outs],
         in_specs=specs,
-        out_specs=[VMEM] * len(outs),
+        out_specs=[(placed or {}).get(i, VMEM) for i in range(len(outs))],
         scratch_shapes=list(scratch),
         compiler_params=pltpu.CompilerParams(vmem_limit_bytes=limit * 1024 * 1024),
         cost_estimate=pl.CostEstimate(flops=flops, bytes_accessed=moved, transcendentals=0),
@@ -53,32 +53,45 @@
     return jnp.sum(first * second, axis=1, keepdims=True)
 
 
-def coarse_kernel(count_ref, right_hbm, vectors_hbm, chunks_ref, right_ref, vectors_ref, sems):
-    copies = [
-        pltpu.make_async_copy(right_hbm, right_ref, sems.at[0]),
-        pltpu.make_async_copy(vectors_hbm, vectors_ref, sems.at[1]),
-    ]
+def levels(values, edges):
+    return dot(values.astype(BF16), edges, 1, 1)
+
+
+def prep_kernel(at_ref, count_hbm, iface_hbm, pattern_hbm, blocks_hbm, right_hbm, vectors_hbm, coupling_hbm, east_hbm,
+                west_hbm, react_hbm, mass_hbm, obs_hbm, inverse_hbm,
+                chunks_ref, dense_hbm, edge_ref, to_west_ref, to_east_ref, near_ref, across_ref,
+                count_ref, iface_ref, pattern_ref, blocks_ref, right_ref, vectors_ref, coupling_ref, east_ref, west_ref,
+                react_ref, mass_ref, obs_ref, inverse_ref, total_ref, dense_ref, in_sems, out_sems):
+    pairs = (
+        (blocks_hbm, blocks_ref), (right_hbm, right_ref), (vectors_hbm, vectors_ref), (coupling_hbm, coupling_ref),
+        (count_hbm, count_ref), (iface_hbm, iface_ref), (pattern_hbm, pattern_ref), (east_hbm, east_ref),
+        (west_hbm, west_ref), (react_hbm, react_ref), (mass_hbm, mass_ref), (obs_hbm, obs_ref),
+        (inverse_hbm, inverse_ref),
+    )
+    copies = [pltpu.make_async_copy(src, dst, in_sems.at[i]) for i, (src, dst) in enumerate(pairs)]
     for copy in copies:
         copy.start()
+    samples, nodes = right_ref.shape
+    count, block, _ = blocks_ref.shape
+    slots = coupling_ref.shape[0]
+    strips = nodes // block
+
+    def clear(i, carry):
+        total_ref[pl.ds(pl.multiple_of(i * block, block), block), :] = jnp.zeros((block, nodes), F32)
+        return carry
+
+    lax.fori_loop(0, strips, clear, 0)
     for copy in copies:
         copy.wait()
-    active = active_of(count_ref, right_ref.shape[1]).astype(BF16)
-    coarse = fold(dot(vectors_ref[...], right_ref[...] * active, 1, 1)).astype(BF16)
+
+    active = active_of(count_ref, nodes)
+    right = active * right_ref[...].astype(F32)
+    coarse = fold(dot(vectors_ref[...], right.astype(BF16), 1, 1)).astype(BF16)
     chunks_ref[...] = jnp.broadcast_to(coarse[None], chunks_ref.shape)
 
-
-def dense_kernel(pattern_ref, blocks_ref, dense_ref, total_ref):
-    count, block, _ = blocks_ref.shape
-    nodes = dense_ref.shape[0]
     unit = (
         lax.broadcasted_iota(jnp.int32, (block, block), 0) == lax.broadcasted_iota(jnp.int32, (block, block), 1)
     ).astype(F32).astype(BF16)
-
-    def clear(i, carry):
-        total_ref[pl.ds(pl.multiple_of(i * block, block), block), :] = jnp.zeros((block, nodes), F32)
-        return carry
-
-    lax.fori_loop(0, nodes // block, clear, 0)
 
     def place(k, carry):
         rows = pl.ds(pl.multiple_of(pattern_ref[k, 0] * block, block), block)
@@ -90,33 +103,54 @@
 
     lax.fori_loop(0, count, place, 0, unroll=8)
 
+    def strip_copy(i):
+        rows = pl.ds(pl.multiple_of(i * block, block), block)
+        return pltpu.make_async_copy(dense_ref.at[rows, :], dense_hbm.at[rows, :], out_sems.at[i])
+
     def narrow(i, carry):
         rows = pl.ds(pl.multiple_of(i * block, block), block)
         dense_ref[rows, :] = total_ref[rows, :].astype(BF16)
+        strip_copy(i).start()
         return carry
 
-    lax.fori_loop(0, nodes // block, narrow, 0)
-
-
-def edge_kernel(iface_ref, coupling_ref, east_ref, west_ref, mass_ref, edge_ref, to_west_ref, to_east_ref):
-    slots = coupling_ref.shape[0]
-    nodes = mass_ref.shape[1]
+    lax.fori_loop(0, strips, narrow, 0)
+
     live_a = lax.broadcasted_iota(jnp.int32, (slots, slots), 0) < iface_ref[0]
     live_b = lax.broadcasted_iota(jnp.int32, (slots, slots), 1) < iface_ref[0]
     link = jnp.where(live_a & live_b, coupling_ref[...], jnp.zeros((slots, slots), BF16))
     node = lax.broadcasted_iota(jnp.int32, (slots, nodes), 1).astype(F32)
-    east = column_of(east_ref[...].astype(F32))
-    west = column_of(west_ref[...].astype(F32))
-    east_hot = jnp.where(node == east, 1.0, 0.0).astype(BF16)
-    west_hot = jnp.where(node == west, 1.0, 0.0).astype(BF16)
+    east_hot = jnp.where(node == column_of(east_ref[...].astype(F32)), 1.0, 0.0).astype(BF16)
+    west_hot = jnp.where(node == column_of(west_ref[...].astype(F32)), 1.0, 0.0).astype(BF16)
     spread = dot(link, east_hot, 0, 0).astype(BF16)
     edge_ref[0:slots, :] = spread
     edge_ref[slots : 2 * slots, :] = west_hot
-    edges = edge_ref[...]
-    scaled = (edges.astype(F32) * (1.0 / mass_ref[...])).astype(BF16)
+    edges = jnp.concatenate([spread, west_hot], axis=0)
+    react, mass = react_ref[...], mass_ref[...]
+    scaled = (edges.astype(F32) * (1.0 / mass)).astype(BF16)
     both = dot(scaled, edges, 1, 1).astype(BF16)
     to_east_ref[...] = both[:, 0:slots]
     to_west_ref[...] = both[:, slots:]
+
+    smooth_right = (right / (obs_ref[...] + react * react / mass)).astype(BF16)
+    masked = vectors_ref[...] * active.astype(BF16)
+    level = levels(jnp.concatenate([masked, smooth_right], axis=0), edges).astype(BF16)
+    rows, width = inverse_ref.shape
+    for ref in (near_ref, across_ref):
+        for j in range(width // LANES):
+            ref[j * rows : (j + 1) * rows, :] = inverse_ref[:, j * LANES : (j + 1) * LANES]
+
+    def send(east_ref, west_ref):
+        east_ref[width // LANES * rows :, :] = level[:, 0:slots]
+        west_ref[width // LANES * rows :, :] = level[:, slots:]
+
+    pl.when(at_ref[0] == 0)(lambda: send(near_ref, across_ref))
+    pl.when(at_ref[0] == 1)(lambda: send(across_ref, near_ref))
+
+    def finish(i, carry):
+        strip_copy(i).wait()
+        return carry
+
+    lax.fori_loop(0, strips, finish, 0)
 
 
 def unfold(lat, count, piece, coarse_ref):
@@ -184,7 +218,7 @@
 
 def image_kernel(at_ref, count_ref, across_ref, beyond_ref, near_ref, far_ref, own_far_ref, own_beyond_ref,
                  z_ref, scaled_ref, dense_ref, edge_ref, react_ref, mass_ref, obs_ref, right_ref, vectors_ref,
-                 image_ref, chunks_ref):
+                 image_ref, chunks_ref, near_out_ref, across_out_ref):
     samples, nodes = z_ref.shape
     active = active_of(count_ref, nodes)
     z = z_ref[...]
@@ -199,9 +233,19 @@
     second_east = from_east[samples : 2 * samples].astype(F32) + dot(east_terms, from_east[2 * samples :])
     second_west = from_west[samples : 2 * samples].astype(F32) + dot(west_terms, from_west[2 * samples :])
     arrived2 = jnp.concatenate([second_east, second_west], axis=1).astype(BF16)
-    stiff = dot(inner.astype(BF16), dense_ref[...]) + dot(arrived2, edges) + react_ref[...] * inner
-    image = active * (stiff + obs_ref[...] * z)
+    react, mass, obs = react_ref[...], mass_ref[...], obs_ref[...]
+    stiff = dot(inner.astype(BF16), dense_ref[...]) + dot(arrived2, edges) + react * inner
+    image = active * (stiff + obs * z)
     image_ref[...] = image
+    level = levels(image / (obs + react * react / mass), edges).astype(BF16)
+    slots = edges.shape[0] // 2
+
+    def send(east_ref, west_ref):
+        east_ref[...] = level[:, 0:slots]
+        west_ref[...] = level[:, slots:]
+
+    pl.when(at_ref[0] == 0)(lambda: send(near_out_ref, across_out_ref))
+    pl.when(at_ref[0] == 1)(lambda: send(across_out_ref, near_out_ref))
     coarse = fold(dot(vectors_ref[...], image.astype(BF16), 1, 1))
     half = coarse.shape[0]
     sums = row_of(row_sum(active * right_ref[...].astype(F32), z), row_sum(z, image))
@@ -210,9 +254,10 @@
     chunks_ref[:, half:, :] = jnp.broadcast_to(sums[None], (count, rows - half, LANES))
 
 
-def middle_kernel(at_ref, count_ref, pieces_ref, others_ref, second_ref, second_others_ref, inverse_ref, right_ref, image_ref, vectors_ref,
+def middle_kernel(at_ref, count_ref, pieces_ref, others_ref, second_ref, second_others_ref, across_ref, near_ref,
+                  across_first_ref, near_first_ref, inverse_ref, right_ref, image_ref, vectors_ref,
                   dense_ref, edge_ref, react_ref, mass_ref, obs_ref,
-                  z_ref, scaled_ref, near_ref, across_ref, sums_ref, coarse_ref):
+                  z_ref, sums_ref, chunks_ref, coarse_ref):
     samples, nodes = right_ref.shape
     count, half, _ = pieces_ref.shape
 
@@ -229,41 +274,41 @@
 
     unfold(at_ref[2], count, piece, coarse_ref)
     active = active_of(count_ref, nodes)
-    react, mass = react_ref[...], mass_ref[...]
+    react, mass, obs = react_ref[...], mass_ref[...], obs_ref[...]
     image = image_ref[...]
-    residual = active * right_ref[...].astype(F32) - column_of(step)[0:samples] * image
-    z = smooth(residual, coarse_ref, inverse_ref, vectors_ref, react, mass, obs_ref[...], active)
+    edges = edge_ref[...]
+    step_column = column_of(step)[0:samples]
+    residual = active * right_ref[...].astype(F32) - step_column * image
+    z = smooth(residual, coarse_ref, inverse_ref, vectors_ref, react, mass, obs, active)
     z_ref[...] = z
-    w = z.astype(BF16)
-    level1 = dot(w, edge_ref[...], 1, 1).astype(BF16)
-    slots = edge_ref.shape[0] // 2
-
-    def send(east_ref, west_ref):
-        east_ref[...] = level1[:, 0:slots]
-        west_ref[...] = level1[:, slots:]
-
-    pl.when(at_ref[0] == 0)(lambda: send(near_ref, across_ref))
-    pl.when(at_ref[0] == 1)(lambda: send(across_ref, near_ref))
-    scaled_ref[...] = dot(w, dense_ref[...]) + react * z
+
+    def arriving(first_ref, change_ref):
+        rows, width = inverse_ref.shape
+        blocks = width // LANES
+        inverse = jnp.concatenate([first_ref[j * rows : (j + 1) * rows, :] for j in range(blocks)], axis=1)
+        fix = dot(inverse, coarse_ref[...]).astype(BF16)
+        level = first_ref[blocks * rows :, :]
+        smooth_level = level[rows:].astype(F32) - step_column * change_ref[...].astype(F32)
+        return smooth_level + dot(fix, level[0:rows], 0, 0)
+
+    from_near, from_across = arriving(near_first_ref, near_ref), arriving(across_first_ref, across_ref)
+    keep = jnp.full((1, 1), at_ref[0], jnp.int32) == 0
+    from_east = jnp.where(keep, from_near, from_across)
+    from_west = jnp.where(keep, from_across, from_near)
+    arrived = jnp.concatenate([from_east, from_west], axis=1).astype(BF16)
+    stiff = dot(z.astype(BF16), dense_ref[...]) + react * z + dot(arrived, edges)
+    curve = jnp.sum(stiff * stiff / mass + obs * z * z, axis=1, keepdims=True)
     products = row_of(row_sum(residual, z), row_sum(z, image))
     row = lax.broadcasted_iota(jnp.int32, (8, LANES), 0)
-    sums_ref[...] = jnp.where(row == 0, products, sums)
-
-
-def last_kernel(at_ref, across_ref, near_ref, z_ref, scaled_ref, edge_ref, mass_ref, obs_ref, sums_ref, chunks_ref):
-    z = z_ref[...]
-    from_east, from_west = pick(at_ref[0], near_ref, across_ref)
-    stiff = scaled_ref[...] + dot(jnp.concatenate([from_east, from_west], axis=1), edge_ref[...])
-    curve = jnp.sum(stiff * stiff / mass_ref[...] + obs_ref[...] * z * z, axis=1, keepdims=True)
-    row = lax.broadcasted_iota(jnp.int32, (8, LANES), 0)
-    chunk = jnp.where(row == 0, sums_ref[0:1, :], row_of(curve, curve))
+    chunk = jnp.where(row == 0, products, row_of(curve, curve))
     chunks_ref[...] = jnp.broadcast_to(chunk[None], chunks_ref.shape)
-
-
-def finish_kernel(sums_ref, chunks_ref, others_ref, first_ref, second_ref, out_ref):
+    sums_ref[...] = jnp.broadcast_to(sums, sums_ref.shape)
+
+
+def finish_kernel(sums_ref, chunks_ref, first_ref, second_ref, out_ref):
     samples = first_ref.shape[0]
     half = LANES // 2
-    totals = jnp.sum(chunks_ref[...] + others_ref[...], axis=0)
+    totals = jnp.sum(chunks_ref[...], axis=0)
     norm0, curve0 = sums_ref[1:2, 0:half], sums_ref[1:2, half:]
     norm1, cross = totals[0:1, 0:half], totals[0:1, half:]
     curve = totals[1:2, 0:half]
@@ -274,8 +319,8 @@
     out_ref[...] = scales[0:samples] * first_ref[...] + scales[samples : 2 * samples] * second_ref[...]
 
 
-def exchange(chunks):
-    return lax.all_to_all(chunks, "lon", split_axis=0, concat_axis=0, tiled=True)
+def exchange(chunks, axes):
+    return lax.all_to_all(chunks, axes, split_axis=0, concat_axis=0, tiled=True)
 
 
 def other_band(array):
@@ -319,28 +364,33 @@
     lon = lax.axis_index("lon")
     at = jnp.stack([lon & 1, (lon >> 1) & 1, lax.axis_index("lat")]).astype(jnp.int32)
 
-    (chunks,) = call(
-        coarse_kernel,
-        [((sectors, half, LANES), BF16)],
-        [SMEM, HBM, HBM],
-        (node_count, right_side, deflation),
-        2 * samples * vectors * nodes,
-        [pltpu.VMEM((samples, nodes), BF16), pltpu.VMEM((vectors, nodes), BF16), pltpu.SemaphoreType.DMA((2,))],
+    blocks = coarse_inverse.shape[1] // LANES
+    static = ((blocks * vectors + vectors + samples, slots), BF16)
+    corr = ((2 * slots, slots), BF16)
+    inputs = (
+        node_count, iface_count, block_pattern, stiffness_blocks, right_side, deflation, coupling, east_rows, west_rows,
+        react, mass, obs, coarse_inverse,
+    )
+    small = 3
+    landing = [
+        pltpu.SMEM(a.shape, a.dtype) if i < small else pltpu.VMEM(a.shape, a.dtype) for i, a in enumerate(inputs)
+    ]
+    chunks, dense, edge, corr_west, corr_east, near_first, across_first = call(
+        prep_kernel,
+        [((sectors, half, LANES), BF16), ((nodes, nodes), BF16), ((2 * slots, nodes), BF16), corr, corr, static, static],
+        [SMEM] + [HBM] * len(inputs),
+        (at,) + inputs,
+        apply_cost,
+        landing + [
+            pltpu.VMEM((nodes, nodes), F32),
+            pltpu.VMEM((nodes, nodes), BF16),
+            pltpu.SemaphoreType.DMA((len(inputs),)),
+            pltpu.SemaphoreType.DMA((nodes // stiffness_blocks.shape[1],)),
+        ],
         64,
-    )
-    edge, corr_west, corr_east = call(
-        edge_kernel,
-        [((2 * slots, nodes), BF16), ((2 * slots, slots), BF16), ((2 * slots, slots), BF16)],
-        [SMEM, VMEM, VMEM, VMEM, VMEM],
-        (iface_count, coupling, east_rows, west_rows, mass),
-        8 * slots * slots * nodes,
-    )
-    (dense,) = call(dense_kernel, [((nodes, nodes), BF16)], [SMEM, VMEM], (block_pattern, stiffness_blocks),
-                    apply_cost, [pltpu.VMEM((nodes, nodes), F32)])
-
-    pieces, dense, edge, corr_west, corr_east = lax.optimization_barrier(
-        (exchange(chunks), dense, edge, corr_west, corr_east)
-    )
+        {1: HBM},
+    )
+    pieces = exchange(chunks, "lon")
     others = other_band(pieces)
     z0, scaled, near, across, far, beyond = call(
         start_kernel,
@@ -353,39 +403,33 @@
     )
     across = swap(across, 1, False)
     got_beyond = swap(beyond, 2, False)
+    near = swap(near, 1, True)
     got_far = swap(far, 2, True)
-    near = swap(near, 1, True)
-    image, chunks = call(
+    across_first = swap(across_first, 1, False)
+    near_first = swap(near_first, 1, True)
+    image, chunks, near_change, across_change = call(
         image_kernel,
-        [field, ((sectors, half + 8, LANES), F32)],
+        [field, ((sectors, half + 8, LANES), F32)] + [((samples, slots), BF16)] * 2,
         [SMEM, SMEM] + [VMEM] * 15,
         (at, node_count, across, got_beyond, near, got_far, far, beyond, z0, scaled, dense, edge,
          react, mass, obs, right_side, deflation),
         apply_cost,
     )
-    second = exchange(chunks)
+    across_change = swap(across_change, 1, False)
+    near_change = swap(near_change, 1, True)
+    second = exchange(chunks, "lon")
     second_others = other_band(second)
-    z1, scaled, near, across, sums = call(
+    z1, sums, chunks = call(
         middle_kernel,
-        [field] * 2 + [((samples, slots), BF16)] * 2 + [((8, LANES), F32)],
-        [SMEM, SMEM] + [VMEM] * 13,
-        (at, node_count, pieces, others, second, second_others, coarse_inverse, right_side, image, deflation, dense,
-         edge, react, mass, obs),
+        [field, ((8, LANES), F32), ((domains, 8, LANES), F32)],
+        [SMEM, SMEM] + [VMEM] * 17,
+        (at, node_count, pieces, others, second, second_others, across_change, near_change, across_first, near_first,
+         coarse_inverse, right_side, image, deflation, dense, edge, react, mass, obs),
         apply_cost,
         [coarse_scratch],
     )
-    across = swap(across, 1, False)
-    near = swap(near, 1, True)
-    (chunks,) = call(
-        last_kernel,
-        [((sectors, 8, LANES), F32)],
-        [SMEM] + [VMEM] * 8,
-        (at, across, near, z1, scaled, edge, mass, obs, sums),
-        apply_cost,
-    )
-    totals = exchange(chunks)
-    other_totals = other_band(totals)
-    (out,) = call(finish_kernel, [field], [VMEM] * 5, (sums, totals, other_totals, z0, z1), 4 * samples * nodes)
+    totals = exchange(chunks, ("lon", "lat"))
+    (out,) = call(finish_kernel, [field], [VMEM] * 4, (sums, totals, z0, z1), 4 * samples * nodes)
     return out
 
 

time: 66.6 us -> 84 us (1.26)
  local copies, waits for them, and re-layouts: 1.94 us -> 14.3 us
  starting transfers between devices: 14.2 us -> 17.8 us
  waiting for transfers between devices: 14.5 us -> 11.2 us
  blocking collectives: 21.4 us -> 24.3 us
  Pallas kernels: 12.7 us -> 13.6 us
    unnamed x21 -> x51, local copies, waits for them, and re-layouts: 1.94 us -> 14.3 us
    ppermute x6 -> x8, starting transfers between devices: 6.8 us -> 14.4 us  [swap(): return lax.ppermute(array, 'lon', pairs)]
    all_to_all x1, starting transfers between devices: 7.4 us -> 3.38 us  [exchange(): return lax.all_to_all(chunks, axes, split_axis=0, concat_axis=0, tiled=True)]
    ppermute x6 -> x8, waiting for transfers between devices: 9.49 us -> 5.82 us  [swap(): return lax.ppermute(array, 'lon', pairs)]
    all_to_all x1, waiting for transfers between devices: 1.2 us -> 4.09 us  [exchange(): return lax.all_to_all(chunks, axes, split_axis=0, concat_axis=0, tiled=True)]
    all_to_all x2, blocking collectives: 21.4 us -> 24.3 us  [exchange(): return lax.all_to_all(chunks, axes, split_axis=0, concat_axis=0, tiled=True)]
    ppermute x3 -> x2, waiting for transfers between devices: 3.77 us -> 1.25 us  [other_band(): return lax.ppermute(array, 'lat', [(0, 1), (1, 0)])]
    pallas_call x8 -> x5, Pallas kernels: 12.7 us -> 13.6 us  [call(): pl.pallas_call(kernel, out_shape=[jax.ShapeDtypeStruct(s, t) for s, t in...]
  transfers between devices with their start and end apart: 10 -> 11, of which waited for: 7 -> 6; matrix products, arithmetic and copies ran while one was open for 1% -> 0% of each run, Pallas kernels for 5% -> 0%
where the time goes in v5:
time: 84 us; the launch traced here: 83.1 us
  blocking collectives  24.3 us (29%)
  starting transfers between devices  17.8 us (21%)
  local copies, waits for them, and re-layouts  14.3 us (17%)
  Pallas kernels  13.6 us (16%)
  waiting for transfers between devices  11.2 us (13%)
  between operations  1.49 us (2%)
    all_to_all x2, blocking collectives, exchange(): return lax.all_to_all(chunks, axes, split_axis=0, concat_axis=0, tiled=True)  24.3 us
    ppermute x8, starting transfers between devices, swap(): return lax.ppermute(array, 'lon', pairs)  14.4 us
    unnamed x51, local copies, waits for them, and re-layouts  14.3 us
    pallas_call x5, Pallas kernels, call(): pl.pallas_call(kernel, out_shape=[jax.ShapeDtypeStruct(s, t) for s, t in...  13.6 us
    ppermute x8, waiting for transfers between devices, swap(): return lax.ppermute(array, 'lon', pairs)  5.82 us
    all_to_all x1, waiting for transfers between devices, exchange(): return lax.all_to_all(chunks, axes, split_axis=0, concat_axis=0, tiled=True)  4.09 us
    all_to_all x1, starting transfers between devices, exchange(): return lax.all_to_all(chunks, axes, split_axis=0, concat_axis=0, tiled=True)  3.38 us
  transfers between devices with their start and end apart: 11, of which 6 were waited for; matrix products, arithmetic and copies ran while one was open for 0% of the time, Pallas kernels for 0%

profile of v5, /device:TPU:0, one launch (start us, length us, event | category | flops | bytes accessed | tf_op | source)
XLA Modules:
  0.0 83.1 jit_solution(6263401746398345729)
XLA Ops:
  1.3 1.4 %copy.14.pattern_hbm = s32[24,2]{1,0:T(8,128)} copy(s32[24,2]{0,1:T(2,128)} %param.15) | data formatting | bytes 384 | tf_op args[2]
  3.2 5.9 %shard_map.127 = (bf16[8,32,128]{2,1,0:T(8,128)(2,1)}, bf16[1024,1024]{1,0:T(8,128)(2,1)}, bf16[256,1024]{1,0:T(8,128)(2,1)}, bf16[256,128]{1,0:T(8,128)(2,1)}, ...) custom-call(s32[3]{0:T(128)} %pad_add_fusion.at_ref, s32[1]{0:T(128)S(6)} %copy.16.count_hbm.count_ref, ...), custom_call_target="tpu_custom_call" | custom-call | flops 134217728 | bytes 1225940 | tf_op jit(solution)/shard_map/pallas_call | solution.py:23
  9.2 14.2 %all_to_all.15.pieces_ref = bf16[8,32,128]{2,1,0:T(8,128)(2,1)S(1)} all-to-all(bf16[8,32,128]{2,1,0:T(8,128)(2,1)} %get-tuple-element.25), channel_id=1, replica_groups=mesh['grp'=2,'lon'=8,'lat'=2] {'lon'}, dimensions={0} | all-to-all | bytes 131072 | tf_op jit(solution)/shard_map/all_to_all | solution.py:323
  23.3 1.3 %collective-permute-done.others_ref = bf16[8,32,128]{2,1,0:T(8,128)(2,1)S(1)} collective-permute-done((bf16[8,32,128]{2,1,0:T(8,128)(2,1)S(1)}, bf16[8,32,128]{2,1,0:T(8,128)(2,1)S(1)}, u32[]{:S(2)}, u32[]{:S(2)}) %collective-permute-start) | collective-permute-done | bytes 65568 | tf_op jit(solution)/shard_map/ppermute | solution.py:327
  24.6 1.6 %copy-done = bf16[1024,1024]{1,0:T(8,128)(2,1)S(1)} copy-done((bf16[1024,1024]{1,0:T(8,128)(2,1)S(1)}, bf16[1024,1024]{1,0:T(8,128)(2,1)}, u32[]{:S(2)}) %copy-start) | copy-done | bytes 2097176
  26.2 1.0 %copy-done.2 = bf16[256,1024]{1,0:T(8,128)(2,1)S(1)} copy-done((bf16[256,1024]{1,0:T(8,128)(2,1)S(1)}, bf16[256,1024]{1,0:T(8,128)(2,1)}, u32[]{:S(2)}) %copy-start.2) | copy-done | bytes 524312
  27.2 0.9 %copy-done.4 = bf16[64,1024]{1,0:T(8,128)(2,1)S(1)} copy-done((bf16[64,1024]{1,0:T(8,128)(2,1)S(1)}, bf16[64,1024]{1,0:T(8,128)(2,1)}, u32[]{:S(2)}) %copy-start.4) | copy-done | bytes 131096
  28.1 0.9 %copy-done.6 = bf16[64,1024]{1,0:T(8,128)(2,1)S(1)} copy-done((bf16[64,1024]{1,0:T(8,128)(2,1)S(1)}, bf16[64,1024]{1,0:T(8,128)(2,1)}, u32[]{:S(2)}) %copy-start.6) | copy-done | bytes 131096
  29.1 0.9 %copy-done.8 = bf16[64,1024]{1,0:T(8,128)(2,1)S(1)} copy-done((bf16[64,1024]{1,0:T(8,128)(2,1)S(1)}, bf16[64,1024]{1,0:T(8,128)(2,1)}, u32[]{:S(2)}) %copy-start.8) | copy-done | bytes 131096
  30.0 0.8 %copy-done.15 = bf16[256,128]{1,0:T(8,128)(2,1)S(1)} copy-done((bf16[256,128]{1,0:T(8,128)(2,1)S(1)}, bf16[256,128]{1,0:T(8,128)(2,1)}, u32[]{:S(2)}) %copy-start.15) | copy-done | bytes 65560
  30.8 0.8 %copy-done.16 = bf16[256,128]{1,0:T(8,128)(2,1)S(1)} copy-done((bf16[256,128]{1,0:T(8,128)(2,1)S(1)}, bf16[256,128]{1,0:T(8,128)(2,1)}, u32[]{:S(2)}) %copy-start.16) | copy-done | bytes 65560
  31.6 0.7 copy-done.17
  32.3 0.7 copy-done.19
  34.3 1.8 %shard_map.128 = (f32[64,1024]{1,0:T(8,128)S(1)}, f32[64,1024]{1,0:T(8,128)S(1)}, bf16[384,128]{1,0:T(8,128)(2,1)S(1)}, bf16[384,128]{1,0:T(8,128)(2,1)S(1)}, bf...) custom-call(s32[3]{0:T(128)S(1)} %copy-done.23, s32[1]{0:T(128)S(6)} %copy.16.count_hbm.count_ref, ...), custom_call_target="tpu_custom_call" | custom-call | flops 134217728 | bytes 3289104 | tf_op jit(solution)/shard_map/pallas_call | solution.py:23
  36.2 0.9 %collective-permute-start.1 = (bf16[384,128]{1,0:T(8,128)(2,1)S(1)}, bf16[384,128]{1,0:T(8,128)(2,1)S(1)}, u32[]{:S(2)}, u32[]{:S(2)}) collective-permute-start(bf16[384,128]{1,0:T(8,128)(2,1)S(1)} %get-tuple-element.30), channel_id=1, source_target_pairs={{0,14},{2,4},{4,2},{6,8},{8,6},{10,12},{12,10},{14,0},{1,15},{3,5}... | collective-permute-start | bytes 294920 | tf_op jit(solution)/shard_map/ppermute | solution.py:336
  37.1 0.8 %collective-permute-start.3 = (bf16[384,128]{1,0:T(8,128)(2,1)S(1)}, bf16[384,128]{1,0:T(8,128)(2,1)S(1)}, u32[]{:S(2)}, u32[]{:S(2)}) collective-permute-start(bf16[384,128]{1,0:T(8,128)(2,1)S(1)} %get-tuple-element.32), channel_id=1, source_target_pairs={{0,2},{2,0},{4,6},{6,4},{8,10},{10,8},{12,14},{14,12},{1,3},{3,1},... | collective-permute-start | bytes 294920 | tf_op jit(solution)/shard_map/ppermute | solution.py:336
  38.0 3.6 %collective-permute-start.2 = (bf16[64,128]{1,0:T(8,128)(2,1)S(1)}, bf16[64,128]{1,0:T(8,128)(2,1)S(1)}, u32[]{:S(2)}, u32[]{:S(2)}) collective-permute-start(bf16[64,128]{1,0:T(8,128)(2,1)S(1)} %get-tuple-element.31.own_beyond_ref), channel_id=1, source_target_pairs={{0,12},{2,14},{4,8},{6,10},{8,4},{10,6},{12,0},{14,2},{1,13},{3,15... | collective-permute-start | bytes 49160 | tf_op jit(solution)/shard_map/ppermute | solution.py:336
  41.6 1.9 %collective-permute-done.2.beyond_ref = bf16[64,128]{1,0:T(8,128)(2,1)S(1)} collective-permute-done((bf16[64,128]{1,0:T(8,128)(2,1)S(1)}, bf16[64,128]{1,0:T(8,128)(2,1)S(1)}, u32[]{:S(2)}, u32[]{:S(2)}) %collective-permute-start.2) | collective-permute-done | bytes 16416 | tf_op jit(solution)/shard_map/ppermute | solution.py:336
  43.5 1.8 %collective-permute-done.4.far_ref = bf16[64,128]{1,0:T(8,128)(2,1)S(1)} collective-permute-done((bf16[64,128]{1,0:T(8,128)(2,1)S(1)}, bf16[64,128]{1,0:T(8,128)(2,1)S(1)}, u32[]{:S(2)}, u32[]{:S(2)}) %collective-permute-start.4) | collective-permute-done | bytes 16416 | tf_op jit(solution)/shard_map/ppermute | solution.py:336
  45.3 1.9 %shard_map.129 = (f32[64,1024]{1,0:T(8,128)S(1)}, f32[8,40,128]{2,1,0:T(8,128)S(1)}, bf16[64,128]{1,0:T(8,128)(2,1)S(1)}, bf16[64,128]{1,0:T(8,128)(2,1)S(1)}) custom-call(s32[3]{0:T(128)S(1)} %copy-done.23, s32[1]{0:T(128)S(6)} %copy.16.count_hbm.count_ref, bf16[384,128]{1,0:T(8,128)(2,1)S(1)} %collective-permute-done.1.across_ref, ...), custom_call_target="tpu_custom_call" | custom-call | flops 134217728 | bytes 3682320 | tf_op jit(solution)/shard_map/pallas_call | solution.py:23
  47.3 0.7 copy-done.12
  48.6 3.4 %all-to-all-start.1 = ((f32[8,40,128]{2,1,0:T(8,128)}), f32[8,40,128]{2,1,0:T(8,128)S(1)}, u32[]{:S(2)}, u32[]{:S(2)}) async-start(f32[8,40,128]{2,1,0:T(8,128)} %copy-done.14), calls=%async_computation.1 | async-start | bytes 327680 | tf_op jit(solution)/shard_map/all_to_all | solution.py:323
  52.0 4.7 %collective-permute-start.8 = (bf16[640,128]{1,0:T(8,128)(2,1)}, bf16[640,128]{1,0:T(8,128)(2,1)}, u32[]{:S(2)}, u32[]{:S(2)}) collective-permute-start(bf16[640,128]{1,0:T(8,128)(2,1)} %get-tuple-element.39), channel_id=1, source_target_pairs={{0,14},{2,4},{4,2},{6,8},{8,6},{10,12},{12,10},{14,0},{1,15},{3,5}... | collective-permute-start | bytes 491528 | tf_op jit(solution)/shard_map/ppermute | solution.py:336
  56.7 4.1 %all-to-all-done.1.second_ref = f32[8,40,128]{2,1,0:T(8,128)S(1)} async-done(((f32[8,40,128]{2,1,0:T(8,128)}), f32[8,40,128]{2,1,0:T(8,128)S(1)}, u32[]{:S(2)}, u32[]{:S(2)}) %all-to-all-start.1) | async-done | bytes 163872 | tf_op jit(solution)/shard_map/all_to_all | solution.py:323
  60.8 0.9 %collective-permute-start.6 = (bf16[64,128]{1,0:T(8,128)(2,1)S(1)}, bf16[64,128]{1,0:T(8,128)(2,1)S(1)}, u32[]{:S(2)}, u32[]{:S(2)}) collective-permute-start(bf16[64,128]{1,0:T(8,128)(2,1)S(1)} %get-tuple-element.37), channel_id=1, source_target_pairs={{0,14},{2,4},{4,2},{6,8},{8,6},{10,12},{12,10},{14,0},{1,15},{3,5}... | collective-permute-start | bytes 49160 | tf_op jit(solution)/shard_map/ppermute | solution.py:336
  61.6 3.5 %collective-permute-start.7 = (bf16[64,128]{1,0:T(8,128)(2,1)S(1)}, bf16[64,128]{1,0:T(8,128)(2,1)S(1)}, u32[]{:S(2)}, u32[]{:S(2)}) collective-permute-start(bf16[64,128]{1,0:T(8,128)(2,1)S(1)} %get-tuple-element.38), channel_id=1, source_target_pairs={{0,2},{2,0},{4,6},{6,4},{8,10},{10,8},{12,14},{14,12},{1,3},{3,1},... | collective-permute-start | bytes 49160 | tf_op jit(solution)/shard_map/ppermute | solution.py:336
  65.5 1.7 %collective-permute-done.6.across_ref = bf16[64,128]{1,0:T(8,128)(2,1)S(1)} collective-permute-done((bf16[64,128]{1,0:T(8,128)(2,1)S(1)}, bf16[64,128]{1,0:T(8,128)(2,1)S(1)}, u32[]{:S(2)}, u32[]{:S(2)}) %collective-permute-start.6) | collective-permute-done | bytes 16416 | tf_op jit(solution)/shard_map/ppermute | solution.py:336
  67.3 0.8 copy-done.11
  68.1 0.9 %copy-done.13 = f32[64,1024]{1,0:T(8,128)S(1)} copy-done((f32[64,1024]{1,0:T(8,128)S(1)}, f32[64,1024]{1,0:T(8,128)}, u32[]{:S(2)}) %copy-start.13) | copy-done | bytes 262168
  69.1 2.8 %shard_map.130 = (f32[64,1024]{1,0:T(8,128)S(1)}, f32[8,128]{1,0:T(8,128)S(1)}, f32[16,8,128]{2,1,0:T(8,128)S(1)}) custom-call(s32[3]{0:T(128)S(1)} %copy-done.24, s32[1]{0:T(128)S(6)} %copy.16.count_hbm.count_ref, bf16[8,32,128]{2,1,0:T(8,128)(2,1)S(1)} %all_to_all.15.pieces_ref, bf16[8,32,128]{2,1,0:T(8,128)(2,1)S(1)} %copy-done.11, ...), custom_call_target="tpu_custom_call" | custom-call | flops 134217728 | bytes 4108304 | tf_op jit(solution)/shard_map/pallas_call | solution.py:23
  71.9 10.1 %all_to_all.16.chunks_ref = f32[16,8,128]{2,1,0:T(8,128)S(1)} all-to-all(f32[16,8,128]{2,1,0:T(8,128)S(1)} %get-tuple-element.43), channel_id=1, replica_groups=mesh['grp'=2,'lon'=8,'lat'=2] {'lon','lat'}, dimensions={0} | all-to-all | bytes 131072 | tf_op jit(solution)/shard_map/all_to_all | solution.py:323
  82.0 1.2 %shard_map.131 = f32[64,1024]{1,0:T(8,128)} custom-call(f32[8,128]{1,0:T(8,128)S(1)} %get-tuple-element.42.sums_ref, f32[16,8,128]{2,1,0:T(8,128)S(1)} %all_to_all.16.chunks_ref, f32[64,1024]{1,0:T(8,128)S(1)} %get-tuple-element.34.z_ref.first_ref, f32[64,1024]{1,0:T(8,128)S(1)} %get-tuple-element.44.second_ref), custom_call_target="tpu_custom_call" | custom-call | flops 262144 | bytes 593920 | tf_op jit(solution)/shard_map/pallas_call | solution.py:23
  (49 shorter events, 3.0 us)
Async XLA Ops:
  23.3 1.3 %collective-permute-start = (bf16[8,32,128]{2,1,0:T(8,128)(2,1)S(1)}, bf16[8,32,128]{2,1,0:T(8,128)(2,1)S(1)}, u32[]{:S(2)}, u32[]{:S(2)}) collective-permute-start(bf16[8,32,128]{2,1,0:T(8,128)(2,1)S(1)} %all_to_all.15.pieces_ref), channel_id=1, source_target_pairs={{0,1},{1,0},{2,3},{3,2},{4,5},{5,4},{6,7},{7,6},{8,9},{9,8},{10,11... | collective-permute-start | bytes 196616 | tf_op jit(solution)/shard_map/ppermute | solution.py:327
  24.6 11.6 %copy-start.10 = (bf16[8,32,128]{2,1,0:T(8,128)(2,1)}, bf16[8,32,128]{2,1,0:T(8,128)(2,1)S(1)}, u32[]{:S(2)}) copy-start(bf16[8,32,128]{2,1,0:T(8,128)(2,1)S(1)} %collective-permute-done.others_ref) | copy-start | bytes 196612
  24.6 1.6 %copy-start = (bf16[1024,1024]{1,0:T(8,128)(2,1)S(1)}, bf16[1024,1024]{1,0:T(8,128)(2,1)}, u32[]{:S(2)}) copy-start(bf16[1024,1024]{1,0:T(8,128)(2,1)} %get-tuple-element.26.dense_ref) | copy-start | bytes 6291460
  26.2 1.0 %copy-start.2 = (bf16[256,1024]{1,0:T(8,128)(2,1)S(1)}, bf16[256,1024]{1,0:T(8,128)(2,1)}, u32[]{:S(2)}) copy-start(bf16[256,1024]{1,0:T(8,128)(2,1)} %get-tuple-element.27.edge_ref) | copy-start | bytes 1572868
  27.2 0.9 %copy-start.4 = (bf16[64,1024]{1,0:T(8,128)(2,1)S(1)}, bf16[64,1024]{1,0:T(8,128)(2,1)}, u32[]{:S(2)}) copy-start(bf16[64,1024]{1,0:T(8,128)(2,1)} %right_ref.5) | copy-start | bytes 393220
  28.1 0.9 %copy-start.6 = (bf16[64,1024]{1,0:T(8,128)(2,1)S(1)}, bf16[64,1024]{1,0:T(8,128)(2,1)}, u32[]{:S(2)}) copy-start(bf16[64,1024]{1,0:T(8,128)(2,1)} %vectors_ref.5) | copy-start | bytes 393220
  29.1 0.9 %copy-start.8 = (bf16[64,1024]{1,0:T(8,128)(2,1)S(1)}, bf16[64,1024]{1,0:T(8,128)(2,1)}, u32[]{:S(2)}) copy-start(bf16[64,1024]{1,0:T(8,128)(2,1)} %inverse_ref.3) | copy-start | bytes 393220
  30.0 0.8 %copy-start.15 = (bf16[256,128]{1,0:T(8,128)(2,1)S(1)}, bf16[256,128]{1,0:T(8,128)(2,1)}, u32[]{:S(2)}) copy-start(bf16[256,128]{1,0:T(8,128)(2,1)} %get-tuple-element.28.to_west_ref) | copy-start | bytes 196612
  30.8 0.8 %copy-start.16 = (bf16[256,128]{1,0:T(8,128)(2,1)S(1)}, bf16[256,128]{1,0:T(8,128)(2,1)}, u32[]{:S(2)}) copy-start(bf16[256,128]{1,0:T(8,128)(2,1)} %get-tuple-element.29.to_east_ref) | copy-start | bytes 196612
  31.6 0.7 copy-start.17
  34.3 11.0 %copy-start.1 = (bf16[1024,1024]{1,0:T(8,128)(2,1)S(1)}, bf16[1024,1024]{1,0:T(8,128)(2,1)}, u32[]{:S(2)}) copy-start(bf16[1024,1024]{1,0:T(8,128)(2,1)} %get-tuple-element.26.dense_ref) | copy-start | bytes 6291460
  34.3 11.0 %copy-start.3 = (bf16[256,1024]{1,0:T(8,128)(2,1)S(1)}, bf16[256,1024]{1,0:T(8,128)(2,1)}, u32[]{:S(2)}) copy-start(bf16[256,1024]{1,0:T(8,128)(2,1)} %get-tuple-element.27.edge_ref) | copy-start | bytes 1572868
  36.2 31.1 %copy-start.5 = (bf16[64,1024]{1,0:T(8,128)(2,1)S(1)}, bf16[64,1024]{1,0:T(8,128)(2,1)}, u32[]{:S(2)}) copy-start(bf16[64,1024]{1,0:T(8,128)(2,1)} %right_ref.5) | copy-start | bytes 393220
  36.2 31.1 %copy-start.7 = (bf16[64,1024]{1,0:T(8,128)(2,1)S(1)}, bf16[64,1024]{1,0:T(8,128)(2,1)}, u32[]{:S(2)}) copy-start(bf16[64,1024]{1,0:T(8,128)(2,1)} %vectors_ref.5) | copy-start | bytes 393220
  36.2 31.1 %copy-start.9 = (bf16[64,1024]{1,0:T(8,128)(2,1)S(1)}, bf16[64,1024]{1,0:T(8,128)(2,1)}, u32[]{:S(2)}) copy-start(bf16[64,1024]{1,0:T(8,128)(2,1)} %inverse_ref.3) | copy-start | bytes 393220
  36.2 31.1 %copy-start.18 = (f32[1024]{0:T(1024)S(1)}, f32[1024]{0:T(1024)}, u32[]{:S(2)}) copy-start(f32[1024]{0:T(1024)} %param.16) | copy-start | bytes 12292
  36.2 31.1 %copy-start.20 = (f32[1024]{0:T(1024)S(1)}, f32[1024]{0:T(1024)}, u32[]{:S(2)}) copy-start(f32[1024]{0:T(1024)} %param.17) | copy-start | bytes 12292
  36.2 31.1 %copy-start.22 = (f32[1024]{0:T(1024)S(1)}, f32[1024]{0:T(1024)}, u32[]{:S(2)}) copy-start(f32[1024]{0:T(1024)} %param.18) | copy-start | bytes 12292
  36.2 31.1 %copy-start.24 = (s32[3]{0:T(128)S(1)}, s32[3]{0:T(128)}, u32[]{:S(2)}) copy-start(s32[3]{0:T(128)} %pad_add_fusion.at_ref) | copy-start | bytes 40
  36.2 9.1 %collective-permute-start.1 = (bf16[384,128]{1,0:T(8,128)(2,1)S(1)}, bf16[384,128]{1,0:T(8,128)(2,1)S(1)}, u32[]{:S(2)}, u32[]{:S(2)}) collective-permute-start(bf16[384,128]{1,0:T(8,128)(2,1)S(1)} %get-tuple-element.30), channel_id=1, source_target_pairs={{0,14},{2,4},{4,2},{6,8},{8,6},{10,12},{12,10},{14,0},{1,15},{3,5}... | collective-permute-start | bytes 294920 | tf_op jit(solution)/shard_map/ppermute | solution.py:336
  37.1 8.2 %collective-permute-start.3 = (bf16[384,128]{1,0:T(8,128)(2,1)S(1)}, bf16[384,128]{1,0:T(8,128)(2,1)S(1)}, u32[]{:S(2)}, u32[]{:S(2)}) collective-permute-start(bf16[384,128]{1,0:T(8,128)(2,1)S(1)} %get-tuple-element.32), channel_id=1, source_target_pairs={{0,2},{2,0},{4,6},{6,4},{8,10},{10,8},{12,14},{14,12},{1,3},{3,1},... | collective-permute-start | bytes 294920 | tf_op jit(solution)/shard_map/ppermute | solution.py:336
  38.0 5.5 %collective-permute-start.2 = (bf16[64,128]{1,0:T(8,128)(2,1)S(1)}, bf16[64,128]{1,0:T(8,128)(2,1)S(1)}, u32[]{:S(2)}, u32[]{:S(2)}) collective-permute-start(bf16[64,128]{1,0:T(8,128)(2,1)S(1)} %get-tuple-element.31.own_beyond_ref), channel_id=1, source_target_pairs={{0,12},{2,14},{4,8},{6,10},{8,4},{10,6},{12,0},{14,2},{1,13},{3,15... | collective-permute-start | bytes 49160 | tf_op jit(solution)/shard_map/ppermute | solution.py:336
  41.6 3.7 %collective-permute-start.4 = (bf16[64,128]{1,0:T(8,128)(2,1)S(1)}, bf16[64,128]{1,0:T(8,128)(2,1)S(1)}, u32[]{:S(2)}, u32[]{:S(2)}) collective-permute-start(bf16[64,128]{1,0:T(8,128)(2,1)S(1)} %get-tuple-element.33.own_far_ref), channel_id=1, source_target_pairs={{0,4},{2,6},{4,0},{6,2},{8,12},{10,14},{12,8},{14,10},{1,5},{3,7},... | collective-permute-start | bytes 49160 | tf_op jit(solution)/shard_map/ppermute | solution.py:336
  47.3 0.7 copy-start.12
  48.6 12.1 %all-to-all-start.1 = ((f32[8,40,128]{2,1,0:T(8,128)}), f32[8,40,128]{2,1,0:T(8,128)S(1)}, u32[]{:S(2)}, u32[]{:S(2)}) async-start(f32[8,40,128]{2,1,0:T(8,128)} %copy-done.14), calls=%async_computation.1 | async-start | bytes 327680 | tf_op jit(solution)/shard_map/all_to_all | solution.py:323
  52.0 13.1 %collective-permute-start.8 = (bf16[640,128]{1,0:T(8,128)(2,1)}, bf16[640,128]{1,0:T(8,128)(2,1)}, u32[]{:S(2)}, u32[]{:S(2)}) collective-permute-start(bf16[640,128]{1,0:T(8,128)(2,1)} %get-tuple-element.39), channel_id=1, source_target_pairs={{0,14},{2,4},{4,2},{6,8},{8,6},{10,12},{12,10},{14,0},{1,15},{3,5}... | collective-permute-start | bytes 491528 | tf_op jit(solution)/shard_map/ppermute | solution.py:336
  56.7 8.8 %collective-permute-start.9 = (bf16[640,128]{1,0:T(8,128)(2,1)}, bf16[640,128]{1,0:T(8,128)(2,1)}, u32[]{:S(2)}, u32[]{:S(2)}) collective-permute-start(bf16[640,128]{1,0:T(8,128)(2,1)} %get-tuple-element.40), channel_id=1, source_target_pairs={{0,2},{2,0},{4,6},{6,4},{8,10},{10,8},{12,14},{14,12},{1,3},{3,1},... | collective-permute-start | bytes 491528 | tf_op jit(solution)/shard_map/ppermute | solution.py:336
  60.8 6.4 %collective-permute-start.5 = (f32[8,40,128]{2,1,0:T(8,128)S(1)}, f32[8,40,128]{2,1,0:T(8,128)S(1)}, u32[]{:S(2)}, u32[]{:S(2)}) collective-permute-start(f32[8,40,128]{2,1,0:T(8,128)S(1)} %all-to-all-done.1.second_ref), channel_id=1, source_target_pairs={{0,1},{1,0},{2,3},{3,2},{4,5},{5,4},{6,7},{7,6},{8,9},{9,8},{10,11... | collective-permute-start | bytes 491528 | tf_op jit(solution)/shard_map/ppermute | solution.py:327
  60.8 6.4 %collective-permute-start.6 = (bf16[64,128]{1,0:T(8,128)(2,1)S(1)}, bf16[64,128]{1,0:T(8,128)(2,1)S(1)}, u32[]{:S(2)}, u32[]{:S(2)}) collective-permute-start(bf16[64,128]{1,0:T(8,128)(2,1)S(1)} %get-tuple-element.37), channel_id=1, source_target_pairs={{0,14},{2,4},{4,2},{6,8},{8,6},{10,12},{12,10},{14,0},{1,15},{3,5}... | collective-permute-start | bytes 49160 | tf_op jit(solution)/shard_map/ppermute | solution.py:336
  61.6 5.6 %collective-permute-start.7 = (bf16[64,128]{1,0:T(8,128)(2,1)S(1)}, bf16[64,128]{1,0:T(8,128)(2,1)S(1)}, u32[]{:S(2)}, u32[]{:S(2)}) collective-permute-start(bf16[64,128]{1,0:T(8,128)(2,1)S(1)} %get-tuple-element.38), channel_id=1, source_target_pairs={{0,2},{2,0},{4,6},{6,4},{8,10},{10,8},{12,14},{14,12},{1,3},{3,1},... | collective-permute-start | bytes 49160 | tf_op jit(solution)/shard_map/ppermute | solution.py:336
  67.3 0.8 %copy-start.11 = (bf16[8,32,128]{2,1,0:T(8,128)(2,1)S(1)}, bf16[8,32,128]{2,1,0:T(8,128)(2,1)}, u32[]{:S(2)}) copy-start(bf16[8,32,128]{2,1,0:T(8,128)(2,1)} %copy-done.10) | copy-start | bytes 196612
  68.1 0.9 %copy-start.13 = (f32[64,1024]{1,0:T(8,128)S(1)}, f32[64,1024]{1,0:T(8,128)}, u32[]{:S(2)}) copy-start(f32[64,1024]{1,0:T(8,128)} %copy-done.12) | copy-start | bytes 786436
  (4 other events, 2.6 us)

commit v6 on v5

v6 whole, which is shorter than its diff:
```python
import jax
import jax.numpy as jnp
import numpy as np
from jax import lax
from jax.experimental import pallas as pl
from jax.experimental.pallas import tpu as pltpu
from jax.sharding import PartitionSpec as P

F32 = jnp.float32
BF16 = jnp.bfloat16
VMEM = pl.BlockSpec(memory_space=pltpu.VMEM)
HBM = pl.BlockSpec(memory_space=pltpu.HBM)
SMEM = pl.BlockSpec(memory_space=pltpu.SMEM)
LANES = 128


def dot(a, b, ca=1, cb=0):
    return lax.dot_general(a, b, (((ca,), (cb,)), ((), ())), preferred_element_type=F32)


def call(kernel, outs, specs, args, flops, scratch=(), keep=False):
    moved = sum(int(np.prod(a.shape)) * a.dtype.itemsize for a in args)
    return pl.pallas_call(
        kernel,
        out_shape=[pltpu.VMEM(s, t) if keep else jax.ShapeDtypeStruct(s, t) for s, t in outs],
        in_specs=specs,
        out_specs=[VMEM] * len(outs),
        scratch_shapes=list(scratch),
        compiler_params=pltpu.CompilerParams(vmem_limit_bytes=32 * 1024 * 1024),
        cost_estimate=pl.CostEstimate(flops=flops, bytes_accessed=moved, transcendentals=0),
    )(*args)


def fold(values):
    half = values.shape[0] // 2
    return jnp.concatenate([values[:half], values[half:]], axis=1)


def column_of(row):
    return jnp.transpose(jnp.broadcast_to(row, (LANES, LANES)))[:, 0:1]


def row_of(first, second):
    both = jnp.concatenate([first, second], axis=0)
    return jnp.transpose(jnp.broadcast_to(both, (LANES, LANES)))[0:1]


def row_sum(first, second):
    return jnp.sum(first * second, axis=1, keepdims=True)


def levels(values, edges):
    return dot(values.astype(BF16), edges, 1, 1)


def by_lon(shift_by, first_ref, second_ref, write):
    bit = (lax.axis_index("lon") >> shift_by) & 1
    pl.when(bit == 0)(lambda: write(first_ref, second_ref))
    pl.when(bit == 1)(lambda: write(second_ref, first_ref))


def pick(shift_by, first, second):
    bit = (lax.axis_index("lon") >> shift_by) & 1
    keep = jnp.full((1, 1), bit, jnp.int32) == 0
    first, second = first.astype(F32), second.astype(F32)
    return jnp.where(keep, first, second).astype(BF16), jnp.where(keep, second, first).astype(BF16)


def load_kernel(count_ref, right_hbm, vectors_hbm, react_hbm, mass_hbm, obs_hbm,
                coupling_hbm, blocks_hbm, east_hbm, west_hbm, inverse_hbm,
                chunks_ref, diag_ref, right_ref, vectors_ref, coupling_ref, blocks_ref, east_ref, west_ref,
                inverse_ref, react_ref, mass_ref, obs_ref, sems):
    pairs = (
        (right_hbm, right_ref), (vectors_hbm, vectors_ref), (react_hbm, react_ref), (mass_hbm, mass_ref),
        (obs_hbm, obs_ref), (coupling_hbm, coupling_ref), (blocks_hbm, blocks_ref), (east_hbm, east_ref),
        (west_hbm, west_ref), (inverse_hbm, inverse_ref),
    )
    copies = [pltpu.make_async_copy(src, dst, sems.at[i]) for i, (src, dst) in enumerate(pairs)]
    for copy in copies:
        copy.start()
    for copy in copies[:5]:
        copy.wait()
    nodes = right_ref.shape[1]
    active = (lax.broadcasted_iota(jnp.int32, (1, nodes), 1) < count_ref[0]).astype(F32)
    coarse = fold(dot(vectors_ref[...], right_ref[...] * active.astype(BF16), 1, 1)).astype(BF16)
    chunks_ref[...] = jnp.broadcast_to(coarse[None], chunks_ref.shape)
    react, mass, obs = react_ref[...], mass_ref[...], obs_ref[...]
    row = lax.broadcasted_iota(jnp.int32, (8, nodes), 0)
    diag = jnp.zeros((8, nodes), F32)
    for i, line in enumerate((active, react, 1.0 / mass, obs, 1.0 / (obs + react * react / mass))):
        diag = jnp.where(row == i, line, diag)
    diag_ref[...] = diag
    for copy in copies[5:]:
        copy.wait()


def lines(diag_ref):
    return tuple(diag_ref[i : i + 1, :] for i in range(5))


def prep_kernel(iface_ref, pattern_ref, blocks_ref, right_ref, vectors_ref, coupling_ref, east_ref, west_ref, diag_ref,
                inverse_ref, dense_ref, edge_ref, to_west_ref, to_east_ref, near_ref, across_ref, total_ref):
    samples, nodes = right_ref.shape
    count, block, _ = blocks_ref.shape
    slots = coupling_ref.shape[0]

    def clear(i, carry):
        total_ref[pl.ds(pl.multiple_of(i * block, block), block), :] = jnp.zeros((block, nodes), F32)
        return carry

    lax.fori_loop(0, nodes // block, clear, 0)
    unit = (
        lax.broadcasted_iota(jnp.int32, (block, block), 0) == lax.broadcasted_iota(jnp.int32, (block, block), 1)
    ).astype(F32).astype(BF16)

    def place(k, carry):
        rows = pl.ds(pl.multiple_of(pattern_ref[k, 0] * block, block), block)
        cols = pl.ds(pl.multiple_of(pattern_ref[k, 1] * block, block), block)
        values = blocks_ref[k]
        total_ref[rows, cols] += values.astype(F32)
        total_ref[cols, rows] += dot(unit, values, 1, 1)
        return carry

    lax.fori_loop(0, count, place, 0, unroll=8)

    def narrow(i, carry):
        rows = pl.ds(pl.multiple_of(i * block, block), block)
        dense_ref[rows, :] = total_ref[rows, :].astype(BF16)
        return carry

    lax.fori_loop(0, nodes // block, narrow, 0)

    active, react, inverse_mass, obs, jacobi = lines(diag_ref)
    node = lax.broadcasted_iota(jnp.int32, (slots, nodes), 1).astype(F32)
    east_hot = jnp.where(node == column_of(east_ref[...].astype(F32)), 1.0, 0.0).astype(BF16)
    west_hot = jnp.where(node == column_of(west_ref[...].astype(F32)), 1.0, 0.0).astype(BF16)
    live_a = lax.broadcasted_iota(jnp.int32, (slots, slots), 0) < iface_ref[0]
    live_b = lax.broadcasted_iota(jnp.int32, (slots, slots), 1) < iface_ref[0]
    link = jnp.where(live_a & live_b, coupling_ref[...], jnp.zeros((slots, slots), BF16))
    spread = dot(link, east_hot, 0, 0).astype(BF16)
    edge_ref[0:slots, :] = spread
    edge_ref[slots : 2 * slots, :] = west_hot
    edges = jnp.concatenate([spread, west_hot], axis=0)
    both = dot((edges.astype(F32) * inverse_mass).astype(BF16), edges, 1, 1).astype(BF16)
    to_east_ref[...] = both[:, 0:slots]
    to_west_ref[...] = both[:, slots:]

    masked = vectors_ref[...] * active.astype(BF16)
    smooth_right = (active * jacobi * right_ref[...].astype(F32)).astype(BF16)
    level = levels(jnp.concatenate([masked, smooth_right], axis=0), edges).astype(BF16)
    rows, width = inverse_ref.shape
    for ref in (near_ref, across_ref):
        for j in range(width // LANES):
            ref[j * rows : (j + 1) * rows, :] = inverse_ref[:, j * LANES : (j + 1) * LANES]

    def send(east_ref, west_ref):
        east_ref[width // LANES * rows :, :] = level[:, 0:slots]
        west_ref[width // LANES * rows :, :] = level[:, slots:]

    by_lon(0, near_ref, across_ref, send)


def unfold(count, piece, coarse_ref):
    half = coarse_ref.shape[0] // count // 4
    lat = lax.axis_index("lat")

    def move(d, carry):
        for side in range(2):
            values = piece(side, d)
            at = pl.multiple_of((2 * d + (lat if side == 0 else 1 - lat)) * 2 * half, 2 * half)
            coarse_ref[pl.ds(at, half), :] = values[:, 0 : LANES // 2]
            coarse_ref[pl.ds(at + half, half), :] = values[:, LANES // 2 :]
        return carry

    lax.fori_loop(0, count, move, 0, unroll=min(count, 8))


def smooth(field, coarse_ref, inverse_ref, vectors_ref, active, jacobi):
    fix = dot(inverse_ref[...], coarse_ref[...]).astype(BF16)
    return active * (field * jacobi + dot(fix, vectors_ref[...], 0, 0))


def start_kernel(pieces_ref, others_ref, inverse_ref, right_ref, vectors_ref, dense_ref, edge_ref, diag_ref,
                 to_west_ref, to_east_ref,
                 z_ref, scaled_ref, near_ref, across_ref, far_ref, beyond_ref, coarse_ref):
    samples, nodes = right_ref.shape
    unfold(pieces_ref.shape[0], lambda side, d: (pieces_ref, others_ref)[side][d], coarse_ref)
    active, react, inverse_mass, obs, jacobi = lines(diag_ref)
    z = smooth(right_ref[...].astype(F32), coarse_ref, inverse_ref, vectors_ref, active, jacobi)
    z_ref[...] = z
    edges = edge_ref[...]
    scaled = (dot(z.astype(BF16), dense_ref[...]) + react * z) * inverse_mass
    scaled_ref[...] = scaled
    level1 = levels(z, edges).astype(BF16)
    level2 = levels(scaled, edges).astype(BF16)
    slots = edges.shape[0] // 2

    def send(east_ref, west_ref):
        for ref, cols, corr_ref in (
            (east_ref, slice(0, slots), to_east_ref),
            (west_ref, slice(slots, 2 * slots), to_west_ref),
        ):
            ref[0:samples, :] = level1[:, cols]
            ref[samples : 2 * samples, :] = level2[:, cols]
            ref[2 * samples :, :] = corr_ref[...]

    def send_far(east_ref, west_ref):
        east_ref[...] = level1[:, 0:slots]
        west_ref[...] = level1[:, slots:]

    by_lon(0, near_ref, across_ref, send)
    by_lon(1, far_ref, beyond_ref, send_far)


def image_kernel(across_ref, beyond_ref, near_ref, far_ref, own_far_ref, own_beyond_ref,
                 z_ref, scaled_ref, dense_ref, edge_ref, diag_ref, right_ref, vectors_ref,
                 image_ref, chunks_ref, near_out_ref, across_out_ref):
    samples, nodes = z_ref.shape
    active, react, inverse_mass, obs, jacobi = lines(diag_ref)
    z = z_ref[...]
    edges = edge_ref[...]
    from_east, from_west = pick(0, near_ref[...], across_ref[...])
    beyond_east, beyond_west = pick(1, far_ref[...], beyond_ref[...])
    own_east, own_west = pick(1, own_far_ref[...], own_beyond_ref[...])
    arrived = jnp.concatenate([from_east[0:samples], from_west[0:samples]], axis=1)
    inner = scaled_ref[...] + dot(arrived, edges) * inverse_mass
    east_terms = jnp.concatenate([beyond_east, own_east], axis=1)
    west_terms = jnp.concatenate([own_west, beyond_west], axis=1)
    second_east = from_east[samples : 2 * samples].astype(F32) + dot(east_terms, from_east[2 * samples :])
    second_west = from_west[samples : 2 * samples].astype(F32) + dot(west_terms, from_west[2 * samples :])
    arrived2 = jnp.concatenate([second_east, second_west], axis=1).astype(BF16)
    stiff = dot(inner.astype(BF16), dense_ref[...]) + dot(arrived2, edges) + react * inner
    image = active * (stiff + obs * z)
    image_ref[...] = image
    level = levels(image * jacobi, edges).astype(BF16)
    slots = edges.shape[0] // 2

    def send(east_ref, west_ref):
        east_ref[...] = level[:, 0:slots]
        west_ref[...] = level[:, slots:]

    by_lon(0, near_out_ref, across_out_ref, send)
    coarse = fold(dot(vectors_ref[...], image.astype(BF16), 1, 1))
    half = coarse.shape[0]
    sums = row_of(row_sum(active * right_ref[...].astype(F32), z), row_sum(z, image))
    count, rows, _ = chunks_ref.shape
    chunks_ref[:, 0:half, :] = jnp.broadcast_to(coarse[None], (count, half, LANES))
    chunks_ref[:, half:, :] = jnp.broadcast_to(sums[None], (count, rows - half, LANES))


def middle_kernel(pieces_ref, others_ref, second_ref, second_others_ref, across_ref, near_ref,
                  across_first_ref, near_first_ref, inverse_ref, right_ref, image_ref, vectors_ref,
                  dense_ref, edge_ref, diag_ref, z_ref, sums_ref, chunks_ref, coarse_ref):
    samples, nodes = right_ref.shape
    count, half, _ = pieces_ref.shape

    def add(d, total):
        return total + second_ref[d, half : half + 1, :] + second_others_ref[d, half : half + 1, :]

    sums = lax.fori_loop(0, count, add, jnp.zeros((1, LANES), F32), unroll=min(count, 8))
    step = sums[:, 0 : LANES // 2] / sums[:, LANES // 2 :]
    step = jnp.concatenate([step, step], axis=1)

    def piece(side, d):
        first, change = ((pieces_ref, second_ref), (others_ref, second_others_ref))[side]
        return (first[d].astype(F32) - step * change[d, 0:half, :]).astype(BF16)

    unfold(count, piece, coarse_ref)
    active, react, inverse_mass, obs, jacobi = lines(diag_ref)
    image = image_ref[...]
    edges = edge_ref[...]
    step_column = column_of(step)[0:samples]
    residual = active * right_ref[...].astype(F32) - step_column * image
    z = smooth(residual, coarse_ref, inverse_ref, vectors_ref, active, jacobi)
    z_ref[...] = z

    def arriving(first_ref, change_ref):
        rows, width = inverse_ref.shape
        blocks = width // LANES
        inverse = jnp.concatenate([first_ref[j * rows : (j + 1) * rows, :] for j in range(blocks)], axis=1)
        fix = dot(inverse, coarse_ref[...]).astype(BF16)
        level = first_ref[blocks * rows :, :]
        smooth_level = level[rows:].astype(F32) - step_column * change_ref[...].astype(F32)
        return smooth_level + dot(fix, level[0:rows], 0, 0)

    from_east, from_west = pick(0, arriving(near_first_ref, near_ref), arriving(across_first_ref, across_ref))
    arrived = jnp.concatenate([from_east, from_west], axis=1)
    stiff = dot(z.astype(BF16), dense_ref[...]) + react * z + dot(arrived, edges)
    curve = jnp.sum(stiff * stiff * inverse_mass + obs * z * z, axis=1, keepdims=True)
    products = row_of(row_sum(residual, z), row_sum(z, image))
    row = lax.broadcasted_iota(jnp.int32, (8, LANES), 0)
    chunk = jnp.where(row == 0, products, row_of(curve, curve))
    chunks_ref[...] = jnp.broadcast_to(chunk[None], chunks_ref.shape)
    sums_ref[...] = jnp.broadcast_to(sums, sums_ref.shape)


def finish_kernel(sums_ref, chunks_ref, first_ref, second_ref, out_ref):
    samples = first_ref.shape[0]
    half = LANES // 2
    totals = jnp.sum(chunks_ref[...], axis=0)
    norm0, curve0 = sums_ref[1:2, 0:half], sums_ref[1:2, half:]
    norm1, cross = totals[0:1, 0:half], totals[0:1, half:]
    curve = totals[1:2, 0:half]
    beta = norm1 / norm0
    step0 = norm0 / curve0
    step1 = norm1 / (curve + beta * (2.0 * cross + beta * curve0))
    scales = column_of(jnp.concatenate([step0 + step1 * beta, step1], axis=1))
    out_ref[...] = scales[0:samples] * first_ref[...] + scales[samples : 2 * samples] * second_ref[...]


def exchange(chunks, axes):
    return lax.all_to_all(chunks, axes, split_axis=0, concat_axis=0, tiled=True)


def other_band(array):
    return lax.ppermute(array, "lat", [(0, 1), (1, 0)])


def swap(array, reach, inner):
    size = lax.axis_size("lon")
    pairs = []
    for i in range(size):
        up = (i // reach) % 2 == (0 if inner else 1)
        pairs.append((i, (i + (reach if up else -reach)) % size))
    return lax.ppermute(array, "lon", pairs)


def body(
    right_side,
    stiffness_blocks,
    block_pattern,
    reaction,
    lumped_mass,
    obs_precision,
    coupling,
    east_rows,
    west_rows,
    iface_count,
    node_count,
    deflation,
    coarse_inverse,
):
    samples, nodes = right_side.shape
    slots = coupling.shape[0]
    vectors = deflation.shape[0]
    sectors = lax.axis_size("lon")
    domains = sectors * lax.axis_size("lat")
    half = vectors // 2
    react, mass, obs = reaction[None], lumped_mass[None], obs_precision[None]
    field = ((samples, nodes), F32)
    coarse_scratch = pltpu.VMEM((domains * vectors, samples), BF16)
    apply_cost = 2 * samples * nodes * nodes
    blocks = coarse_inverse.shape[1] // LANES
    static = ((blocks * vectors + vectors + samples, slots), BF16)
    corr = ((2 * slots, slots), BF16)
    kept = (right_side, deflation, coupling, stiffness_blocks, east_rows, west_rows, coarse_inverse)
    inputs = (right_side, deflation, react, mass, obs, coupling, stiffness_blocks, east_rows, west_rows, coarse_inverse)
    line = pltpu.VMEM((1, nodes), F32)
    chunks, diag, right, basis, link, stored, east, west, inverse = call(
        load_kernel,
        [((sectors, half, LANES), BF16), ((8, nodes), F32)] + [(a.shape, a.dtype) for a in kept],
        [SMEM] + [HBM] * len(inputs),
        [node_count] + [pltpu.with_memory_space_constraint(a, pltpu.HBM) for a in inputs],
        2 * samples * vectors * nodes,
        [line, line, line, pltpu.SemaphoreType.DMA((len(inputs),))],
        keep=True,
    )
    dense, edge, corr_west, corr_east, near_first, across_first = call(
        prep_kernel,
        [((nodes, nodes), BF16), ((2 * slots, nodes), BF16), corr, corr, static, static],
        [SMEM, SMEM] + [VMEM] * 8,
        (iface_count, block_pattern, stored, right, basis, link, east, west, diag, inverse),
        apply_cost,
        [pltpu.VMEM((nodes, nodes), F32)],
        keep=True,
    )
    pieces, dense, edge, corr_west, corr_east, near_first, across_first = lax.optimization_barrier(
        (exchange(chunks, "lon"), dense, edge, corr_west, corr_east, near_first, across_first)
    )
    others = other_band(pieces)
    z0, scaled, near, across, far, beyond = call(
        start_kernel,
        [field] * 2 + [((2 * samples + 2 * slots, slots), BF16)] * 2 + [((samples, slots), BF16)] * 2,
        [VMEM] * 10,
        (pieces, others, inverse, right, basis, dense, edge, diag, corr_west, corr_east),
        apply_cost,
        [coarse_scratch],
    )
    across = swap(across, 1, False)
    got_beyond = swap(beyond, 2, False)
    near = swap(near, 1, True)
    got_far = swap(far, 2, True)
    across_first = swap(across_first, 1, False)
    near_first = swap(near_first, 1, True)
    image, chunks, near_change, across_change = call(
        image_kernel,
        [field, ((sectors, half + 8, LANES), F32)] + [((samples, slots), BF16)] * 2,
        [VMEM] * 13,
        (across, got_beyond, near, got_far, far, beyond, z0, scaled, dense, edge, diag, right, basis),
        apply_cost,
    )
    second, across_change, near_change, across_first, near_first = lax.optimization_barrier(
        (exchange(chunks, "lon"), swap(across_change, 1, False), swap(near_change, 1, True), across_first, near_first)
    )
    second_others = other_band(second)
    z1, sums, chunks = call(
        middle_kernel,
        [field, ((8, LANES), F32), ((domains, 8, LANES), F32)],
        [VMEM] * 15,
        (pieces, others, second, second_others, across_change, near_change, across_first, near_first,
         inverse, right, image, basis, dense, edge, diag),
        apply_cost,
        [coarse_scratch],
    )
    totals = exchange(chunks, ("lon", "lat"))
    (out,) = call(finish_kernel, [field], [VMEM] * 4, (sums, totals, z0, z1), 4 * samples * nodes)
    return out


def solution(mesh):
    placed = (
        P(None, ("grp", "lon", "lat")),
        P(("grp", "lon", "lat"), None, None),
        P(("grp", "lon", "lat"), None),
        P(("grp", "lon", "lat")),
        P(("grp", "lon", "lat")),
        P(("grp", "lon", "lat")),
        P(("grp", "lon", "lat"), None),
        P(("grp", "lon", "lat"), None),
        P(("grp", "lon", "lat"), None),
        P(("grp", "lon", "lat")),
        P(("grp", "lon", "lat")),
        P(None, ("grp", "lon", "lat")),
        P(("grp", "lon", "lat"), None),
    )
    return jax.shard_map(
        body, mesh=mesh, in_specs=placed, out_specs=P(None, ("grp", "lon", "lat")), check_vma=False
    )
```

time: 84 us -> 72.9 us (0.87)
  blocking collectives: 24.3 us -> 9.49 us
  starting transfers between devices: 17.8 us -> 25.2 us
  Pallas kernels: 13.6 us -> 10.9 us
  local copies, waits for them, and re-layouts: 14.3 us -> 12.9 us
  waiting for transfers between devices: 11.2 us -> 12.3 us
    all_to_all x2 -> x1, blocking collectives: 24.3 us -> 9.49 us  [exchange(): return lax.all_to_all(chunks, axes, split_axis=0, concat_axis=0, tiled=True)]
    all_to_all x1 -> x2, starting transfers between devices: 3.38 us -> 12 us  [exchange(): return lax.all_to_all(chunks, axes, split_axis=0, concat_axis=0, tiled=True)]
    all_to_all x1 -> x2, waiting for transfers between devices: 4.09 us -> 0.01 us  [exchange(): return lax.all_to_all(chunks, axes, split_axis=0, concat_axis=0, tiled=True)]
    ppermute x8, waiting for transfers between devices: 5.82 us -> 9.67 us  [swap(): return lax.ppermute(array, 'lon', pairs)]
    pallas_call x5 -> x6, Pallas kernels: 13.6 us -> 10.9 us  [call(): pl.pallas_call(kernel, out_shape=[pltpu.VMEM(s, t) if keep else jax.Shape...]
    ppermute x2, waiting for transfers between devices: 1.25 us -> 2.64 us  [other_band(): return lax.ppermute(array, 'lat', [(0, 1), (1, 0)])]
    unnamed x51 -> x35, local copies, waits for them, and re-layouts: 14.3 us -> 12.9 us
    ppermute x8, starting transfers between devices: 14.4 us -> 13.2 us  [swap(): return lax.ppermute(array, 'lon', pairs)]
  transfers between devices with their start and end apart: 11 -> 12, of which waited for: 6 -> 5; matrix products, arithmetic and copies ran while one was open for 0% -> 1% of each run, Pallas kernels for 0% -> 4%
where the time goes in v6:
time: 72.9 us; the launch traced here: 72.3 us
  starting transfers between devices  25.2 us (35%)
  local copies, waits for them, and re-layouts  12.9 us (18%)
  waiting for transfers between devices  12.3 us (17%)
  Pallas kernels  10.9 us (15%)
  blocking collectives  9.49 us (13%)
  between operations  1.39 us (2%)
    ppermute x8, starting transfers between devices, swap(): return lax.ppermute(array, 'lon', pairs)  13.2 us
    unnamed x35, local copies, waits for them, and re-layouts  12.9 us
    all_to_all x2, starting transfers between devices, exchange(): return lax.all_to_all(chunks, axes, split_axis=0, concat_axis=0, tiled=True)  12 us
    pallas_call x6, Pallas kernels, call(): pl.pallas_call(kernel, out_shape=[pltpu.VMEM(s, t) if keep else jax.Shape...  10.9 us
    ppermute x8, waiting for transfers between devices, swap(): return lax.ppermute(array, 'lon', pairs)  9.67 us
    all_to_all x1, blocking collectives, exchange(): return lax.all_to_all(chunks, axes, split_axis=0, concat_axis=0, tiled=True)  9.49 us
    ppermute x2, waiting for transfers between devices, other_band(): return lax.ppermute(array, 'lat', [(0, 1), (1, 0)])  2.64 us
  transfers between devices with their start and end apart: 12, of which 5 were waited for; matrix products, arithmetic and copies ran while one was open for 1% of the time, Pallas kernels for 4%

profile of v6, /device:TPU:0, one launch (start us, length us, event | category | flops | bytes accessed | tf_op | source)
XLA Modules:
  0.0 72.3 jit_solution(13970460566036787610)
XLA Ops:
  0.7 2.1 %shard_map.127 = (bf16[8,32,128]{2,1,0:T(8,128)(2,1)}, f32[8,1024]{1,0:T(8,128)S(1)}, bf16[64,1024]{1,0:T(8,128)(2,1)S(1)}, bf16[64,1024]{1,0:T(8,128)(2,1)S(1)}...) custom-call(s32[1]{0:T(128)S(6)} %copy.16.count_ref, ...), custom_call_target="tpu_custom_call" | custom-call | flops 8388608 | bytes 1225732 | tf_op jit(solution)/shard_map/pallas_call | solution.py:23
  2.8 0.9 %copy-done = bf16[24,128,128]{2,1,0:T(8,128)(2,1)} copy-done((bf16[24,128,128]{2,1,0:T(8,128)(2,1)}, bf16[24,128,128]{2,1,0:T(8,128)(2,1)S(1)}, u32[]{:S(2)}) %copy-start) | copy-done | bytes 786456
  3.6 7.3 %all-to-all-start = ((bf16[8,32,128]{2,1,0:T(8,128)(2,1)}), bf16[8,32,128]{2,1,0:T(8,128)(2,1)S(1)}, u32[]{:S(2)}, u32[]{:S(2)}) async-start(bf16[8,32,128]{2,1,0:T(8,128)(2,1)} %get-tuple-element.45), calls=%async_computation | async-start | bytes 131072 | tf_op jit(solution)/shard_map/all_to_all | solution.py:312
  11.5 0.8 %copy.14.pattern_ref = s32[24,2]{1,0:T(8,128)S(1)} copy(s32[24,2]{0,1:T(2,128)} %param.15) | data formatting | bytes 384 | tf_op args[2]
  12.3 1.1 %copy-done.1 = bf16[24,128,128]{2,1,0:T(8,128)(2,1)S(1)} copy-done((bf16[24,128,128]{2,1,0:T(8,128)(2,1)S(1)}, bf16[24,128,128]{2,1,0:T(8,128)(2,1)}, u32[]{:S(2)}) %copy-start.1) | copy-done | bytes 786456
  13.4 3.2 %shard_map.128 = (bf16[1024,1024]{1,0:T(8,128)(2,1)S(1)}, bf16[256,1024]{1,0:T(8,128)(2,1)S(1)}, bf16[256,128]{1,0:T(8,128)(2,1)S(1)}, bf16[256,128]{1,0:T(8,128...) custom-call(s32[1]{0:T(128)S(6)} %copy.15.iface_ref, s32[24,2]{1,0:T(8,128)S(1)} %copy.14.pattern_ref, ...), custom_call_target="tpu_custom_call" | custom-call | flops 134217728 | bytes 1246404 | tf_op jit(solution)/shard_map/pallas_call | solution.py:23
  16.7 0.7 copy-done.13
  17.3 0.7 copy-done.14
  18.0 1.3 %collective-permute-done.others_ref = bf16[8,32,128]{2,1,0:T(8,128)(2,1)S(1)} collective-permute-done((bf16[8,32,128]{2,1,0:T(8,128)(2,1)S(1)}, bf16[8,32,128]{2,1,0:T(8,128)(2,1)S(1)}, u32[]{:S(2)}, u32[]{:S(2)}) %collective-permute-start) | collective-permute-done | bytes 65568 | tf_op jit(solution)/shard_map/ppermute | solution.py:316
  19.2 1.3 %shard_map.129 = (f32[64,1024]{1,0:T(8,128)S(1)}, f32[64,1024]{1,0:T(8,128)S(1)}, bf16[384,128]{1,0:T(8,128)(2,1)S(1)}, bf16[384,128]{1,0:T(8,128)(2,1)S(1)}, bf...) custom-call(bf16[8,32,128]{2,1,0:T(8,128)(2,1)S(1)} %all-to-all-done.pieces_ref, ...), custom_call_target="tpu_custom_call" | custom-call | flops 134217728 | bytes 3309568 | tf_op jit(solution)/shard_map/pallas_call | solution.py:23
  20.5 4.8 %collective-permute-start.1 = (bf16[384,128]{1,0:T(8,128)(2,1)S(1)}, bf16[384,128]{1,0:T(8,128)(2,1)S(1)}, u32[]{:S(2)}, u32[]{:S(2)}) collective-permute-start(bf16[384,128]{1,0:T(8,128)(2,1)S(1)} %get-tuple-element.65), channel_id=1, source_target_pairs={{0,14},{2,4},{4,2},{6,8},{8,6},{10,12},{12,10},{14,0},{1,15},{3,5}... | collective-permute-start | bytes 294920 | tf_op jit(solution)/shard_map/ppermute | solution.py:325
  25.9 1.0 %collective-permute-start.4 = (bf16[64,128]{1,0:T(8,128)(2,1)S(1)}, bf16[64,128]{1,0:T(8,128)(2,1)S(1)}, u32[]{:S(2)}, u32[]{:S(2)}) collective-permute-start(bf16[64,128]{1,0:T(8,128)(2,1)S(1)} %get-tuple-element.68.own_far_ref), channel_id=1, source_target_pairs={{0,4},{2,6},{4,0},{6,2},{8,12},{10,14},{12,8},{14,10},{1,5},{3,7},... | collective-permute-start | bytes 49160 | tf_op jit(solution)/shard_map/ppermute | solution.py:325
  27.0 3.9 %collective-permute-done.2.beyond_ref = bf16[64,128]{1,0:T(8,128)(2,1)S(1)} collective-permute-done((bf16[64,128]{1,0:T(8,128)(2,1)S(1)}, bf16[64,128]{1,0:T(8,128)(2,1)S(1)}, u32[]{:S(2)}, u32[]{:S(2)}) %collective-permute-start.2) | collective-permute-done | bytes 16416 | tf_op jit(solution)/shard_map/ppermute | solution.py:325
  30.9 1.4 %shard_map.130 = (f32[64,1024]{1,0:T(8,128)S(1)}, f32[8,40,128]{2,1,0:T(8,128)S(1)}, bf16[64,128]{1,0:T(8,128)(2,1)S(1)}, bf16[64,128]{1,0:T(8,128)(2,1)S(1)}) custom-call(bf16[384,128]{1,0:T(8,128)(2,1)S(1)} %collective-permute-done.1.across_ref, bf16[64,128]{1,0:T(8,128)(2,1)S(1)} %collective-permute-done.2.beyond_ref, ...), custom_call_target="tpu_custom_call" | custom-call | flops 134217728 | bytes 3702784 | tf_op jit(solution)/shard_map/pallas_call | solution.py:23
  32.2 0.7 copy-done.4
  33.0 0.7 copy-done.10
  34.8 4.8 %all-to-all-start.1 = ((f32[8,40,128]{2,1,0:T(8,128)}), f32[8,40,128]{2,1,0:T(8,128)S(1)}, u32[]{:S(2)}, u32[]{:S(2)}) async-start(f32[8,40,128]{2,1,0:T(8,128)} %copy-done.10), calls=%async_computation.1 | async-start | bytes 327680 | tf_op jit(solution)/shard_map/all_to_all | solution.py:312
  39.6 4.7 %collective-permute-start.7 = (bf16[640,128]{1,0:T(8,128)(2,1)}, bf16[640,128]{1,0:T(8,128)(2,1)S(1)}, u32[]{:S(2)}, u32[]{:S(2)}) collective-permute-start(bf16[640,128]{1,0:T(8,128)(2,1)} %copy-done.14), channel_id=1, source_target_pairs={{0,14},{2,4},{4,2},{6,8},{8,6},{10,12},{12,10},{14,0},{1,15},{3,5}... | collective-permute-start | bytes 491528 | tf_op jit(solution)/shard_map/ppermute | solution.py:325
  44.3 2.0 %collective-permute-start.5 = (bf16[64,128]{1,0:T(8,128)(2,1)}, bf16[64,128]{1,0:T(8,128)(2,1)S(1)}, u32[]{:S(2)}, u32[]{:S(2)}) collective-permute-start(bf16[64,128]{1,0:T(8,128)(2,1)} %copy-done.16), channel_id=1, source_target_pairs={{0,14},{2,4},{4,2},{6,8},{8,6},{10,12},{12,10},{14,0},{1,15},{3,5}... | collective-permute-start | bytes 49160 | tf_op jit(solution)/shard_map/ppermute | solution.py:325
  46.3 3.3 %collective-permute-done.7.across_first_ref = bf16[640,128]{1,0:T(8,128)(2,1)S(1)} collective-permute-done((bf16[640,128]{1,0:T(8,128)(2,1)}, bf16[640,128]{1,0:T(8,128)(2,1)S(1)}, u32[]{:S(2)}, u32[]{:S(2)}) %collective-permute-start.7) | collective-permute-done | bytes 163872 | tf_op jit(solution)/shard_map/ppermute | solution.py:325
  49.6 0.7 copy-done.6
  50.3 2.5 %collective-permute-done.8.near_first_ref = bf16[640,128]{1,0:T(8,128)(2,1)S(1)} collective-permute-done((bf16[640,128]{1,0:T(8,128)(2,1)}, bf16[640,128]{1,0:T(8,128)(2,1)S(1)}, u32[]{:S(2)}, u32[]{:S(2)}) %collective-permute-start.8) | collective-permute-done | bytes 163872 | tf_op jit(solution)/shard_map/ppermute | solution.py:325
  52.8 0.7 copy-done.8
  54.1 1.4 %collective-permute-done.9.second_others_ref = f32[8,40,128]{2,1,0:T(8,128)S(1)} collective-permute-done((f32[8,40,128]{2,1,0:T(8,128)S(1)}, f32[8,40,128]{2,1,0:T(8,128)S(1)}, u32[]{:S(2)}, u32[]{:S(2)}) %collective-permute-start.9) | collective-permute-done | bytes 163872 | tf_op jit(solution)/shard_map/ppermute | solution.py:316
  55.5 0.8 %copy-done.3 = bf16[8,32,128]{2,1,0:T(8,128)(2,1)S(1)} copy-done((bf16[8,32,128]{2,1,0:T(8,128)(2,1)S(1)}, bf16[8,32,128]{2,1,0:T(8,128)(2,1)}, u32[]{:S(2)}) %copy-start.3) | copy-done | bytes 65560
  56.3 0.9 %copy-done.5 = f32[64,1024]{1,0:T(8,128)S(1)} copy-done((f32[64,1024]{1,0:T(8,128)S(1)}, f32[64,1024]{1,0:T(8,128)}, u32[]{:S(2)}) %copy-start.5) | copy-done | bytes 262168
  57.2 0.9 %copy-done.7 = bf16[640,128]{1,0:T(8,128)(2,1)S(1)} copy-done((bf16[640,128]{1,0:T(8,128)(2,1)S(1)}, bf16[640,128]{1,0:T(8,128)(2,1)}, u32[]{:S(2)}) %copy-start.7) | copy-done | bytes 163864
  58.2 0.9 %copy-done.9 = bf16[640,128]{1,0:T(8,128)(2,1)S(1)} copy-done((bf16[640,128]{1,0:T(8,128)(2,1)S(1)}, bf16[640,128]{1,0:T(8,128)(2,1)}, u32[]{:S(2)}) %copy-start.9) | copy-done | bytes 163864
  59.1 0.7 copy-done.12
  59.8 1.8 %shard_map.131 = (f32[64,1024]{1,0:T(8,128)S(1)}, f32[8,128]{1,0:T(8,128)S(1)}, f32[16,8,128]{2,1,0:T(8,128)S(1)}) custom-call(bf16[8,32,128]{2,1,0:T(8,128)(2,1)S(1)} %all-to-all-done.pieces_ref, bf16[8,32,128]{2,1,0:T(8,128)(2,1)S(1)} %copy-done.3, f32[8,40,128]{2,1,0:T(8,128)S(1)} %all-to-all-done.1.second_ref, ...), custom_call_target="tpu_custom_call" | custom-call | flops 134217728 | bytes 4128768 | tf_op jit(solution)/shard_map/pallas_call | solution.py:23
  61.6 9.5 %all_to_all.15.chunks_ref = f32[16,8,128]{2,1,0:T(8,128)S(1)} all-to-all(f32[16,8,128]{2,1,0:T(8,128)S(1)} %get-tuple-element.83), channel_id=1, replica_groups=mesh['grp'=2,'lon'=8,'lat'=2] {'lon','lat'}, dimensions={0} | all-to-all | bytes 131072 | tf_op jit(solution)/shard_map/all_to_all | solution.py:312
  71.1 1.2 %shard_map.132 = f32[64,1024]{1,0:T(8,128)} custom-call(f32[8,128]{1,0:T(8,128)S(1)} %get-tuple-element.82.sums_ref, f32[16,8,128]{2,1,0:T(8,128)S(1)} %all_to_all.15.chunks_ref, f32[64,1024]{1,0:T(8,128)S(1)} %get-tuple-element.69.z_ref.first_ref, f32[64,1024]{1,0:T(8,128)S(1)} %get-tuple-element.84.second_ref), custom_call_target="tpu_custom_call" | custom-call | flops 262144 | bytes 593920 | tf_op jit(solution)/shard_map/pallas_call | solution.py:23
  (34 shorter events, 2.5 us)
Async XLA Ops:
  2.7 0.9 %copy-start = (bf16[24,128,128]{2,1,0:T(8,128)(2,1)}, bf16[24,128,128]{2,1,0:T(8,128)(2,1)S(1)}, u32[]{:S(2)}) copy-start(bf16[24,128,128]{2,1,0:T(8,128)(2,1)S(1)} %get-tuple-element.46.blocks_ref) | copy-start | bytes 2359300
  3.6 14.3 %all-to-all-start = ((bf16[8,32,128]{2,1,0:T(8,128)(2,1)}), bf16[8,32,128]{2,1,0:T(8,128)(2,1)S(1)}, u32[]{:S(2)}, u32[]{:S(2)}) async-start(bf16[8,32,128]{2,1,0:T(8,128)(2,1)} %get-tuple-element.45), calls=%async_computation | async-start | bytes 131072 | tf_op jit(solution)/shard_map/all_to_all | solution.py:312
  12.3 1.1 %copy-start.1 = (bf16[24,128,128]{2,1,0:T(8,128)(2,1)S(1)}, bf16[24,128,128]{2,1,0:T(8,128)(2,1)}, u32[]{:S(2)}) copy-start(bf16[24,128,128]{2,1,0:T(8,128)(2,1)} %copy-done) | copy-start | bytes 2359300
  16.7 0.7 copy-start.13
  17.3 0.7 copy-start.14
  18.0 1.3 %collective-permute-start = (bf16[8,32,128]{2,1,0:T(8,128)(2,1)S(1)}, bf16[8,32,128]{2,1,0:T(8,128)(2,1)S(1)}, u32[]{:S(2)}, u32[]{:S(2)}) collective-permute-start(bf16[8,32,128]{2,1,0:T(8,128)(2,1)S(1)} %all-to-all-done.pieces_ref), channel_id=1, source_target_pairs={{0,1},{1,0},{2,3},{3,2},{4,5},{5,4},{6,7},{7,6},{8,9},{9,8},{10,11... | collective-permute-start | bytes 196616 | tf_op jit(solution)/shard_map/ppermute | solution.py:316
  19.2 13.0 %copy-start.2 = (bf16[8,32,128]{2,1,0:T(8,128)(2,1)}, bf16[8,32,128]{2,1,0:T(8,128)(2,1)S(1)}, u32[]{:S(2)}) copy-start(bf16[8,32,128]{2,1,0:T(8,128)(2,1)S(1)} %collective-permute-done.others_ref) | copy-start | bytes 196612
  20.5 10.3 %collective-permute-start.1 = (bf16[384,128]{1,0:T(8,128)(2,1)S(1)}, bf16[384,128]{1,0:T(8,128)(2,1)S(1)}, u32[]{:S(2)}, u32[]{:S(2)}) collective-permute-start(bf16[384,128]{1,0:T(8,128)(2,1)S(1)} %get-tuple-element.65), channel_id=1, source_target_pairs={{0,14},{2,4},{4,2},{6,8},{8,6},{10,12},{12,10},{14,0},{1,15},{3,5}... | collective-permute-start | bytes 294920 | tf_op jit(solution)/shard_map/ppermute | solution.py:325
  25.3 5.5 %collective-permute-start.3 = (bf16[384,128]{1,0:T(8,128)(2,1)S(1)}, bf16[384,128]{1,0:T(8,128)(2,1)S(1)}, u32[]{:S(2)}, u32[]{:S(2)}) collective-permute-start(bf16[384,128]{1,0:T(8,128)(2,1)S(1)} %get-tuple-element.67), channel_id=1, source_target_pairs={{0,2},{2,0},{4,6},{6,4},{8,10},{10,8},{12,14},{14,12},{1,3},{3,1},... | collective-permute-start | bytes 294920 | tf_op jit(solution)/shard_map/ppermute | solution.py:325
  25.3 5.5 %collective-permute-start.2 = (bf16[64,128]{1,0:T(8,128)(2,1)S(1)}, bf16[64,128]{1,0:T(8,128)(2,1)S(1)}, u32[]{:S(2)}, u32[]{:S(2)}) collective-permute-start(bf16[64,128]{1,0:T(8,128)(2,1)S(1)} %get-tuple-element.66.own_beyond_ref), channel_id=1, source_target_pairs={{0,12},{2,14},{4,8},{6,10},{8,4},{10,6},{12,0},{14,2},{1,13},{3,15... | collective-permute-start | bytes 49160 | tf_op jit(solution)/shard_map/ppermute | solution.py:325
  25.9 4.9 %collective-permute-start.4 = (bf16[64,128]{1,0:T(8,128)(2,1)S(1)}, bf16[64,128]{1,0:T(8,128)(2,1)S(1)}, u32[]{:S(2)}, u32[]{:S(2)}) collective-permute-start(bf16[64,128]{1,0:T(8,128)(2,1)S(1)} %get-tuple-element.68.own_far_ref), channel_id=1, source_target_pairs={{0,4},{2,6},{4,0},{6,2},{8,12},{10,14},{12,8},{14,10},{1,5},{3,7},... | collective-permute-start | bytes 49160 | tf_op jit(solution)/shard_map/ppermute | solution.py:325
  32.2 0.7 copy-start.4
  33.0 0.7 copy-start.10
  33.6 0.6 copy-start.15
  34.2 0.6 copy-start.16
  34.8 19.2 %all-to-all-start.1 = ((f32[8,40,128]{2,1,0:T(8,128)}), f32[8,40,128]{2,1,0:T(8,128)S(1)}, u32[]{:S(2)}, u32[]{:S(2)}) async-start(f32[8,40,128]{2,1,0:T(8,128)} %copy-done.10), calls=%async_computation.1 | async-start | bytes 327680 | tf_op jit(solution)/shard_map/all_to_all | solution.py:312
  39.6 10.1 %collective-permute-start.7 = (bf16[640,128]{1,0:T(8,128)(2,1)}, bf16[640,128]{1,0:T(8,128)(2,1)S(1)}, u32[]{:S(2)}, u32[]{:S(2)}) collective-permute-start(bf16[640,128]{1,0:T(8,128)(2,1)} %copy-done.14), channel_id=1, source_target_pairs={{0,14},{2,4},{4,2},{6,8},{8,6},{10,12},{12,10},{14,0},{1,15},{3,5}... | collective-permute-start | bytes 491528 | tf_op jit(solution)/shard_map/ppermute | solution.py:325
  44.3 8.5 %collective-permute-start.8 = (bf16[640,128]{1,0:T(8,128)(2,1)}, bf16[640,128]{1,0:T(8,128)(2,1)S(1)}, u32[]{:S(2)}, u32[]{:S(2)}) collective-permute-start(bf16[640,128]{1,0:T(8,128)(2,1)} %copy-done.13), channel_id=1, source_target_pairs={{0,2},{2,0},{4,6},{6,4},{8,10},{10,8},{12,14},{14,12},{1,3},{3,1},... | collective-permute-start | bytes 491528 | tf_op jit(solution)/shard_map/ppermute | solution.py:325
  44.3 9.1 %collective-permute-start.5 = (bf16[64,128]{1,0:T(8,128)(2,1)}, bf16[64,128]{1,0:T(8,128)(2,1)S(1)}, u32[]{:S(2)}, u32[]{:S(2)}) collective-permute-start(bf16[64,128]{1,0:T(8,128)(2,1)} %copy-done.16), channel_id=1, source_target_pairs={{0,14},{2,4},{4,2},{6,8},{8,6},{10,12},{12,10},{14,0},{1,15},{3,5}... | collective-permute-start | bytes 49160 | tf_op jit(solution)/shard_map/ppermute | solution.py:325
  46.3 7.1 %collective-permute-start.6 = (bf16[64,128]{1,0:T(8,128)(2,1)}, bf16[64,128]{1,0:T(8,128)(2,1)S(1)}, u32[]{:S(2)}, u32[]{:S(2)}) collective-permute-start(bf16[64,128]{1,0:T(8,128)(2,1)} %copy-done.15), channel_id=1, source_target_pairs={{0,2},{2,0},{4,6},{6,4},{8,10},{10,8},{12,14},{14,12},{1,3},{3,1},... | collective-permute-start | bytes 49160 | tf_op jit(solution)/shard_map/ppermute | solution.py:325
  49.6 0.7 copy-start.6
  52.8 0.7 copy-start.8
  53.4 0.6 copy-start.11
  54.1 1.4 %collective-permute-start.9 = (f32[8,40,128]{2,1,0:T(8,128)S(1)}, f32[8,40,128]{2,1,0:T(8,128)S(1)}, u32[]{:S(2)}, u32[]{:S(2)}) collective-permute-start(f32[8,40,128]{2,1,0:T(8,128)S(1)} %all-to-all-done.1.second_ref), channel_id=1, source_target_pairs={{0,1},{1,0},{2,3},{3,2},{4,5},{5,4},{6,7},{7,6},{8,9},{9,8},{10,11... | collective-permute-start | bytes 491528 | tf_op jit(solution)/shard_map/ppermute | solution.py:316
  55.5 0.8 %copy-start.3 = (bf16[8,32,128]{2,1,0:T(8,128)(2,1)S(1)}, bf16[8,32,128]{2,1,0:T(8,128)(2,1)}, u32[]{:S(2)}) copy-start(bf16[8,32,128]{2,1,0:T(8,128)(2,1)} %copy-done.2) | copy-start | bytes 196612
  56.3 0.9 %copy-start.5 = (f32[64,1024]{1,0:T(8,128)S(1)}, f32[64,1024]{1,0:T(8,128)}, u32[]{:S(2)}) copy-start(f32[64,1024]{1,0:T(8,128)} %copy-done.4) | copy-start | bytes 786436
  57.2 0.9 %copy-start.7 = (bf16[640,128]{1,0:T(8,128)(2,1)S(1)}, bf16[640,128]{1,0:T(8,128)(2,1)}, u32[]{:S(2)}) copy-start(bf16[640,128]{1,0:T(8,128)(2,1)} %copy-done.6) | copy-start | bytes 491524
  58.2 0.9 %copy-start.9 = (bf16[640,128]{1,0:T(8,128)(2,1)S(1)}, bf16[640,128]{1,0:T(8,128)(2,1)}, u32[]{:S(2)}) copy-start(bf16[640,128]{1,0:T(8,128)(2,1)} %copy-done.8) | copy-start | bytes 491524
  59.1 0.7 copy-start.12

commit v7 on v6

--- a/solution.py
+++ b/solution.py
@@ -363,7 +363,6 @@
         [node_count] + [pltpu.with_memory_space_constraint(a, pltpu.HBM) for a in inputs],
         2 * samples * vectors * nodes,
         [line, line, line, pltpu.SemaphoreType.DMA((len(inputs),))],
-        keep=True,
     )
     dense, edge, corr_west, corr_east, near_first, across_first = call(
         prep_kernel,
@@ -372,7 +371,6 @@
         (iface_count, block_pattern, stored, right, basis, link, east, west, diag, inverse),
         apply_cost,
         [pltpu.VMEM((nodes, nodes), F32)],
-        keep=True,
     )
     pieces, dense, edge, corr_west, corr_east, near_first, across_first = lax.optimization_barrier(
         (exchange(chunks, "lon"), dense, edge, corr_west, corr_east, near_first, across_first)

time: 72.9 us -> 72.9 us (level)
  no operation moved by 1% of the time
where the time goes in v7:
time: 72.9 us; the launch traced here: 72.3 us
  starting transfers between devices  25.2 us (35%)
  local copies, waits for them, and re-layouts  12.9 us (18%)
  waiting for transfers between devices  12.3 us (17%)
  Pallas kernels  10.9 us (15%)
  blocking collectives  9.49 us (13%)
  between operations  1.39 us (2%)
    ppermute x8, starting transfers between devices, swap(): return lax.ppermute(array, 'lon', pairs)  13.2 us
    unnamed x35, local copies, waits for them, and re-layouts  12.9 us
    all_to_all x2, starting transfers between devices, exchange(): return lax.all_to_all(chunks, axes, split_axis=0, concat_axis=0, tiled=True)  12 us
    pallas_call x6, Pallas kernels, call(): pl.pallas_call(kernel, out_shape=[pltpu.VMEM(s, t) if keep else jax.Shape...  10.9 us
    ppermute x8, waiting for transfers between devices, swap(): return lax.ppermute(array, 'lon', pairs)  9.67 us
    all_to_all x1, blocking collectives, exchange(): return lax.all_to_all(chunks, axes, split_axis=0, concat_axis=0, tiled=True)  9.49 us
    ppermute x2, waiting for transfers between devices, other_band(): return lax.ppermute(array, 'lat', [(0, 1), (1, 0)])  2.64 us
  transfers between devices with their start and end apart: 12, of which 5 were waited for; matrix products, arithmetic and copies ran while one was open for 1% of the time, Pallas kernels for 4%

profile of v7, /device:TPU:0, one launch (start us, length us, event | category | flops | bytes accessed | tf_op | source)
XLA Modules:
  0.0 72.3 jit_solution(13970460566036787610)
XLA Ops:
  0.7 2.1 %shard_map.127 = (bf16[8,32,128]{2,1,0:T(8,128)(2,1)}, f32[8,1024]{1,0:T(8,128)S(1)}, bf16[64,1024]{1,0:T(8,128)(2,1)S(1)}, bf16[64,1024]{1,0:T(8,128)(2,1)S(1)}...) custom-call(s32[1]{0:T(128)S(6)} %copy.16.count_ref, ...), custom_call_target="tpu_custom_call" | custom-call | flops 8388608 | bytes 1225732 | tf_op jit(solution)/shard_map/pallas_call | solution.py:23
  2.8 0.9 %copy-done = bf16[24,128,128]{2,1,0:T(8,128)(2,1)} copy-done((bf16[24,128,128]{2,1,0:T(8,128)(2,1)}, bf16[24,128,128]{2,1,0:T(8,128)(2,1)S(1)}, u32[]{:S(2)}) %copy-start) | copy-done | bytes 786456
  3.6 7.3 %all-to-all-start = ((bf16[8,32,128]{2,1,0:T(8,128)(2,1)}), bf16[8,32,128]{2,1,0:T(8,128)(2,1)S(1)}, u32[]{:S(2)}, u32[]{:S(2)}) async-start(bf16[8,32,128]{2,1,0:T(8,128)(2,1)} %get-tuple-element.45), calls=%async_computation | async-start | bytes 131072 | tf_op jit(solution)/shard_map/all_to_all | solution.py:312
  11.5 0.8 %copy.14.pattern_ref = s32[24,2]{1,0:T(8,128)S(1)} copy(s32[24,2]{0,1:T(2,128)} %param.15) | data formatting | bytes 384 | tf_op args[2]
  12.3 1.1 %copy-done.1 = bf16[24,128,128]{2,1,0:T(8,128)(2,1)S(1)} copy-done((bf16[24,128,128]{2,1,0:T(8,128)(2,1)S(1)}, bf16[24,128,128]{2,1,0:T(8,128)(2,1)}, u32[]{:S(2)}) %copy-start.1) | copy-done | bytes 786456
  13.4 3.2 %shard_map.128 = (bf16[1024,1024]{1,0:T(8,128)(2,1)S(1)}, bf16[256,1024]{1,0:T(8,128)(2,1)S(1)}, bf16[256,128]{1,0:T(8,128)(2,1)S(1)}, bf16[256,128]{1,0:T(8,128...) custom-call(s32[1]{0:T(128)S(6)} %copy.15.iface_ref, s32[24,2]{1,0:T(8,128)S(1)} %copy.14.pattern_ref, ...), custom_call_target="tpu_custom_call" | custom-call | flops 134217728 | bytes 1246404 | tf_op jit(solution)/shard_map/pallas_call | solution.py:23
  16.7 0.7 copy-done.13
  17.3 0.7 copy-done.14
  18.0 1.3 %collective-permute-done.others_ref = bf16[8,32,128]{2,1,0:T(8,128)(2,1)S(1)} collective-permute-done((bf16[8,32,128]{2,1,0:T(8,128)(2,1)S(1)}, bf16[8,32,128]{2,1,0:T(8,128)(2,1)S(1)}, u32[]{:S(2)}, u32[]{:S(2)}) %collective-permute-start) | collective-permute-done | bytes 65568 | tf_op jit(solution)/shard_map/ppermute | solution.py:316
  19.2 1.3 %shard_map.129 = (f32[64,1024]{1,0:T(8,128)S(1)}, f32[64,1024]{1,0:T(8,128)S(1)}, bf16[384,128]{1,0:T(8,128)(2,1)S(1)}, bf16[384,128]{1,0:T(8,128)(2,1)S(1)}, bf...) custom-call(bf16[8,32,128]{2,1,0:T(8,128)(2,1)S(1)} %all-to-all-done.pieces_ref, ...), custom_call_target="tpu_custom_call" | custom-call | flops 134217728 | bytes 3309568 | tf_op jit(solution)/shard_map/pallas_call | solution.py:23
  20.5 4.8 %collective-permute-start.1 = (bf16[384,128]{1,0:T(8,128)(2,1)S(1)}, bf16[384,128]{1,0:T(8,128)(2,1)S(1)}, u32[]{:S(2)}, u32[]{:S(2)}) collective-permute-start(bf16[384,128]{1,0:T(8,128)(2,1)S(1)} %get-tuple-element.65), channel_id=1, source_target_pairs={{0,14},{2,4},{4,2},{6,8},{8,6},{10,12},{12,10},{14,0},{1,15},{3,5}... | collective-permute-start | bytes 294920 | tf_op jit(solution)/shard_map/ppermute | solution.py:325
  26.0 1.0 %collective-permute-start.4 = (bf16[64,128]{1,0:T(8,128)(2,1)S(1)}, bf16[64,128]{1,0:T(8,128)(2,1)S(1)}, u32[]{:S(2)}, u32[]{:S(2)}) collective-permute-start(bf16[64,128]{1,0:T(8,128)(2,1)S(1)} %get-tuple-element.68.own_far_ref), channel_id=1, source_target_pairs={{0,4},{2,6},{4,0},{6,2},{8,12},{10,14},{12,8},{14,10},{1,5},{3,7},... | collective-permute-start | bytes 49160 | tf_op jit(solution)/shard_map/ppermute | solution.py:325
  27.0 3.9 %collective-permute-done.2.beyond_ref = bf16[64,128]{1,0:T(8,128)(2,1)S(1)} collective-permute-done((bf16[64,128]{1,0:T(8,128)(2,1)S(1)}, bf16[64,128]{1,0:T(8,128)(2,1)S(1)}, u32[]{:S(2)}, u32[]{:S(2)}) %collective-permute-start.2) | collective-permute-done | bytes 16416 | tf_op jit(solution)/shard_map/ppermute | solution.py:325
  30.9 1.4 %shard_map.130 = (f32[64,1024]{1,0:T(8,128)S(1)}, f32[8,40,128]{2,1,0:T(8,128)S(1)}, bf16[64,128]{1,0:T(8,128)(2,1)S(1)}, bf16[64,128]{1,0:T(8,128)(2,1)S(1)}) custom-call(bf16[384,128]{1,0:T(8,128)(2,1)S(1)} %collective-permute-done.1.across_ref, bf16[64,128]{1,0:T(8,128)(2,1)S(1)} %collective-permute-done.2.beyond_ref, ...), custom_call_target="tpu_custom_call" | custom-call | flops 134217728 | bytes 3702784 | tf_op jit(solution)/shard_map/pallas_call | solution.py:23
  32.3 0.7 copy-done.4
  33.0 0.7 copy-done.10
  34.8 4.8 %all-to-all-start.1 = ((f32[8,40,128]{2,1,0:T(8,128)}), f32[8,40,128]{2,1,0:T(8,128)S(1)}, u32[]{:S(2)}, u32[]{:S(2)}) async-start(f32[8,40,128]{2,1,0:T(8,128)} %copy-done.10), calls=%async_computation.1 | async-start | bytes 327680 | tf_op jit(solution)/shard_map/all_to_all | solution.py:312
  39.6 4.7 %collective-permute-start.7 = (bf16[640,128]{1,0:T(8,128)(2,1)}, bf16[640,128]{1,0:T(8,128)(2,1)S(1)}, u32[]{:S(2)}, u32[]{:S(2)}) collective-permute-start(bf16[640,128]{1,0:T(8,128)(2,1)} %copy-done.14), channel_id=1, source_target_pairs={{0,14},{2,4},{4,2},{6,8},{8,6},{10,12},{12,10},{14,0},{1,15},{3,5}... | collective-permute-start | bytes 491528 | tf_op jit(solution)/shard_map/ppermute | solution.py:325
  44.3 2.0 %collective-permute-start.5 = (bf16[64,128]{1,0:T(8,128)(2,1)}, bf16[64,128]{1,0:T(8,128)(2,1)S(1)}, u32[]{:S(2)}, u32[]{:S(2)}) collective-permute-start(bf16[64,128]{1,0:T(8,128)(2,1)} %copy-done.16), channel_id=1, source_target_pairs={{0,14},{2,4},{4,2},{6,8},{8,6},{10,12},{12,10},{14,0},{1,15},{3,5}... | collective-permute-start | bytes 49160 | tf_op jit(solution)/shard_map/ppermute | solution.py:325
  46.3 3.3 %collective-permute-done.7.across_first_ref = bf16[640,128]{1,0:T(8,128)(2,1)S(1)} collective-permute-done((bf16[640,128]{1,0:T(8,128)(2,1)}, bf16[640,128]{1,0:T(8,128)(2,1)S(1)}, u32[]{:S(2)}, u32[]{:S(2)}) %collective-permute-start.7) | collective-permute-done | bytes 163872 | tf_op jit(solution)/shard_map/ppermute | solution.py:325
  49.6 0.7 copy-done.6
  50.3 2.5 %collective-permute-done.8.near_first_ref = bf16[640,128]{1,0:T(8,128)(2,1)S(1)} collective-permute-done((bf16[640,128]{1,0:T(8,128)(2,1)}, bf16[640,128]{1,0:T(8,128)(2,1)S(1)}, u32[]{:S(2)}, u32[]{:S(2)}) %collective-permute-start.8) | collective-permute-done | bytes 163872 | tf_op jit(solution)/shard_map/ppermute | solution.py:325
  52.8 0.7 copy-done.8
  54.1 1.4 %collective-permute-done.9.second_others_ref = f32[8,40,128]{2,1,0:T(8,128)S(1)} collective-permute-done((f32[8,40,128]{2,1,0:T(8,128)S(1)}, f32[8,40,128]{2,1,0:T(8,128)S(1)}, u32[]{:S(2)}, u32[]{:S(2)}) %collective-permute-start.9) | collective-permute-done | bytes 163872 | tf_op jit(solution)/shard_map/ppermute | solution.py:316
  55.5 0.8 %copy-done.3 = bf16[8,32,128]{2,1,0:T(8,128)(2,1)S(1)} copy-done((bf16[8,32,128]{2,1,0:T(8,128)(2,1)S(1)}, bf16[8,32,128]{2,1,0:T(8,128)(2,1)}, u32[]{:S(2)}) %copy-start.3) | copy-done | bytes 65560
  56.3 0.9 %copy-done.5 = f32[64,1024]{1,0:T(8,128)S(1)} copy-done((f32[64,1024]{1,0:T(8,128)S(1)}, f32[64,1024]{1,0:T(8,128)}, u32[]{:S(2)}) %copy-start.5) | copy-done | bytes 262168
  57.3 0.9 %copy-done.7 = bf16[640,128]{1,0:T(8,128)(2,1)S(1)} copy-done((bf16[640,128]{1,0:T(8,128)(2,1)S(1)}, bf16[640,128]{1,0:T(8,128)(2,1)}, u32[]{:S(2)}) %copy-start.7) | copy-done | bytes 163864
  58.2 0.9 %copy-done.9 = bf16[640,128]{1,0:T(8,128)(2,1)S(1)} copy-done((bf16[640,128]{1,0:T(8,128)(2,1)S(1)}, bf16[640,128]{1,0:T(8,128)(2,1)}, u32[]{:S(2)}) %copy-start.9) | copy-done | bytes 163864
  59.1 0.7 copy-done.12
  59.8 1.8 %shard_map.131 = (f32[64,1024]{1,0:T(8,128)S(1)}, f32[8,128]{1,0:T(8,128)S(1)}, f32[16,8,128]{2,1,0:T(8,128)S(1)}) custom-call(bf16[8,32,128]{2,1,0:T(8,128)(2,1)S(1)} %all-to-all-done.pieces_ref, bf16[8,32,128]{2,1,0:T(8,128)(2,1)S(1)} %copy-done.3, f32[8,40,128]{2,1,0:T(8,128)S(1)} %all-to-all-done.1.second_ref, ...), custom_call_target="tpu_custom_call" | custom-call | flops 134217728 | bytes 4128768 | tf_op jit(solution)/shard_map/pallas_call | solution.py:23
  61.6 9.5 %all_to_all.15.chunks_ref = f32[16,8,128]{2,1,0:T(8,128)S(1)} all-to-all(f32[16,8,128]{2,1,0:T(8,128)S(1)} %get-tuple-element.83), channel_id=1, replica_groups=mesh['grp'=2,'lon'=8,'lat'=2] {'lon','lat'}, dimensions={0} | all-to-all | bytes 131072 | tf_op jit(solution)/shard_map/all_to_all | solution.py:312
  71.1 1.2 %shard_map.132 = f32[64,1024]{1,0:T(8,128)} custom-call(f32[8,128]{1,0:T(8,128)S(1)} %get-tuple-element.82.sums_ref, f32[16,8,128]{2,1,0:T(8,128)S(1)} %all_to_all.15.chunks_ref, f32[64,1024]{1,0:T(8,128)S(1)} %get-tuple-element.69.z_ref.first_ref, f32[64,1024]{1,0:T(8,128)S(1)} %get-tuple-element.84.second_ref), custom_call_target="tpu_custom_call" | custom-call | flops 262144 | bytes 593920 | tf_op jit(solution)/shard_map/pallas_call | solution.py:23
  (34 shorter events, 2.5 us)
Async XLA Ops:
  2.7 0.9 %copy-start = (bf16[24,128,128]{2,1,0:T(8,128)(2,1)}, bf16[24,128,128]{2,1,0:T(8,128)(2,1)S(1)}, u32[]{:S(2)}) copy-start(bf16[24,128,128]{2,1,0:T(8,128)(2,1)S(1)} %get-tuple-element.46.blocks_ref) | copy-start | bytes 2359300
  3.6 14.3 %all-to-all-start = ((bf16[8,32,128]{2,1,0:T(8,128)(2,1)}), bf16[8,32,128]{2,1,0:T(8,128)(2,1)S(1)}, u32[]{:S(2)}, u32[]{:S(2)}) async-start(bf16[8,32,128]{2,1,0:T(8,128)(2,1)} %get-tuple-element.45), calls=%async_computation | async-start | bytes 131072 | tf_op jit(solution)/shard_map/all_to_all | solution.py:312
  12.3 1.1 %copy-start.1 = (bf16[24,128,128]{2,1,0:T(8,128)(2,1)S(1)}, bf16[24,128,128]{2,1,0:T(8,128)(2,1)}, u32[]{:S(2)}) copy-start(bf16[24,128,128]{2,1,0:T(8,128)(2,1)} %copy-done) | copy-start | bytes 2359300
  16.6 0.7 copy-start.13
  17.3 0.7 copy-start.14
  18.0 1.3 %collective-permute-start = (bf16[8,32,128]{2,1,0:T(8,128)(2,1)S(1)}, bf16[8,32,128]{2,1,0:T(8,128)(2,1)S(1)}, u32[]{:S(2)}, u32[]{:S(2)}) collective-permute-start(bf16[8,32,128]{2,1,0:T(8,128)(2,1)S(1)} %all-to-all-done.pieces_ref), channel_id=1, source_target_pairs={{0,1},{1,0},{2,3},{3,2},{4,5},{5,4},{6,7},{7,6},{8,9},{9,8},{10,11... | collective-permute-start | bytes 196616 | tf_op jit(solution)/shard_map/ppermute | solution.py:316
  19.2 13.0 %copy-start.2 = (bf16[8,32,128]{2,1,0:T(8,128)(2,1)}, bf16[8,32,128]{2,1,0:T(8,128)(2,1)S(1)}, u32[]{:S(2)}) copy-start(bf16[8,32,128]{2,1,0:T(8,128)(2,1)S(1)} %collective-permute-done.others_ref) | copy-start | bytes 196612
  20.5 10.3 %collective-permute-start.1 = (bf16[384,128]{1,0:T(8,128)(2,1)S(1)}, bf16[384,128]{1,0:T(8,128)(2,1)S(1)}, u32[]{:S(2)}, u32[]{:S(2)}) collective-permute-start(bf16[384,128]{1,0:T(8,128)(2,1)S(1)} %get-tuple-element.65), channel_id=1, source_target_pairs={{0,14},{2,4},{4,2},{6,8},{8,6},{10,12},{12,10},{14,0},{1,15},{3,5}... | collective-permute-start | bytes 294920 | tf_op jit(solution)/shard_map/ppermute | solution.py:325
  25.3 5.5 %collective-permute-start.3 = (bf16[384,128]{1,0:T(8,128)(2,1)S(1)}, bf16[384,128]{1,0:T(8,128)(2,1)S(1)}, u32[]{:S(2)}, u32[]{:S(2)}) collective-permute-start(bf16[384,128]{1,0:T(8,128)(2,1)S(1)} %get-tuple-element.67), channel_id=1, source_target_pairs={{0,2},{2,0},{4,6},{6,4},{8,10},{10,8},{12,14},{14,12},{1,3},{3,1},... | collective-permute-start | bytes 294920 | tf_op jit(solution)/shard_map/ppermute | solution.py:325
  25.3 5.5 %collective-permute-start.2 = (bf16[64,128]{1,0:T(8,128)(2,1)S(1)}, bf16[64,128]{1,0:T(8,128)(2,1)S(1)}, u32[]{:S(2)}, u32[]{:S(2)}) collective-permute-start(bf16[64,128]{1,0:T(8,128)(2,1)S(1)} %get-tuple-element.66.own_beyond_ref), channel_id=1, source_target_pairs={{0,12},{2,14},{4,8},{6,10},{8,4},{10,6},{12,0},{14,2},{1,13},{3,15... | collective-permute-start | bytes 49160 | tf_op jit(solution)/shard_map/ppermute | solution.py:325
  26.0 4.9 %collective-permute-start.4 = (bf16[64,128]{1,0:T(8,128)(2,1)S(1)}, bf16[64,128]{1,0:T(8,128)(2,1)S(1)}, u32[]{:S(2)}, u32[]{:S(2)}) collective-permute-start(bf16[64,128]{1,0:T(8,128)(2,1)S(1)} %get-tuple-element.68.own_far_ref), channel_id=1, source_target_pairs={{0,4},{2,6},{4,0},{6,2},{8,12},{10,14},{12,8},{14,10},{1,5},{3,7},... | collective-permute-start | bytes 49160 | tf_op jit(solution)/shard_map/ppermute | solution.py:325
  32.3 0.7 copy-start.4
  33.0 0.7 copy-start.10
  33.6 0.6 copy-start.15
  34.2 0.6 copy-start.16
  34.8 19.2 %all-to-all-start.1 = ((f32[8,40,128]{2,1,0:T(8,128)}), f32[8,40,128]{2,1,0:T(8,128)S(1)}, u32[]{:S(2)}, u32[]{:S(2)}) async-start(f32[8,40,128]{2,1,0:T(8,128)} %copy-done.10), calls=%async_computation.1 | async-start | bytes 327680 | tf_op jit(solution)/shard_map/all_to_all | solution.py:312
  39.6 10.1 %collective-permute-start.7 = (bf16[640,128]{1,0:T(8,128)(2,1)}, bf16[640,128]{1,0:T(8,128)(2,1)S(1)}, u32[]{:S(2)}, u32[]{:S(2)}) collective-permute-start(bf16[640,128]{1,0:T(8,128)(2,1)} %copy-done.14), channel_id=1, source_target_pairs={{0,14},{2,4},{4,2},{6,8},{8,6},{10,12},{12,10},{14,0},{1,15},{3,5}... | collective-permute-start | bytes 491528 | tf_op jit(solution)/shard_map/ppermute | solution.py:325
  44.3 8.5 %collective-permute-start.8 = (bf16[640,128]{1,0:T(8,128)(2,1)}, bf16[640,128]{1,0:T(8,128)(2,1)S(1)}, u32[]{:S(2)}, u32[]{:S(2)}) collective-permute-start(bf16[640,128]{1,0:T(8,128)(2,1)} %copy-done.13), channel_id=1, source_target_pairs={{0,2},{2,0},{4,6},{6,4},{8,10},{10,8},{12,14},{14,12},{1,3},{3,1},... | collective-permute-start | bytes 491528 | tf_op jit(solution)/shard_map/ppermute | solution.py:325
  44.3 9.1 %collective-permute-start.5 = (bf16[64,128]{1,0:T(8,128)(2,1)}, bf16[64,128]{1,0:T(8,128)(2,1)S(1)}, u32[]{:S(2)}, u32[]{:S(2)}) collective-permute-start(bf16[64,128]{1,0:T(8,128)(2,1)} %copy-done.16), channel_id=1, source_target_pairs={{0,14},{2,4},{4,2},{6,8},{8,6},{10,12},{12,10},{14,0},{1,15},{3,5}... | collective-permute-start | bytes 49160 | tf_op jit(solution)/shard_map/ppermute | solution.py:325
  46.3 7.1 %collective-permute-start.6 = (bf16[64,128]{1,0:T(8,128)(2,1)}, bf16[64,128]{1,0:T(8,128)(2,1)S(1)}, u32[]{:S(2)}, u32[]{:S(2)}) collective-permute-start(bf16[64,128]{1,0:T(8,128)(2,1)} %copy-done.15), channel_id=1, source_target_pairs={{0,2},{2,0},{4,6},{6,4},{8,10},{10,8},{12,14},{14,12},{1,3},{3,1},... | collective-permute-start | bytes 49160 | tf_op jit(solution)/shard_map/ppermute | solution.py:325
  49.6 0.7 copy-start.6
  52.8 0.7 copy-start.8
  53.5 0.6 copy-start.11
  54.1 1.4 %collective-permute-start.9 = (f32[8,40,128]{2,1,0:T(8,128)S(1)}, f32[8,40,128]{2,1,0:T(8,128)S(1)}, u32[]{:S(2)}, u32[]{:S(2)}) collective-permute-start(f32[8,40,128]{2,1,0:T(8,128)S(1)} %all-to-all-done.1.second_ref), channel_id=1, source_target_pairs={{0,1},{1,0},{2,3},{3,2},{4,5},{5,4},{6,7},{7,6},{8,9},{9,8},{10,11... | collective-permute-start | bytes 491528 | tf_op jit(solution)/shard_map/ppermute | solution.py:316
  55.5 0.8 %copy-start.3 = (bf16[8,32,128]{2,1,0:T(8,128)(2,1)S(1)}, bf16[8,32,128]{2,1,0:T(8,128)(2,1)}, u32[]{:S(2)}) copy-start(bf16[8,32,128]{2,1,0:T(8,128)(2,1)} %copy-done.2) | copy-start | bytes 196612
  56.3 0.9 %copy-start.5 = (f32[64,1024]{1,0:T(8,128)S(1)}, f32[64,1024]{1,0:T(8,128)}, u32[]{:S(2)}) copy-start(f32[64,1024]{1,0:T(8,128)} %copy-done.4) | copy-start | bytes 786436
  57.2 0.9 %copy-start.7 = (bf16[640,128]{1,0:T(8,128)(2,1)S(1)}, bf16[640,128]{1,0:T(8,128)(2,1)}, u32[]{:S(2)}) copy-start(bf16[640,128]{1,0:T(8,128)(2,1)} %copy-done.6) | copy-start | bytes 491524
  58.2 0.9 %copy-start.9 = (bf16[640,128]{1,0:T(8,128)(2,1)S(1)}, bf16[640,128]{1,0:T(8,128)(2,1)}, u32[]{:S(2)}) copy-start(bf16[640,128]{1,0:T(8,128)(2,1)} %copy-done.8) | copy-start | bytes 491524
  59.1 0.7 copy-start.12

commit v8 on v7

--- a/solution.py
+++ b/solution.py
@@ -12,17 +12,18 @@
 HBM = pl.BlockSpec(memory_space=pltpu.HBM)
 SMEM = pl.BlockSpec(memory_space=pltpu.SMEM)
 LANES = 128
+SUM_ROWS = 16
 
 
 def dot(a, b, ca=1, cb=0):
     return lax.dot_general(a, b, (((ca,), (cb,)), ((), ())), preferred_element_type=F32)
 
 
-def call(kernel, outs, specs, args, flops, scratch=(), keep=False):
+def call(kernel, outs, specs, args, flops, scratch=()):
     moved = sum(int(np.prod(a.shape)) * a.dtype.itemsize for a in args)
     return pl.pallas_call(
         kernel,
-        out_shape=[pltpu.VMEM(s, t) if keep else jax.ShapeDtypeStruct(s, t) for s, t in outs],
+        out_shape=[jax.ShapeDtypeStruct(s, t) for s, t in outs],
         in_specs=specs,
         out_specs=[VMEM] * len(outs),
         scratch_shapes=list(scratch),
@@ -68,8 +69,8 @@
 
 def load_kernel(count_ref, right_hbm, vectors_hbm, react_hbm, mass_hbm, obs_hbm,
                 coupling_hbm, blocks_hbm, east_hbm, west_hbm, inverse_hbm,
-                chunks_ref, diag_ref, right_ref, vectors_ref, coupling_ref, blocks_ref, east_ref, west_ref,
-                inverse_ref, react_ref, mass_ref, obs_ref, sems):
+                chunks_ref, diag_ref, link_ref, right_ref, vectors_ref, blocks_ref, east_ref, west_ref,
+                inverse_ref, react_ref, mass_ref, obs_ref, coupling_ref, sems):
     pairs = (
         (right_hbm, right_ref), (vectors_hbm, vectors_ref), (react_hbm, react_ref), (mass_hbm, mass_ref),
         (obs_hbm, obs_ref), (coupling_hbm, coupling_ref), (blocks_hbm, blocks_ref), (east_hbm, east_ref),
@@ -78,7 +79,7 @@
     copies = [pltpu.make_async_copy(src, dst, sems.at[i]) for i, (src, dst) in enumerate(pairs)]
     for copy in copies:
         copy.start()
-    for copy in copies[:5]:
+    for copy in copies[:6]:
         copy.wait()
     nodes = right_ref.shape[1]
     active = (lax.broadcasted_iota(jnp.int32, (1, nodes), 1) < count_ref[0]).astype(F32)
@@ -90,7 +91,11 @@
     for i, line in enumerate((active, react, 1.0 / mass, obs, 1.0 / (obs + react * react / mass))):
         diag = jnp.where(row == i, line, diag)
     diag_ref[...] = diag
-    for copy in copies[5:]:
+    slots = coupling_ref.shape[0]
+    live_a = lax.broadcasted_iota(jnp.int32, (slots, slots), 0) < count_ref[1]
+    live_b = lax.broadcasted_iota(jnp.int32, (slots, slots), 1) < count_ref[1]
+    link_ref[...] = jnp.where(live_a & live_b, coupling_ref[...], jnp.zeros((slots, slots), BF16))
+    for copy in copies[6:]:
         copy.wait()
 
 
@@ -98,24 +103,27 @@
     return tuple(diag_ref[i : i + 1, :] for i in range(5))
 
 
-def prep_kernel(iface_ref, pattern_ref, blocks_ref, right_ref, vectors_ref, coupling_ref, east_ref, west_ref, diag_ref,
-                inverse_ref, dense_ref, edge_ref, to_west_ref, to_east_ref, near_ref, across_ref, total_ref):
+def prep_kernel(pattern_hbm, blocks_ref, right_ref, vectors_ref, link_ref, east_ref, west_ref, diag_ref, inverse_ref,
+                dense_ref, edge_ref, to_west_ref, to_east_ref, near_ref, across_ref, pattern_ref, total_ref, sem):
+    copy = pltpu.make_async_copy(pattern_hbm, pattern_ref, sem)
+    copy.start()
     samples, nodes = right_ref.shape
     count, block, _ = blocks_ref.shape
-    slots = coupling_ref.shape[0]
+    slots = link_ref.shape[0]
 
     def clear(i, carry):
         total_ref[pl.ds(pl.multiple_of(i * block, block), block), :] = jnp.zeros((block, nodes), F32)
         return carry
 
     lax.fori_loop(0, nodes // block, clear, 0)
+    copy.wait()
     unit = (
         lax.broadcasted_iota(jnp.int32, (block, block), 0) == lax.broadcasted_iota(jnp.int32, (block, block), 1)
     ).astype(F32).astype(BF16)
 
     def place(k, carry):
-        rows = pl.ds(pl.multiple_of(pattern_ref[k, 0] * block, block), block)
-        cols = pl.ds(pl.multiple_of(pattern_ref[k, 1] * block, block), block)
+        rows = pl.ds(pl.multiple_of(pattern_ref[0, k] * block, block), block)
+        cols = pl.ds(pl.multiple_of(pattern_ref[1, k] * block, block), block)
         values = blocks_ref[k]
         total_ref[rows, cols] += values.astype(F32)
         total_ref[cols, rows] += dot(unit, values, 1, 1)
@@ -134,10 +142,7 @@
     node = lax.broadcasted_iota(jnp.int32, (slots, nodes), 1).astype(F32)
     east_hot = jnp.where(node == column_of(east_ref[...].astype(F32)), 1.0, 0.0).astype(BF16)
     west_hot = jnp.where(node == column_of(west_ref[...].astype(F32)), 1.0, 0.0).astype(BF16)
-    live_a = lax.broadcasted_iota(jnp.int32, (slots, slots), 0) < iface_ref[0]
-    live_b = lax.broadcasted_iota(jnp.int32, (slots, slots), 1) < iface_ref[0]
-    link = jnp.where(live_a & live_b, coupling_ref[...], jnp.zeros((slots, slots), BF16))
-    spread = dot(link, east_hot, 0, 0).astype(BF16)
+    spread = dot(link_ref[...], east_hot, 0, 0).astype(BF16)
     edge_ref[0:slots, :] = spread
     edge_ref[slots : 2 * slots, :] = west_hot
     edges = jnp.concatenate([spread, west_hot], axis=0)
@@ -214,7 +219,7 @@
 
 def image_kernel(across_ref, beyond_ref, near_ref, far_ref, own_far_ref, own_beyond_ref,
                  z_ref, scaled_ref, dense_ref, edge_ref, diag_ref, right_ref, vectors_ref,
-                 image_ref, chunks_ref, near_out_ref, across_out_ref):
+                 image_ref, chunks_ref):
     samples, nodes = z_ref.shape
     active, react, inverse_mass, obs, jacobi = lines(diag_ref)
     z = z_ref[...]
@@ -233,37 +238,43 @@
     image = active * (stiff + obs * z)
     image_ref[...] = image
     level = levels(image * jacobi, edges).astype(BF16)
-    slots = edges.shape[0] // 2
-
-    def send(east_ref, west_ref):
-        east_ref[...] = level[:, 0:slots]
-        west_ref[...] = level[:, slots:]
-
-    by_lon(0, near_out_ref, across_out_ref, send)
     coarse = fold(dot(vectors_ref[...], image.astype(BF16), 1, 1))
-    half = coarse.shape[0]
+    high = coarse.astype(BF16)
+    low = (coarse - high.astype(F32)).astype(BF16)
     sums = row_of(row_sum(active * right_ref[...].astype(F32), z), row_sum(z, image))
+    row = lax.broadcasted_iota(jnp.int32, (SUM_ROWS, LANES), 0)
+    tail = jnp.zeros((SUM_ROWS, LANES), F32)
+    for i in range(3):
+        part = sums.astype(BF16).astype(F32)
+        tail = jnp.where(row == i, part, tail)
+        sums = sums - part
     count, rows, _ = chunks_ref.shape
-    chunks_ref[:, 0:half, :] = jnp.broadcast_to(coarse[None], (count, half, LANES))
-    chunks_ref[:, half:, :] = jnp.broadcast_to(sums[None], (count, rows - half, LANES))
-
-
-def middle_kernel(pieces_ref, others_ref, second_ref, second_others_ref, across_ref, near_ref,
+    slots = level.shape[1] // 2
+    common = jnp.concatenate([high, low, tail.astype(BF16), level[:, 0:slots]], axis=0)
+    chunks_ref[...] = jnp.broadcast_to(common[None], chunks_ref.shape)
+    before = lax.rem(lax.axis_index("lon") + count - 1, count)
+    chunks_ref[before, rows - samples :, :] = level[:, slots:]
+
+
+def middle_kernel(pieces_ref, others_ref, second_ref, second_others_ref,
                   across_first_ref, near_first_ref, inverse_ref, right_ref, image_ref, vectors_ref,
                   dense_ref, edge_ref, diag_ref, z_ref, sums_ref, chunks_ref, coarse_ref):
     samples, nodes = right_ref.shape
     count, half, _ = pieces_ref.shape
+    tail = slice(2 * half, 2 * half + SUM_ROWS)
 
     def add(d, total):
-        return total + second_ref[d, half : half + 1, :] + second_others_ref[d, half : half + 1, :]
-
-    sums = lax.fori_loop(0, count, add, jnp.zeros((1, LANES), F32), unroll=min(count, 8))
+        return total + second_ref[d, tail, :].astype(F32) + second_others_ref[d, tail, :].astype(F32)
+
+    parts = lax.fori_loop(0, count, add, jnp.zeros((SUM_ROWS, LANES), F32), unroll=min(count, 8))
+    sums = parts[2:3] + parts[1:2] + parts[0:1]
     step = sums[:, 0 : LANES // 2] / sums[:, LANES // 2 :]
     step = jnp.concatenate([step, step], axis=1)
 
     def piece(side, d):
         first, change = ((pieces_ref, second_ref), (others_ref, second_others_ref))[side]
-        return (first[d].astype(F32) - step * change[d, 0:half, :]).astype(BF16)
+        moved = change[d, 0:half, :].astype(F32) + change[d, half : 2 * half, :].astype(F32)
+        return (first[d].astype(F32) - step * moved).astype(BF16)
 
     unfold(count, piece, coarse_ref)
     active, react, inverse_mass, obs, jacobi = lines(diag_ref)
@@ -274,16 +285,20 @@
     z = smooth(residual, coarse_ref, inverse_ref, vectors_ref, active, jacobi)
     z_ref[...] = z
 
-    def arriving(first_ref, change_ref):
+    def arriving(first, change):
         rows, width = inverse_ref.shape
         blocks = width // LANES
-        inverse = jnp.concatenate([first_ref[j * rows : (j + 1) * rows, :] for j in range(blocks)], axis=1)
+        inverse = jnp.concatenate([first[j * rows : (j + 1) * rows] for j in range(blocks)], axis=1)
         fix = dot(inverse, coarse_ref[...]).astype(BF16)
-        level = first_ref[blocks * rows :, :]
-        smooth_level = level[rows:].astype(F32) - step_column * change_ref[...].astype(F32)
-        return smooth_level + dot(fix, level[0:rows], 0, 0)
-
-    from_east, from_west = pick(0, arriving(near_first_ref, near_ref), arriving(across_first_ref, across_ref))
+        level = first[blocks * rows :]
+        smooth_level = level[rows:].astype(F32) - step_column * change.astype(F32)
+        return (smooth_level + dot(fix, level[0:rows], 0, 0)).astype(BF16)
+
+    lon = lax.axis_index("lon")
+    ahead, before = lax.rem(lon + 1, count), lax.rem(lon + count - 1, count)
+    east_first, west_first = pick(0, near_first_ref[...], across_first_ref[...])
+    from_east = arriving(east_first, second_ref[ahead, 2 * half + SUM_ROWS :, :])
+    from_west = arriving(west_first, second_ref[before, 2 * half + SUM_ROWS :, :])
     arrived = jnp.concatenate([from_east, from_west], axis=1)
     stiff = dot(z.astype(BF16), dense_ref[...]) + react * z + dot(arrived, edges)
     curve = jnp.sum(stiff * stiff * inverse_mass + obs * z * z, axis=1, keepdims=True)
@@ -353,27 +368,26 @@
     blocks = coarse_inverse.shape[1] // LANES
     static = ((blocks * vectors + vectors + samples, slots), BF16)
     corr = ((2 * slots, slots), BF16)
-    kept = (right_side, deflation, coupling, stiffness_blocks, east_rows, west_rows, coarse_inverse)
+    kept = (right_side, deflation, stiffness_blocks, east_rows, west_rows, coarse_inverse)
     inputs = (right_side, deflation, react, mass, obs, coupling, stiffness_blocks, east_rows, west_rows, coarse_inverse)
     line = pltpu.VMEM((1, nodes), F32)
-    chunks, diag, right, basis, link, stored, east, west, inverse = call(
+    chunks, diag, link, right, basis, stored, east, west, inverse = call(
         load_kernel,
-        [((sectors, half, LANES), BF16), ((8, nodes), F32)] + [(a.shape, a.dtype) for a in kept],
+        [((sectors, half, LANES), BF16), ((8, nodes), F32), (coupling.shape, BF16)] + [(a.shape, a.dtype) for a in kept],
         [SMEM] + [HBM] * len(inputs),
-        [node_count] + [pltpu.with_memory_space_constraint(a, pltpu.HBM) for a in inputs],
+        [jnp.concatenate([node_count, iface_count])] + [pltpu.with_memory_space_constraint(a, pltpu.HBM) for a in inputs],
         2 * samples * vectors * nodes,
-        [line, line, line, pltpu.SemaphoreType.DMA((len(inputs),))],
-    )
+        [line, line, line, pltpu.VMEM(coupling.shape, BF16), pltpu.SemaphoreType.DMA((len(inputs),))],
+    )
+    pieces, stored = lax.optimization_barrier((exchange(chunks, "lon"), stored))
+    pattern = pltpu.with_memory_space_constraint(block_pattern.T, pltpu.HBM)
     dense, edge, corr_west, corr_east, near_first, across_first = call(
         prep_kernel,
         [((nodes, nodes), BF16), ((2 * slots, nodes), BF16), corr, corr, static, static],
-        [SMEM, SMEM] + [VMEM] * 8,
-        (iface_count, block_pattern, stored, right, basis, link, east, west, diag, inverse),
+        [HBM] + [VMEM] * 8,
+        (pattern, stored, right, basis, link, east, west, diag, inverse),
         apply_cost,
-        [pltpu.VMEM((nodes, nodes), F32)],
-    )
-    pieces, dense, edge, corr_west, corr_east, near_first, across_first = lax.optimization_barrier(
-        (exchange(chunks, "lon"), dense, edge, corr_west, corr_east, near_first, across_first)
+        [pltpu.SMEM((2, block_pattern.shape[0]), jnp.int32), pltpu.VMEM((nodes, nodes), F32), pltpu.SemaphoreType.DMA],
     )
     others = other_band(pieces)
     z0, scaled, near, across, far, beyond = call(
@@ -390,22 +404,21 @@
     got_far = swap(far, 2, True)
     across_first = swap(across_first, 1, False)
     near_first = swap(near_first, 1, True)
-    image, chunks, near_change, across_change = call(
+    image, chunks = call(
         image_kernel,
-        [field, ((sectors, half + 8, LANES), F32)] + [((samples, slots), BF16)] * 2,
+        [field, ((sectors, 2 * half + SUM_ROWS + samples, LANES), BF16)],
         [VMEM] * 13,
         (across, got_beyond, near, got_far, far, beyond, z0, scaled, dense, edge, diag, right, basis),
         apply_cost,
     )
-    second, across_change, near_change, across_first, near_first = lax.optimization_barrier(
-        (exchange(chunks, "lon"), swap(across_change, 1, False), swap(near_change, 1, True), across_first, near_first)
-    )
+    chunks, across_first, near_first = lax.optimization_barrier((chunks, across_first, near_first))
+    second = exchange(chunks, "lon")
     second_others = other_band(second)
     z1, sums, chunks = call(
         middle_kernel,
         [field, ((8, LANES), F32), ((domains, 8, LANES), F32)],
-        [VMEM] * 15,
-        (pieces, others, second, second_others, across_change, near_change, across_first, near_first,
+        [VMEM] * 13,
+        (pieces, others, second, second_others, across_first, near_first,
          inverse, right, image, basis, dense, edge, diag),
         apply_cost,
         [coarse_scratch],

time: 72.9 us -> 65.5 us (0.90)
  blocking collectives: 9.49 us -> 37.7 us
  starting transfers between devices: 25.2 us -> 7.11 us
  local copies, waits for them, and re-layouts: 12.9 us -> 0 us
  waiting for transfers between devices: 12.3 us -> 8.64 us
    all_to_all x1 -> x3, blocking collectives: 9.49 us -> 37.7 us  [exchange(): return lax.all_to_all(chunks, axes, split_axis=0, concat_axis=0, tiled=True)]
    unnamed x35 -> x0, local copies, waits for them, and re-layouts: 12.9 us -> none
    all_to_all x2 -> x0, starting transfers between devices: 12 us -> none  [exchange(): return lax.all_to_all(chunks, axes, split_axis=0, concat_axis=0, tiled=True)]
    ppermute x8 -> x6, starting transfers between devices: 13.2 us -> 7.11 us  [swap(): return lax.ppermute(array, 'lon', pairs)]
    ppermute x8 -> x6, waiting for transfers between devices: 9.67 us -> 7.05 us  [swap(): return lax.ppermute(array, 'lon', pairs)]
    ppermute x2, waiting for transfers between devices: 2.64 us -> 1.58 us  [other_band(): return lax.ppermute(array, 'lat', [(0, 1), (1, 0)])]
  transfers between devices with their start and end apart: 12 -> 8, of which waited for: 5 -> 3; matrix products, arithmetic and copies ran while one was open for 1% -> 0% of each run, Pallas kernels for 4% -> 8%
where the time goes in v8:
time: 65.5 us; the launch traced here: 65.2 us
  blocking collectives  37.7 us (58%)
  Pallas kernels  10.3 us (16%)
  waiting for transfers between devices  8.64 us (13%)
  starting transfers between devices  7.11 us (11%)
  between operations  1.34 us (2%)
    all_to_all x3, blocking collectives, exchange(): return lax.all_to_all(chunks, axes, split_axis=0, concat_axis=0, tiled=True)  37.7 us
    pallas_call x6, Pallas kernels, call(): pl.pallas_call(kernel, out_shape=[jax.ShapeDtypeStruct(s, t) for s, t in...  10.3 us
    ppermute x6, starting transfers between devices, swap(): return lax.ppermute(array, 'lon', pairs)  7.11 us
    ppermute x6, waiting for transfers between devices, swap(): return lax.ppermute(array, 'lon', pairs)  7.05 us
    ppermute x2, waiting for transfers between devices, other_band(): return lax.ppermute(array, 'lat', [(0, 1), (1, 0)])  1.58 us
  transfers between devices with their start and end apart: 8, of which 3 were waited for; matrix products, arithmetic and copies ran while one was open for 0% of the time, Pallas kernels for 8%

profile of v8, /device:TPU:0, one launch (start us, length us, event | category | flops | bytes accessed | tf_op | source)
XLA Modules:
  0.0 65.2 jit_solution(12458809743787693450)
XLA Ops:
  1.3 0.1 pad_add_fusion.count_ref
  1.4 2.0 %shard_map.127 = (bf16[8,32,128]{2,1,0:T(8,128)(2,1)S(1)}, f32[8,1024]{1,0:T(8,128)S(1)}, bf16[128,128]{1,0:T(8,128)(2,1)S(1)}, bf16[64,1024]{1,0:T(8,128)(2,1)S...) custom-call(s32[2]{0:T(128)S(1)} %pad_add_fusion.count_ref, ...), custom_call_target="tpu_custom_call" | custom-call | flops 8388608 | bytes 1225736 | tf_op jit(solution)/shard_map/pallas_call | solution.py:24
  3.4 14.0 %all_to_all.15.pieces_ref = bf16[8,32,128]{2,1,0:T(8,128)(2,1)S(1)} all-to-all(bf16[8,32,128]{2,1,0:T(8,128)(2,1)S(1)} %get-tuple-element.36), channel_id=1, replica_groups=mesh['grp'=2,'lon'=8,'lat'=2] {'lon'}, dimensions={0} | all-to-all | bytes 131072 | tf_op jit(solution)/shard_map/all_to_all | solution.py:327
  17.3 0.0 collective-permute-start
  17.3 2.9 %shard_map.128 = (bf16[1024,1024]{1,0:T(8,128)(2,1)S(1)}, bf16[256,1024]{1,0:T(8,128)(2,1)S(1)}, bf16[256,128]{1,0:T(8,128)(2,1)S(1)}, bf16[256,128]{1,0:T(8,128...) custom-call(s32[2,24]{1,0:T(2,128)} %bitcast.7, ...), custom_call_target="tpu_custom_call" | custom-call | flops 134217728 | bytes 1246400 | tf_op jit(solution)/shard_map/pallas_call | solution.py:24
  20.2 0.9 %collective-permute-start.5 = (bf16[640,128]{1,0:T(8,128)(2,1)S(1)}, bf16[640,128]{1,0:T(8,128)(2,1)S(1)}, u32[]{:S(2)}, u32[]{:S(2)}) collective-permute-start(bf16[640,128]{1,0:T(8,128)(2,1)S(1)} %get-tuple-element.58), channel_id=1, source_target_pairs={{0,14},{2,4},{4,2},{6,8},{8,6},{10,12},{12,10},{14,0},{1,15},{3,5}... | collective-permute-start | bytes 491528 | tf_op jit(solution)/shard_map/ppermute | solution.py:340
  21.1 0.9 %collective-permute-start.6 = (bf16[640,128]{1,0:T(8,128)(2,1)S(1)}, bf16[640,128]{1,0:T(8,128)(2,1)S(1)}, u32[]{:S(2)}, u32[]{:S(2)}) collective-permute-start(bf16[640,128]{1,0:T(8,128)(2,1)S(1)} %get-tuple-element.59), channel_id=1, source_target_pairs={{0,2},{2,0},{4,6},{6,4},{8,10},{10,8},{12,14},{14,12},{1,3},{3,1},... | collective-permute-start | bytes 491528 | tf_op jit(solution)/shard_map/ppermute | solution.py:340
  22.0 0.0 collective-permute-done.others_ref
  22.0 1.3 %shard_map.129 = (f32[64,1024]{1,0:T(8,128)S(1)}, f32[64,1024]{1,0:T(8,128)S(1)}, bf16[384,128]{1,0:T(8,128)(2,1)S(1)}, bf16[384,128]{1,0:T(8,128)(2,1)S(1)}, bf...) custom-call(bf16[8,32,128]{2,1,0:T(8,128)(2,1)S(1)} %all_to_all.15.pieces_ref, ...), custom_call_target="tpu_custom_call" | custom-call | flops 134217728 | bytes 3309568 | tf_op jit(solution)/shard_map/pallas_call | solution.py:24
  23.3 3.1 %collective-permute-start.1 = (bf16[384,128]{1,0:T(8,128)(2,1)S(1)}, bf16[384,128]{1,0:T(8,128)(2,1)S(1)}, u32[]{:S(2)}, u32[]{:S(2)}) collective-permute-start(bf16[384,128]{1,0:T(8,128)(2,1)S(1)} %get-tuple-element.51), channel_id=1, source_target_pairs={{0,14},{2,4},{4,2},{6,8},{8,6},{10,12},{12,10},{14,0},{1,15},{3,5}... | collective-permute-start | bytes 294920 | tf_op jit(solution)/shard_map/ppermute | solution.py:340
  26.4 0.0 collective-permute-start.3
  26.4 2.2 %collective-permute-start.2 = (bf16[64,128]{1,0:T(8,128)(2,1)S(1)}, bf16[64,128]{1,0:T(8,128)(2,1)S(1)}, u32[]{:S(2)}, u32[]{:S(2)}) collective-permute-start(bf16[64,128]{1,0:T(8,128)(2,1)S(1)} %get-tuple-element.52.own_beyond_ref), channel_id=1, source_target_pairs={{0,12},{2,14},{4,8},{6,10},{8,4},{10,6},{12,0},{14,2},{1,13},{3,15... | collective-permute-start | bytes 49160 | tf_op jit(solution)/shard_map/ppermute | solution.py:340
  28.6 3.3 %collective-permute-done.2.beyond_ref = bf16[64,128]{1,0:T(8,128)(2,1)S(1)} collective-permute-done((bf16[64,128]{1,0:T(8,128)(2,1)S(1)}, bf16[64,128]{1,0:T(8,128)(2,1)S(1)}, u32[]{:S(2)}, u32[]{:S(2)}) %collective-permute-start.2) | collective-permute-done | bytes 16416 | tf_op jit(solution)/shard_map/ppermute | solution.py:340
  31.9 0.0 collective-permute-start.4
  32.0 3.7 %collective-permute-done.4.far_ref = bf16[64,128]{1,0:T(8,128)(2,1)S(1)} collective-permute-done((bf16[64,128]{1,0:T(8,128)(2,1)S(1)}, bf16[64,128]{1,0:T(8,128)(2,1)S(1)}, u32[]{:S(2)}, u32[]{:S(2)}) %collective-permute-start.4) | collective-permute-done | bytes 16416 | tf_op jit(solution)/shard_map/ppermute | solution.py:340
  35.7 0.0 collective-permute-done.1.across_ref
  35.7 0.0 collective-permute-done.3.near_ref
  35.7 1.1 %shard_map.130 = (f32[64,1024]{1,0:T(8,128)S(1)}, bf16[8,144,128]{2,1,0:T(8,128)(2,1)S(1)}) custom-call(bf16[384,128]{1,0:T(8,128)(2,1)S(1)} %collective-permute-done.1.across_ref, bf16[64,128]{1,0:T(8,128)(2,1)S(1)} %collective-permute-done.2.beyond_ref, bf16[384,128]{1,0:T(8,128)(2,1)S(1)} %collective-permute-done.3.near_ref, ...), custom_call_target="tpu_custom_call" | custom-call | flops 134217728 | bytes 3702784 | tf_op jit(solution)/shard_map/pallas_call | solution.py:24
  36.8 0.0 collective-permute-done.5.across_first_ref
  36.8 0.0 collective-permute-done.6.near_first_ref
  36.8 14.1 %all_to_all.16.second_ref = bf16[8,144,128]{2,1,0:T(8,128)(2,1)S(1)} all-to-all(bf16[8,144,128]{2,1,0:T(8,128)(2,1)S(1)} %get-tuple-element.60), channel_id=1, replica_groups=mesh['grp'=2,'lon'=8,'lat'=2] {'lon'}, dimensions={0} | all-to-all | bytes 589824 | tf_op jit(solution)/shard_map/all_to_all | solution.py:327
  50.9 0.0 collective-permute-start.7
  50.9 1.6 %collective-permute-done.7.second_others_ref = bf16[8,144,128]{2,1,0:T(8,128)(2,1)S(1)} collective-permute-done((bf16[8,144,128]{2,1,0:T(8,128)(2,1)S(1)}, bf16[8,144,128]{2,1,0:T(8,128)(2,1)S(1)}, u32[]{:S(2)}, u32[]{:S(2)}) %collective-permute-start.7) | collective-permute-done | bytes 294944 | tf_op jit(solution)/shard_map/ppermute | solution.py:331
  52.5 1.8 %shard_map.131 = (f32[64,1024]{1,0:T(8,128)S(1)}, f32[8,128]{1,0:T(8,128)S(1)}, f32[16,8,128]{2,1,0:T(8,128)S(1)}) custom-call(bf16[8,32,128]{2,1,0:T(8,128)(2,1)S(1)} %all_to_all.15.pieces_ref, bf16[8,32,128]{2,1,0:T(8,128)(2,1)S(1)} %collective-permute-done.others_ref, bf16[8,144,128]{2,1,0:T(8,128)(2,1)S(1)} %all_to_all.16.second_ref, ...), custom_call_target="tpu_custom_call" | custom-call | flops 134217728 | bytes 4358144 | tf_op jit(solution)/shard_map/pallas_call | solution.py:24
  54.3 9.7 %all_to_all.17.chunks_ref = f32[16,8,128]{2,1,0:T(8,128)S(1)} all-to-all(f32[16,8,128]{2,1,0:T(8,128)S(1)} %get-tuple-element.65), channel_id=1, replica_groups=mesh['grp'=2,'lon'=8,'lat'=2] {'lon','lat'}, dimensions={0} | all-to-all | bytes 131072 | tf_op jit(solution)/shard_map/all_to_all | solution.py:327
  64.0 1.2 %shard_map.132 = f32[64,1024]{1,0:T(8,128)} custom-call(f32[8,128]{1,0:T(8,128)S(1)} %get-tuple-element.64.sums_ref, f32[16,8,128]{2,1,0:T(8,128)S(1)} %all_to_all.17.chunks_ref, f32[64,1024]{1,0:T(8,128)S(1)} %get-tuple-element.55.z_ref.first_ref, f32[64,1024]{1,0:T(8,128)S(1)} %get-tuple-element.66.second_ref), custom_call_target="tpu_custom_call" | custom-call | flops 262144 | bytes 593920 | tf_op jit(solution)/shard_map/pallas_call | solution.py:24
Async XLA Ops:
  17.3 4.7 %collective-permute-start = (bf16[8,32,128]{2,1,0:T(8,128)(2,1)S(1)}, bf16[8,32,128]{2,1,0:T(8,128)(2,1)S(1)}, u32[]{:S(2)}, u32[]{:S(2)}) collective-permute-start(bf16[8,32,128]{2,1,0:T(8,128)(2,1)S(1)} %all_to_all.15.pieces_ref), channel_id=1, source_target_pairs={{0,1},{1,0},{2,3},{3,2},{4,5},{5,4},{6,7},{7,6},{8,9},{9,8},{10,11... | collective-permute-start | bytes 196616 | tf_op jit(solution)/shard_map/ppermute | solution.py:331
  20.2 16.6 %collective-permute-start.5 = (bf16[640,128]{1,0:T(8,128)(2,1)S(1)}, bf16[640,128]{1,0:T(8,128)(2,1)S(1)}, u32[]{:S(2)}, u32[]{:S(2)}) collective-permute-start(bf16[640,128]{1,0:T(8,128)(2,1)S(1)} %get-tuple-element.58), channel_id=1, source_target_pairs={{0,14},{2,4},{4,2},{6,8},{8,6},{10,12},{12,10},{14,0},{1,15},{3,5}... | collective-permute-start | bytes 491528 | tf_op jit(solution)/shard_map/ppermute | solution.py:340
  21.1 15.7 %collective-permute-start.6 = (bf16[640,128]{1,0:T(8,128)(2,1)S(1)}, bf16[640,128]{1,0:T(8,128)(2,1)S(1)}, u32[]{:S(2)}, u32[]{:S(2)}) collective-permute-start(bf16[640,128]{1,0:T(8,128)(2,1)S(1)} %get-tuple-element.59), channel_id=1, source_target_pairs={{0,2},{2,0},{4,6},{6,4},{8,10},{10,8},{12,14},{14,12},{1,3},{3,1},... | collective-permute-start | bytes 491528 | tf_op jit(solution)/shard_map/ppermute | solution.py:340
  23.3 12.4 %collective-permute-start.1 = (bf16[384,128]{1,0:T(8,128)(2,1)S(1)}, bf16[384,128]{1,0:T(8,128)(2,1)S(1)}, u32[]{:S(2)}, u32[]{:S(2)}) collective-permute-start(bf16[384,128]{1,0:T(8,128)(2,1)S(1)} %get-tuple-element.51), channel_id=1, source_target_pairs={{0,14},{2,4},{4,2},{6,8},{8,6},{10,12},{12,10},{14,0},{1,15},{3,5}... | collective-permute-start | bytes 294920 | tf_op jit(solution)/shard_map/ppermute | solution.py:340
  26.4 9.3 %collective-permute-start.3 = (bf16[384,128]{1,0:T(8,128)(2,1)S(1)}, bf16[384,128]{1,0:T(8,128)(2,1)S(1)}, u32[]{:S(2)}, u32[]{:S(2)}) collective-permute-start(bf16[384,128]{1,0:T(8,128)(2,1)S(1)} %get-tuple-element.53), channel_id=1, source_target_pairs={{0,2},{2,0},{4,6},{6,4},{8,10},{10,8},{12,14},{14,12},{1,3},{3,1},... | collective-permute-start | bytes 294920 | tf_op jit(solution)/shard_map/ppermute | solution.py:340
  26.4 5.5 %collective-permute-start.2 = (bf16[64,128]{1,0:T(8,128)(2,1)S(1)}, bf16[64,128]{1,0:T(8,128)(2,1)S(1)}, u32[]{:S(2)}, u32[]{:S(2)}) collective-permute-start(bf16[64,128]{1,0:T(8,128)(2,1)S(1)} %get-tuple-element.52.own_beyond_ref), channel_id=1, source_target_pairs={{0,12},{2,14},{4,8},{6,10},{8,4},{10,6},{12,0},{14,2},{1,13},{3,15... | collective-permute-start | bytes 49160 | tf_op jit(solution)/shard_map/ppermute | solution.py:340
  31.9 3.7 %collective-permute-start.4 = (bf16[64,128]{1,0:T(8,128)(2,1)S(1)}, bf16[64,128]{1,0:T(8,128)(2,1)S(1)}, u32[]{:S(2)}, u32[]{:S(2)}) collective-permute-start(bf16[64,128]{1,0:T(8,128)(2,1)S(1)} %get-tuple-element.54.own_far_ref), channel_id=1, source_target_pairs={{0,4},{2,6},{4,0},{6,2},{8,12},{10,14},{12,8},{14,10},{1,5},{3,7},... | collective-permute-start | bytes 49160 | tf_op jit(solution)/shard_map/ppermute | solution.py:340
  50.9 1.6 %collective-permute-start.7 = (bf16[8,144,128]{2,1,0:T(8,128)(2,1)S(1)}, bf16[8,144,128]{2,1,0:T(8,128)(2,1)S(1)}, u32[]{:S(2)}, u32[]{:S(2)}) collective-permute-start(bf16[8,144,128]{2,1,0:T(8,128)(2,1)S(1)} %all_to_all.16.second_ref), channel_id=1, source_target_pairs={{0,1},{1,0},{2,3},{3,2},{4,5},{5,4},{6,7},{7,6},{8,9},{9,8},{10,11... | collective-permute-start | bytes 884744 | tf_op jit(solution)/shard_map/ppermute | solution.py:331

commit v9 on v8

--- a/solution.py
+++ b/solution.py
@@ -69,8 +69,8 @@
 
 def load_kernel(count_ref, right_hbm, vectors_hbm, react_hbm, mass_hbm, obs_hbm,
                 coupling_hbm, blocks_hbm, east_hbm, west_hbm, inverse_hbm,
-                chunks_ref, diag_ref, link_ref, right_ref, vectors_ref, blocks_ref, east_ref, west_ref,
-                inverse_ref, react_ref, mass_ref, obs_ref, coupling_ref, sems):
+                chunks_ref, diag_ref, right_ref, vectors_ref, coupling_ref, blocks_ref, east_ref, west_ref,
+                inverse_ref, react_ref, mass_ref, obs_ref, sems):
     pairs = (
         (right_hbm, right_ref), (vectors_hbm, vectors_ref), (react_hbm, react_ref), (mass_hbm, mass_ref),
         (obs_hbm, obs_ref), (coupling_hbm, coupling_ref), (blocks_hbm, blocks_ref), (east_hbm, east_ref),
@@ -79,7 +79,7 @@
     copies = [pltpu.make_async_copy(src, dst, sems.at[i]) for i, (src, dst) in enumerate(pairs)]
     for copy in copies:
         copy.start()
-    for copy in copies[:6]:
+    for copy in copies[:5]:
         copy.wait()
     nodes = right_ref.shape[1]
     active = (lax.broadcasted_iota(jnp.int32, (1, nodes), 1) < count_ref[0]).astype(F32)
@@ -91,11 +91,7 @@
     for i, line in enumerate((active, react, 1.0 / mass, obs, 1.0 / (obs + react * react / mass))):
         diag = jnp.where(row == i, line, diag)
     diag_ref[...] = diag
-    slots = coupling_ref.shape[0]
-    live_a = lax.broadcasted_iota(jnp.int32, (slots, slots), 0) < count_ref[1]
-    live_b = lax.broadcasted_iota(jnp.int32, (slots, slots), 1) < count_ref[1]
-    link_ref[...] = jnp.where(live_a & live_b, coupling_ref[...], jnp.zeros((slots, slots), BF16))
-    for copy in copies[6:]:
+    for copy in copies[5:]:
         copy.wait()
 
 
@@ -103,13 +99,13 @@
     return tuple(diag_ref[i : i + 1, :] for i in range(5))
 
 
-def prep_kernel(pattern_hbm, blocks_ref, right_ref, vectors_ref, link_ref, east_ref, west_ref, diag_ref, inverse_ref,
-                dense_ref, edge_ref, to_west_ref, to_east_ref, near_ref, across_ref, pattern_ref, total_ref, sem):
+def prep_kernel(iface_ref, pattern_hbm, blocks_ref, right_ref, vectors_ref, coupling_ref, east_ref, west_ref, diag_ref,
+                dense_ref, edge_ref, to_west_ref, to_east_ref, pattern_ref, total_ref, sem):
     copy = pltpu.make_async_copy(pattern_hbm, pattern_ref, sem)
     copy.start()
     samples, nodes = right_ref.shape
     count, block, _ = blocks_ref.shape
-    slots = link_ref.shape[0]
+    slots = coupling_ref.shape[0]
 
     def clear(i, carry):
         total_ref[pl.ds(pl.multiple_of(i * block, block), block), :] = jnp.zeros((block, nodes), F32)
@@ -142,27 +138,21 @@
     node = lax.broadcasted_iota(jnp.int32, (slots, nodes), 1).astype(F32)
     east_hot = jnp.where(node == column_of(east_ref[...].astype(F32)), 1.0, 0.0).astype(BF16)
     west_hot = jnp.where(node == column_of(west_ref[...].astype(F32)), 1.0, 0.0).astype(BF16)
-    spread = dot(link_ref[...], east_hot, 0, 0).astype(BF16)
+    live_a = lax.broadcasted_iota(jnp.int32, (slots, slots), 0) < iface_ref[0]
+    live_b = lax.broadcasted_iota(jnp.int32, (slots, slots), 1) < iface_ref[0]
+    link = jnp.where(live_a & live_b, coupling_ref[...], jnp.zeros((slots, slots), BF16))
+    spread = dot(link, east_hot, 0, 0).astype(BF16)
     edge_ref[0:slots, :] = spread
     edge_ref[slots : 2 * slots, :] = west_hot
     edges = jnp.concatenate([spread, west_hot], axis=0)
     both = dot((edges.astype(F32) * inverse_mass).astype(BF16), edges, 1, 1).astype(BF16)
-    to_east_ref[...] = both[:, 0:slots]
-    to_west_ref[...] = both[:, slots:]
-
     masked = vectors_ref[...] * active.astype(BF16)
     smooth_right = (active * jacobi * right_ref[...].astype(F32)).astype(BF16)
     level = levels(jnp.concatenate([masked, smooth_right], axis=0), edges).astype(BF16)
-    rows, width = inverse_ref.shape
-    for ref in (near_ref, across_ref):
-        for j in range(width // LANES):
-            ref[j * rows : (j + 1) * rows, :] = inverse_ref[:, j * LANES : (j + 1) * LANES]
-
-    def send(east_ref, west_ref):
-        east_ref[width // LANES * rows :, :] = level[:, 0:slots]
-        west_ref[width // LANES * rows :, :] = level[:, slots:]
-
-    by_lon(0, near_ref, across_ref, send)
+    to_east_ref[0 : 2 * slots, :] = both[:, 0:slots]
+    to_west_ref[0 : 2 * slots, :] = both[:, slots:]
+    to_east_ref[2 * slots :, :] = level[:, 0:slots]
+    to_west_ref[2 * slots :, :] = level[:, slots:]
 
 
 def unfold(count, piece, coarse_ref):
@@ -224,15 +214,16 @@
     active, react, inverse_mass, obs, jacobi = lines(diag_ref)
     z = z_ref[...]
     edges = edge_ref[...]
-    from_east, from_west = pick(0, near_ref[...], across_ref[...])
+    fixed = 2 * samples + edges.shape[0]
+    from_east, from_west = pick(0, near_ref[0:fixed, :], across_ref[0:fixed, :])
     beyond_east, beyond_west = pick(1, far_ref[...], beyond_ref[...])
     own_east, own_west = pick(1, own_far_ref[...], own_beyond_ref[...])
     arrived = jnp.concatenate([from_east[0:samples], from_west[0:samples]], axis=1)
     inner = scaled_ref[...] + dot(arrived, edges) * inverse_mass
     east_terms = jnp.concatenate([beyond_east, own_east], axis=1)
     west_terms = jnp.concatenate([own_west, beyond_west], axis=1)
-    second_east = from_east[samples : 2 * samples].astype(F32) + dot(east_terms, from_east[2 * samples :])
-    second_west = from_west[samples : 2 * samples].astype(F32) + dot(west_terms, from_west[2 * samples :])
+    second_east = from_east[samples : 2 * samples].astype(F32) + dot(east_terms, from_east[2 * samples : fixed])
+    second_west = from_west[samples : 2 * samples].astype(F32) + dot(west_terms, from_west[2 * samples : fixed])
     arrived2 = jnp.concatenate([second_east, second_west], axis=1).astype(BF16)
     stiff = dot(inner.astype(BF16), dense_ref[...]) + dot(arrived2, edges) + react * inner
     image = active * (stiff + obs * z)
@@ -257,7 +248,7 @@
 
 
 def middle_kernel(pieces_ref, others_ref, second_ref, second_others_ref,
-                  across_first_ref, near_first_ref, inverse_ref, right_ref, image_ref, vectors_ref,
+                  across_ref, near_ref, across_inverse_ref, near_inverse_ref, inverse_ref, right_ref, image_ref, vectors_ref,
                   dense_ref, edge_ref, diag_ref, z_ref, sums_ref, chunks_ref, coarse_ref):
     samples, nodes = right_ref.shape
     count, half, _ = pieces_ref.shape
@@ -285,20 +276,18 @@
     z = smooth(residual, coarse_ref, inverse_ref, vectors_ref, active, jacobi)
     z_ref[...] = z
 
-    def arriving(first, change):
-        rows, width = inverse_ref.shape
-        blocks = width // LANES
-        inverse = jnp.concatenate([first[j * rows : (j + 1) * rows] for j in range(blocks)], axis=1)
+    def arriving(level, inverse, change):
         fix = dot(inverse, coarse_ref[...]).astype(BF16)
-        level = first[blocks * rows :]
-        smooth_level = level[rows:].astype(F32) - step_column * change.astype(F32)
-        return (smooth_level + dot(fix, level[0:rows], 0, 0)).astype(BF16)
+        spread = dot(fix, level[0 : fix.shape[0]], 0, 0)
+        return (level[fix.shape[0] :].astype(F32) - step_column * change.astype(F32) + spread).astype(BF16)
 
     lon = lax.axis_index("lon")
     ahead, before = lax.rem(lon + 1, count), lax.rem(lon + count - 1, count)
-    east_first, west_first = pick(0, near_first_ref[...], across_first_ref[...])
-    from_east = arriving(east_first, second_ref[ahead, 2 * half + SUM_ROWS :, :])
-    from_west = arriving(west_first, second_ref[before, 2 * half + SUM_ROWS :, :])
+    fixed = 2 * samples + edges.shape[0]
+    east_level, west_level = pick(0, near_ref[fixed:, :], across_ref[fixed:, :])
+    east_inverse, west_inverse = pick(0, near_inverse_ref[...], across_inverse_ref[...])
+    from_east = arriving(east_level, east_inverse, second_ref[ahead, 2 * half + SUM_ROWS :, :])
+    from_west = arriving(west_level, west_inverse, second_ref[before, 2 * half + SUM_ROWS :, :])
     arrived = jnp.concatenate([from_east, from_west], axis=1)
     stiff = dot(z.astype(BF16), dense_ref[...]) + react * z + dot(arrived, edges)
     curve = jnp.sum(stiff * stiff * inverse_mass + obs * z * z, axis=1, keepdims=True)
@@ -365,34 +354,35 @@
     field = ((samples, nodes), F32)
     coarse_scratch = pltpu.VMEM((domains * vectors, samples), BF16)
     apply_cost = 2 * samples * nodes * nodes
-    blocks = coarse_inverse.shape[1] // LANES
-    static = ((blocks * vectors + vectors + samples, slots), BF16)
-    corr = ((2 * slots, slots), BF16)
-    kept = (right_side, deflation, stiffness_blocks, east_rows, west_rows, coarse_inverse)
+    corr = ((2 * slots + vectors + samples, slots), BF16)
+    kept = (right_side, deflation, coupling, stiffness_blocks, east_rows, west_rows, coarse_inverse)
     inputs = (right_side, deflation, react, mass, obs, coupling, stiffness_blocks, east_rows, west_rows, coarse_inverse)
     line = pltpu.VMEM((1, nodes), F32)
-    chunks, diag, link, right, basis, stored, east, west, inverse = call(
+    chunks, diag, right, basis, link, stored, east, west, inverse = call(
         load_kernel,
-        [((sectors, half, LANES), BF16), ((8, nodes), F32), (coupling.shape, BF16)] + [(a.shape, a.dtype) for a in kept],
+        [((sectors, half, LANES), BF16), ((8, nodes), F32)] + [(a.shape, a.dtype) for a in kept],
         [SMEM] + [HBM] * len(inputs),
-        [jnp.concatenate([node_count, iface_count])] + [pltpu.with_memory_space_constraint(a, pltpu.HBM) for a in inputs],
+        [node_count] + [pltpu.with_memory_space_constraint(a, pltpu.HBM) for a in inputs],
         2 * samples * vectors * nodes,
-        [line, line, line, pltpu.VMEM(coupling.shape, BF16), pltpu.SemaphoreType.DMA((len(inputs),))],
-    )
-    pieces, stored = lax.optimization_barrier((exchange(chunks, "lon"), stored))
+        [line, line, line, pltpu.SemaphoreType.DMA((len(inputs),))],
+    )
+    across_inverse, near_inverse = swap(coarse_inverse, 1, False), swap(coarse_inverse, 1, True)
+    pieces, stored, iface, across_inverse, near_inverse = lax.optimization_barrier(
+        (exchange(chunks, "lon"), stored, iface_count, across_inverse, near_inverse)
+    )
     pattern = pltpu.with_memory_space_constraint(block_pattern.T, pltpu.HBM)
-    dense, edge, corr_west, corr_east, near_first, across_first = call(
+    dense, edge, corr_west, corr_east = call(
         prep_kernel,
-        [((nodes, nodes), BF16), ((2 * slots, nodes), BF16), corr, corr, static, static],
-        [HBM] + [VMEM] * 8,
-        (pattern, stored, right, basis, link, east, west, diag, inverse),
+        [((nodes, nodes), BF16), ((2 * slots, nodes), BF16), corr, corr],
+        [SMEM, HBM] + [VMEM] * 7,
+        (iface, pattern, stored, right, basis, link, east, west, diag),
         apply_cost,
         [pltpu.SMEM((2, block_pattern.shape[0]), jnp.int32), pltpu.VMEM((nodes, nodes), F32), pltpu.SemaphoreType.DMA],
     )
     others = other_band(pieces)
     z0, scaled, near, across, far, beyond = call(
         start_kernel,
-        [field] * 2 + [((2 * samples + 2 * slots, slots), BF16)] * 2 + [((samples, slots), BF16)] * 2,
+        [field] * 2 + [((2 * samples + corr[0][0], slots), BF16)] * 2 + [((samples, slots), BF16)] * 2,
         [VMEM] * 10,
         (pieces, others, inverse, right, basis, dense, edge, diag, corr_west, corr_east),
         apply_cost,
@@ -402,8 +392,6 @@
     got_beyond = swap(beyond, 2, False)
     near = swap(near, 1, True)
     got_far = swap(far, 2, True)
-    across_first = swap(across_first, 1, False)
-    near_first = swap(near_first, 1, True)
     image, chunks = call(
         image_kernel,
         [field, ((sectors, 2 * half + SUM_ROWS + samples, LANES), BF16)],
@@ -411,14 +399,13 @@
         (across, got_beyond, near, got_far, far, beyond, z0, scaled, dense, edge, diag, right, basis),
         apply_cost,
     )
-    chunks, across_first, near_first = lax.optimization_barrier((chunks, across_first, near_first))
     second = exchange(chunks, "lon")
     second_others = other_band(second)
     z1, sums, chunks = call(
         middle_kernel,
         [field, ((8, LANES), F32), ((domains, 8, LANES), F32)],
-        [VMEM] * 13,
-        (pieces, others, second, second_others, across_first, near_first,
+        [VMEM] * 15,
+        (pieces, others, second, second_others, across, near, across_inverse, near_inverse,
          inverse, right, image, basis, dense, edge, diag),
         apply_cost,
         [coarse_scratch],

time: 65.5 us -> 62.6 us (0.956)
  starting transfers between devices: 7.11 us -> 11.9 us
  blocking collectives: 37.7 us -> 33.8 us
  waiting for transfers between devices: 8.64 us -> 5.55 us
    ppermute x6, starting transfers between devices: 7.11 us -> 11.9 us  [swap(): return lax.ppermute(array, 'lon', pairs)]
    all_to_all x3, blocking collectives: 37.7 us -> 33.8 us  [exchange(): return lax.all_to_all(chunks, axes, split_axis=0, concat_axis=0, tiled=True)]
    ppermute x6, waiting for transfers between devices: 7.05 us -> 3.97 us  [swap(): return lax.ppermute(array, 'lon', pairs)]
  transfers between devices with their start and end apart: 8 -> 8, of which waited for: 3 -> 4; matrix products, arithmetic and copies ran while one was open for 0% -> 0% of each run, Pallas kernels for 8% -> 7%
where the time goes in v9:
time: 62.6 us; the launch traced here: 62.3 us
  blocking collectives  33.8 us (54%)
  starting transfers between devices  11.9 us (19%)
  Pallas kernels  9.74 us (16%)
  waiting for transfers between devices  5.55 us (9%)
  between operations  1.35 us (2%)
    all_to_all x3, blocking collectives, exchange(): return lax.all_to_all(chunks, axes, split_axis=0, concat_axis=0, tiled=True)  33.8 us
    ppermute x6, starting transfers between devices, swap(): return lax.ppermute(array, 'lon', pairs)  11.9 us
    pallas_call x6, Pallas kernels, call(): pl.pallas_call(kernel, out_shape=[jax.ShapeDtypeStruct(s, t) for s, t in...  9.74 us
    ppermute x6, waiting for transfers between devices, swap(): return lax.ppermute(array, 'lon', pairs)  3.97 us
    ppermute x2, waiting for transfers between devices, other_band(): return lax.ppermute(array, 'lat', [(0, 1), (1, 0)])  1.58 us
  transfers between devices with their start and end apart: 8, of which 4 were waited for; matrix products, arithmetic and copies ran while one was open for 0% of the time, Pallas kernels for 7%

profile of v9, /device:TPU:0, one launch (start us, length us, event | category | flops | bytes accessed | tf_op | source)
XLA Modules:
  0.0 62.3 jit_solution(6209880221603364233)
XLA Ops:
  0.0 2.9 %collective-permute-start.1 = (bf16[64,1024]{1,0:T(8,128)(2,1)}, bf16[64,1024]{1,0:T(8,128)(2,1)S(1)}, u32[]{:S(2)}, u32[]{:S(2)}) collective-permute-start(bf16[64,1024]{1,0:T(8,128)(2,1)} %inverse_hbm.1), channel_id=1, source_target_pairs={{0,2},{2,0},{4,6},{6,4},{8,10},{10,8},{12,14},{14,12},{1,3},{3,1},... | collective-permute-start | bytes 393224 | tf_op jit(solution)/shard_map/ppermute | solution.py:329
  2.9 3.6 %collective-permute-start = (bf16[64,1024]{1,0:T(8,128)(2,1)}, bf16[64,1024]{1,0:T(8,128)(2,1)S(1)}, u32[]{:S(2)}, u32[]{:S(2)}) collective-permute-start(bf16[64,1024]{1,0:T(8,128)(2,1)} %inverse_hbm.1), channel_id=1, source_target_pairs={{0,14},{2,4},{4,2},{6,8},{8,6},{10,12},{12,10},{14,0},{1,15},{3,5}... | collective-permute-start | bytes 393224 | tf_op jit(solution)/shard_map/ppermute | solution.py:329
  7.2 1.5 %shard_map.127 = (bf16[8,32,128]{2,1,0:T(8,128)(2,1)S(1)}, f32[8,1024]{1,0:T(8,128)S(1)}, bf16[64,1024]{1,0:T(8,128)(2,1)S(1)}, bf16[64,1024]{1,0:T(8,128)(2,1)S...) custom-call(s32[1]{0:T(128)S(6)} %copy.15.count_ref, ...), custom_call_target="tpu_custom_call" | custom-call | flops 8388608 | bytes 1225732 | tf_op jit(solution)/shard_map/pallas_call | solution.py:24
  8.6 9.5 %all_to_all.15.pieces_ref = bf16[8,32,128]{2,1,0:T(8,128)(2,1)S(1)} all-to-all(bf16[8,32,128]{2,1,0:T(8,128)(2,1)S(1)} %get-tuple-element.34), channel_id=1, replica_groups=mesh['grp'=2,'lon'=8,'lat'=2] {'lon'}, dimensions={0} | all-to-all | bytes 131072 | tf_op jit(solution)/shard_map/all_to_all | solution.py:316
  18.1 0.0 collective-permute-done.1.near_inverse_ref
  18.1 0.0 collective-permute-done.across_inverse_ref
  18.1 0.0 collective-permute-start.2
  18.8 2.9 %shard_map.128 = (bf16[1024,1024]{1,0:T(8,128)(2,1)S(1)}, bf16[256,1024]{1,0:T(8,128)(2,1)S(1)}, bf16[384,128]{1,0:T(8,128)(2,1)S(1)}, bf16[384,128]{1,0:T(8,128)(2,1)S(1)}) custom-call(s32[1]{0:T(128)S(6)} %copy.14.iface_ref, s32[2,24]{1,0:T(2,128)} %bitcast.7, bf16[24,128,128]{2,1,0:T(8,128)(2,1)S(1)} %get-tuple-element.41.blocks_ref, ...), custom_call_target="tpu_custom_call" | custom-call | flops 134217728 | bytes 1115332 | tf_op jit(solution)/shard_map/pallas_call | solution.py:24
  21.7 0.0 collective-permute-done.2.others_ref
  21.7 1.3 %shard_map.129 = (f32[64,1024]{1,0:T(8,128)S(1)}, f32[64,1024]{1,0:T(8,128)S(1)}, bf16[512,128]{1,0:T(8,128)(2,1)S(1)}, bf16[512,128]{1,0:T(8,128)(2,1)S(1)}, bf...) custom-call(bf16[8,32,128]{2,1,0:T(8,128)(2,1)S(1)} %all_to_all.15.pieces_ref, ...), custom_call_target="tpu_custom_call" | custom-call | flops 134217728 | bytes 3375104 | tf_op jit(solution)/shard_map/pallas_call | solution.py:24
  23.0 0.9 %collective-permute-start.3 = (bf16[512,128]{1,0:T(8,128)(2,1)S(1)}, bf16[512,128]{1,0:T(8,128)(2,1)S(1)}, u32[]{:S(2)}, u32[]{:S(2)}) collective-permute-start(bf16[512,128]{1,0:T(8,128)(2,1)S(1)} %get-tuple-element.50), channel_id=1, source_target_pairs={{0,14},{2,4},{4,2},{6,8},{8,6},{10,12},{12,10},{14,0},{1,15},{3,5}... | collective-permute-start | bytes 393224 | tf_op jit(solution)/shard_map/ppermute | solution.py:329
  23.9 0.8 %collective-permute-start.5 = (bf16[512,128]{1,0:T(8,128)(2,1)S(1)}, bf16[512,128]{1,0:T(8,128)(2,1)S(1)}, u32[]{:S(2)}, u32[]{:S(2)}) collective-permute-start(bf16[512,128]{1,0:T(8,128)(2,1)S(1)} %get-tuple-element.52), channel_id=1, source_target_pairs={{0,2},{2,0},{4,6},{6,4},{8,10},{10,8},{12,14},{14,12},{1,3},{3,1},... | collective-permute-start | bytes 393224 | tf_op jit(solution)/shard_map/ppermute | solution.py:329
  24.7 3.6 %collective-permute-start.4 = (bf16[64,128]{1,0:T(8,128)(2,1)S(1)}, bf16[64,128]{1,0:T(8,128)(2,1)S(1)}, u32[]{:S(2)}, u32[]{:S(2)}) collective-permute-start(bf16[64,128]{1,0:T(8,128)(2,1)S(1)} %get-tuple-element.51.own_beyond_ref), channel_id=1, source_target_pairs={{0,12},{2,14},{4,8},{6,10},{8,4},{10,6},{12,0},{14,2},{1,13},{3,15... | collective-permute-start | bytes 49160 | tf_op jit(solution)/shard_map/ppermute | solution.py:329
  28.3 0.0 collective-permute-start.6
  28.3 1.9 %collective-permute-done.4.beyond_ref = bf16[64,128]{1,0:T(8,128)(2,1)S(1)} collective-permute-done((bf16[64,128]{1,0:T(8,128)(2,1)S(1)}, bf16[64,128]{1,0:T(8,128)(2,1)S(1)}, u32[]{:S(2)}, u32[]{:S(2)}) %collective-permute-start.4) | collective-permute-done | bytes 16416 | tf_op jit(solution)/shard_map/ppermute | solution.py:329
  30.2 1.8 %collective-permute-done.6.far_ref = bf16[64,128]{1,0:T(8,128)(2,1)S(1)} collective-permute-done((bf16[64,128]{1,0:T(8,128)(2,1)S(1)}, bf16[64,128]{1,0:T(8,128)(2,1)S(1)}, u32[]{:S(2)}, u32[]{:S(2)}) %collective-permute-start.6) | collective-permute-done | bytes 16416 | tf_op jit(solution)/shard_map/ppermute | solution.py:329
  32.1 0.0 collective-permute-done.3.across_ref
  32.1 0.2 collective-permute-done.5.near_ref
  32.3 1.1 %shard_map.130 = (f32[64,1024]{1,0:T(8,128)S(1)}, bf16[8,144,128]{2,1,0:T(8,128)(2,1)S(1)}) custom-call(bf16[512,128]{1,0:T(8,128)(2,1)S(1)} %collective-permute-done.3.across_ref, bf16[64,128]{1,0:T(8,128)(2,1)S(1)} %collective-permute-done.4.beyond_ref, bf16[512,128]{1,0:T(8,128)(2,1)S(1)} %collective-permute-done.5.near_ref, ...), custom_call_target="tpu_custom_call" | custom-call | flops 134217728 | bytes 3768320 | tf_op jit(solution)/shard_map/pallas_call | solution.py:24
  33.4 14.6 %all_to_all.16.second_ref = bf16[8,144,128]{2,1,0:T(8,128)(2,1)S(1)} all-to-all(bf16[8,144,128]{2,1,0:T(8,128)(2,1)S(1)} %get-tuple-element.56), channel_id=1, replica_groups=mesh['grp'=2,'lon'=8,'lat'=2] {'lon'}, dimensions={0} | all-to-all | bytes 589824 | tf_op jit(solution)/shard_map/all_to_all | solution.py:316
  48.0 0.0 collective-permute-start.7
  48.0 1.6 %collective-permute-done.7.second_others_ref = bf16[8,144,128]{2,1,0:T(8,128)(2,1)S(1)} collective-permute-done((bf16[8,144,128]{2,1,0:T(8,128)(2,1)S(1)}, bf16[8,144,128]{2,1,0:T(8,128)(2,1)S(1)}, u32[]{:S(2)}, u32[]{:S(2)}) %collective-permute-start.7) | collective-permute-done | bytes 294944 | tf_op jit(solution)/shard_map/ppermute | solution.py:320
  49.6 1.8 %shard_map.131 = (f32[64,1024]{1,0:T(8,128)S(1)}, f32[8,128]{1,0:T(8,128)S(1)}, f32[16,8,128]{2,1,0:T(8,128)S(1)}) custom-call(bf16[8,32,128]{2,1,0:T(8,128)(2,1)S(1)} %all_to_all.15.pieces_ref, bf16[8,32,128]{2,1,0:T(8,128)(2,1)S(1)} %collective-permute-done.2.others_ref, bf16[8,144,128]{2,1,0:T(8,128)(2,1)S(1)} %all_to_all.16.second_ref, ...), custom_call_target="tpu_custom_call" | custom-call | flops 134217728 | bytes 4554752 | tf_op jit(solution)/shard_map/pallas_call | solution.py:24
  51.4 9.7 %all_to_all.17.chunks_ref = f32[16,8,128]{2,1,0:T(8,128)S(1)} all-to-all(f32[16,8,128]{2,1,0:T(8,128)S(1)} %get-tuple-element.61), channel_id=1, replica_groups=mesh['grp'=2,'lon'=8,'lat'=2] {'lon','lat'}, dimensions={0} | all-to-all | bytes 131072 | tf_op jit(solution)/shard_map/all_to_all | solution.py:316
  61.1 1.2 %shard_map.132 = f32[64,1024]{1,0:T(8,128)} custom-call(f32[8,128]{1,0:T(8,128)S(1)} %get-tuple-element.60.sums_ref, f32[16,8,128]{2,1,0:T(8,128)S(1)} %all_to_all.17.chunks_ref, f32[64,1024]{1,0:T(8,128)S(1)} %get-tuple-element.54.z_ref.first_ref, f32[64,1024]{1,0:T(8,128)S(1)} %get-tuple-element.62.second_ref), custom_call_target="tpu_custom_call" | custom-call | flops 262144 | bytes 593920 | tf_op jit(solution)/shard_map/pallas_call | solution.py:24
Async XLA Ops:
  0.0 18.1 %collective-permute-start.1 = (bf16[64,1024]{1,0:T(8,128)(2,1)}, bf16[64,1024]{1,0:T(8,128)(2,1)S(1)}, u32[]{:S(2)}, u32[]{:S(2)}) collective-permute-start(bf16[64,1024]{1,0:T(8,128)(2,1)} %inverse_hbm.1), channel_id=1, source_target_pairs={{0,2},{2,0},{4,6},{6,4},{8,10},{10,8},{12,14},{14,12},{1,3},{3,1},... | collective-permute-start | bytes 393224 | tf_op jit(solution)/shard_map/ppermute | solution.py:329
  2.9 15.2 %collective-permute-start = (bf16[64,1024]{1,0:T(8,128)(2,1)}, bf16[64,1024]{1,0:T(8,128)(2,1)S(1)}, u32[]{:S(2)}, u32[]{:S(2)}) collective-permute-start(bf16[64,1024]{1,0:T(8,128)(2,1)} %inverse_hbm.1), channel_id=1, source_target_pairs={{0,14},{2,4},{4,2},{6,8},{8,6},{10,12},{12,10},{14,0},{1,15},{3,5}... | collective-permute-start | bytes 393224 | tf_op jit(solution)/shard_map/ppermute | solution.py:329
  18.1 3.6 %collective-permute-start.2 = (bf16[8,32,128]{2,1,0:T(8,128)(2,1)S(1)}, bf16[8,32,128]{2,1,0:T(8,128)(2,1)S(1)}, u32[]{:S(2)}, u32[]{:S(2)}) collective-permute-start(bf16[8,32,128]{2,1,0:T(8,128)(2,1)S(1)} %all_to_all.15.pieces_ref), channel_id=1, source_target_pairs={{0,1},{1,0},{2,3},{3,2},{4,5},{5,4},{6,7},{7,6},{8,9},{9,8},{10,11... | collective-permute-start | bytes 196616 | tf_op jit(solution)/shard_map/ppermute | solution.py:320
  23.0 9.1 %collective-permute-start.3 = (bf16[512,128]{1,0:T(8,128)(2,1)S(1)}, bf16[512,128]{1,0:T(8,128)(2,1)S(1)}, u32[]{:S(2)}, u32[]{:S(2)}) collective-permute-start(bf16[512,128]{1,0:T(8,128)(2,1)S(1)} %get-tuple-element.50), channel_id=1, source_target_pairs={{0,14},{2,4},{4,2},{6,8},{8,6},{10,12},{12,10},{14,0},{1,15},{3,5}... | collective-permute-start | bytes 393224 | tf_op jit(solution)/shard_map/ppermute | solution.py:329
  23.9 8.4 %collective-permute-start.5 = (bf16[512,128]{1,0:T(8,128)(2,1)S(1)}, bf16[512,128]{1,0:T(8,128)(2,1)S(1)}, u32[]{:S(2)}, u32[]{:S(2)}) collective-permute-start(bf16[512,128]{1,0:T(8,128)(2,1)S(1)} %get-tuple-element.52), channel_id=1, source_target_pairs={{0,2},{2,0},{4,6},{6,4},{8,10},{10,8},{12,14},{14,12},{1,3},{3,1},... | collective-permute-start | bytes 393224 | tf_op jit(solution)/shard_map/ppermute | solution.py:329
  24.7 5.5 %collective-permute-start.4 = (bf16[64,128]{1,0:T(8,128)(2,1)S(1)}, bf16[64,128]{1,0:T(8,128)(2,1)S(1)}, u32[]{:S(2)}, u32[]{:S(2)}) collective-permute-start(bf16[64,128]{1,0:T(8,128)(2,1)S(1)} %get-tuple-element.51.own_beyond_ref), channel_id=1, source_target_pairs={{0,12},{2,14},{4,8},{6,10},{8,4},{10,6},{12,0},{14,2},{1,13},{3,15... | collective-permute-start | bytes 49160 | tf_op jit(solution)/shard_map/ppermute | solution.py:329
  28.3 3.7 %collective-permute-start.6 = (bf16[64,128]{1,0:T(8,128)(2,1)S(1)}, bf16[64,128]{1,0:T(8,128)(2,1)S(1)}, u32[]{:S(2)}, u32[]{:S(2)}) collective-permute-start(bf16[64,128]{1,0:T(8,128)(2,1)S(1)} %get-tuple-element.53.own_far_ref), channel_id=1, source_target_pairs={{0,4},{2,6},{4,0},{6,2},{8,12},{10,14},{12,8},{14,10},{1,5},{3,7},... | collective-permute-start | bytes 49160 | tf_op jit(solution)/shard_map/ppermute | solution.py:329
  48.0 1.6 %collective-permute-start.7 = (bf16[8,144,128]{2,1,0:T(8,128)(2,1)S(1)}, bf16[8,144,128]{2,1,0:T(8,128)(2,1)S(1)}, u32[]{:S(2)}, u32[]{:S(2)}) collective-permute-start(bf16[8,144,128]{2,1,0:T(8,128)(2,1)S(1)} %all_to_all.16.second_ref), channel_id=1, source_target_pairs={{0,1},{1,0},{2,3},{3,2},{4,5},{5,4},{6,7},{7,6},{8,9},{9,8},{10,11... | collective-permute-start | bytes 884744 | tf_op jit(solution)/shard_map/ppermute | solution.py:320

commit v10 on v9

--- a/solution.py
+++ b/solution.py
@@ -67,45 +67,70 @@
     return jnp.where(keep, first, second).astype(BF16), jnp.where(keep, second, first).astype(BF16)
 
 
-def load_kernel(count_ref, right_hbm, vectors_hbm, react_hbm, mass_hbm, obs_hbm,
-                coupling_hbm, blocks_hbm, east_hbm, west_hbm, inverse_hbm,
-                chunks_ref, diag_ref, right_ref, vectors_ref, coupling_ref, blocks_ref, east_ref, west_ref,
-                inverse_ref, react_ref, mass_ref, obs_ref, sems):
+def lines(diag_ref):
+    return tuple(diag_ref[i : i + 1, :] for i in range(5))
+
+
+def load_kernel(count_ref, right_hbm, vectors_hbm, react_hbm, mass_hbm, obs_hbm, coupling_hbm, east_hbm, west_hbm,
+                blocks_hbm, inverse_hbm,
+                chunks_ref, diag_ref, edge_ref, near_ref, across_ref, right_ref, vectors_ref, blocks_ref, inverse_ref,
+                react_ref, mass_ref, obs_ref, coupling_ref, east_ref, west_ref, sems):
     pairs = (
         (right_hbm, right_ref), (vectors_hbm, vectors_ref), (react_hbm, react_ref), (mass_hbm, mass_ref),
-        (obs_hbm, obs_ref), (coupling_hbm, coupling_ref), (blocks_hbm, blocks_ref), (east_hbm, east_ref),
-        (west_hbm, west_ref), (inverse_hbm, inverse_ref),
+        (obs_hbm, obs_ref), (coupling_hbm, coupling_ref), (east_hbm, east_ref), (west_hbm, west_ref),
+        (inverse_hbm, inverse_ref), (blocks_hbm, blocks_ref),
     )
     copies = [pltpu.make_async_copy(src, dst, sems.at[i]) for i, (src, dst) in enumerate(pairs)]
     for copy in copies:
         copy.start()
-    for copy in copies[:5]:
+    for copy in copies[:9]:
         copy.wait()
     nodes = right_ref.shape[1]
+    slots = coupling_ref.shape[0]
     active = (lax.broadcasted_iota(jnp.int32, (1, nodes), 1) < count_ref[0]).astype(F32)
-    coarse = fold(dot(vectors_ref[...], right_ref[...] * active.astype(BF16), 1, 1)).astype(BF16)
+    right = active * right_ref[...].astype(F32)
+    coarse = fold(dot(vectors_ref[...], right.astype(BF16), 1, 1)).astype(BF16)
     chunks_ref[...] = jnp.broadcast_to(coarse[None], chunks_ref.shape)
     react, mass, obs = react_ref[...], mass_ref[...], obs_ref[...]
+    inverse_mass, jacobi = 1.0 / mass, 1.0 / (obs + react * react / mass)
     row = lax.broadcasted_iota(jnp.int32, (8, nodes), 0)
     diag = jnp.zeros((8, nodes), F32)
-    for i, line in enumerate((active, react, 1.0 / mass, obs, 1.0 / (obs + react * react / mass))):
+    for i, line in enumerate((active, react, inverse_mass, obs, jacobi)):
         diag = jnp.where(row == i, line, diag)
     diag_ref[...] = diag
-    for copy in copies[5:]:
-        copy.wait()
-
-
-def lines(diag_ref):
-    return tuple(diag_ref[i : i + 1, :] for i in range(5))
-
-
-def prep_kernel(iface_ref, pattern_hbm, blocks_ref, right_ref, vectors_ref, coupling_ref, east_ref, west_ref, diag_ref,
-                dense_ref, edge_ref, to_west_ref, to_east_ref, pattern_ref, total_ref, sem):
+
+    node = lax.broadcasted_iota(jnp.int32, (slots, nodes), 1).astype(F32)
+    east_hot = jnp.where(node == column_of(east_ref[...].astype(F32)), 1.0, 0.0).astype(BF16)
+    west_hot = jnp.where(node == column_of(west_ref[...].astype(F32)), 1.0, 0.0).astype(BF16)
+    live_a = lax.broadcasted_iota(jnp.int32, (slots, slots), 0) < count_ref[1]
+    live_b = lax.broadcasted_iota(jnp.int32, (slots, slots), 1) < count_ref[1]
+    link = jnp.where(live_a & live_b, coupling_ref[...], jnp.zeros((slots, slots), BF16))
+    edges = jnp.concatenate([dot(link, east_hot, 0, 0).astype(BF16), west_hot], axis=0)
+    edge_ref[...] = edges
+    rows = [
+        (edges.astype(F32) * inverse_mass).astype(BF16),
+        vectors_ref[...] * active.astype(BF16),
+        (jacobi * right).astype(BF16),
+    ]
+    level = dot(jnp.concatenate(rows, axis=0), edges, 1, 1).astype(BF16)
+    kept, width = inverse_ref.shape
+    fixed = width // LANES * kept
+
+    def send(east_ref, west_ref):
+        for ref, cols in ((east_ref, slice(0, slots)), (west_ref, slice(slots, 2 * slots))):
+            for j in range(width // LANES):
+                ref[j * kept : (j + 1) * kept, :] = inverse_ref[:, j * LANES : (j + 1) * LANES]
+            ref[fixed:, :] = level[:, cols]
+
+    by_lon(0, near_ref, across_ref, send)
+    copies[9].wait()
+
+
+def prep_kernel(pattern_hbm, blocks_ref, dense_ref, pattern_ref, total_ref, sem):
     copy = pltpu.make_async_copy(pattern_hbm, pattern_ref, sem)
     copy.start()
-    samples, nodes = right_ref.shape
+    nodes = dense_ref.shape[0]
     count, block, _ = blocks_ref.shape
-    slots = coupling_ref.shape[0]
 
     def clear(i, carry):
         total_ref[pl.ds(pl.multiple_of(i * block, block), block), :] = jnp.zeros((block, nodes), F32)
@@ -134,26 +159,6 @@
 
     lax.fori_loop(0, nodes // block, narrow, 0)
 
-    active, react, inverse_mass, obs, jacobi = lines(diag_ref)
-    node = lax.broadcasted_iota(jnp.int32, (slots, nodes), 1).astype(F32)
-    east_hot = jnp.where(node == column_of(east_ref[...].astype(F32)), 1.0, 0.0).astype(BF16)
-    west_hot = jnp.where(node == column_of(west_ref[...].astype(F32)), 1.0, 0.0).astype(BF16)
-    live_a = lax.broadcasted_iota(jnp.int32, (slots, slots), 0) < iface_ref[0]
-    live_b = lax.broadcasted_iota(jnp.int32, (slots, slots), 1) < iface_ref[0]
-    link = jnp.where(live_a & live_b, coupling_ref[...], jnp.zeros((slots, slots), BF16))
-    spread = dot(link, east_hot, 0, 0).astype(BF16)
-    edge_ref[0:slots, :] = spread
-    edge_ref[slots : 2 * slots, :] = west_hot
-    edges = jnp.concatenate([spread, west_hot], axis=0)
-    both = dot((edges.astype(F32) * inverse_mass).astype(BF16), edges, 1, 1).astype(BF16)
-    masked = vectors_ref[...] * active.astype(BF16)
-    smooth_right = (active * jacobi * right_ref[...].astype(F32)).astype(BF16)
-    level = levels(jnp.concatenate([masked, smooth_right], axis=0), edges).astype(BF16)
-    to_east_ref[0 : 2 * slots, :] = both[:, 0:slots]
-    to_west_ref[0 : 2 * slots, :] = both[:, slots:]
-    to_east_ref[2 * slots :, :] = level[:, 0:slots]
-    to_west_ref[2 * slots :, :] = level[:, slots:]
-
 
 def unfold(count, piece, coarse_ref):
     half = coarse_ref.shape[0] // count // 4
@@ -176,7 +181,6 @@
 
 
 def start_kernel(pieces_ref, others_ref, inverse_ref, right_ref, vectors_ref, dense_ref, edge_ref, diag_ref,
-                 to_west_ref, to_east_ref,
                  z_ref, scaled_ref, near_ref, across_ref, far_ref, beyond_ref, coarse_ref):
     samples, nodes = right_ref.shape
     unfold(pieces_ref.shape[0], lambda side, d: (pieces_ref, others_ref)[side][d], coarse_ref)
@@ -191,13 +195,9 @@
     slots = edges.shape[0] // 2
 
     def send(east_ref, west_ref):
-        for ref, cols, corr_ref in (
-            (east_ref, slice(0, slots), to_east_ref),
-            (west_ref, slice(slots, 2 * slots), to_west_ref),
-        ):
+        for ref, cols in ((east_ref, slice(0, slots)), (west_ref, slice(slots, 2 * slots))):
             ref[0:samples, :] = level1[:, cols]
-            ref[samples : 2 * samples, :] = level2[:, cols]
-            ref[2 * samples :, :] = corr_ref[...]
+            ref[samples:, :] = level2[:, cols]
 
     def send_far(east_ref, west_ref):
         east_ref[...] = level1[:, 0:slots]
@@ -207,23 +207,25 @@
     by_lon(1, far_ref, beyond_ref, send_far)
 
 
-def image_kernel(across_ref, beyond_ref, near_ref, far_ref, own_far_ref, own_beyond_ref,
+def image_kernel(across_ref, beyond_ref, near_ref, far_ref, own_far_ref, own_beyond_ref, across_corr_ref, near_corr_ref,
                  z_ref, scaled_ref, dense_ref, edge_ref, diag_ref, right_ref, vectors_ref,
                  image_ref, chunks_ref):
     samples, nodes = z_ref.shape
     active, react, inverse_mass, obs, jacobi = lines(diag_ref)
     z = z_ref[...]
     edges = edge_ref[...]
-    fixed = 2 * samples + edges.shape[0]
-    from_east, from_west = pick(0, near_ref[0:fixed, :], across_ref[0:fixed, :])
+    from_east, from_west = pick(0, near_ref[...], across_ref[...])
+    fixed = near_corr_ref.shape[0] - edges.shape[0] - vectors_ref.shape[0] - samples
+    corr = slice(fixed, fixed + edges.shape[0])
+    corr_east, corr_west = pick(0, near_corr_ref[corr, :], across_corr_ref[corr, :])
     beyond_east, beyond_west = pick(1, far_ref[...], beyond_ref[...])
     own_east, own_west = pick(1, own_far_ref[...], own_beyond_ref[...])
     arrived = jnp.concatenate([from_east[0:samples], from_west[0:samples]], axis=1)
     inner = scaled_ref[...] + dot(arrived, edges) * inverse_mass
     east_terms = jnp.concatenate([beyond_east, own_east], axis=1)
     west_terms = jnp.concatenate([own_west, beyond_west], axis=1)
-    second_east = from_east[samples : 2 * samples].astype(F32) + dot(east_terms, from_east[2 * samples : fixed])
-    second_west = from_west[samples : 2 * samples].astype(F32) + dot(west_terms, from_west[2 * samples : fixed])
+    second_east = from_east[samples:].astype(F32) + dot(east_terms, corr_east)
+    second_west = from_west[samples:].astype(F32) + dot(west_terms, corr_west)
     arrived2 = jnp.concatenate([second_east, second_west], axis=1).astype(BF16)
     stiff = dot(inner.astype(BF16), dense_ref[...]) + dot(arrived2, edges) + react * inner
     image = active * (stiff + obs * z)
@@ -248,7 +250,7 @@
 
 
 def middle_kernel(pieces_ref, others_ref, second_ref, second_others_ref,
-                  across_ref, near_ref, across_inverse_ref, near_inverse_ref, inverse_ref, right_ref, image_ref, vectors_ref,
+                  across_ref, near_ref, inverse_ref, right_ref, image_ref, vectors_ref,
                   dense_ref, edge_ref, diag_ref, z_ref, sums_ref, chunks_ref, coarse_ref):
     samples, nodes = right_ref.shape
     count, half, _ = pieces_ref.shape
@@ -276,18 +278,20 @@
     z = smooth(residual, coarse_ref, inverse_ref, vectors_ref, active, jacobi)
     z_ref[...] = z
 
-    def arriving(level, inverse, change):
+    kept, width = inverse_ref.shape
+    fixed = width // LANES * kept + edges.shape[0]
+
+    def arriving(static, change):
+        inverse = jnp.concatenate([static[j * kept : (j + 1) * kept] for j in range(width // LANES)], axis=1)
         fix = dot(inverse, coarse_ref[...]).astype(BF16)
-        spread = dot(fix, level[0 : fix.shape[0]], 0, 0)
-        return (level[fix.shape[0] :].astype(F32) - step_column * change.astype(F32) + spread).astype(BF16)
+        spread = dot(fix, static[fixed : fixed + kept], 0, 0)
+        return (static[fixed + kept :].astype(F32) - step_column * change.astype(F32) + spread).astype(BF16)
 
     lon = lax.axis_index("lon")
     ahead, before = lax.rem(lon + 1, count), lax.rem(lon + count - 1, count)
-    fixed = 2 * samples + edges.shape[0]
-    east_level, west_level = pick(0, near_ref[fixed:, :], across_ref[fixed:, :])
-    east_inverse, west_inverse = pick(0, near_inverse_ref[...], across_inverse_ref[...])
-    from_east = arriving(east_level, east_inverse, second_ref[ahead, 2 * half + SUM_ROWS :, :])
-    from_west = arriving(west_level, west_inverse, second_ref[before, 2 * half + SUM_ROWS :, :])
+    east_static, west_static = pick(0, near_ref[...], across_ref[...])
+    from_east = arriving(east_static, second_ref[ahead, 2 * half + SUM_ROWS :, :])
+    from_west = arriving(west_static, second_ref[before, 2 * half + SUM_ROWS :, :])
     arrived = jnp.concatenate([from_east, from_west], axis=1)
     stiff = dot(z.astype(BF16), dense_ref[...]) + react * z + dot(arrived, edges)
     curve = jnp.sum(stiff * stiff * inverse_mass + obs * z * z, axis=1, keepdims=True)
@@ -354,37 +358,37 @@
     field = ((samples, nodes), F32)
     coarse_scratch = pltpu.VMEM((domains * vectors, samples), BF16)
     apply_cost = 2 * samples * nodes * nodes
-    corr = ((2 * slots + vectors + samples, slots), BF16)
-    kept = (right_side, deflation, coupling, stiffness_blocks, east_rows, west_rows, coarse_inverse)
-    inputs = (right_side, deflation, react, mass, obs, coupling, stiffness_blocks, east_rows, west_rows, coarse_inverse)
+    static = ((coarse_inverse.size // LANES + 2 * slots + vectors + samples, slots), BF16)
+    inputs = (right_side, deflation, react, mass, obs, coupling, east_rows, west_rows, stiffness_blocks, coarse_inverse)
     line = pltpu.VMEM((1, nodes), F32)
-    chunks, diag, right, basis, link, stored, east, west, inverse = call(
+    chunks, diag, edge, near_static, across_static, right, basis, stored, inverse = call(
         load_kernel,
-        [((sectors, half, LANES), BF16), ((8, nodes), F32)] + [(a.shape, a.dtype) for a in kept],
+        [((sectors, half, LANES), BF16), ((8, nodes), F32), ((2 * slots, nodes), BF16), static, static]
+        + [(a.shape, a.dtype) for a in (right_side, deflation, stiffness_blocks, coarse_inverse)],
         [SMEM] + [HBM] * len(inputs),
-        [node_count] + [pltpu.with_memory_space_constraint(a, pltpu.HBM) for a in inputs],
+        [jnp.concatenate([node_count, iface_count])] + [pltpu.with_memory_space_constraint(a, pltpu.HBM) for a in inputs],
         2 * samples * vectors * nodes,
-        [line, line, line, pltpu.SemaphoreType.DMA((len(inputs),))],
-    )
-    across_inverse, near_inverse = swap(coarse_inverse, 1, False), swap(coarse_inverse, 1, True)
-    pieces, stored, iface, across_inverse, near_inverse = lax.optimization_barrier(
-        (exchange(chunks, "lon"), stored, iface_count, across_inverse, near_inverse)
+        [line, line, line] + [pltpu.VMEM(a.shape, a.dtype) for a in (coupling, east_rows, west_rows)]
+        + [pltpu.SemaphoreType.DMA((len(inputs),))],
+    )
+    pieces, stored, across_static, near_static = lax.optimization_barrier(
+        (exchange(chunks, "lon"), stored, swap(across_static, 1, False), swap(near_static, 1, True))
     )
     pattern = pltpu.with_memory_space_constraint(block_pattern.T, pltpu.HBM)
-    dense, edge, corr_west, corr_east = call(
+    (dense,) = call(
         prep_kernel,
-        [((nodes, nodes), BF16), ((2 * slots, nodes), BF16), corr, corr],
-        [SMEM, HBM] + [VMEM] * 7,
-        (iface, pattern, stored, right, basis, link, east, west, diag),
+        [((nodes, nodes), BF16)],
+        [HBM, VMEM],
+        (pattern, stored),
         apply_cost,
         [pltpu.SMEM((2, block_pattern.shape[0]), jnp.int32), pltpu.VMEM((nodes, nodes), F32), pltpu.SemaphoreType.DMA],
     )
     others = other_band(pieces)
     z0, scaled, near, across, far, beyond = call(
         start_kernel,
-        [field] * 2 + [((2 * samples + corr[0][0], slots), BF16)] * 2 + [((samples, slots), BF16)] * 2,
-        [VMEM] * 10,
-        (pieces, others, inverse, right, basis, dense, edge, diag, corr_west, corr_east),
+        [field] * 2 + [((2 * samples, slots), BF16)] * 2 + [((samples, slots), BF16)] * 2,
+        [VMEM] * 8,
+        (pieces, others, inverse, right, basis, dense, edge, diag),
         apply_cost,
         [coarse_scratch],
     )
@@ -395,8 +399,8 @@
     image, chunks = call(
         image_kernel,
         [field, ((sectors, 2 * half + SUM_ROWS + samples, LANES), BF16)],
-        [VMEM] * 13,
-        (across, got_beyond, near, got_far, far, beyond, z0, scaled, dense, edge, diag, right, basis),
+        [VMEM] * 15,
+        (across, got_beyond, near, got_far, far, beyond, across_static, near_static, z0, scaled, dense, edge, diag, right, basis),
         apply_cost,
     )
     second = exchange(chunks, "lon")
@@ -404,8 +408,8 @@
     z1, sums, chunks = call(
         middle_kernel,
         [field, ((8, LANES), F32), ((domains, 8, LANES), F32)],
-        [VMEM] * 15,
-        (pieces, others, second, second_others, across, near, across_inverse, near_inverse,
+        [VMEM] * 13,
+        (pieces, others, second, second_others, across_static, near_static,
          inverse, right, image, basis, dense, edge, diag),
         apply_cost,
         [coarse_scratch],

time: 62.6 us -> 61.7 us (0.986)
  transfers between devices with their start and end apart: 8 -> 8, of which waited for: 4 -> 3; matrix products, arithmetic and copies ran while one was open for 0% -> 0% of each run, Pallas kernels for 7% -> 3%
where the time goes in v10:
time: 61.7 us; the launch traced here: 61.4 us
  blocking collectives  33.2 us (54%)
  starting transfers between devices  11.4 us (18%)
  Pallas kernels  10 us (16%)
  waiting for transfers between devices  5.33 us (9%)
  between operations  1.34 us (2%)
    all_to_all x3, blocking collectives, exchange(): return lax.all_to_all(chunks, axes, split_axis=0, concat_axis=0, tiled=True)  33.2 us
    ppermute x6, starting transfers between devices, swap(): return lax.ppermute(array, 'lon', pairs)  11.4 us
    pallas_call x6, Pallas kernels, call(): pl.pallas_call(kernel, out_shape=[jax.ShapeDtypeStruct(s, t) for s, t in...  10 us
    ppermute x6, waiting for transfers between devices, swap(): return lax.ppermute(array, 'lon', pairs)  3.75 us
    ppermute x2, waiting for transfers between devices, other_band(): return lax.ppermute(array, 'lat', [(0, 1), (1, 0)])  1.58 us
  transfers between devices with their start and end apart: 8, of which 3 were waited for; matrix products, arithmetic and copies ran while one was open for 0% of the time, Pallas kernels for 3%

profile of v10, /device:TPU:0, one launch (start us, length us, event | category | flops | bytes accessed | tf_op | source)
XLA Modules:
  0.0 61.4 jit_solution(16303418258032746344)
XLA Ops:
  1.3 0.1 pad_add_fusion.count_ref
  1.4 2.5 %shard_map.127 = (bf16[8,32,128]{2,1,0:T(8,128)(2,1)S(1)}, f32[8,1024]{1,0:T(8,128)S(1)}, bf16[256,1024]{1,0:T(8,128)(2,1)S(1)}, bf16[896,128]{1,0:T(8,128)(2,1)...) custom-call(s32[2]{0:T(128)S(1)} %pad_add_fusion.count_ref, ...), custom_call_target="tpu_custom_call" | custom-call | flops 8388608 | bytes 1225736 | tf_op jit(solution)/shard_map/pallas_call | solution.py:24
  3.9 6.0 %collective-permute-start = (bf16[896,128]{1,0:T(8,128)(2,1)S(1)}, bf16[896,128]{1,0:T(8,128)(2,1)S(1)}, u32[]{:S(2)}, u32[]{:S(2)}) collective-permute-start(bf16[896,128]{1,0:T(8,128)(2,1)S(1)} %get-tuple-element.31), channel_id=1, source_target_pairs={{0,14},{2,4},{4,2},{6,8},{8,6},{10,12},{12,10},{14,0},{1,15},{3,5}... | collective-permute-start | bytes 688136 | tf_op jit(solution)/shard_map/ppermute | solution.py:333
  10.0 0.0 collective-permute-start.1
  10.0 11.2 %all_to_all.15.pieces_ref = bf16[8,32,128]{2,1,0:T(8,128)(2,1)S(1)} all-to-all(bf16[8,32,128]{2,1,0:T(8,128)(2,1)S(1)} %get-tuple-element.29), channel_id=1, replica_groups=mesh['grp'=2,'lon'=8,'lat'=2] {'lon'}, dimensions={0} | all-to-all | bytes 131072 | tf_op jit(solution)/shard_map/all_to_all | solution.py:320
  21.2 0.0 collective-permute-done.across_corr_ref.across_ref
  21.2 0.0 collective-permute-done.1.near_corr_ref.near_ref
  21.2 0.0 collective-permute-start.2
  21.2 2.1 %shard_map.128.dense_ref = bf16[1024,1024]{1,0:T(8,128)(2,1)S(1)} custom-call(s32[2,24]{1,0:T(2,128)} %bitcast.7, bf16[24,128,128]{2,1,0:T(8,128)(2,1)S(1)} %get-tuple-element.37.blocks_ref), custom_call_target="tpu_custom_call" | custom-call | flops 134217728 | bytes 786624 | tf_op jit(solution)/shard_map/pallas_call | solution.py:24
  23.3 0.0 collective-permute-done.2.others_ref
  23.3 1.3 %shard_map.129 = (f32[64,1024]{1,0:T(8,128)S(1)}, f32[64,1024]{1,0:T(8,128)S(1)}, bf16[128,128]{1,0:T(8,128)(2,1)S(1)}, bf16[128,128]{1,0:T(8,128)(2,1)S(1)}, bf...) custom-call(bf16[8,32,128]{2,1,0:T(8,128)(2,1)S(1)} %all_to_all.15.pieces_ref, ...), custom_call_target="tpu_custom_call" | custom-call | flops 134217728 | bytes 3178496 | tf_op jit(solution)/shard_map/pallas_call | solution.py:24
  24.6 1.9 %collective-permute-start.3 = (bf16[128,128]{1,0:T(8,128)(2,1)S(1)}, bf16[128,128]{1,0:T(8,128)(2,1)S(1)}, u32[]{:S(2)}, u32[]{:S(2)}) collective-permute-start(bf16[128,128]{1,0:T(8,128)(2,1)S(1)} %get-tuple-element.40), channel_id=1, source_target_pairs={{0,14},{2,4},{4,2},{6,8},{8,6},{10,12},{12,10},{14,0},{1,15},{3,5}... | collective-permute-start | bytes 98312 | tf_op jit(solution)/shard_map/ppermute | solution.py:333
  26.5 0.0 collective-permute-start.5
  26.5 3.5 %collective-permute-start.4 = (bf16[64,128]{1,0:T(8,128)(2,1)S(1)}, bf16[64,128]{1,0:T(8,128)(2,1)S(1)}, u32[]{:S(2)}, u32[]{:S(2)}) collective-permute-start(bf16[64,128]{1,0:T(8,128)(2,1)S(1)} %get-tuple-element.41.own_beyond_ref), channel_id=1, source_target_pairs={{0,12},{2,14},{4,8},{6,10},{8,4},{10,6},{12,0},{14,2},{1,13},{3,15... | collective-permute-start | bytes 49160 | tf_op jit(solution)/shard_map/ppermute | solution.py:333
  30.0 0.0 collective-permute-start.6
  30.0 2.1 %collective-permute-done.4.beyond_ref = bf16[64,128]{1,0:T(8,128)(2,1)S(1)} collective-permute-done((bf16[64,128]{1,0:T(8,128)(2,1)S(1)}, bf16[64,128]{1,0:T(8,128)(2,1)S(1)}, u32[]{:S(2)}, u32[]{:S(2)}) %collective-permute-start.4) | collective-permute-done | bytes 16416 | tf_op jit(solution)/shard_map/ppermute | solution.py:333
  32.0 1.7 %collective-permute-done.6.far_ref = bf16[64,128]{1,0:T(8,128)(2,1)S(1)} collective-permute-done((bf16[64,128]{1,0:T(8,128)(2,1)S(1)}, bf16[64,128]{1,0:T(8,128)(2,1)S(1)}, u32[]{:S(2)}, u32[]{:S(2)}) %collective-permute-start.6) | collective-permute-done | bytes 16416 | tf_op jit(solution)/shard_map/ppermute | solution.py:333
  33.7 0.0 collective-permute-done.3.across_ref
  33.7 0.0 collective-permute-done.5.near_ref
  33.7 1.1 %shard_map.130 = (f32[64,1024]{1,0:T(8,128)S(1)}, bf16[8,144,128]{2,1,0:T(8,128)(2,1)S(1)}) custom-call(bf16[128,128]{1,0:T(8,128)(2,1)S(1)} %collective-permute-done.3.across_ref, bf16[64,128]{1,0:T(8,128)(2,1)S(1)} %collective-permute-done.4.beyond_ref, bf16[128,128]{1,0:T(8,128)(2,1)S(1)} %collective-permute-done.5.near_ref, ...), custom_call_target="tpu_custom_call" | custom-call | flops 134217728 | bytes 4030464 | tf_op jit(solution)/shard_map/pallas_call | solution.py:24
  34.8 12.4 %all_to_all.16.second_ref = bf16[8,144,128]{2,1,0:T(8,128)(2,1)S(1)} all-to-all(bf16[8,144,128]{2,1,0:T(8,128)(2,1)S(1)} %get-tuple-element.48), channel_id=1, replica_groups=mesh['grp'=2,'lon'=8,'lat'=2] {'lon'}, dimensions={0} | all-to-all | bytes 589824 | tf_op jit(solution)/shard_map/all_to_all | solution.py:320
  47.2 0.0 collective-permute-start.7
  47.2 1.6 %collective-permute-done.7.second_others_ref = bf16[8,144,128]{2,1,0:T(8,128)(2,1)S(1)} collective-permute-done((bf16[8,144,128]{2,1,0:T(8,128)(2,1)S(1)}, bf16[8,144,128]{2,1,0:T(8,128)(2,1)S(1)}, u32[]{:S(2)}, u32[]{:S(2)}) %collective-permute-start.7) | collective-permute-done | bytes 294944 | tf_op jit(solution)/shard_map/ppermute | solution.py:324
  48.8 1.8 %shard_map.131 = (f32[64,1024]{1,0:T(8,128)S(1)}, f32[8,128]{1,0:T(8,128)S(1)}, f32[16,8,128]{2,1,0:T(8,128)S(1)}) custom-call(bf16[8,32,128]{2,1,0:T(8,128)(2,1)S(1)} %all_to_all.15.pieces_ref, bf16[8,32,128]{2,1,0:T(8,128)(2,1)S(1)} %collective-permute-done.2.others_ref, bf16[8,144,128]{2,1,0:T(8,128)(2,1)S(1)} %all_to_all.16.second_ref, ...), custom_call_target="tpu_custom_call" | custom-call | flops 134217728 | bytes 4489216 | tf_op jit(solution)/shard_map/pallas_call | solution.py:24
  50.6 9.7 %all_to_all.17.chunks_ref = f32[16,8,128]{2,1,0:T(8,128)S(1)} all-to-all(f32[16,8,128]{2,1,0:T(8,128)S(1)} %get-tuple-element.51), channel_id=1, replica_groups=mesh['grp'=2,'lon'=8,'lat'=2] {'lon','lat'}, dimensions={0} | all-to-all | bytes 131072 | tf_op jit(solution)/shard_map/all_to_all | solution.py:320
  60.3 1.2 %shard_map.132 = f32[64,1024]{1,0:T(8,128)} custom-call(f32[8,128]{1,0:T(8,128)S(1)} %get-tuple-element.50.sums_ref, f32[16,8,128]{2,1,0:T(8,128)S(1)} %all_to_all.17.chunks_ref, f32[64,1024]{1,0:T(8,128)S(1)} %get-tuple-element.46.z_ref.first_ref, f32[64,1024]{1,0:T(8,128)S(1)} %get-tuple-element.52.second_ref), custom_call_target="tpu_custom_call" | custom-call | flops 262144 | bytes 593920 | tf_op jit(solution)/shard_map/pallas_call | solution.py:24
Async XLA Ops:
  3.9 17.3 %collective-permute-start = (bf16[896,128]{1,0:T(8,128)(2,1)S(1)}, bf16[896,128]{1,0:T(8,128)(2,1)S(1)}, u32[]{:S(2)}, u32[]{:S(2)}) collective-permute-start(bf16[896,128]{1,0:T(8,128)(2,1)S(1)} %get-tuple-element.31), channel_id=1, source_target_pairs={{0,14},{2,4},{4,2},{6,8},{8,6},{10,12},{12,10},{14,0},{1,15},{3,5}... | collective-permute-start | bytes 688136 | tf_op jit(solution)/shard_map/ppermute | solution.py:333
  10.0 11.2 %collective-permute-start.1 = (bf16[896,128]{1,0:T(8,128)(2,1)S(1)}, bf16[896,128]{1,0:T(8,128)(2,1)S(1)}, u32[]{:S(2)}, u32[]{:S(2)}) collective-permute-start(bf16[896,128]{1,0:T(8,128)(2,1)S(1)} %get-tuple-element.32), channel_id=1, source_target_pairs={{0,2},{2,0},{4,6},{6,4},{8,10},{10,8},{12,14},{14,12},{1,3},{3,1},... | collective-permute-start | bytes 688136 | tf_op jit(solution)/shard_map/ppermute | solution.py:333
  21.2 2.1 %collective-permute-start.2 = (bf16[8,32,128]{2,1,0:T(8,128)(2,1)S(1)}, bf16[8,32,128]{2,1,0:T(8,128)(2,1)S(1)}, u32[]{:S(2)}, u32[]{:S(2)}) collective-permute-start(bf16[8,32,128]{2,1,0:T(8,128)(2,1)S(1)} %all_to_all.15.pieces_ref), channel_id=1, source_target_pairs={{0,1},{1,0},{2,3},{3,2},{4,5},{5,4},{6,7},{7,6},{8,9},{9,8},{10,11... | collective-permute-start | bytes 196616 | tf_op jit(solution)/shard_map/ppermute | solution.py:324
  24.6 9.1 %collective-permute-start.3 = (bf16[128,128]{1,0:T(8,128)(2,1)S(1)}, bf16[128,128]{1,0:T(8,128)(2,1)S(1)}, u32[]{:S(2)}, u32[]{:S(2)}) collective-permute-start(bf16[128,128]{1,0:T(8,128)(2,1)S(1)} %get-tuple-element.40), channel_id=1, source_target_pairs={{0,14},{2,4},{4,2},{6,8},{8,6},{10,12},{12,10},{14,0},{1,15},{3,5}... | collective-permute-start | bytes 98312 | tf_op jit(solution)/shard_map/ppermute | solution.py:333
  26.5 7.2 %collective-permute-start.5 = (bf16[128,128]{1,0:T(8,128)(2,1)S(1)}, bf16[128,128]{1,0:T(8,128)(2,1)S(1)}, u32[]{:S(2)}, u32[]{:S(2)}) collective-permute-start(bf16[128,128]{1,0:T(8,128)(2,1)S(1)} %get-tuple-element.42), channel_id=1, source_target_pairs={{0,2},{2,0},{4,6},{6,4},{8,10},{10,8},{12,14},{14,12},{1,3},{3,1},... | collective-permute-start | bytes 98312 | tf_op jit(solution)/shard_map/ppermute | solution.py:333
  26.5 5.5 %collective-permute-start.4 = (bf16[64,128]{1,0:T(8,128)(2,1)S(1)}, bf16[64,128]{1,0:T(8,128)(2,1)S(1)}, u32[]{:S(2)}, u32[]{:S(2)}) collective-permute-start(bf16[64,128]{1,0:T(8,128)(2,1)S(1)} %get-tuple-element.41.own_beyond_ref), channel_id=1, source_target_pairs={{0,12},{2,14},{4,8},{6,10},{8,4},{10,6},{12,0},{14,2},{1,13},{3,15... | collective-permute-start | bytes 49160 | tf_op jit(solution)/shard_map/ppermute | solution.py:333
  30.0 3.7 %collective-permute-start.6 = (bf16[64,128]{1,0:T(8,128)(2,1)S(1)}, bf16[64,128]{1,0:T(8,128)(2,1)S(1)}, u32[]{:S(2)}, u32[]{:S(2)}) collective-permute-start(bf16[64,128]{1,0:T(8,128)(2,1)S(1)} %get-tuple-element.43.own_far_ref), channel_id=1, source_target_pairs={{0,4},{2,6},{4,0},{6,2},{8,12},{10,14},{12,8},{14,10},{1,5},{3,7},... | collective-permute-start | bytes 49160 | tf_op jit(solution)/shard_map/ppermute | solution.py:333
  47.2 1.6 %collective-permute-start.7 = (bf16[8,144,128]{2,1,0:T(8,128)(2,1)S(1)}, bf16[8,144,128]{2,1,0:T(8,128)(2,1)S(1)}, u32[]{:S(2)}, u32[]{:S(2)}) collective-permute-start(bf16[8,144,128]{2,1,0:T(8,128)(2,1)S(1)} %all_to_all.16.second_ref), channel_id=1, source_target_pairs={{0,1},{1,0},{2,3},{3,2},{4,5},{5,4},{6,7},{7,6},{8,9},{9,8},{10,11... | collective-permute-start | bytes 884744 | tf_op jit(solution)/shard_map/ppermute | solution.py:324

commit v11 on v10

--- a/solution.py
+++ b/solution.py
@@ -181,7 +181,7 @@
 
 
 def start_kernel(pieces_ref, others_ref, inverse_ref, right_ref, vectors_ref, dense_ref, edge_ref, diag_ref,
-                 z_ref, scaled_ref, near_ref, across_ref, far_ref, beyond_ref, coarse_ref):
+                 z_ref, scaled_ref, own_ref, near_ref, across_ref, far_ref, beyond_ref, coarse_ref):
     samples, nodes = right_ref.shape
     unfold(pieces_ref.shape[0], lambda side, d: (pieces_ref, others_ref)[side][d], coarse_ref)
     active, react, inverse_mass, obs, jacobi = lines(diag_ref)
@@ -192,6 +192,7 @@
     scaled_ref[...] = scaled
     level1 = levels(z, edges).astype(BF16)
     level2 = levels(scaled, edges).astype(BF16)
+    own_ref[...] = level1
     slots = edges.shape[0] // 2
 
     def send(east_ref, west_ref):
@@ -199,15 +200,11 @@
             ref[0:samples, :] = level1[:, cols]
             ref[samples:, :] = level2[:, cols]
 
-    def send_far(east_ref, west_ref):
-        east_ref[...] = level1[:, 0:slots]
-        west_ref[...] = level1[:, slots:]
-
     by_lon(0, near_ref, across_ref, send)
-    by_lon(1, far_ref, beyond_ref, send_far)
-
-
-def image_kernel(across_ref, beyond_ref, near_ref, far_ref, own_far_ref, own_beyond_ref, across_corr_ref, near_corr_ref,
+    by_lon(1, far_ref, beyond_ref, send)
+
+
+def image_kernel(across_ref, beyond_ref, near_ref, far_ref, own_ref, across_corr_ref, near_corr_ref,
                  z_ref, scaled_ref, dense_ref, edge_ref, diag_ref, right_ref, vectors_ref,
                  image_ref, chunks_ref):
     samples, nodes = z_ref.shape
@@ -218,8 +215,9 @@
     fixed = near_corr_ref.shape[0] - edges.shape[0] - vectors_ref.shape[0] - samples
     corr = slice(fixed, fixed + edges.shape[0])
     corr_east, corr_west = pick(0, near_corr_ref[corr, :], across_corr_ref[corr, :])
-    beyond_east, beyond_west = pick(1, far_ref[...], beyond_ref[...])
-    own_east, own_west = pick(1, own_far_ref[...], own_beyond_ref[...])
+    beyond_east, beyond_west = pick(1, far_ref[0:samples, :], beyond_ref[0:samples, :])
+    slots = edges.shape[0] // 2
+    own_east, own_west = own_ref[:, 0:slots], own_ref[:, slots:]
     arrived = jnp.concatenate([from_east[0:samples], from_west[0:samples]], axis=1)
     inner = scaled_ref[...] + dot(arrived, edges) * inverse_mass
     east_terms = jnp.concatenate([beyond_east, own_east], axis=1)
@@ -288,10 +286,12 @@
         return (static[fixed + kept :].astype(F32) - step_column * change.astype(F32) + spread).astype(BF16)
 
     lon = lax.axis_index("lon")
+    odd = lon & 1
     ahead, before = lax.rem(lon + 1, count), lax.rem(lon + count - 1, count)
-    east_static, west_static = pick(0, near_ref[...], across_ref[...])
-    from_east = arriving(east_static, second_ref[ahead, 2 * half + SUM_ROWS :, :])
-    from_west = arriving(west_static, second_ref[before, 2 * half + SUM_ROWS :, :])
+    change = slice(2 * half + SUM_ROWS, second_ref.shape[1])
+    from_near = arriving(near_ref[...], second_ref[ahead + odd * (before - ahead), change, :])
+    from_across = arriving(across_ref[...], second_ref[before + odd * (ahead - before), change, :])
+    from_east, from_west = pick(0, from_near, from_across)
     arrived = jnp.concatenate([from_east, from_west], axis=1)
     stiff = dot(z.astype(BF16), dense_ref[...]) + react * z + dot(arrived, edges)
     curve = jnp.sum(stiff * stiff * inverse_mass + obs * z * z, axis=1, keepdims=True)
@@ -384,9 +384,9 @@
         [pltpu.SMEM((2, block_pattern.shape[0]), jnp.int32), pltpu.VMEM((nodes, nodes), F32), pltpu.SemaphoreType.DMA],
     )
     others = other_band(pieces)
-    z0, scaled, near, across, far, beyond = call(
+    z0, scaled, own, near, across, far, beyond = call(
         start_kernel,
-        [field] * 2 + [((2 * samples, slots), BF16)] * 2 + [((samples, slots), BF16)] * 2,
+        [field] * 2 + [((samples, 2 * slots), BF16)] + [((2 * samples, slots), BF16)] * 4,
         [VMEM] * 8,
         (pieces, others, inverse, right, basis, dense, edge, diag),
         apply_cost,
@@ -399,8 +399,8 @@
     image, chunks = call(
         image_kernel,
         [field, ((sectors, 2 * half + SUM_ROWS + samples, LANES), BF16)],
-        [VMEM] * 15,
-        (across, got_beyond, near, got_far, far, beyond, across_static, near_static, z0, scaled, dense, edge, diag, right, basis),
+        [VMEM] * 14,
+        (across, got_beyond, near, got_far, own, across_static, near_static, z0, scaled, dense, edge, diag, right, basis),
         apply_cost,
     )
     second = exchange(chunks, "lon")

time: 61.7 us -> 62 us (level)
  transfers between devices with their start and end apart: 8 -> 8, of which waited for: 3 -> 4; matrix products, arithmetic and copies ran while one was open for 0% -> 0% of each run, Pallas kernels for 3% -> 3%
where the time goes in v11:
time: 62 us; the launch traced here: 61.8 us
  blocking collectives  33.4 us (54%)
  starting transfers between devices  11.4 us (18%)
  Pallas kernels  10 us (16%)
  waiting for transfers between devices  5.5 us (9%)
  between operations  1.34 us (2%)
    all_to_all x3, blocking collectives, exchange(): return lax.all_to_all(chunks, axes, split_axis=0, concat_axis=0, tiled=True)  33.4 us
    ppermute x6, starting transfers between devices, swap(): return lax.ppermute(array, 'lon', pairs)  11.4 us
    pallas_call x6, Pallas kernels, call(): pl.pallas_call(kernel, out_shape=[jax.ShapeDtypeStruct(s, t) for s, t in...  10 us
    ppermute x6, waiting for transfers between devices, swap(): return lax.ppermute(array, 'lon', pairs)  3.92 us
    ppermute x2, waiting for transfers between devices, other_band(): return lax.ppermute(array, 'lat', [(0, 1), (1, 0)])  1.58 us
  transfers between devices with their start and end apart: 8, of which 4 were waited for; matrix products, arithmetic and copies ran while one was open for 0% of the time, Pallas kernels for 3%

profile of v11, /device:TPU:0, one launch (start us, length us, event | category | flops | bytes accessed | tf_op | source)
XLA Modules:
  0.0 61.8 jit_solution(6173928440236462617)
XLA Ops:
  1.3 0.1 pad_add_fusion.count_ref
  1.4 2.5 %shard_map.127 = (bf16[8,32,128]{2,1,0:T(8,128)(2,1)S(1)}, f32[8,1024]{1,0:T(8,128)S(1)}, bf16[256,1024]{1,0:T(8,128)(2,1)S(1)}, bf16[896,128]{1,0:T(8,128)(2,1)...) custom-call(s32[2]{0:T(128)S(1)} %pad_add_fusion.count_ref, ...), custom_call_target="tpu_custom_call" | custom-call | flops 8388608 | bytes 1225736 | tf_op jit(solution)/shard_map/pallas_call | solution.py:24
  3.9 6.0 %collective-permute-start = (bf16[896,128]{1,0:T(8,128)(2,1)S(1)}, bf16[896,128]{1,0:T(8,128)(2,1)S(1)}, u32[]{:S(2)}, u32[]{:S(2)}) collective-permute-start(bf16[896,128]{1,0:T(8,128)(2,1)S(1)} %get-tuple-element.32), channel_id=1, source_target_pairs={{0,14},{2,4},{4,2},{6,8},{8,6},{10,12},{12,10},{14,0},{1,15},{3,5}... | collective-permute-start | bytes 688136 | tf_op jit(solution)/shard_map/ppermute | solution.py:333
  10.0 0.0 collective-permute-start.1
  10.0 11.2 %all_to_all.15.pieces_ref = bf16[8,32,128]{2,1,0:T(8,128)(2,1)S(1)} all-to-all(bf16[8,32,128]{2,1,0:T(8,128)(2,1)S(1)} %get-tuple-element.30), channel_id=1, replica_groups=mesh['grp'=2,'lon'=8,'lat'=2] {'lon'}, dimensions={0} | all-to-all | bytes 131072 | tf_op jit(solution)/shard_map/all_to_all | solution.py:320
  21.2 0.0 collective-permute-done.across_corr_ref.across_ref
  21.2 0.0 collective-permute-done.1.near_corr_ref.near_ref
  21.2 0.0 collective-permute-start.2
  21.2 2.1 %shard_map.128.dense_ref = bf16[1024,1024]{1,0:T(8,128)(2,1)S(1)} custom-call(s32[2,24]{1,0:T(2,128)} %bitcast.7, bf16[24,128,128]{2,1,0:T(8,128)(2,1)S(1)} %get-tuple-element.38.blocks_ref), custom_call_target="tpu_custom_call" | custom-call | flops 134217728 | bytes 786624 | tf_op jit(solution)/shard_map/pallas_call | solution.py:24
  23.3 0.0 collective-permute-done.2.others_ref
  23.3 1.3 %shard_map.129 = (f32[64,1024]{1,0:T(8,128)S(1)}, f32[64,1024]{1,0:T(8,128)S(1)}, bf16[64,256]{1,0:T(8,128)(2,1)S(1)}, bf16[128,128]{1,0:T(8,128)(2,1)S(1)}, bf1...) custom-call(bf16[8,32,128]{2,1,0:T(8,128)(2,1)S(1)} %all_to_all.15.pieces_ref, ...), custom_call_target="tpu_custom_call" | custom-call | flops 134217728 | bytes 3178496 | tf_op jit(solution)/shard_map/pallas_call | solution.py:24
  24.6 1.9 %collective-permute-start.3 = (bf16[128,128]{1,0:T(8,128)(2,1)S(1)}, bf16[128,128]{1,0:T(8,128)(2,1)S(1)}, u32[]{:S(2)}, u32[]{:S(2)}) collective-permute-start(bf16[128,128]{1,0:T(8,128)(2,1)S(1)} %get-tuple-element.41), channel_id=1, source_target_pairs={{0,14},{2,4},{4,2},{6,8},{8,6},{10,12},{12,10},{14,0},{1,15},{3,5}... | collective-permute-start | bytes 98312 | tf_op jit(solution)/shard_map/ppermute | solution.py:333
  26.5 1.3 %collective-permute-start.4 = (bf16[128,128]{1,0:T(8,128)(2,1)S(1)}, bf16[128,128]{1,0:T(8,128)(2,1)S(1)}, u32[]{:S(2)}, u32[]{:S(2)}) collective-permute-start(bf16[128,128]{1,0:T(8,128)(2,1)S(1)} %get-tuple-element.42), channel_id=1, source_target_pairs={{0,12},{2,14},{4,8},{6,10},{8,4},{10,6},{12,0},{14,2},{1,13},{3,15... | collective-permute-start | bytes 98312 | tf_op jit(solution)/shard_map/ppermute | solution.py:333
  27.8 2.2 %collective-permute-start.5 = (bf16[128,128]{1,0:T(8,128)(2,1)S(1)}, bf16[128,128]{1,0:T(8,128)(2,1)S(1)}, u32[]{:S(2)}, u32[]{:S(2)}) collective-permute-start(bf16[128,128]{1,0:T(8,128)(2,1)S(1)} %get-tuple-element.43), channel_id=1, source_target_pairs={{0,2},{2,0},{4,6},{6,4},{8,10},{10,8},{12,14},{14,12},{1,3},{3,1},... | collective-permute-start | bytes 98312 | tf_op jit(solution)/shard_map/ppermute | solution.py:333
  30.0 0.0 collective-permute-start.6
  30.0 1.6 %collective-permute-done.3.across_ref = bf16[128,128]{1,0:T(8,128)(2,1)S(1)} collective-permute-done((bf16[128,128]{1,0:T(8,128)(2,1)S(1)}, bf16[128,128]{1,0:T(8,128)(2,1)S(1)}, u32[]{:S(2)}, u32[]{:S(2)}) %collective-permute-start.3) | collective-permute-done | bytes 32800 | tf_op jit(solution)/shard_map/ppermute | solution.py:333
  31.5 0.7 %collective-permute-done.4.beyond_ref = bf16[128,128]{1,0:T(8,128)(2,1)S(1)} collective-permute-done((bf16[128,128]{1,0:T(8,128)(2,1)S(1)}, bf16[128,128]{1,0:T(8,128)(2,1)S(1)}, u32[]{:S(2)}, u32[]{:S(2)}) %collective-permute-start.4) | collective-permute-done | bytes 32800 | tf_op jit(solution)/shard_map/ppermute | solution.py:333
  32.2 0.0 collective-permute-done.5.near_ref
  32.2 1.7 %collective-permute-done.6.far_ref = bf16[128,128]{1,0:T(8,128)(2,1)S(1)} collective-permute-done((bf16[128,128]{1,0:T(8,128)(2,1)S(1)}, bf16[128,128]{1,0:T(8,128)(2,1)S(1)}, u32[]{:S(2)}, u32[]{:S(2)}) %collective-permute-start.6) | collective-permute-done | bytes 32800 | tf_op jit(solution)/shard_map/ppermute | solution.py:333
  33.9 1.1 %shard_map.130 = (f32[64,1024]{1,0:T(8,128)S(1)}, bf16[8,144,128]{2,1,0:T(8,128)(2,1)S(1)}) custom-call(bf16[128,128]{1,0:T(8,128)(2,1)S(1)} %collective-permute-done.3.across_ref, bf16[128,128]{1,0:T(8,128)(2,1)S(1)} %collective-permute-done.4.beyond_ref, bf16[128,128]{1,0:T(8,128)(2,1)S(1)} %collective-permute-done.5.near_ref, ...), custom_call_target="tpu_custom_call" | custom-call | flops 134217728 | bytes 4063232 | tf_op jit(solution)/shard_map/pallas_call | solution.py:24
  35.0 12.5 %all_to_all.16.second_ref = bf16[8,144,128]{2,1,0:T(8,128)(2,1)S(1)} all-to-all(bf16[8,144,128]{2,1,0:T(8,128)(2,1)S(1)} %get-tuple-element.50), channel_id=1, replica_groups=mesh['grp'=2,'lon'=8,'lat'=2] {'lon'}, dimensions={0} | all-to-all | bytes 589824 | tf_op jit(solution)/shard_map/all_to_all | solution.py:320
  47.5 0.0 collective-permute-start.7
  47.5 1.6 %collective-permute-done.7.second_others_ref = bf16[8,144,128]{2,1,0:T(8,128)(2,1)S(1)} collective-permute-done((bf16[8,144,128]{2,1,0:T(8,128)(2,1)S(1)}, bf16[8,144,128]{2,1,0:T(8,128)(2,1)S(1)}, u32[]{:S(2)}, u32[]{:S(2)}) %collective-permute-start.7) | collective-permute-done | bytes 294944 | tf_op jit(solution)/shard_map/ppermute | solution.py:324
  49.1 1.8 %shard_map.131 = (f32[64,1024]{1,0:T(8,128)S(1)}, f32[8,128]{1,0:T(8,128)S(1)}, f32[16,8,128]{2,1,0:T(8,128)S(1)}) custom-call(bf16[8,32,128]{2,1,0:T(8,128)(2,1)S(1)} %all_to_all.15.pieces_ref, bf16[8,32,128]{2,1,0:T(8,128)(2,1)S(1)} %collective-permute-done.2.others_ref, bf16[8,144,128]{2,1,0:T(8,128)(2,1)S(1)} %all_to_all.16.second_ref, ...), custom_call_target="tpu_custom_call" | custom-call | flops 134217728 | bytes 4489216 | tf_op jit(solution)/shard_map/pallas_call | solution.py:24
  50.9 9.7 %all_to_all.17.chunks_ref = f32[16,8,128]{2,1,0:T(8,128)S(1)} all-to-all(f32[16,8,128]{2,1,0:T(8,128)S(1)} %get-tuple-element.53), channel_id=1, replica_groups=mesh['grp'=2,'lon'=8,'lat'=2] {'lon','lat'}, dimensions={0} | all-to-all | bytes 131072 | tf_op jit(solution)/shard_map/all_to_all | solution.py:320
  60.6 1.2 %shard_map.132 = f32[64,1024]{1,0:T(8,128)} custom-call(f32[8,128]{1,0:T(8,128)S(1)} %get-tuple-element.52.sums_ref, f32[16,8,128]{2,1,0:T(8,128)S(1)} %all_to_all.17.chunks_ref, f32[64,1024]{1,0:T(8,128)S(1)} %get-tuple-element.48.z_ref.first_ref, f32[64,1024]{1,0:T(8,128)S(1)} %get-tuple-element.54.second_ref), custom_call_target="tpu_custom_call" | custom-call | flops 262144 | bytes 593920 | tf_op jit(solution)/shard_map/pallas_call | solution.py:24
Async XLA Ops:
  3.9 17.3 %collective-permute-start = (bf16[896,128]{1,0:T(8,128)(2,1)S(1)}, bf16[896,128]{1,0:T(8,128)(2,1)S(1)}, u32[]{:S(2)}, u32[]{:S(2)}) collective-permute-start(bf16[896,128]{1,0:T(8,128)(2,1)S(1)} %get-tuple-element.32), channel_id=1, source_target_pairs={{0,14},{2,4},{4,2},{6,8},{8,6},{10,12},{12,10},{14,0},{1,15},{3,5}... | collective-permute-start | bytes 688136 | tf_op jit(solution)/shard_map/ppermute | solution.py:333
  10.0 11.2 %collective-permute-start.1 = (bf16[896,128]{1,0:T(8,128)(2,1)S(1)}, bf16[896,128]{1,0:T(8,128)(2,1)S(1)}, u32[]{:S(2)}, u32[]{:S(2)}) collective-permute-start(bf16[896,128]{1,0:T(8,128)(2,1)S(1)} %get-tuple-element.33), channel_id=1, source_target_pairs={{0,2},{2,0},{4,6},{6,4},{8,10},{10,8},{12,14},{14,12},{1,3},{3,1},... | collective-permute-start | bytes 688136 | tf_op jit(solution)/shard_map/ppermute | solution.py:333
  21.2 2.1 %collective-permute-start.2 = (bf16[8,32,128]{2,1,0:T(8,128)(2,1)S(1)}, bf16[8,32,128]{2,1,0:T(8,128)(2,1)S(1)}, u32[]{:S(2)}, u32[]{:S(2)}) collective-permute-start(bf16[8,32,128]{2,1,0:T(8,128)(2,1)S(1)} %all_to_all.15.pieces_ref), channel_id=1, source_target_pairs={{0,1},{1,0},{2,3},{3,2},{4,5},{5,4},{6,7},{7,6},{8,9},{9,8},{10,11... | collective-permute-start | bytes 196616 | tf_op jit(solution)/shard_map/ppermute | solution.py:324
  24.6 6.9 %collective-permute-start.3 = (bf16[128,128]{1,0:T(8,128)(2,1)S(1)}, bf16[128,128]{1,0:T(8,128)(2,1)S(1)}, u32[]{:S(2)}, u32[]{:S(2)}) collective-permute-start(bf16[128,128]{1,0:T(8,128)(2,1)S(1)} %get-tuple-element.41), channel_id=1, source_target_pairs={{0,14},{2,4},{4,2},{6,8},{8,6},{10,12},{12,10},{14,0},{1,15},{3,5}... | collective-permute-start | bytes 98312 | tf_op jit(solution)/shard_map/ppermute | solution.py:333
  26.5 5.7 %collective-permute-start.4 = (bf16[128,128]{1,0:T(8,128)(2,1)S(1)}, bf16[128,128]{1,0:T(8,128)(2,1)S(1)}, u32[]{:S(2)}, u32[]{:S(2)}) collective-permute-start(bf16[128,128]{1,0:T(8,128)(2,1)S(1)} %get-tuple-element.42), channel_id=1, source_target_pairs={{0,12},{2,14},{4,8},{6,10},{8,4},{10,6},{12,0},{14,2},{1,13},{3,15... | collective-permute-start | bytes 98312 | tf_op jit(solution)/shard_map/ppermute | solution.py:333
  27.8 4.4 %collective-permute-start.5 = (bf16[128,128]{1,0:T(8,128)(2,1)S(1)}, bf16[128,128]{1,0:T(8,128)(2,1)S(1)}, u32[]{:S(2)}, u32[]{:S(2)}) collective-permute-start(bf16[128,128]{1,0:T(8,128)(2,1)S(1)} %get-tuple-element.43), channel_id=1, source_target_pairs={{0,2},{2,0},{4,6},{6,4},{8,10},{10,8},{12,14},{14,12},{1,3},{3,1},... | collective-permute-start | bytes 98312 | tf_op jit(solution)/shard_map/ppermute | solution.py:333
  30.0 3.9 %collective-permute-start.6 = (bf16[128,128]{1,0:T(8,128)(2,1)S(1)}, bf16[128,128]{1,0:T(8,128)(2,1)S(1)}, u32[]{:S(2)}, u32[]{:S(2)}) collective-permute-start(bf16[128,128]{1,0:T(8,128)(2,1)S(1)} %get-tuple-element.44), channel_id=1, source_target_pairs={{0,4},{2,6},{4,0},{6,2},{8,12},{10,14},{12,8},{14,10},{1,5},{3,7},... | collective-permute-start | bytes 98312 | tf_op jit(solution)/shard_map/ppermute | solution.py:333
  47.5 1.6 %collective-permute-start.7 = (bf16[8,144,128]{2,1,0:T(8,128)(2,1)S(1)}, bf16[8,144,128]{2,1,0:T(8,128)(2,1)S(1)}, u32[]{:S(2)}, u32[]{:S(2)}) collective-permute-start(bf16[8,144,128]{2,1,0:T(8,128)(2,1)S(1)} %all_to_all.16.second_ref), channel_id=1, source_target_pairs={{0,1},{1,0},{2,3},{3,2},{4,5},{5,4},{6,7},{7,6},{8,9},{9,8},{10,11... | collective-permute-start | bytes 884744 | tf_op jit(solution)/shard_map/ppermute | solution.py:324

commit v12 on v10

--- a/solution.py
+++ b/solution.py
@@ -71,26 +71,23 @@
     return tuple(diag_ref[i : i + 1, :] for i in range(5))
 
 
-def load_kernel(count_ref, right_hbm, vectors_hbm, react_hbm, mass_hbm, obs_hbm, coupling_hbm, east_hbm, west_hbm,
-                blocks_hbm, inverse_hbm,
-                chunks_ref, diag_ref, edge_ref, near_ref, across_ref, right_ref, vectors_ref, blocks_ref, inverse_ref,
-                react_ref, mass_ref, obs_ref, coupling_ref, east_ref, west_ref, sems):
+def load_kernel(node_count_ref, iface_count_ref, coupling_hbm, east_hbm, west_hbm, react_hbm, mass_hbm, obs_hbm,
+                right_hbm, vectors_hbm, inverse_hbm, blocks_hbm,
+                chunks_ref, diag_ref, edge_ref, near_ref, across_ref, right_ref, vectors_ref, blocks_ref,
+                inverse_ref, react_ref, mass_ref, obs_ref, coupling_ref, east_ref, west_ref, sems):
     pairs = (
-        (right_hbm, right_ref), (vectors_hbm, vectors_ref), (react_hbm, react_ref), (mass_hbm, mass_ref),
-        (obs_hbm, obs_ref), (coupling_hbm, coupling_ref), (east_hbm, east_ref), (west_hbm, west_ref),
+        (coupling_hbm, coupling_ref), (east_hbm, east_ref), (west_hbm, west_ref), (react_hbm, react_ref),
+        (mass_hbm, mass_ref), (obs_hbm, obs_ref), (right_hbm, right_ref), (vectors_hbm, vectors_ref),
         (inverse_hbm, inverse_ref), (blocks_hbm, blocks_ref),
     )
     copies = [pltpu.make_async_copy(src, dst, sems.at[i]) for i, (src, dst) in enumerate(pairs)]
     for copy in copies:
         copy.start()
-    for copy in copies[:9]:
-        copy.wait()
     nodes = right_ref.shape[1]
     slots = coupling_ref.shape[0]
-    active = (lax.broadcasted_iota(jnp.int32, (1, nodes), 1) < count_ref[0]).astype(F32)
-    right = active * right_ref[...].astype(F32)
-    coarse = fold(dot(vectors_ref[...], right.astype(BF16), 1, 1)).astype(BF16)
-    chunks_ref[...] = jnp.broadcast_to(coarse[None], chunks_ref.shape)
+    for copy in copies[:6]:
+        copy.wait()
+    active = (lax.broadcasted_iota(jnp.int32, (1, nodes), 1) < node_count_ref[0]).astype(F32)
     react, mass, obs = react_ref[...], mass_ref[...], obs_ref[...]
     inverse_mass, jacobi = 1.0 / mass, 1.0 / (obs + react * react / mass)
     row = lax.broadcasted_iota(jnp.int32, (8, nodes), 0)
@@ -102,11 +99,16 @@
     node = lax.broadcasted_iota(jnp.int32, (slots, nodes), 1).astype(F32)
     east_hot = jnp.where(node == column_of(east_ref[...].astype(F32)), 1.0, 0.0).astype(BF16)
     west_hot = jnp.where(node == column_of(west_ref[...].astype(F32)), 1.0, 0.0).astype(BF16)
-    live_a = lax.broadcasted_iota(jnp.int32, (slots, slots), 0) < count_ref[1]
-    live_b = lax.broadcasted_iota(jnp.int32, (slots, slots), 1) < count_ref[1]
+    live_a = lax.broadcasted_iota(jnp.int32, (slots, slots), 0) < iface_count_ref[0]
+    live_b = lax.broadcasted_iota(jnp.int32, (slots, slots), 1) < iface_count_ref[0]
     link = jnp.where(live_a & live_b, coupling_ref[...], jnp.zeros((slots, slots), BF16))
     edges = jnp.concatenate([dot(link, east_hot, 0, 0).astype(BF16), west_hot], axis=0)
     edge_ref[...] = edges
+    for copy in copies[6:9]:
+        copy.wait()
+    right = active * right_ref[...].astype(F32)
+    coarse = fold(dot(vectors_ref[...], right.astype(BF16), 1, 1)).astype(BF16)
+    chunks_ref[...] = jnp.broadcast_to(coarse[None], chunks_ref.shape)
     rows = [
         (edges.astype(F32) * inverse_mass).astype(BF16),
         vectors_ref[...] * active.astype(BF16),
@@ -288,10 +290,12 @@
         return (static[fixed + kept :].astype(F32) - step_column * change.astype(F32) + spread).astype(BF16)
 
     lon = lax.axis_index("lon")
+    odd = lon & 1
     ahead, before = lax.rem(lon + 1, count), lax.rem(lon + count - 1, count)
-    east_static, west_static = pick(0, near_ref[...], across_ref[...])
-    from_east = arriving(east_static, second_ref[ahead, 2 * half + SUM_ROWS :, :])
-    from_west = arriving(west_static, second_ref[before, 2 * half + SUM_ROWS :, :])
+    change = slice(2 * half + SUM_ROWS, second_ref.shape[1])
+    from_near = arriving(near_ref[...], second_ref[ahead + odd * (before - ahead), change, :])
+    from_across = arriving(across_ref[...], second_ref[before + odd * (ahead - before), change, :])
+    from_east, from_west = pick(0, from_near, from_across)
     arrived = jnp.concatenate([from_east, from_west], axis=1)
     stiff = dot(z.astype(BF16), dense_ref[...]) + react * z + dot(arrived, edges)
     curve = jnp.sum(stiff * stiff * inverse_mass + obs * z * z, axis=1, keepdims=True)
@@ -359,14 +363,14 @@
     coarse_scratch = pltpu.VMEM((domains * vectors, samples), BF16)
     apply_cost = 2 * samples * nodes * nodes
     static = ((coarse_inverse.size // LANES + 2 * slots + vectors + samples, slots), BF16)
-    inputs = (right_side, deflation, react, mass, obs, coupling, east_rows, west_rows, stiffness_blocks, coarse_inverse)
+    inputs = (coupling, east_rows, west_rows, react, mass, obs, right_side, deflation, coarse_inverse, stiffness_blocks)
     line = pltpu.VMEM((1, nodes), F32)
     chunks, diag, edge, near_static, across_static, right, basis, stored, inverse = call(
         load_kernel,
         [((sectors, half, LANES), BF16), ((8, nodes), F32), ((2 * slots, nodes), BF16), static, static]
         + [(a.shape, a.dtype) for a in (right_side, deflation, stiffness_blocks, coarse_inverse)],
-        [SMEM] + [HBM] * len(inputs),
-        [jnp.concatenate([node_count, iface_count])] + [pltpu.with_memory_space_constraint(a, pltpu.HBM) for a in inputs],
+        [SMEM, SMEM] + [HBM] * len(inputs),
+        [node_count, iface_count] + [pltpu.with_memory_space_constraint(a, pltpu.HBM) for a in inputs],
         2 * samples * vectors * nodes,
         [line, line, line] + [pltpu.VMEM(a.shape, a.dtype) for a in (coupling, east_rows, west_rows)]
         + [pltpu.SemaphoreType.DMA((len(inputs),))],

time: 61.7 us -> 60.8 us (0.985)
  Pallas kernels: 10 us -> 9.19 us
    pallas_call x6, Pallas kernels: 10 us -> 9.19 us  [call(): pl.pallas_call(kernel, out_shape=[jax.ShapeDtypeStruct(s, t) for s, t in...]
where the time goes in v12:
time: 60.8 us; the launch traced here: 60.5 us
  blocking collectives  33.3 us (55%)
  starting transfers between devices  11.4 us (19%)
  Pallas kernels  9.19 us (15%)
  waiting for transfers between devices  5.33 us (9%)
  between operations  1.34 us (2%)
    all_to_all x3, blocking collectives, exchange(): return lax.all_to_all(chunks, axes, split_axis=0, concat_axis=0, tiled=True)  33.3 us
    ppermute x6, starting transfers between devices, swap(): return lax.ppermute(array, 'lon', pairs)  11.4 us
    pallas_call x6, Pallas kernels, call(): pl.pallas_call(kernel, out_shape=[jax.ShapeDtypeStruct(s, t) for s, t in...  9.19 us
    ppermute x6, waiting for transfers between devices, swap(): return lax.ppermute(array, 'lon', pairs)  3.75 us
    ppermute x2, waiting for transfers between devices, other_band(): return lax.ppermute(array, 'lat', [(0, 1), (1, 0)])  1.58 us
  transfers between devices with their start and end apart: 8, of which 3 were waited for; matrix products, arithmetic and copies ran while one was open for 0% of the time, Pallas kernels for 3%

profile of v12, /device:TPU:0, one launch (start us, length us, event | category | flops | bytes accessed | tf_op | source)
XLA Modules:
  0.0 60.5 jit_solution(14244718233258011158)
XLA Ops:
  1.3 1.7 %shard_map.127 = (bf16[8,32,128]{2,1,0:T(8,128)(2,1)S(1)}, f32[8,1024]{1,0:T(8,128)S(1)}, bf16[256,1024]{1,0:T(8,128)(2,1)S(1)}, bf16[896,128]{1,0:T(8,128)(2,1)...) custom-call(s32[1]{0:T(128)S(6)} %copy.15.node_count_ref, ...), custom_call_target="tpu_custom_call" | custom-call | flops 8388608 | bytes 1225736 | tf_op jit(solution)/shard_map/pallas_call | solution.py:24
  3.0 6.0 %collective-permute-start = (bf16[896,128]{1,0:T(8,128)(2,1)S(1)}, bf16[896,128]{1,0:T(8,128)(2,1)S(1)}, u32[]{:S(2)}, u32[]{:S(2)}) collective-permute-start(bf16[896,128]{1,0:T(8,128)(2,1)S(1)} %get-tuple-element.31), channel_id=1, source_target_pairs={{0,14},{2,4},{4,2},{6,8},{8,6},{10,12},{12,10},{14,0},{1,15},{3,5}... | collective-permute-start | bytes 688136 | tf_op jit(solution)/shard_map/ppermute | solution.py:337
  9.1 0.0 collective-permute-start.1
  9.1 11.2 %all_to_all.15.pieces_ref = bf16[8,32,128]{2,1,0:T(8,128)(2,1)S(1)} all-to-all(bf16[8,32,128]{2,1,0:T(8,128)(2,1)S(1)} %get-tuple-element.29), channel_id=1, replica_groups=mesh['grp'=2,'lon'=8,'lat'=2] {'lon'}, dimensions={0} | all-to-all | bytes 131072 | tf_op jit(solution)/shard_map/all_to_all | solution.py:324
  20.3 0.0 collective-permute-done.across_corr_ref.across_ref
  20.3 0.0 collective-permute-done.1.near_corr_ref.near_ref
  20.3 0.0 collective-permute-start.2
  20.3 2.1 %shard_map.128.dense_ref = bf16[1024,1024]{1,0:T(8,128)(2,1)S(1)} custom-call(s32[2,24]{1,0:T(2,128)} %bitcast.7, bf16[24,128,128]{2,1,0:T(8,128)(2,1)S(1)} %get-tuple-element.37.blocks_ref), custom_call_target="tpu_custom_call" | custom-call | flops 134217728 | bytes 786624 | tf_op jit(solution)/shard_map/pallas_call | solution.py:24
  22.4 0.0 collective-permute-done.2.others_ref
  22.4 1.3 %shard_map.129 = (f32[64,1024]{1,0:T(8,128)S(1)}, f32[64,1024]{1,0:T(8,128)S(1)}, bf16[128,128]{1,0:T(8,128)(2,1)S(1)}, bf16[128,128]{1,0:T(8,128)(2,1)S(1)}, bf...) custom-call(bf16[8,32,128]{2,1,0:T(8,128)(2,1)S(1)} %all_to_all.15.pieces_ref, ...), custom_call_target="tpu_custom_call" | custom-call | flops 134217728 | bytes 3178496 | tf_op jit(solution)/shard_map/pallas_call | solution.py:24
  23.7 1.9 %collective-permute-start.3 = (bf16[128,128]{1,0:T(8,128)(2,1)S(1)}, bf16[128,128]{1,0:T(8,128)(2,1)S(1)}, u32[]{:S(2)}, u32[]{:S(2)}) collective-permute-start(bf16[128,128]{1,0:T(8,128)(2,1)S(1)} %get-tuple-element.40), channel_id=1, source_target_pairs={{0,14},{2,4},{4,2},{6,8},{8,6},{10,12},{12,10},{14,0},{1,15},{3,5}... | collective-permute-start | bytes 98312 | tf_op jit(solution)/shard_map/ppermute | solution.py:337
  25.6 0.0 collective-permute-start.5
  25.6 3.5 %collective-permute-start.4 = (bf16[64,128]{1,0:T(8,128)(2,1)S(1)}, bf16[64,128]{1,0:T(8,128)(2,1)S(1)}, u32[]{:S(2)}, u32[]{:S(2)}) collective-permute-start(bf16[64,128]{1,0:T(8,128)(2,1)S(1)} %get-tuple-element.41.own_beyond_ref), channel_id=1, source_target_pairs={{0,12},{2,14},{4,8},{6,10},{8,4},{10,6},{12,0},{14,2},{1,13},{3,15... | collective-permute-start | bytes 49160 | tf_op jit(solution)/shard_map/ppermute | solution.py:337
  29.1 0.0 collective-permute-start.6
  29.1 2.1 %collective-permute-done.4.beyond_ref = bf16[64,128]{1,0:T(8,128)(2,1)S(1)} collective-permute-done((bf16[64,128]{1,0:T(8,128)(2,1)S(1)}, bf16[64,128]{1,0:T(8,128)(2,1)S(1)}, u32[]{:S(2)}, u32[]{:S(2)}) %collective-permute-start.4) | collective-permute-done | bytes 16416 | tf_op jit(solution)/shard_map/ppermute | solution.py:337
  31.1 1.7 %collective-permute-done.6.far_ref = bf16[64,128]{1,0:T(8,128)(2,1)S(1)} collective-permute-done((bf16[64,128]{1,0:T(8,128)(2,1)S(1)}, bf16[64,128]{1,0:T(8,128)(2,1)S(1)}, u32[]{:S(2)}, u32[]{:S(2)}) %collective-permute-start.6) | collective-permute-done | bytes 16416 | tf_op jit(solution)/shard_map/ppermute | solution.py:337
  32.8 0.0 collective-permute-done.3.across_ref
  32.8 0.0 collective-permute-done.5.near_ref
  32.8 1.1 %shard_map.130 = (f32[64,1024]{1,0:T(8,128)S(1)}, bf16[8,144,128]{2,1,0:T(8,128)(2,1)S(1)}) custom-call(bf16[128,128]{1,0:T(8,128)(2,1)S(1)} %collective-permute-done.3.across_ref, bf16[64,128]{1,0:T(8,128)(2,1)S(1)} %collective-permute-done.4.beyond_ref, bf16[128,128]{1,0:T(8,128)(2,1)S(1)} %collective-permute-done.5.near_ref, ...), custom_call_target="tpu_custom_call" | custom-call | flops 134217728 | bytes 4030464 | tf_op jit(solution)/shard_map/pallas_call | solution.py:24
  33.9 12.4 %all_to_all.16.second_ref = bf16[8,144,128]{2,1,0:T(8,128)(2,1)S(1)} all-to-all(bf16[8,144,128]{2,1,0:T(8,128)(2,1)S(1)} %get-tuple-element.48), channel_id=1, replica_groups=mesh['grp'=2,'lon'=8,'lat'=2] {'lon'}, dimensions={0} | all-to-all | bytes 589824 | tf_op jit(solution)/shard_map/all_to_all | solution.py:324
  46.3 0.0 collective-permute-start.7
  46.3 1.6 %collective-permute-done.7.second_others_ref = bf16[8,144,128]{2,1,0:T(8,128)(2,1)S(1)} collective-permute-done((bf16[8,144,128]{2,1,0:T(8,128)(2,1)S(1)}, bf16[8,144,128]{2,1,0:T(8,128)(2,1)S(1)}, u32[]{:S(2)}, u32[]{:S(2)}) %collective-permute-start.7) | collective-permute-done | bytes 294944 | tf_op jit(solution)/shard_map/ppermute | solution.py:328
  47.9 1.8 %shard_map.131 = (f32[64,1024]{1,0:T(8,128)S(1)}, f32[8,128]{1,0:T(8,128)S(1)}, f32[16,8,128]{2,1,0:T(8,128)S(1)}) custom-call(bf16[8,32,128]{2,1,0:T(8,128)(2,1)S(1)} %all_to_all.15.pieces_ref, bf16[8,32,128]{2,1,0:T(8,128)(2,1)S(1)} %collective-permute-done.2.others_ref, bf16[8,144,128]{2,1,0:T(8,128)(2,1)S(1)} %all_to_all.16.second_ref, ...), custom_call_target="tpu_custom_call" | custom-call | flops 134217728 | bytes 4489216 | tf_op jit(solution)/shard_map/pallas_call | solution.py:24
  49.7 9.7 %all_to_all.17.chunks_ref = f32[16,8,128]{2,1,0:T(8,128)S(1)} all-to-all(f32[16,8,128]{2,1,0:T(8,128)S(1)} %get-tuple-element.51), channel_id=1, replica_groups=mesh['grp'=2,'lon'=8,'lat'=2] {'lon','lat'}, dimensions={0} | all-to-all | bytes 131072 | tf_op jit(solution)/shard_map/all_to_all | solution.py:324
  59.4 1.2 %shard_map.132 = f32[64,1024]{1,0:T(8,128)} custom-call(f32[8,128]{1,0:T(8,128)S(1)} %get-tuple-element.50.sums_ref, f32[16,8,128]{2,1,0:T(8,128)S(1)} %all_to_all.17.chunks_ref, f32[64,1024]{1,0:T(8,128)S(1)} %get-tuple-element.46.z_ref.first_ref, f32[64,1024]{1,0:T(8,128)S(1)} %get-tuple-element.52.second_ref), custom_call_target="tpu_custom_call" | custom-call | flops 262144 | bytes 593920 | tf_op jit(solution)/shard_map/pallas_call | solution.py:24
Async XLA Ops:
  3.0 17.3 %collective-permute-start = (bf16[896,128]{1,0:T(8,128)(2,1)S(1)}, bf16[896,128]{1,0:T(8,128)(2,1)S(1)}, u32[]{:S(2)}, u32[]{:S(2)}) collective-permute-start(bf16[896,128]{1,0:T(8,128)(2,1)S(1)} %get-tuple-element.31), channel_id=1, source_target_pairs={{0,14},{2,4},{4,2},{6,8},{8,6},{10,12},{12,10},{14,0},{1,15},{3,5}... | collective-permute-start | bytes 688136 | tf_op jit(solution)/shard_map/ppermute | solution.py:337
  9.1 11.2 %collective-permute-start.1 = (bf16[896,128]{1,0:T(8,128)(2,1)S(1)}, bf16[896,128]{1,0:T(8,128)(2,1)S(1)}, u32[]{:S(2)}, u32[]{:S(2)}) collective-permute-start(bf16[896,128]{1,0:T(8,128)(2,1)S(1)} %get-tuple-element.32), channel_id=1, source_target_pairs={{0,2},{2,0},{4,6},{6,4},{8,10},{10,8},{12,14},{14,12},{1,3},{3,1},... | collective-permute-start | bytes 688136 | tf_op jit(solution)/shard_map/ppermute | solution.py:337
  20.3 2.1 %collective-permute-start.2 = (bf16[8,32,128]{2,1,0:T(8,128)(2,1)S(1)}, bf16[8,32,128]{2,1,0:T(8,128)(2,1)S(1)}, u32[]{:S(2)}, u32[]{:S(2)}) collective-permute-start(bf16[8,32,128]{2,1,0:T(8,128)(2,1)S(1)} %all_to_all.15.pieces_ref), channel_id=1, source_target_pairs={{0,1},{1,0},{2,3},{3,2},{4,5},{5,4},{6,7},{7,6},{8,9},{9,8},{10,11... | collective-permute-start | bytes 196616 | tf_op jit(solution)/shard_map/ppermute | solution.py:328
  23.7 9.1 %collective-permute-start.3 = (bf16[128,128]{1,0:T(8,128)(2,1)S(1)}, bf16[128,128]{1,0:T(8,128)(2,1)S(1)}, u32[]{:S(2)}, u32[]{:S(2)}) collective-permute-start(bf16[128,128]{1,0:T(8,128)(2,1)S(1)} %get-tuple-element.40), channel_id=1, source_target_pairs={{0,14},{2,4},{4,2},{6,8},{8,6},{10,12},{12,10},{14,0},{1,15},{3,5}... | collective-permute-start | bytes 98312 | tf_op jit(solution)/shard_map/ppermute | solution.py:337
  25.6 7.2 %collective-permute-start.5 = (bf16[128,128]{1,0:T(8,128)(2,1)S(1)}, bf16[128,128]{1,0:T(8,128)(2,1)S(1)}, u32[]{:S(2)}, u32[]{:S(2)}) collective-permute-start(bf16[128,128]{1,0:T(8,128)(2,1)S(1)} %get-tuple-element.42), channel_id=1, source_target_pairs={{0,2},{2,0},{4,6},{6,4},{8,10},{10,8},{12,14},{14,12},{1,3},{3,1},... | collective-permute-start | bytes 98312 | tf_op jit(solution)/shard_map/ppermute | solution.py:337
  25.6 5.5 %collective-permute-start.4 = (bf16[64,128]{1,0:T(8,128)(2,1)S(1)}, bf16[64,128]{1,0:T(8,128)(2,1)S(1)}, u32[]{:S(2)}, u32[]{:S(2)}) collective-permute-start(bf16[64,128]{1,0:T(8,128)(2,1)S(1)} %get-tuple-element.41.own_beyond_ref), channel_id=1, source_target_pairs={{0,12},{2,14},{4,8},{6,10},{8,4},{10,6},{12,0},{14,2},{1,13},{3,15... | collective-permute-start | bytes 49160 | tf_op jit(solution)/shard_map/ppermute | solution.py:337
  29.1 3.7 %collective-permute-start.6 = (bf16[64,128]{1,0:T(8,128)(2,1)S(1)}, bf16[64,128]{1,0:T(8,128)(2,1)S(1)}, u32[]{:S(2)}, u32[]{:S(2)}) collective-permute-start(bf16[64,128]{1,0:T(8,128)(2,1)S(1)} %get-tuple-element.43.own_far_ref), channel_id=1, source_target_pairs={{0,4},{2,6},{4,0},{6,2},{8,12},{10,14},{12,8},{14,10},{1,5},{3,7},... | collective-permute-start | bytes 49160 | tf_op jit(solution)/shard_map/ppermute | solution.py:337
  46.3 1.6 %collective-permute-start.7 = (bf16[8,144,128]{2,1,0:T(8,128)(2,1)S(1)}, bf16[8,144,128]{2,1,0:T(8,128)(2,1)S(1)}, u32[]{:S(2)}, u32[]{:S(2)}) collective-permute-start(bf16[8,144,128]{2,1,0:T(8,128)(2,1)S(1)} %all_to_all.16.second_ref), channel_id=1, source_target_pairs={{0,1},{1,0},{2,3},{3,2},{4,5},{5,4},{6,7},{7,6},{8,9},{9,8},{10,11... | collective-permute-start | bytes 884744 | tf_op jit(solution)/shard_map/ppermute | solution.py:328

commit v13 on v12

--- a/solution.py
+++ b/solution.py
@@ -152,7 +152,7 @@
         total_ref[cols, rows] += dot(unit, values, 1, 1)
         return carry
 
-    lax.fori_loop(0, count, place, 0, unroll=8)
+    lax.fori_loop(0, count, place, 0, unroll=True)
 
     def narrow(i, carry):
         rows = pl.ds(pl.multiple_of(i * block, block), block)
@@ -192,8 +192,8 @@
     edges = edge_ref[...]
     scaled = (dot(z.astype(BF16), dense_ref[...]) + react * z) * inverse_mass
     scaled_ref[...] = scaled
-    level1 = levels(z, edges).astype(BF16)
-    level2 = levels(scaled, edges).astype(BF16)
+    level = levels(jnp.concatenate([z, scaled], axis=0), edges).astype(BF16)
+    level1, level2 = level[0:samples], level[samples:]
     slots = edges.shape[0] // 2
 
     def send(east_ref, west_ref):
@@ -216,19 +216,20 @@
     active, react, inverse_mass, obs, jacobi = lines(diag_ref)
     z = z_ref[...]
     edges = edge_ref[...]
-    from_east, from_west = pick(0, near_ref[...], across_ref[...])
     fixed = near_corr_ref.shape[0] - edges.shape[0] - vectors_ref.shape[0] - samples
     corr = slice(fixed, fixed + edges.shape[0])
-    corr_east, corr_west = pick(0, near_corr_ref[corr, :], across_corr_ref[corr, :])
+    arrived = jnp.concatenate(pick(0, near_ref[0:samples, :], across_ref[0:samples, :]), axis=1)
+    inner = scaled_ref[...] + dot(arrived, edges) * inverse_mass
     beyond_east, beyond_west = pick(1, far_ref[...], beyond_ref[...])
     own_east, own_west = pick(1, own_far_ref[...], own_beyond_ref[...])
-    arrived = jnp.concatenate([from_east[0:samples], from_west[0:samples]], axis=1)
-    inner = scaled_ref[...] + dot(arrived, edges) * inverse_mass
-    east_terms = jnp.concatenate([beyond_east, own_east], axis=1)
-    west_terms = jnp.concatenate([own_west, beyond_west], axis=1)
-    second_east = from_east[samples:].astype(F32) + dot(east_terms, corr_east)
-    second_west = from_west[samples:].astype(F32) + dot(west_terms, corr_west)
-    arrived2 = jnp.concatenate([second_east, second_west], axis=1).astype(BF16)
+    near_terms, across_terms = pick(
+        0,
+        jnp.concatenate([beyond_east, own_east], axis=1),
+        jnp.concatenate([own_west, beyond_west], axis=1),
+    )
+    second_near = near_ref[samples:, :].astype(F32) + dot(near_terms, near_corr_ref[corr, :])
+    second_across = across_ref[samples:, :].astype(F32) + dot(across_terms, across_corr_ref[corr, :])
+    arrived2 = jnp.concatenate(pick(0, second_near, second_across), axis=1)
     stiff = dot(inner.astype(BF16), dense_ref[...]) + dot(arrived2, edges) + react * inner
     image = active * (stiff + obs * z)
     image_ref[...] = image
@@ -277,24 +278,27 @@
     edges = edge_ref[...]
     step_column = column_of(step)[0:samples]
     residual = active * right_ref[...].astype(F32) - step_column * image
-    z = smooth(residual, coarse_ref, inverse_ref, vectors_ref, active, jacobi)
-    z_ref[...] = z
-
     kept, width = inverse_ref.shape
     fixed = width // LANES * kept + edges.shape[0]
 
-    def arriving(static, change):
-        inverse = jnp.concatenate([static[j * kept : (j + 1) * kept] for j in range(width // LANES)], axis=1)
-        fix = dot(inverse, coarse_ref[...]).astype(BF16)
-        spread = dot(fix, static[fixed : fixed + kept], 0, 0)
-        return (static[fixed + kept :].astype(F32) - step_column * change.astype(F32) + spread).astype(BF16)
+    def rows_of(static_ref):
+        return jnp.concatenate([static_ref[j * kept : (j + 1) * kept, :] for j in range(width // LANES)], axis=1)
+
+    inverses = jnp.concatenate([inverse_ref[...], rows_of(near_ref), rows_of(across_ref)], axis=0)
+    fixes = dot(inverses, coarse_ref[...]).astype(BF16)
+    z = active * (residual * jacobi + dot(fixes[0:kept], vectors_ref[...], 0, 0))
+    z_ref[...] = z
+
+    def arriving(static_ref, fix, change):
+        smooth_level = static_ref[fixed + kept :, :].astype(F32) - step_column * change.astype(F32)
+        return (smooth_level + dot(fix, static_ref[fixed : fixed + kept, :], 0, 0)).astype(BF16)
 
     lon = lax.axis_index("lon")
     odd = lon & 1
     ahead, before = lax.rem(lon + 1, count), lax.rem(lon + count - 1, count)
     change = slice(2 * half + SUM_ROWS, second_ref.shape[1])
-    from_near = arriving(near_ref[...], second_ref[ahead + odd * (before - ahead), change, :])
-    from_across = arriving(across_ref[...], second_ref[before + odd * (ahead - before), change, :])
+    from_near = arriving(near_ref, fixes[kept : 2 * kept], second_ref[ahead + odd * (before - ahead), change, :])
+    from_across = arriving(across_ref, fixes[2 * kept :], second_ref[before + odd * (ahead - before), change, :])
     from_east, from_west = pick(0, from_near, from_across)
     arrived = jnp.concatenate([from_east, from_west], axis=1)
     stiff = dot(z.astype(BF16), dense_ref[...]) + react * z + dot(arrived, edges)

time: 60.8 us -> 60.1 us (0.988)
  Pallas kernels: 9.19 us -> 8.52 us
    pallas_call x6, Pallas kernels: 9.19 us -> 8.52 us  [call(): pl.pallas_call(kernel, out_shape=[jax.ShapeDtypeStruct(s, t) for s, t in...]
where the time goes in v13:
time: 60.1 us; the launch traced here: 59.8 us
  blocking collectives  33.2 us (55%)
  starting transfers between devices  11.4 us (19%)
  Pallas kernels  8.52 us (14%)
  waiting for transfers between devices  5.33 us (9%)
  between operations  1.34 us (2%)
    all_to_all x3, blocking collectives, exchange(): return lax.all_to_all(chunks, axes, split_axis=0, concat_axis=0, tiled=True)  33.2 us
    ppermute x6, starting transfers between devices, swap(): return lax.ppermute(array, 'lon', pairs)  11.4 us
    pallas_call x6, Pallas kernels, call(): pl.pallas_call(kernel, out_shape=[jax.ShapeDtypeStruct(s, t) for s, t in...  8.52 us
    ppermute x6, waiting for transfers between devices, swap(): return lax.ppermute(array, 'lon', pairs)  3.75 us
    ppermute x2, waiting for transfers between devices, other_band(): return lax.ppermute(array, 'lat', [(0, 1), (1, 0)])  1.58 us
  transfers between devices with their start and end apart: 8, of which 3 were waited for; matrix products, arithmetic and copies ran while one was open for 0% of the time, Pallas kernels for 3%

profile of v13, /device:TPU:0, one launch (start us, length us, event | category | flops | bytes accessed | tf_op | source)
XLA Modules:
  0.0 59.8 jit_solution(8300445362066398348)
XLA Ops:
  1.3 1.7 %shard_map.127 = (bf16[8,32,128]{2,1,0:T(8,128)(2,1)S(1)}, f32[8,1024]{1,0:T(8,128)S(1)}, bf16[256,1024]{1,0:T(8,128)(2,1)S(1)}, bf16[896,128]{1,0:T(8,128)(2,1)...) custom-call(s32[1]{0:T(128)S(6)} %copy.15.node_count_ref, ...), custom_call_target="tpu_custom_call" | custom-call | flops 8388608 | bytes 1225736 | tf_op jit(solution)/shard_map/pallas_call | solution.py:24
  3.0 6.0 %collective-permute-start = (bf16[896,128]{1,0:T(8,128)(2,1)S(1)}, bf16[896,128]{1,0:T(8,128)(2,1)S(1)}, u32[]{:S(2)}, u32[]{:S(2)}) collective-permute-start(bf16[896,128]{1,0:T(8,128)(2,1)S(1)} %get-tuple-element.31), channel_id=1, source_target_pairs={{0,14},{2,4},{4,2},{6,8},{8,6},{10,12},{12,10},{14,0},{1,15},{3,5}... | collective-permute-start | bytes 688136 | tf_op jit(solution)/shard_map/ppermute | solution.py:341
  9.1 0.0 collective-permute-start.1
  9.1 11.2 %all_to_all.15.pieces_ref = bf16[8,32,128]{2,1,0:T(8,128)(2,1)S(1)} all-to-all(bf16[8,32,128]{2,1,0:T(8,128)(2,1)S(1)} %get-tuple-element.29), channel_id=1, replica_groups=mesh['grp'=2,'lon'=8,'lat'=2] {'lon'}, dimensions={0} | all-to-all | bytes 131072 | tf_op jit(solution)/shard_map/all_to_all | solution.py:328
  20.3 0.0 collective-permute-done.across_corr_ref.across_ref
  20.3 0.0 collective-permute-done.1.near_corr_ref.near_ref
  20.3 0.0 collective-permute-start.2
  20.3 1.9 %shard_map.128.dense_ref = bf16[1024,1024]{1,0:T(8,128)(2,1)S(1)} custom-call(s32[2,24]{1,0:T(2,128)} %bitcast.7, bf16[24,128,128]{2,1,0:T(8,128)(2,1)S(1)} %get-tuple-element.37.blocks_ref), custom_call_target="tpu_custom_call" | custom-call | flops 134217728 | bytes 786624 | tf_op jit(solution)/shard_map/pallas_call | solution.py:24
  22.2 0.0 collective-permute-done.2.others_ref
  22.2 1.2 %shard_map.129 = (f32[64,1024]{1,0:T(8,128)S(1)}, f32[64,1024]{1,0:T(8,128)S(1)}, bf16[128,128]{1,0:T(8,128)(2,1)S(1)}, bf16[128,128]{1,0:T(8,128)(2,1)S(1)}, bf...) custom-call(bf16[8,32,128]{2,1,0:T(8,128)(2,1)S(1)} %all_to_all.15.pieces_ref, ...), custom_call_target="tpu_custom_call" | custom-call | flops 134217728 | bytes 3178496 | tf_op jit(solution)/shard_map/pallas_call | solution.py:24
  23.4 1.9 %collective-permute-start.3 = (bf16[128,128]{1,0:T(8,128)(2,1)S(1)}, bf16[128,128]{1,0:T(8,128)(2,1)S(1)}, u32[]{:S(2)}, u32[]{:S(2)}) collective-permute-start(bf16[128,128]{1,0:T(8,128)(2,1)S(1)} %get-tuple-element.40), channel_id=1, source_target_pairs={{0,14},{2,4},{4,2},{6,8},{8,6},{10,12},{12,10},{14,0},{1,15},{3,5}... | collective-permute-start | bytes 98312 | tf_op jit(solution)/shard_map/ppermute | solution.py:341
  25.2 0.0 collective-permute-start.5
  25.2 3.5 %collective-permute-start.4 = (bf16[64,128]{1,0:T(8,128)(2,1)S(1)}, bf16[64,128]{1,0:T(8,128)(2,1)S(1)}, u32[]{:S(2)}, u32[]{:S(2)}) collective-permute-start(bf16[64,128]{1,0:T(8,128)(2,1)S(1)} %get-tuple-element.41.own_beyond_ref), channel_id=1, source_target_pairs={{0,12},{2,14},{4,8},{6,10},{8,4},{10,6},{12,0},{14,2},{1,13},{3,15... | collective-permute-start | bytes 49160 | tf_op jit(solution)/shard_map/ppermute | solution.py:341
  28.7 0.0 collective-permute-start.6
  28.7 2.1 %collective-permute-done.4.beyond_ref = bf16[64,128]{1,0:T(8,128)(2,1)S(1)} collective-permute-done((bf16[64,128]{1,0:T(8,128)(2,1)S(1)}, bf16[64,128]{1,0:T(8,128)(2,1)S(1)}, u32[]{:S(2)}, u32[]{:S(2)}) %collective-permute-start.4) | collective-permute-done | bytes 16416 | tf_op jit(solution)/shard_map/ppermute | solution.py:341
  30.8 1.7 %collective-permute-done.6.far_ref = bf16[64,128]{1,0:T(8,128)(2,1)S(1)} collective-permute-done((bf16[64,128]{1,0:T(8,128)(2,1)S(1)}, bf16[64,128]{1,0:T(8,128)(2,1)S(1)}, u32[]{:S(2)}, u32[]{:S(2)}) %collective-permute-start.6) | collective-permute-done | bytes 16416 | tf_op jit(solution)/shard_map/ppermute | solution.py:341
  32.5 0.0 collective-permute-done.3.across_ref
  32.5 0.0 collective-permute-done.5.near_ref
  32.5 1.1 %shard_map.130 = (f32[64,1024]{1,0:T(8,128)S(1)}, bf16[8,144,128]{2,1,0:T(8,128)(2,1)S(1)}) custom-call(bf16[128,128]{1,0:T(8,128)(2,1)S(1)} %collective-permute-done.3.across_ref, bf16[64,128]{1,0:T(8,128)(2,1)S(1)} %collective-permute-done.4.beyond_ref, bf16[128,128]{1,0:T(8,128)(2,1)S(1)} %collective-permute-done.5.near_ref, ...), custom_call_target="tpu_custom_call" | custom-call | flops 134217728 | bytes 4030464 | tf_op jit(solution)/shard_map/pallas_call | solution.py:24
  33.6 12.4 %all_to_all.16.second_ref = bf16[8,144,128]{2,1,0:T(8,128)(2,1)S(1)} all-to-all(bf16[8,144,128]{2,1,0:T(8,128)(2,1)S(1)} %get-tuple-element.48), channel_id=1, replica_groups=mesh['grp'=2,'lon'=8,'lat'=2] {'lon'}, dimensions={0} | all-to-all | bytes 589824 | tf_op jit(solution)/shard_map/all_to_all | solution.py:328
  45.9 0.0 collective-permute-start.7
  45.9 1.6 %collective-permute-done.7.second_others_ref = bf16[8,144,128]{2,1,0:T(8,128)(2,1)S(1)} collective-permute-done((bf16[8,144,128]{2,1,0:T(8,128)(2,1)S(1)}, bf16[8,144,128]{2,1,0:T(8,128)(2,1)S(1)}, u32[]{:S(2)}, u32[]{:S(2)}) %collective-permute-start.7) | collective-permute-done | bytes 294944 | tf_op jit(solution)/shard_map/ppermute | solution.py:332
  47.5 1.5 %shard_map.131 = (f32[64,1024]{1,0:T(8,128)S(1)}, f32[8,128]{1,0:T(8,128)S(1)}, f32[16,8,128]{2,1,0:T(8,128)S(1)}) custom-call(bf16[8,32,128]{2,1,0:T(8,128)(2,1)S(1)} %all_to_all.15.pieces_ref, bf16[8,32,128]{2,1,0:T(8,128)(2,1)S(1)} %collective-permute-done.2.others_ref, bf16[8,144,128]{2,1,0:T(8,128)(2,1)S(1)} %all_to_all.16.second_ref, ...), custom_call_target="tpu_custom_call" | custom-call | flops 134217728 | bytes 4489216 | tf_op jit(solution)/shard_map/pallas_call | solution.py:24
  49.0 9.7 %all_to_all.17.chunks_ref = f32[16,8,128]{2,1,0:T(8,128)S(1)} all-to-all(f32[16,8,128]{2,1,0:T(8,128)S(1)} %get-tuple-element.51), channel_id=1, replica_groups=mesh['grp'=2,'lon'=8,'lat'=2] {'lon','lat'}, dimensions={0} | all-to-all | bytes 131072 | tf_op jit(solution)/shard_map/all_to_all | solution.py:328
  58.7 1.2 %shard_map.132 = f32[64,1024]{1,0:T(8,128)} custom-call(f32[8,128]{1,0:T(8,128)S(1)} %get-tuple-element.50.sums_ref, f32[16,8,128]{2,1,0:T(8,128)S(1)} %all_to_all.17.chunks_ref, f32[64,1024]{1,0:T(8,128)S(1)} %get-tuple-element.46.z_ref.first_ref, f32[64,1024]{1,0:T(8,128)S(1)} %get-tuple-element.52.second_ref), custom_call_target="tpu_custom_call" | custom-call | flops 262144 | bytes 593920 | tf_op jit(solution)/shard_map/pallas_call | solution.py:24
Async XLA Ops:
  3.0 17.3 %collective-permute-start = (bf16[896,128]{1,0:T(8,128)(2,1)S(1)}, bf16[896,128]{1,0:T(8,128)(2,1)S(1)}, u32[]{:S(2)}, u32[]{:S(2)}) collective-permute-start(bf16[896,128]{1,0:T(8,128)(2,1)S(1)} %get-tuple-element.31), channel_id=1, source_target_pairs={{0,14},{2,4},{4,2},{6,8},{8,6},{10,12},{12,10},{14,0},{1,15},{3,5}... | collective-permute-start | bytes 688136 | tf_op jit(solution)/shard_map/ppermute | solution.py:341
  9.1 11.2 %collective-permute-start.1 = (bf16[896,128]{1,0:T(8,128)(2,1)S(1)}, bf16[896,128]{1,0:T(8,128)(2,1)S(1)}, u32[]{:S(2)}, u32[]{:S(2)}) collective-permute-start(bf16[896,128]{1,0:T(8,128)(2,1)S(1)} %get-tuple-element.32), channel_id=1, source_target_pairs={{0,2},{2,0},{4,6},{6,4},{8,10},{10,8},{12,14},{14,12},{1,3},{3,1},... | collective-permute-start | bytes 688136 | tf_op jit(solution)/shard_map/ppermute | solution.py:341
  20.3 1.9 %collective-permute-start.2 = (bf16[8,32,128]{2,1,0:T(8,128)(2,1)S(1)}, bf16[8,32,128]{2,1,0:T(8,128)(2,1)S(1)}, u32[]{:S(2)}, u32[]{:S(2)}) collective-permute-start(bf16[8,32,128]{2,1,0:T(8,128)(2,1)S(1)} %all_to_all.15.pieces_ref), channel_id=1, source_target_pairs={{0,1},{1,0},{2,3},{3,2},{4,5},{5,4},{6,7},{7,6},{8,9},{9,8},{10,11... | collective-permute-start | bytes 196616 | tf_op jit(solution)/shard_map/ppermute | solution.py:332
  23.4 9.1 %collective-permute-start.3 = (bf16[128,128]{1,0:T(8,128)(2,1)S(1)}, bf16[128,128]{1,0:T(8,128)(2,1)S(1)}, u32[]{:S(2)}, u32[]{:S(2)}) collective-permute-start(bf16[128,128]{1,0:T(8,128)(2,1)S(1)} %get-tuple-element.40), channel_id=1, source_target_pairs={{0,14},{2,4},{4,2},{6,8},{8,6},{10,12},{12,10},{14,0},{1,15},{3,5}... | collective-permute-start | bytes 98312 | tf_op jit(solution)/shard_map/ppermute | solution.py:341
  25.2 7.2 %collective-permute-start.5 = (bf16[128,128]{1,0:T(8,128)(2,1)S(1)}, bf16[128,128]{1,0:T(8,128)(2,1)S(1)}, u32[]{:S(2)}, u32[]{:S(2)}) collective-permute-start(bf16[128,128]{1,0:T(8,128)(2,1)S(1)} %get-tuple-element.42), channel_id=1, source_target_pairs={{0,2},{2,0},{4,6},{6,4},{8,10},{10,8},{12,14},{14,12},{1,3},{3,1},... | collective-permute-start | bytes 98312 | tf_op jit(solution)/shard_map/ppermute | solution.py:341
  25.2 5.5 %collective-permute-start.4 = (bf16[64,128]{1,0:T(8,128)(2,1)S(1)}, bf16[64,128]{1,0:T(8,128)(2,1)S(1)}, u32[]{:S(2)}, u32[]{:S(2)}) collective-permute-start(bf16[64,128]{1,0:T(8,128)(2,1)S(1)} %get-tuple-element.41.own_beyond_ref), channel_id=1, source_target_pairs={{0,12},{2,14},{4,8},{6,10},{8,4},{10,6},{12,0},{14,2},{1,13},{3,15... | collective-permute-start | bytes 49160 | tf_op jit(solution)/shard_map/ppermute | solution.py:341
  28.7 3.7 %collective-permute-start.6 = (bf16[64,128]{1,0:T(8,128)(2,1)S(1)}, bf16[64,128]{1,0:T(8,128)(2,1)S(1)}, u32[]{:S(2)}, u32[]{:S(2)}) collective-permute-start(bf16[64,128]{1,0:T(8,128)(2,1)S(1)} %get-tuple-element.43.own_far_ref), channel_id=1, source_target_pairs={{0,4},{2,6},{4,0},{6,2},{8,12},{10,14},{12,8},{14,10},{1,5},{3,7},... | collective-permute-start | bytes 49160 | tf_op jit(solution)/shard_map/ppermute | solution.py:341
  45.9 1.6 %collective-permute-start.7 = (bf16[8,144,128]{2,1,0:T(8,128)(2,1)S(1)}, bf16[8,144,128]{2,1,0:T(8,128)(2,1)S(1)}, u32[]{:S(2)}, u32[]{:S(2)}) collective-permute-start(bf16[8,144,128]{2,1,0:T(8,128)(2,1)S(1)} %all_to_all.16.second_ref), channel_id=1, source_target_pairs={{0,1},{1,0},{2,3},{3,2},{4,5},{5,4},{6,7},{7,6},{8,9},{9,8},{10,11... | collective-permute-start | bytes 884744 | tf_op jit(solution)/shard_map/ppermute | solution.py:332

commit v14 on v13

--- a/solution.py
+++ b/solution.py
@@ -72,13 +72,13 @@
 
 
 def load_kernel(node_count_ref, iface_count_ref, coupling_hbm, east_hbm, west_hbm, react_hbm, mass_hbm, obs_hbm,
-                right_hbm, vectors_hbm, inverse_hbm, blocks_hbm,
+                right_hbm, vectors_hbm, inverse_hbm, blocks_hbm, pattern_hbm,
                 chunks_ref, diag_ref, edge_ref, near_ref, across_ref, right_ref, vectors_ref, blocks_ref,
-                inverse_ref, react_ref, mass_ref, obs_ref, coupling_ref, east_ref, west_ref, sems):
+                inverse_ref, pattern_ref, react_ref, mass_ref, obs_ref, coupling_ref, east_ref, west_ref, sems):
     pairs = (
         (coupling_hbm, coupling_ref), (east_hbm, east_ref), (west_hbm, west_ref), (react_hbm, react_ref),
         (mass_hbm, mass_ref), (obs_hbm, obs_ref), (right_hbm, right_ref), (vectors_hbm, vectors_ref),
-        (inverse_hbm, inverse_ref), (blocks_hbm, blocks_ref),
+        (inverse_hbm, inverse_ref), (blocks_hbm, blocks_ref), (pattern_hbm, pattern_ref),
     )
     copies = [pltpu.make_async_copy(src, dst, sems.at[i]) for i, (src, dst) in enumerate(pairs)]
     for copy in copies:
@@ -125,11 +125,12 @@
             ref[fixed:, :] = level[:, cols]
 
     by_lon(0, near_ref, across_ref, send)
-    copies[9].wait()
-
-
-def prep_kernel(pattern_hbm, blocks_ref, dense_ref, pattern_ref, total_ref, sem):
-    copy = pltpu.make_async_copy(pattern_hbm, pattern_ref, sem)
+    for copy in copies[9:]:
+        copy.wait()
+
+
+def prep_kernel(pattern_vmem, blocks_ref, dense_ref, pattern_ref, total_ref, sem):
+    copy = pltpu.make_async_copy(pattern_vmem, pattern_ref, sem)
     copy.start()
     nodes = dense_ref.shape[0]
     count, block, _ = blocks_ref.shape
@@ -367,12 +368,13 @@
     coarse_scratch = pltpu.VMEM((domains * vectors, samples), BF16)
     apply_cost = 2 * samples * nodes * nodes
     static = ((coarse_inverse.size // LANES + 2 * slots + vectors + samples, slots), BF16)
-    inputs = (coupling, east_rows, west_rows, react, mass, obs, right_side, deflation, coarse_inverse, stiffness_blocks)
+    inputs = (coupling, east_rows, west_rows, react, mass, obs, right_side, deflation, coarse_inverse, stiffness_blocks,
+              block_pattern.T)
     line = pltpu.VMEM((1, nodes), F32)
-    chunks, diag, edge, near_static, across_static, right, basis, stored, inverse = call(
+    chunks, diag, edge, near_static, across_static, right, basis, stored, inverse, pattern = call(
         load_kernel,
         [((sectors, half, LANES), BF16), ((8, nodes), F32), ((2 * slots, nodes), BF16), static, static]
-        + [(a.shape, a.dtype) for a in (right_side, deflation, stiffness_blocks, coarse_inverse)],
+        + [(a.shape, a.dtype) for a in (right_side, deflation, stiffness_blocks, coarse_inverse, inputs[-1])],
         [SMEM, SMEM] + [HBM] * len(inputs),
         [node_count, iface_count] + [pltpu.with_memory_space_constraint(a, pltpu.HBM) for a in inputs],
         2 * samples * vectors * nodes,
@@ -382,11 +384,10 @@
     pieces, stored, across_static, near_static = lax.optimization_barrier(
         (exchange(chunks, "lon"), stored, swap(across_static, 1, False), swap(near_static, 1, True))
     )
-    pattern = pltpu.with_memory_space_constraint(block_pattern.T, pltpu.HBM)
     (dense,) = call(
         prep_kernel,
         [((nodes, nodes), BF16)],
-        [HBM, VMEM],
+        [VMEM, VMEM],
         (pattern, stored),
         apply_cost,
         [pltpu.SMEM((2, block_pattern.shape[0]), jnp.int32), pltpu.VMEM((nodes, nodes), F32), pltpu.SemaphoreType.DMA],

time: 60.1 us -> 60 us (level)
  no operation moved by 1% of the time
where the time goes in v14:
time: 60 us; the launch traced here: 59.7 us
  blocking collectives  33.2 us (55%)
  starting transfers between devices  11.4 us (19%)
  Pallas kernels  8.43 us (14%)
  waiting for transfers between devices  5.33 us (9%)
  between operations  1.34 us (2%)
    all_to_all x3, blocking collectives, exchange(): return lax.all_to_all(chunks, axes, split_axis=0, concat_axis=0, tiled=True)  33.2 us
    ppermute x6, starting transfers between devices, swap(): return lax.ppermute(array, 'lon', pairs)  11.4 us
    pallas_call x6, Pallas kernels, call(): pl.pallas_call(kernel, out_shape=[jax.ShapeDtypeStruct(s, t) for s, t in...  8.43 us
    ppermute x6, waiting for transfers between devices, swap(): return lax.ppermute(array, 'lon', pairs)  3.75 us
    ppermute x2, waiting for transfers between devices, other_band(): return lax.ppermute(array, 'lat', [(0, 1), (1, 0)])  1.58 us
  transfers between devices with their start and end apart: 8, of which 3 were waited for; matrix products, arithmetic and copies ran while one was open for 0% of the time, Pallas kernels for 3%

profile of v14, /device:TPU:0, one launch (start us, length us, event | category | flops | bytes accessed | tf_op | source)
XLA Modules:
  0.0 59.7 jit_solution(227614415625946385)
XLA Ops:
  1.3 1.7 %shard_map.127 = (bf16[8,32,128]{2,1,0:T(8,128)(2,1)S(1)}, f32[8,1024]{1,0:T(8,128)S(1)}, bf16[256,1024]{1,0:T(8,128)(2,1)S(1)}, bf16[896,128]{1,0:T(8,128)(2,1)...) custom-call(s32[1]{0:T(128)S(6)} %copy.15.node_count_ref, ...), custom_call_target="tpu_custom_call" | custom-call | flops 8388608 | bytes 1225928 | tf_op jit(solution)/shard_map/pallas_call | solution.py:24
  3.0 6.0 %collective-permute-start = (bf16[896,128]{1,0:T(8,128)(2,1)S(1)}, bf16[896,128]{1,0:T(8,128)(2,1)S(1)}, u32[]{:S(2)}, u32[]{:S(2)}) collective-permute-start(bf16[896,128]{1,0:T(8,128)(2,1)S(1)} %get-tuple-element.32), channel_id=1, source_target_pairs={{0,14},{2,4},{4,2},{6,8},{8,6},{10,12},{12,10},{14,0},{1,15},{3,5}... | collective-permute-start | bytes 688136 | tf_op jit(solution)/shard_map/ppermute | solution.py:342
  9.1 0.0 collective-permute-start.1
  9.1 11.2 %all_to_all.15.pieces_ref = bf16[8,32,128]{2,1,0:T(8,128)(2,1)S(1)} all-to-all(bf16[8,32,128]{2,1,0:T(8,128)(2,1)S(1)} %get-tuple-element.30), channel_id=1, replica_groups=mesh['grp'=2,'lon'=8,'lat'=2] {'lon'}, dimensions={0} | all-to-all | bytes 131072 | tf_op jit(solution)/shard_map/all_to_all | solution.py:329
  20.3 0.0 collective-permute-done.across_corr_ref.across_ref
  20.3 0.0 collective-permute-done.1.near_corr_ref.near_ref
  20.3 0.0 collective-permute-start.2
  20.3 1.7 %shard_map.128.dense_ref = bf16[1024,1024]{1,0:T(8,128)(2,1)S(1)} custom-call(s32[2,24]{1,0:T(2,128)S(1)} %get-tuple-element.38.pattern_vmem, bf16[24,128,128]{2,1,0:T(8,128)(2,1)S(1)} %get-tuple-element.39.blocks_ref), custom_call_target="tpu_custom_call" | custom-call | flops 134217728 | bytes 786624 | tf_op jit(solution)/shard_map/pallas_call | solution.py:24
  22.1 0.0 collective-permute-done.2.others_ref
  22.1 1.2 %shard_map.129 = (f32[64,1024]{1,0:T(8,128)S(1)}, f32[64,1024]{1,0:T(8,128)S(1)}, bf16[128,128]{1,0:T(8,128)(2,1)S(1)}, bf16[128,128]{1,0:T(8,128)(2,1)S(1)}, bf...) custom-call(bf16[8,32,128]{2,1,0:T(8,128)(2,1)S(1)} %all_to_all.15.pieces_ref, ...), custom_call_target="tpu_custom_call" | custom-call | flops 134217728 | bytes 3178496 | tf_op jit(solution)/shard_map/pallas_call | solution.py:24
  23.3 1.8 %collective-permute-start.3 = (bf16[128,128]{1,0:T(8,128)(2,1)S(1)}, bf16[128,128]{1,0:T(8,128)(2,1)S(1)}, u32[]{:S(2)}, u32[]{:S(2)}) collective-permute-start(bf16[128,128]{1,0:T(8,128)(2,1)S(1)} %get-tuple-element.42), channel_id=1, source_target_pairs={{0,14},{2,4},{4,2},{6,8},{8,6},{10,12},{12,10},{14,0},{1,15},{3,5}... | collective-permute-start | bytes 98312 | tf_op jit(solution)/shard_map/ppermute | solution.py:342
  25.1 0.0 collective-permute-start.5
  25.1 3.5 %collective-permute-start.4 = (bf16[64,128]{1,0:T(8,128)(2,1)S(1)}, bf16[64,128]{1,0:T(8,128)(2,1)S(1)}, u32[]{:S(2)}, u32[]{:S(2)}) collective-permute-start(bf16[64,128]{1,0:T(8,128)(2,1)S(1)} %get-tuple-element.43.own_beyond_ref), channel_id=1, source_target_pairs={{0,12},{2,14},{4,8},{6,10},{8,4},{10,6},{12,0},{14,2},{1,13},{3,15... | collective-permute-start | bytes 49160 | tf_op jit(solution)/shard_map/ppermute | solution.py:342
  28.6 0.0 collective-permute-start.6
  28.6 2.0 %collective-permute-done.4.beyond_ref = bf16[64,128]{1,0:T(8,128)(2,1)S(1)} collective-permute-done((bf16[64,128]{1,0:T(8,128)(2,1)S(1)}, bf16[64,128]{1,0:T(8,128)(2,1)S(1)}, u32[]{:S(2)}, u32[]{:S(2)}) %collective-permute-start.4) | collective-permute-done | bytes 16416 | tf_op jit(solution)/shard_map/ppermute | solution.py:342
  30.6 1.7 %collective-permute-done.6.far_ref = bf16[64,128]{1,0:T(8,128)(2,1)S(1)} collective-permute-done((bf16[64,128]{1,0:T(8,128)(2,1)S(1)}, bf16[64,128]{1,0:T(8,128)(2,1)S(1)}, u32[]{:S(2)}, u32[]{:S(2)}) %collective-permute-start.6) | collective-permute-done | bytes 16416 | tf_op jit(solution)/shard_map/ppermute | solution.py:342
  32.4 0.0 collective-permute-done.3.across_ref
  32.4 0.0 collective-permute-done.5.near_ref
  32.4 1.1 %shard_map.130 = (f32[64,1024]{1,0:T(8,128)S(1)}, bf16[8,144,128]{2,1,0:T(8,128)(2,1)S(1)}) custom-call(bf16[128,128]{1,0:T(8,128)(2,1)S(1)} %collective-permute-done.3.across_ref, bf16[64,128]{1,0:T(8,128)(2,1)S(1)} %collective-permute-done.4.beyond_ref, bf16[128,128]{1,0:T(8,128)(2,1)S(1)} %collective-permute-done.5.near_ref, ...), custom_call_target="tpu_custom_call" | custom-call | flops 134217728 | bytes 4030464 | tf_op jit(solution)/shard_map/pallas_call | solution.py:24
  33.5 12.3 %all_to_all.16.second_ref = bf16[8,144,128]{2,1,0:T(8,128)(2,1)S(1)} all-to-all(bf16[8,144,128]{2,1,0:T(8,128)(2,1)S(1)} %get-tuple-element.50), channel_id=1, replica_groups=mesh['grp'=2,'lon'=8,'lat'=2] {'lon'}, dimensions={0} | all-to-all | bytes 589824 | tf_op jit(solution)/shard_map/all_to_all | solution.py:329
  45.8 0.0 collective-permute-start.7
  45.8 1.6 %collective-permute-done.7.second_others_ref = bf16[8,144,128]{2,1,0:T(8,128)(2,1)S(1)} collective-permute-done((bf16[8,144,128]{2,1,0:T(8,128)(2,1)S(1)}, bf16[8,144,128]{2,1,0:T(8,128)(2,1)S(1)}, u32[]{:S(2)}, u32[]{:S(2)}) %collective-permute-start.7) | collective-permute-done | bytes 294944 | tf_op jit(solution)/shard_map/ppermute | solution.py:333
  47.4 1.5 %shard_map.131 = (f32[64,1024]{1,0:T(8,128)S(1)}, f32[8,128]{1,0:T(8,128)S(1)}, f32[16,8,128]{2,1,0:T(8,128)S(1)}) custom-call(bf16[8,32,128]{2,1,0:T(8,128)(2,1)S(1)} %all_to_all.15.pieces_ref, bf16[8,32,128]{2,1,0:T(8,128)(2,1)S(1)} %collective-permute-done.2.others_ref, bf16[8,144,128]{2,1,0:T(8,128)(2,1)S(1)} %all_to_all.16.second_ref, ...), custom_call_target="tpu_custom_call" | custom-call | flops 134217728 | bytes 4489216 | tf_op jit(solution)/shard_map/pallas_call | solution.py:24
  48.9 9.7 %all_to_all.17.chunks_ref = f32[16,8,128]{2,1,0:T(8,128)S(1)} all-to-all(f32[16,8,128]{2,1,0:T(8,128)S(1)} %get-tuple-element.53), channel_id=1, replica_groups=mesh['grp'=2,'lon'=8,'lat'=2] {'lon','lat'}, dimensions={0} | all-to-all | bytes 131072 | tf_op jit(solution)/shard_map/all_to_all | solution.py:329
  58.6 1.2 %shard_map.132 = f32[64,1024]{1,0:T(8,128)} custom-call(f32[8,128]{1,0:T(8,128)S(1)} %get-tuple-element.52.sums_ref, f32[16,8,128]{2,1,0:T(8,128)S(1)} %all_to_all.17.chunks_ref, f32[64,1024]{1,0:T(8,128)S(1)} %get-tuple-element.48.z_ref.first_ref, f32[64,1024]{1,0:T(8,128)S(1)} %get-tuple-element.54.second_ref), custom_call_target="tpu_custom_call" | custom-call | flops 262144 | bytes 593920 | tf_op jit(solution)/shard_map/pallas_call | solution.py:24
Async XLA Ops:
  3.0 17.3 %collective-permute-start = (bf16[896,128]{1,0:T(8,128)(2,1)S(1)}, bf16[896,128]{1,0:T(8,128)(2,1)S(1)}, u32[]{:S(2)}, u32[]{:S(2)}) collective-permute-start(bf16[896,128]{1,0:T(8,128)(2,1)S(1)} %get-tuple-element.32), channel_id=1, source_target_pairs={{0,14},{2,4},{4,2},{6,8},{8,6},{10,12},{12,10},{14,0},{1,15},{3,5}... | collective-permute-start | bytes 688136 | tf_op jit(solution)/shard_map/ppermute | solution.py:342
  9.1 11.2 %collective-permute-start.1 = (bf16[896,128]{1,0:T(8,128)(2,1)S(1)}, bf16[896,128]{1,0:T(8,128)(2,1)S(1)}, u32[]{:S(2)}, u32[]{:S(2)}) collective-permute-start(bf16[896,128]{1,0:T(8,128)(2,1)S(1)} %get-tuple-element.33), channel_id=1, source_target_pairs={{0,2},{2,0},{4,6},{6,4},{8,10},{10,8},{12,14},{14,12},{1,3},{3,1},... | collective-permute-start | bytes 688136 | tf_op jit(solution)/shard_map/ppermute | solution.py:342
  20.3 1.8 %collective-permute-start.2 = (bf16[8,32,128]{2,1,0:T(8,128)(2,1)S(1)}, bf16[8,32,128]{2,1,0:T(8,128)(2,1)S(1)}, u32[]{:S(2)}, u32[]{:S(2)}) collective-permute-start(bf16[8,32,128]{2,1,0:T(8,128)(2,1)S(1)} %all_to_all.15.pieces_ref), channel_id=1, source_target_pairs={{0,1},{1,0},{2,3},{3,2},{4,5},{5,4},{6,7},{7,6},{8,9},{9,8},{10,11... | collective-permute-start | bytes 196616 | tf_op jit(solution)/shard_map/ppermute | solution.py:333
  23.3 9.1 %collective-permute-start.3 = (bf16[128,128]{1,0:T(8,128)(2,1)S(1)}, bf16[128,128]{1,0:T(8,128)(2,1)S(1)}, u32[]{:S(2)}, u32[]{:S(2)}) collective-permute-start(bf16[128,128]{1,0:T(8,128)(2,1)S(1)} %get-tuple-element.42), channel_id=1, source_target_pairs={{0,14},{2,4},{4,2},{6,8},{8,6},{10,12},{12,10},{14,0},{1,15},{3,5}... | collective-permute-start | bytes 98312 | tf_op jit(solution)/shard_map/ppermute | solution.py:342
  25.1 7.3 %collective-permute-start.5 = (bf16[128,128]{1,0:T(8,128)(2,1)S(1)}, bf16[128,128]{1,0:T(8,128)(2,1)S(1)}, u32[]{:S(2)}, u32[]{:S(2)}) collective-permute-start(bf16[128,128]{1,0:T(8,128)(2,1)S(1)} %get-tuple-element.44), channel_id=1, source_target_pairs={{0,2},{2,0},{4,6},{6,4},{8,10},{10,8},{12,14},{14,12},{1,3},{3,1},... | collective-permute-start | bytes 98312 | tf_op jit(solution)/shard_map/ppermute | solution.py:342
  25.1 5.5 %collective-permute-start.4 = (bf16[64,128]{1,0:T(8,128)(2,1)S(1)}, bf16[64,128]{1,0:T(8,128)(2,1)S(1)}, u32[]{:S(2)}, u32[]{:S(2)}) collective-permute-start(bf16[64,128]{1,0:T(8,128)(2,1)S(1)} %get-tuple-element.43.own_beyond_ref), channel_id=1, source_target_pairs={{0,12},{2,14},{4,8},{6,10},{8,4},{10,6},{12,0},{14,2},{1,13},{3,15... | collective-permute-start | bytes 49160 | tf_op jit(solution)/shard_map/ppermute | solution.py:342
  28.6 3.7 %collective-permute-start.6 = (bf16[64,128]{1,0:T(8,128)(2,1)S(1)}, bf16[64,128]{1,0:T(8,128)(2,1)S(1)}, u32[]{:S(2)}, u32[]{:S(2)}) collective-permute-start(bf16[64,128]{1,0:T(8,128)(2,1)S(1)} %get-tuple-element.45.own_far_ref), channel_id=1, source_target_pairs={{0,4},{2,6},{4,0},{6,2},{8,12},{10,14},{12,8},{14,10},{1,5},{3,7},... | collective-permute-start | bytes 49160 | tf_op jit(solution)/shard_map/ppermute | solution.py:342
  45.8 1.6 %collective-permute-start.7 = (bf16[8,144,128]{2,1,0:T(8,128)(2,1)S(1)}, bf16[8,144,128]{2,1,0:T(8,128)(2,1)S(1)}, u32[]{:S(2)}, u32[]{:S(2)}) collective-permute-start(bf16[8,144,128]{2,1,0:T(8,128)(2,1)S(1)} %all_to_all.16.second_ref), channel_id=1, source_target_pairs={{0,1},{1,0},{2,3},{3,2},{4,5},{5,4},{6,7},{7,6},{8,9},{9,8},{10,11... | collective-permute-start | bytes 884744 | tf_op jit(solution)/shard_map/ppermute | solution.py:333

commit v15 on v14

--- a/solution.py
+++ b/solution.py
@@ -381,8 +381,10 @@
         [line, line, line] + [pltpu.VMEM(a.shape, a.dtype) for a in (coupling, east_rows, west_rows)]
         + [pltpu.SemaphoreType.DMA((len(inputs),))],
     )
-    pieces, stored, across_static, near_static = lax.optimization_barrier(
-        (exchange(chunks, "lon"), stored, swap(across_static, 1, False), swap(near_static, 1, True))
+    near_static = swap(near_static, 1, True)
+    across_static = swap(across_static, 1, False)
+    near_static, across_static, pieces, stored = lax.optimization_barrier(
+        (near_static, across_static, exchange(chunks, "lon"), stored)
     )
     (dense,) = call(
         prep_kernel,

time: 60 us -> 59.5 us (level)
  blocking collectives: 33.2 us -> 32.2 us
    all_to_all x3, blocking collectives: 33.2 us -> 32.2 us  [exchange(): return lax.all_to_all(chunks, axes, split_axis=0, concat_axis=0, tiled=True)]
where the time goes in v15:
time: 59.5 us; the launch traced here: 59.3 us
  blocking collectives  32.2 us (54%)
  starting transfers between devices  11.9 us (20%)
  Pallas kernels  8.42 us (14%)
  waiting for transfers between devices  5.33 us (9%)
  between operations  1.35 us (2%)
    all_to_all x3, blocking collectives, exchange(): return lax.all_to_all(chunks, axes, split_axis=0, concat_axis=0, tiled=True)  32.2 us
    ppermute x6, starting transfers between devices, swap(): return lax.ppermute(array, 'lon', pairs)  11.9 us
    pallas_call x6, Pallas kernels, call(): pl.pallas_call(kernel, out_shape=[jax.ShapeDtypeStruct(s, t) for s, t in...  8.42 us
    ppermute x6, waiting for transfers between devices, swap(): return lax.ppermute(array, 'lon', pairs)  3.75 us
    ppermute x2, waiting for transfers between devices, other_band(): return lax.ppermute(array, 'lat', [(0, 1), (1, 0)])  1.58 us
  transfers between devices with their start and end apart: 8, of which 3 were waited for; matrix products, arithmetic and copies ran while one was open for 0% of the time, Pallas kernels for 3%

profile of v15, /device:TPU:0, one launch (start us, length us, event | category | flops | bytes accessed | tf_op | source)
XLA Modules:
  0.0 59.3 jit_solution(2484083344211236313)
XLA Ops:
  1.3 1.7 %shard_map.127 = (bf16[8,32,128]{2,1,0:T(8,128)(2,1)S(1)}, f32[8,1024]{1,0:T(8,128)S(1)}, bf16[256,1024]{1,0:T(8,128)(2,1)S(1)}, bf16[896,128]{1,0:T(8,128)(2,1)...) custom-call(s32[1]{0:T(128)S(6)} %copy.15.node_count_ref, ...), custom_call_target="tpu_custom_call" | custom-call | flops 8388608 | bytes 1225928 | tf_op jit(solution)/shard_map/pallas_call | solution.py:24
  3.0 3.0 %collective-permute-start = (bf16[896,128]{1,0:T(8,128)(2,1)S(1)}, bf16[896,128]{1,0:T(8,128)(2,1)S(1)}, u32[]{:S(2)}, u32[]{:S(2)}) collective-permute-start(bf16[896,128]{1,0:T(8,128)(2,1)S(1)} %get-tuple-element.30), channel_id=1, source_target_pairs={{0,2},{2,0},{4,6},{6,4},{8,10},{10,8},{12,14},{14,12},{1,3},{3,1},... | collective-permute-start | bytes 688136 | tf_op jit(solution)/shard_map/ppermute | solution.py:342
  6.0 3.6 %collective-permute-start.1 = (bf16[896,128]{1,0:T(8,128)(2,1)S(1)}, bf16[896,128]{1,0:T(8,128)(2,1)S(1)}, u32[]{:S(2)}, u32[]{:S(2)}) collective-permute-start(bf16[896,128]{1,0:T(8,128)(2,1)S(1)} %get-tuple-element.31), channel_id=1, source_target_pairs={{0,14},{2,4},{4,2},{6,8},{8,6},{10,12},{12,10},{14,0},{1,15},{3,5}... | collective-permute-start | bytes 688136 | tf_op jit(solution)/shard_map/ppermute | solution.py:342
  9.6 9.5 %all_to_all.15.pieces_ref = bf16[8,32,128]{2,1,0:T(8,128)(2,1)S(1)} all-to-all(bf16[8,32,128]{2,1,0:T(8,128)(2,1)S(1)} %get-tuple-element.32), channel_id=1, replica_groups=mesh['grp'=2,'lon'=8,'lat'=2] {'lon'}, dimensions={0} | all-to-all | bytes 131072 | tf_op jit(solution)/shard_map/all_to_all | solution.py:329
  19.1 0.0 collective-permute-done.near_corr_ref.near_ref
  19.1 0.0 collective-permute-done.1.across_corr_ref.across_ref
  19.1 0.0 collective-permute-start.2
  19.1 1.7 %shard_map.128.dense_ref = bf16[1024,1024]{1,0:T(8,128)(2,1)S(1)} custom-call(s32[2,24]{1,0:T(2,128)S(1)} %get-tuple-element.38.pattern_vmem, bf16[24,128,128]{2,1,0:T(8,128)(2,1)S(1)} %get-tuple-element.39.blocks_ref), custom_call_target="tpu_custom_call" | custom-call | flops 134217728 | bytes 786624 | tf_op jit(solution)/shard_map/pallas_call | solution.py:24
  20.8 0.0 collective-permute-done.2.others_ref
  20.9 1.2 %shard_map.129 = (f32[64,1024]{1,0:T(8,128)S(1)}, f32[64,1024]{1,0:T(8,128)S(1)}, bf16[128,128]{1,0:T(8,128)(2,1)S(1)}, bf16[128,128]{1,0:T(8,128)(2,1)S(1)}, bf...) custom-call(bf16[8,32,128]{2,1,0:T(8,128)(2,1)S(1)} %all_to_all.15.pieces_ref, ...), custom_call_target="tpu_custom_call" | custom-call | flops 134217728 | bytes 3178496 | tf_op jit(solution)/shard_map/pallas_call | solution.py:24
  22.0 3.0 %collective-permute-start.3 = (bf16[128,128]{1,0:T(8,128)(2,1)S(1)}, bf16[128,128]{1,0:T(8,128)(2,1)S(1)}, u32[]{:S(2)}, u32[]{:S(2)}) collective-permute-start(bf16[128,128]{1,0:T(8,128)(2,1)S(1)} %get-tuple-element.42), channel_id=1, source_target_pairs={{0,14},{2,4},{4,2},{6,8},{8,6},{10,12},{12,10},{14,0},{1,15},{3,5}... | collective-permute-start | bytes 98312 | tf_op jit(solution)/shard_map/ppermute | solution.py:342
  25.1 0.0 collective-permute-start.5
  25.1 2.3 %collective-permute-start.4 = (bf16[64,128]{1,0:T(8,128)(2,1)S(1)}, bf16[64,128]{1,0:T(8,128)(2,1)S(1)}, u32[]{:S(2)}, u32[]{:S(2)}) collective-permute-start(bf16[64,128]{1,0:T(8,128)(2,1)S(1)} %get-tuple-element.43.own_beyond_ref), channel_id=1, source_target_pairs={{0,12},{2,14},{4,8},{6,10},{8,4},{10,6},{12,0},{14,2},{1,13},{3,15... | collective-permute-start | bytes 49160 | tf_op jit(solution)/shard_map/ppermute | solution.py:342
  27.4 0.0 collective-permute-start.6
  27.4 3.2 %collective-permute-done.4.beyond_ref = bf16[64,128]{1,0:T(8,128)(2,1)S(1)} collective-permute-done((bf16[64,128]{1,0:T(8,128)(2,1)S(1)}, bf16[64,128]{1,0:T(8,128)(2,1)S(1)}, u32[]{:S(2)}, u32[]{:S(2)}) %collective-permute-start.4) | collective-permute-done | bytes 16416 | tf_op jit(solution)/shard_map/ppermute | solution.py:342
  30.6 0.5 collective-permute-done.6.far_ref
  31.1 0.0 collective-permute-done.3.across_ref
  31.1 0.0 collective-permute-done.5.near_ref
  31.1 1.1 %shard_map.130 = (f32[64,1024]{1,0:T(8,128)S(1)}, bf16[8,144,128]{2,1,0:T(8,128)(2,1)S(1)}) custom-call(bf16[128,128]{1,0:T(8,128)(2,1)S(1)} %collective-permute-done.3.across_ref, bf16[64,128]{1,0:T(8,128)(2,1)S(1)} %collective-permute-done.4.beyond_ref, bf16[128,128]{1,0:T(8,128)(2,1)S(1)} %collective-permute-done.5.near_ref, ...), custom_call_target="tpu_custom_call" | custom-call | flops 134217728 | bytes 4030464 | tf_op jit(solution)/shard_map/pallas_call | solution.py:24
  32.2 13.1 %all_to_all.16.second_ref = bf16[8,144,128]{2,1,0:T(8,128)(2,1)S(1)} all-to-all(bf16[8,144,128]{2,1,0:T(8,128)(2,1)S(1)} %get-tuple-element.50), channel_id=1, replica_groups=mesh['grp'=2,'lon'=8,'lat'=2] {'lon'}, dimensions={0} | all-to-all | bytes 589824 | tf_op jit(solution)/shard_map/all_to_all | solution.py:329
  45.3 0.0 collective-permute-start.7
  45.3 1.6 %collective-permute-done.7.second_others_ref = bf16[8,144,128]{2,1,0:T(8,128)(2,1)S(1)} collective-permute-done((bf16[8,144,128]{2,1,0:T(8,128)(2,1)S(1)}, bf16[8,144,128]{2,1,0:T(8,128)(2,1)S(1)}, u32[]{:S(2)}, u32[]{:S(2)}) %collective-permute-start.7) | collective-permute-done | bytes 294944 | tf_op jit(solution)/shard_map/ppermute | solution.py:333
  46.9 1.5 %shard_map.131 = (f32[64,1024]{1,0:T(8,128)S(1)}, f32[8,128]{1,0:T(8,128)S(1)}, f32[16,8,128]{2,1,0:T(8,128)S(1)}) custom-call(bf16[8,32,128]{2,1,0:T(8,128)(2,1)S(1)} %all_to_all.15.pieces_ref, bf16[8,32,128]{2,1,0:T(8,128)(2,1)S(1)} %collective-permute-done.2.others_ref, bf16[8,144,128]{2,1,0:T(8,128)(2,1)S(1)} %all_to_all.16.second_ref, ...), custom_call_target="tpu_custom_call" | custom-call | flops 134217728 | bytes 4489216 | tf_op jit(solution)/shard_map/pallas_call | solution.py:24
  48.4 9.7 %all_to_all.17.chunks_ref = f32[16,8,128]{2,1,0:T(8,128)S(1)} all-to-all(f32[16,8,128]{2,1,0:T(8,128)S(1)} %get-tuple-element.53), channel_id=1, replica_groups=mesh['grp'=2,'lon'=8,'lat'=2] {'lon','lat'}, dimensions={0} | all-to-all | bytes 131072 | tf_op jit(solution)/shard_map/all_to_all | solution.py:329
  58.1 1.2 %shard_map.132 = f32[64,1024]{1,0:T(8,128)} custom-call(f32[8,128]{1,0:T(8,128)S(1)} %get-tuple-element.52.sums_ref, f32[16,8,128]{2,1,0:T(8,128)S(1)} %all_to_all.17.chunks_ref, f32[64,1024]{1,0:T(8,128)S(1)} %get-tuple-element.48.z_ref.first_ref, f32[64,1024]{1,0:T(8,128)S(1)} %get-tuple-element.54.second_ref), custom_call_target="tpu_custom_call" | custom-call | flops 262144 | bytes 593920 | tf_op jit(solution)/shard_map/pallas_call | solution.py:24
Async XLA Ops:
  3.0 16.0 %collective-permute-start = (bf16[896,128]{1,0:T(8,128)(2,1)S(1)}, bf16[896,128]{1,0:T(8,128)(2,1)S(1)}, u32[]{:S(2)}, u32[]{:S(2)}) collective-permute-start(bf16[896,128]{1,0:T(8,128)(2,1)S(1)} %get-tuple-element.30), channel_id=1, source_target_pairs={{0,2},{2,0},{4,6},{6,4},{8,10},{10,8},{12,14},{14,12},{1,3},{3,1},... | collective-permute-start | bytes 688136 | tf_op jit(solution)/shard_map/ppermute | solution.py:342
  6.0 13.0 %collective-permute-start.1 = (bf16[896,128]{1,0:T(8,128)(2,1)S(1)}, bf16[896,128]{1,0:T(8,128)(2,1)S(1)}, u32[]{:S(2)}, u32[]{:S(2)}) collective-permute-start(bf16[896,128]{1,0:T(8,128)(2,1)S(1)} %get-tuple-element.31), channel_id=1, source_target_pairs={{0,14},{2,4},{4,2},{6,8},{8,6},{10,12},{12,10},{14,0},{1,15},{3,5}... | collective-permute-start | bytes 688136 | tf_op jit(solution)/shard_map/ppermute | solution.py:342
  19.1 1.8 %collective-permute-start.2 = (bf16[8,32,128]{2,1,0:T(8,128)(2,1)S(1)}, bf16[8,32,128]{2,1,0:T(8,128)(2,1)S(1)}, u32[]{:S(2)}, u32[]{:S(2)}) collective-permute-start(bf16[8,32,128]{2,1,0:T(8,128)(2,1)S(1)} %all_to_all.15.pieces_ref), channel_id=1, source_target_pairs={{0,1},{1,0},{2,3},{3,2},{4,5},{5,4},{6,7},{7,6},{8,9},{9,8},{10,11... | collective-permute-start | bytes 196616 | tf_op jit(solution)/shard_map/ppermute | solution.py:333
  22.0 9.1 %collective-permute-start.3 = (bf16[128,128]{1,0:T(8,128)(2,1)S(1)}, bf16[128,128]{1,0:T(8,128)(2,1)S(1)}, u32[]{:S(2)}, u32[]{:S(2)}) collective-permute-start(bf16[128,128]{1,0:T(8,128)(2,1)S(1)} %get-tuple-element.42), channel_id=1, source_target_pairs={{0,14},{2,4},{4,2},{6,8},{8,6},{10,12},{12,10},{14,0},{1,15},{3,5}... | collective-permute-start | bytes 98312 | tf_op jit(solution)/shard_map/ppermute | solution.py:342
  25.1 6.1 %collective-permute-start.5 = (bf16[128,128]{1,0:T(8,128)(2,1)S(1)}, bf16[128,128]{1,0:T(8,128)(2,1)S(1)}, u32[]{:S(2)}, u32[]{:S(2)}) collective-permute-start(bf16[128,128]{1,0:T(8,128)(2,1)S(1)} %get-tuple-element.44), channel_id=1, source_target_pairs={{0,2},{2,0},{4,6},{6,4},{8,10},{10,8},{12,14},{14,12},{1,3},{3,1},... | collective-permute-start | bytes 98312 | tf_op jit(solution)/shard_map/ppermute | solution.py:342
  25.1 5.5 %collective-permute-start.4 = (bf16[64,128]{1,0:T(8,128)(2,1)S(1)}, bf16[64,128]{1,0:T(8,128)(2,1)S(1)}, u32[]{:S(2)}, u32[]{:S(2)}) collective-permute-start(bf16[64,128]{1,0:T(8,128)(2,1)S(1)} %get-tuple-element.43.own_beyond_ref), channel_id=1, source_target_pairs={{0,12},{2,14},{4,8},{6,10},{8,4},{10,6},{12,0},{14,2},{1,13},{3,15... | collective-permute-start | bytes 49160 | tf_op jit(solution)/shard_map/ppermute | solution.py:342
  27.4 3.7 %collective-permute-start.6 = (bf16[64,128]{1,0:T(8,128)(2,1)S(1)}, bf16[64,128]{1,0:T(8,128)(2,1)S(1)}, u32[]{:S(2)}, u32[]{:S(2)}) collective-permute-start(bf16[64,128]{1,0:T(8,128)(2,1)S(1)} %get-tuple-element.45.own_far_ref), channel_id=1, source_target_pairs={{0,4},{2,6},{4,0},{6,2},{8,12},{10,14},{12,8},{14,10},{1,5},{3,7},... | collective-permute-start | bytes 49160 | tf_op jit(solution)/shard_map/ppermute | solution.py:342
  45.3 1.6 %collective-permute-start.7 = (bf16[8,144,128]{2,1,0:T(8,128)(2,1)S(1)}, bf16[8,144,128]{2,1,0:T(8,128)(2,1)S(1)}, u32[]{:S(2)}, u32[]{:S(2)}) collective-permute-start(bf16[8,144,128]{2,1,0:T(8,128)(2,1)S(1)} %all_to_all.16.second_ref), channel_id=1, source_target_pairs={{0,1},{1,0},{2,3},{3,2},{4,5},{5,4},{6,7},{7,6},{8,9},{9,8},{10,11... | collective-permute-start | bytes 884744 | tf_op jit(solution)/shard_map/ppermute | solution.py:333

commit v16 on v15

--- a/solution.py
+++ b/solution.py
@@ -210,7 +210,7 @@
     by_lon(1, far_ref, beyond_ref, send_far)
 
 
-def image_kernel(across_ref, beyond_ref, near_ref, far_ref, own_far_ref, own_beyond_ref, across_corr_ref, near_corr_ref,
+def image_kernel(near_ref, across_ref, beyond_ref, far_ref, own_far_ref, own_beyond_ref, across_corr_ref, near_corr_ref,
                  z_ref, scaled_ref, dense_ref, edge_ref, diag_ref, right_ref, vectors_ref,
                  image_ref, chunks_ref):
     samples, nodes = z_ref.shape
@@ -411,7 +411,7 @@
         image_kernel,
         [field, ((sectors, 2 * half + SUM_ROWS + samples, LANES), BF16)],
         [VMEM] * 15,
-        (across, got_beyond, near, got_far, far, beyond, across_static, near_static, z0, scaled, dense, edge, diag, right, basis),
+        (near, across, got_beyond, got_far, far, beyond, across_static, near_static, z0, scaled, dense, edge, diag, right, basis),
         apply_cost,
     )
     second = exchange(chunks, "lon")

time: 59.5 us -> 58.6 us (0.985)
  waiting for transfers between devices: 5.33 us -> 6.66 us
  starting transfers between devices: 11.9 us -> 10.6 us
  blocking collectives: 32.2 us -> 31.3 us
    ppermute x6, waiting for transfers between devices: 3.75 us -> 5.08 us  [swap(): return lax.ppermute(array, 'lon', pairs)]
    ppermute x6, starting transfers between devices: 11.9 us -> 10.6 us  [swap(): return lax.ppermute(array, 'lon', pairs)]
    all_to_all x3, blocking collectives: 32.2 us -> 31.3 us  [exchange(): return lax.all_to_all(chunks, axes, split_axis=0, concat_axis=0, tiled=True)]
  transfers between devices with their start and end apart: 8 -> 8, of which waited for: 3 -> 2; matrix products, arithmetic and copies ran while one was open for 0% -> 0% of each run, Pallas kernels for 3% -> 3%
where the time goes in v16:
time: 58.6 us; the launch traced here: 58.4 us
  blocking collectives  31.3 us (53%)
  starting transfers between devices  10.6 us (18%)
  Pallas kernels  8.41 us (14%)
  waiting for transfers between devices  6.66 us (11%)
  between operations  1.35 us (2%)
    all_to_all x3, blocking collectives, exchange(): return lax.all_to_all(chunks, axes, split_axis=0, concat_axis=0, tiled=True)  31.3 us
    ppermute x6, starting transfers between devices, swap(): return lax.ppermute(array, 'lon', pairs)  10.6 us
    pallas_call x6, Pallas kernels, call(): pl.pallas_call(kernel, out_shape=[jax.ShapeDtypeStruct(s, t) for s, t in...  8.41 us
    ppermute x6, waiting for transfers between devices, swap(): return lax.ppermute(array, 'lon', pairs)  5.08 us
    ppermute x2, waiting for transfers between devices, other_band(): return lax.ppermute(array, 'lat', [(0, 1), (1, 0)])  1.58 us
  transfers between devices with their start and end apart: 8, of which 2 were waited for; matrix products, arithmetic and copies ran while one was open for 0% of the time, Pallas kernels for 3%

profile of v16, /device:TPU:0, one launch (start us, length us, event | category | flops | bytes accessed | tf_op | source)
XLA Modules:
  0.0 58.4 jit_solution(5555076665964199479)
XLA Ops:
  1.3 1.7 %shard_map.127 = (bf16[8,32,128]{2,1,0:T(8,128)(2,1)S(1)}, f32[8,1024]{1,0:T(8,128)S(1)}, bf16[256,1024]{1,0:T(8,128)(2,1)S(1)}, bf16[896,128]{1,0:T(8,128)(2,1)...) custom-call(s32[1]{0:T(128)S(6)} %copy.15.node_count_ref, ...), custom_call_target="tpu_custom_call" | custom-call | flops 8388608 | bytes 1225928 | tf_op jit(solution)/shard_map/pallas_call | solution.py:24
  3.0 3.0 %collective-permute-start = (bf16[896,128]{1,0:T(8,128)(2,1)S(1)}, bf16[896,128]{1,0:T(8,128)(2,1)S(1)}, u32[]{:S(2)}, u32[]{:S(2)}) collective-permute-start(bf16[896,128]{1,0:T(8,128)(2,1)S(1)} %get-tuple-element.30), channel_id=1, source_target_pairs={{0,2},{2,0},{4,6},{6,4},{8,10},{10,8},{12,14},{14,12},{1,3},{3,1},... | collective-permute-start | bytes 688136 | tf_op jit(solution)/shard_map/ppermute | solution.py:342
  6.0 3.6 %collective-permute-start.1 = (bf16[896,128]{1,0:T(8,128)(2,1)S(1)}, bf16[896,128]{1,0:T(8,128)(2,1)S(1)}, u32[]{:S(2)}, u32[]{:S(2)}) collective-permute-start(bf16[896,128]{1,0:T(8,128)(2,1)S(1)} %get-tuple-element.31), channel_id=1, source_target_pairs={{0,14},{2,4},{4,2},{6,8},{8,6},{10,12},{12,10},{14,0},{1,15},{3,5}... | collective-permute-start | bytes 688136 | tf_op jit(solution)/shard_map/ppermute | solution.py:342
  9.6 9.5 %all_to_all.15.pieces_ref = bf16[8,32,128]{2,1,0:T(8,128)(2,1)S(1)} all-to-all(bf16[8,32,128]{2,1,0:T(8,128)(2,1)S(1)} %get-tuple-element.32), channel_id=1, replica_groups=mesh['grp'=2,'lon'=8,'lat'=2] {'lon'}, dimensions={0} | all-to-all | bytes 131072 | tf_op jit(solution)/shard_map/all_to_all | solution.py:329
  19.1 0.0 collective-permute-done.near_corr_ref.near_ref
  19.1 0.0 collective-permute-done.1.across_corr_ref.across_ref
  19.1 0.0 collective-permute-start.2
  19.1 1.7 %shard_map.128.dense_ref = bf16[1024,1024]{1,0:T(8,128)(2,1)S(1)} custom-call(s32[2,24]{1,0:T(2,128)S(1)} %get-tuple-element.38.pattern_vmem, bf16[24,128,128]{2,1,0:T(8,128)(2,1)S(1)} %get-tuple-element.39.blocks_ref), custom_call_target="tpu_custom_call" | custom-call | flops 134217728 | bytes 786624 | tf_op jit(solution)/shard_map/pallas_call | solution.py:24
  20.8 0.0 collective-permute-done.2.others_ref
  20.8 1.2 %shard_map.129 = (f32[64,1024]{1,0:T(8,128)S(1)}, f32[64,1024]{1,0:T(8,128)S(1)}, bf16[128,128]{1,0:T(8,128)(2,1)S(1)}, bf16[128,128]{1,0:T(8,128)(2,1)S(1)}, bf...) custom-call(bf16[8,32,128]{2,1,0:T(8,128)(2,1)S(1)} %all_to_all.15.pieces_ref, ...), custom_call_target="tpu_custom_call" | custom-call | flops 134217728 | bytes 3178496 | tf_op jit(solution)/shard_map/pallas_call | solution.py:24
  22.0 0.5 collective-permute-start.3
  22.5 3.1 %collective-permute-start.4 = (bf16[128,128]{1,0:T(8,128)(2,1)S(1)}, bf16[128,128]{1,0:T(8,128)(2,1)S(1)}, u32[]{:S(2)}, u32[]{:S(2)}) collective-permute-start(bf16[128,128]{1,0:T(8,128)(2,1)S(1)} %get-tuple-element.43), channel_id=1, source_target_pairs={{0,14},{2,4},{4,2},{6,8},{8,6},{10,12},{12,10},{14,0},{1,15},{3,5}... | collective-permute-start | bytes 98312 | tf_op jit(solution)/shard_map/ppermute | solution.py:342
  25.6 0.5 collective-permute-start.5
  26.0 0.0 collective-permute-start.6
  26.0 5.1 %collective-permute-done.5.beyond_ref = bf16[64,128]{1,0:T(8,128)(2,1)S(1)} collective-permute-done((bf16[64,128]{1,0:T(8,128)(2,1)S(1)}, bf16[64,128]{1,0:T(8,128)(2,1)S(1)}, u32[]{:S(2)}, u32[]{:S(2)}) %collective-permute-start.5) | collective-permute-done | bytes 16416 | tf_op jit(solution)/shard_map/ppermute | solution.py:342
  31.1 0.0 collective-permute-done.6.far_ref
  31.1 0.0 collective-permute-done.3.near_ref
  31.1 0.0 collective-permute-done.4.across_ref
  31.1 1.1 %shard_map.130 = (f32[64,1024]{1,0:T(8,128)S(1)}, bf16[8,144,128]{2,1,0:T(8,128)(2,1)S(1)}) custom-call(bf16[128,128]{1,0:T(8,128)(2,1)S(1)} %collective-permute-done.3.near_ref, bf16[128,128]{1,0:T(8,128)(2,1)S(1)} %collective-permute-done.4.across_ref, bf16[64,128]{1,0:T(8,128)(2,1)S(1)} %collective-permute-done.5.beyond_ref, ...), custom_call_target="tpu_custom_call" | custom-call | flops 134217728 | bytes 4030464 | tf_op jit(solution)/shard_map/pallas_call | solution.py:24
  32.2 12.2 %all_to_all.16.second_ref = bf16[8,144,128]{2,1,0:T(8,128)(2,1)S(1)} all-to-all(bf16[8,144,128]{2,1,0:T(8,128)(2,1)S(1)} %get-tuple-element.50), channel_id=1, replica_groups=mesh['grp'=2,'lon'=8,'lat'=2] {'lon'}, dimensions={0} | all-to-all | bytes 589824 | tf_op jit(solution)/shard_map/all_to_all | solution.py:329
  44.4 0.0 collective-permute-start.7
  44.4 1.6 %collective-permute-done.7.second_others_ref = bf16[8,144,128]{2,1,0:T(8,128)(2,1)S(1)} collective-permute-done((bf16[8,144,128]{2,1,0:T(8,128)(2,1)S(1)}, bf16[8,144,128]{2,1,0:T(8,128)(2,1)S(1)}, u32[]{:S(2)}, u32[]{:S(2)}) %collective-permute-start.7) | collective-permute-done | bytes 294944 | tf_op jit(solution)/shard_map/ppermute | solution.py:333
  46.0 1.5 %shard_map.131 = (f32[64,1024]{1,0:T(8,128)S(1)}, f32[8,128]{1,0:T(8,128)S(1)}, f32[16,8,128]{2,1,0:T(8,128)S(1)}) custom-call(bf16[8,32,128]{2,1,0:T(8,128)(2,1)S(1)} %all_to_all.15.pieces_ref, bf16[8,32,128]{2,1,0:T(8,128)(2,1)S(1)} %collective-permute-done.2.others_ref, bf16[8,144,128]{2,1,0:T(8,128)(2,1)S(1)} %all_to_all.16.second_ref, ...), custom_call_target="tpu_custom_call" | custom-call | flops 134217728 | bytes 4489216 | tf_op jit(solution)/shard_map/pallas_call | solution.py:24
  47.5 9.7 %all_to_all.17.chunks_ref = f32[16,8,128]{2,1,0:T(8,128)S(1)} all-to-all(f32[16,8,128]{2,1,0:T(8,128)S(1)} %get-tuple-element.53), channel_id=1, replica_groups=mesh['grp'=2,'lon'=8,'lat'=2] {'lon','lat'}, dimensions={0} | all-to-all | bytes 131072 | tf_op jit(solution)/shard_map/all_to_all | solution.py:329
  57.2 1.2 %shard_map.132 = f32[64,1024]{1,0:T(8,128)} custom-call(f32[8,128]{1,0:T(8,128)S(1)} %get-tuple-element.52.sums_ref, f32[16,8,128]{2,1,0:T(8,128)S(1)} %all_to_all.17.chunks_ref, f32[64,1024]{1,0:T(8,128)S(1)} %get-tuple-element.48.z_ref.first_ref, f32[64,1024]{1,0:T(8,128)S(1)} %get-tuple-element.54.second_ref), custom_call_target="tpu_custom_call" | custom-call | flops 262144 | bytes 593920 | tf_op jit(solution)/shard_map/pallas_call | solution.py:24
Async XLA Ops:
  3.0 16.0 %collective-permute-start = (bf16[896,128]{1,0:T(8,128)(2,1)S(1)}, bf16[896,128]{1,0:T(8,128)(2,1)S(1)}, u32[]{:S(2)}, u32[]{:S(2)}) collective-permute-start(bf16[896,128]{1,0:T(8,128)(2,1)S(1)} %get-tuple-element.30), channel_id=1, source_target_pairs={{0,2},{2,0},{4,6},{6,4},{8,10},{10,8},{12,14},{14,12},{1,3},{3,1},... | collective-permute-start | bytes 688136 | tf_op jit(solution)/shard_map/ppermute | solution.py:342
  6.0 13.0 %collective-permute-start.1 = (bf16[896,128]{1,0:T(8,128)(2,1)S(1)}, bf16[896,128]{1,0:T(8,128)(2,1)S(1)}, u32[]{:S(2)}, u32[]{:S(2)}) collective-permute-start(bf16[896,128]{1,0:T(8,128)(2,1)S(1)} %get-tuple-element.31), channel_id=1, source_target_pairs={{0,14},{2,4},{4,2},{6,8},{8,6},{10,12},{12,10},{14,0},{1,15},{3,5}... | collective-permute-start | bytes 688136 | tf_op jit(solution)/shard_map/ppermute | solution.py:342
  19.1 1.7 %collective-permute-start.2 = (bf16[8,32,128]{2,1,0:T(8,128)(2,1)S(1)}, bf16[8,32,128]{2,1,0:T(8,128)(2,1)S(1)}, u32[]{:S(2)}, u32[]{:S(2)}) collective-permute-start(bf16[8,32,128]{2,1,0:T(8,128)(2,1)S(1)} %all_to_all.15.pieces_ref), channel_id=1, source_target_pairs={{0,1},{1,0},{2,3},{3,2},{4,5},{5,4},{6,7},{7,6},{8,9},{9,8},{10,11... | collective-permute-start | bytes 196616 | tf_op jit(solution)/shard_map/ppermute | solution.py:333
  22.0 9.1 %collective-permute-start.3 = (bf16[128,128]{1,0:T(8,128)(2,1)S(1)}, bf16[128,128]{1,0:T(8,128)(2,1)S(1)}, u32[]{:S(2)}, u32[]{:S(2)}) collective-permute-start(bf16[128,128]{1,0:T(8,128)(2,1)S(1)} %get-tuple-element.42), channel_id=1, source_target_pairs={{0,2},{2,0},{4,6},{6,4},{8,10},{10,8},{12,14},{14,12},{1,3},{3,1},... | collective-permute-start | bytes 98312 | tf_op jit(solution)/shard_map/ppermute | solution.py:342
  22.5 8.7 %collective-permute-start.4 = (bf16[128,128]{1,0:T(8,128)(2,1)S(1)}, bf16[128,128]{1,0:T(8,128)(2,1)S(1)}, u32[]{:S(2)}, u32[]{:S(2)}) collective-permute-start(bf16[128,128]{1,0:T(8,128)(2,1)S(1)} %get-tuple-element.43), channel_id=1, source_target_pairs={{0,14},{2,4},{4,2},{6,8},{8,6},{10,12},{12,10},{14,0},{1,15},{3,5}... | collective-permute-start | bytes 98312 | tf_op jit(solution)/shard_map/ppermute | solution.py:342
  25.6 5.5 %collective-permute-start.5 = (bf16[64,128]{1,0:T(8,128)(2,1)S(1)}, bf16[64,128]{1,0:T(8,128)(2,1)S(1)}, u32[]{:S(2)}, u32[]{:S(2)}) collective-permute-start(bf16[64,128]{1,0:T(8,128)(2,1)S(1)} %get-tuple-element.44.own_beyond_ref), channel_id=1, source_target_pairs={{0,12},{2,14},{4,8},{6,10},{8,4},{10,6},{12,0},{14,2},{1,13},{3,15... | collective-permute-start | bytes 49160 | tf_op jit(solution)/shard_map/ppermute | solution.py:342
  26.0 5.1 %collective-permute-start.6 = (bf16[64,128]{1,0:T(8,128)(2,1)S(1)}, bf16[64,128]{1,0:T(8,128)(2,1)S(1)}, u32[]{:S(2)}, u32[]{:S(2)}) collective-permute-start(bf16[64,128]{1,0:T(8,128)(2,1)S(1)} %get-tuple-element.45.own_far_ref), channel_id=1, source_target_pairs={{0,4},{2,6},{4,0},{6,2},{8,12},{10,14},{12,8},{14,10},{1,5},{3,7},... | collective-permute-start | bytes 49160 | tf_op jit(solution)/shard_map/ppermute | solution.py:342
  44.4 1.6 %collective-permute-start.7 = (bf16[8,144,128]{2,1,0:T(8,128)(2,1)S(1)}, bf16[8,144,128]{2,1,0:T(8,128)(2,1)S(1)}, u32[]{:S(2)}, u32[]{:S(2)}) collective-permute-start(bf16[8,144,128]{2,1,0:T(8,128)(2,1)S(1)} %all_to_all.16.second_ref), channel_id=1, source_target_pairs={{0,1},{1,0},{2,3},{3,2},{4,5},{5,4},{6,7},{7,6},{8,9},{9,8},{10,11... | collective-permute-start | bytes 884744 | tf_op jit(solution)/shard_map/ppermute | solution.py:333
